TPU v7x, 512 devices: a whole 4x8x8 slice. The times are simulated.
512 devices in a mesh: pp: 4 (over x), ep: 32 (over y_hi, z), tp: 4 (over y_lo, core).
Axes of the slice: x: 4, y: 8 (y_hi: 4, y_lo: 2; y = y_hi * 2 + y_lo), z: 8, core: 2. Of those that a mesh axis runs over, the one named last changes fastest.
Arguments:
- trunk_in: bfloat16 [4, 4096, 2048], P('pp', 'ep'), may hold values from -6 to 6
- expert_ids: int32 [4, 4096, 8], P('pp', 'ep'), may hold values from 0 to 31, all different within a row; in each aligned block of 128 rows (0 to 127, 128 to 255, ..., all dimensions but the last counted through in order) at most 40 rows name the same one
- gate_scores: float32 [4, 4096, 8], P('pp', 'ep'), may hold values from 0.05 to 1
- trunk_gain: float32 [4, 2048], P('pp'), may hold values from 0.1 to 1.9
- w_gate: bfloat16 [4, 32, 2048, 768], P('pp', 'ep', None, 'tp'), may hold values from -0.125 to 0.125
- w_up: bfloat16 [4, 32, 2048, 768], P('pp', 'ep', None, 'tp'), may hold values from -0.125 to 0.125
- w_down: bfloat16 [4, 32, 768, 2048], P('pp', 'ep', 'tp'), may hold values from -0.21875 to 0.21875
- image_in: bfloat16 [4, 128, 3200], P('pp', ('ep', 'tp')), may hold values from -6 to 6
- image_gain: float32 [4, 3200], P('pp'), may hold values from 0.1 to 1.9
- fc_in: bfloat16 [4, 3200, 12800], P('pp', None, ('ep', 'tp')), may hold values from -0.109375 to 0.109375
- fc_out: bfloat16 [4, 12800, 3200], P('pp', ('ep', 'tp')), may hold values from -0.0546875 to 0.0546875
- layer_scale: float32 [4, 3200], P('pp'), may hold values from 0.5 to 1.5
Outputs:
- trunk_out: bfloat16 [4, 4096, 2048], P('pp', 'ep')
- image_out: bfloat16 [4, 128, 3200], P('pp', ('ep', 'tp'))
Inputs may be any that keep to these rules, and one draw needn't show every extreme that they name: `expert_ids`: within each aligned block of 128 rows of one section (the rows of one device), no expert is named by more than 40 rows, a bound that some block reaches.
All inputs are finite; a program needn't handle non-finite values.
Results may differ from a plain program's by a relative error of at most 0.008.
Values may be sent and summed in bfloat16 or wider, within the bound.
No kernel may reach another device: no remote copies, remote signals or barrier semaphores. Data moves between devices by JAX's collectives and lax.ppermute only.
A program may use at most 64 MiB of HBM per device.

v0:
```python
import jax
import jax.numpy as jnp
from jax import lax
from jax.sharding import PartitionSpec as P


def passed_along(value, axis, steps):
    count = lax.axis_size(axis)
    pairs = [(source, (source + steps) % count) for source in range(count)]
    return lax.ppermute(value, axis, pairs)


def rms_scale(values, gain):
    wide = values.astype(jnp.float32)
    return wide * lax.rsqrt(jnp.mean(wide * wide, axis=-1, keepdims=True) + 1e-06) * gain


def place(dest, n_exp, cap):
    onehot = (dest[:, None] == jnp.arange(n_exp, dtype=jnp.int32)[None, :]).astype(jnp.int32)
    rank = jnp.sum((jnp.cumsum(onehot, axis=0) - onehot) * onehot, axis=1)
    return dest * cap + rank


def owners(slot, count, rows, topk):
    entry_token = jnp.arange(slot.shape[0], dtype=jnp.int32) // topk
    return jnp.full((count,), rows, jnp.int32).at[slot].set(entry_token)


def expert_partial(rows, gate_w, up_w, down_w):
    flat = rows.reshape(-1, rows.shape[-1])
    gate = jnp.dot(flat, gate_w, preferred_element_type=jnp.float32)
    upval = jnp.dot(flat, up_w, preferred_element_type=jnp.float32)
    hidden = (jax.nn.silu(gate) * upval).astype(jnp.bfloat16)
    made = jnp.dot(hidden, down_w, preferred_element_type=jnp.float32).astype(jnp.bfloat16)
    return made.reshape(rows.shape)


def body(
    trunk_in,
    expert_ids,
    gate_scores,
    trunk_gain,
    w_gate,
    w_up,
    w_down,
    image_in,
    image_gain,
    fc_in,
    fc_out,
    layer_scale,
):
    n_expert = lax.axis_size("ep")
    n_split = lax.axis_size("tp")
    tok_rows = trunk_in.shape[1]
    width = trunk_in.shape[2]
    topk = expert_ids.shape[2]
    capacity = min(tok_rows, n_split * (tok_rows * topk * 9 // (8 * n_expert * n_split) + 1))
    tokens = trunk_in[0]
    normed = rms_scale(tokens, trunk_gain[0]).astype(jnp.bfloat16)
    slot = place(expert_ids[0].reshape(-1), n_expert, capacity)
    table = owners(slot, n_expert * capacity, tok_rows, topk)
    padded = jnp.concatenate([normed, jnp.zeros((1, width), jnp.bfloat16)], axis=0)
    slots = padded[table].reshape(n_expert, capacity, width)
    gate_w = w_gate[0, 0]
    up_w = w_up[0, 0]
    down_w = w_down[0, 0]
    scores = gate_scores[0]
    weights = scores / jnp.sum(scores, axis=-1, keepdims=True)
    returned = lax.all_to_all(
        expert_partial(
            lax.all_to_all(slots, "ep", split_axis=0, concat_axis=0, tiled=True),
            gate_w,
            up_w,
            down_w,
        ),
        "ep",
        split_axis=0,
        concat_axis=0,
        tiled=True,
    )
    picked = returned.reshape(-1, width)[slot].reshape(tok_rows, topk, width)
    weighted = jnp.sum(picked.astype(jnp.float32) * weights[:, :, None], axis=1)
    total = lax.psum(weighted.astype(jnp.bfloat16), "tp").astype(jnp.float32)
    layer = (tokens.astype(jnp.float32) + total).astype(jnp.bfloat16)
    trunk_out = passed_along(layer[None], "pp", 1)
    image = image_in[0]
    image_normed = rms_scale(image, image_gain[0]).astype(jnp.bfloat16)
    all_rows = lax.all_gather(image_normed, ("ep", "tp"), axis=0, tiled=True)
    first = fc_in[0]
    second = fc_out[0]
    hidden = jax.nn.gelu(
        jnp.dot(all_rows, first, preferred_element_type=jnp.float32), approximate=False
    ).astype(jnp.bfloat16)
    summed = lax.psum_scatter(
        jnp.dot(hidden, second, preferred_element_type=jnp.float32),
        ("ep", "tp"),
        scatter_dimension=0,
        tiled=True,
    )
    encoded = (image.astype(jnp.float32) + layer_scale[0] * summed).astype(jnp.bfloat16)
    image_out = passed_along(encoded[None], "pp", -1)
    return (trunk_out, image_out)


def solution(mesh):
    return jax.shard_map(
        body,
        mesh=mesh,
        in_specs=(
            P("pp", "ep", None),
            P("pp", "ep", None),
            P("pp", "ep", None),
            P("pp", None),
            P("pp", "ep", None, "tp"),
            P("pp", "ep", None, "tp"),
            P("pp", "ep", "tp", None),
            P("pp", ("ep", "tp"), None),
            P("pp", None),
            P("pp", None, ("ep", "tp")),
            P("pp", ("ep", "tp"), None),
            P("pp", None),
        ),
        out_specs=(P("pp", "ep", None), P("pp", ("ep", "tp"), None)),
        check_vma=False,
    )
```

profile of v0, /device:TPU:1, one launch (start us, length us, event | category | flops | bytes accessed | tf_op | source)
XLA Modules:
  0.0 726.6 jit_solution(5370912785028602910)
XLA Ops:
  7.2 0.0 copy-start
  7.2 0.9 copy.22
  8.0 0.1 eq.29
  8.1 0.1 eq.25
  8.2 0.7 broadcast_multiply_fusion
  8.9 9.0 %reduce-window.6 = s32[32,8,128]{2,1,0:T(8,128)S(1)} reduce-window(s32[32,8,128]{2,1,0:T(8,128)S(1)} %fusion.27, s32[]{:T(128)} %constant.20.clone.1), window={size=1x1x128 pad=0_0x0_0x127_0}, to_apply=%region_1.0 | reduce-window | flops 4161536 | bytes 262148 | tf_op jit(solution)/shard_map/reduce-window
  18.0 0.1 slice.12
  18.0 0.1 copy.24
  18.2 0.1 copy.25
  18.3 0.1 broadcast_add_fusion
  18.4 0.1 copy.21
  18.5 0.1 mul.111
  18.7 4.3 scatter_custom_fusion
  23.0 1.2 fusion.2
  24.3 1.2 fusion.4
  25.5 6.1 gather_fusion
  31.7 0.0 copy-start.7
  31.7 145.0 %all_to_all.10 = bf16[32,40,2048]{2,1,0:T(8,128)(2,1)S(1)} all-to-all(bf16[32,40,2048]{2,1,0:T(8,128)(2,1)} %bitcast.78), channel_id=1, replica_groups=mesh['pp'=4,'ep'=32,'tp'=4] {'ep'}, dimensions={0} | all-to-all | bytes 10485760 | tf_op jit(solution)/shard_map/all_to_all | solution.py:71
  176.6 0.0 copy-start.1
  176.6 0.0 copy-start.8
  176.6 2.3 copy-done.1
  178.9 0.0 copy-done.7
  178.9 1.9 fusion.17
  180.8 0.0 copy-done
  180.8 0.0 copy-done.8
  180.8 8.5 %convolution_convert_fusion = bf16[1280,2048]{1,0:T(8,128)(2,1)} fusion(bf16[1280,2048]{1,0:T(8,128)(2,1)} %bitcast.81, f32[1280,192]{0,1:T(8,128)S(1)} %fusion.17, bf16[1,1,192,2048]{3,2,1,0:T(8,128)(2,1)S(1)} %copy-done, bf16[1,1,2048,192]{2,3,1,0:T(8,128)(2,1)S(1)} %copy-done.8), kind=kOutput, calls=%fused_computation.5 | convolution fusion | flops 2017361920 | bytes 13041664 | tf_op jit(solution)/shard_map/dot_general | solution.py:34
  189.3 0.0 copy-start.4
  189.3 0.0 copy-start.3
  189.3 0.0 copy-start.5
  189.3 8.2 %all-to-all-start.1 = ((bf16[32,40,2048]{2,1,0:T(8,128)(2,1)}), bf16[32,40,2048]{2,1,0:T(8,128)(2,1)}, u32[]{:S(2)}, u32[]{:S(2)}) async-start(bf16[32,40,2048]{2,1,0:T(8,128)(2,1)} %bitcast.79), calls=%async_computation.1 | async-start | bytes 10485760 | tf_op jit(solution)/shard_map/all_to_all | solution.py:69
  197.5 0.2 all-reduce.5.cloned.1.call-start
  197.7 0.0 copy-done.4
  197.8 0.1 copy.26
  197.9 0.0 copy-done.3
  197.9 0.6 fusion.77
  199.2 0.0 copy-done.5
  199.3 144.9 %all-to-all-done.1 = bf16[32,40,2048]{2,1,0:T(8,128)(2,1)} async-done(((bf16[32,40,2048]{2,1,0:T(8,128)(2,1)}), bf16[32,40,2048]{2,1,0:T(8,128)(2,1)}, u32[]{:S(2)}, u32[]{:S(2)}) %all-to-all-start.1) | async-done | bytes 5242912 | tf_op jit(solution)/shard_map/all_to_all | solution.py:69
  344.1 12.0 %gather_fusion.1 = bf16[1024,2048]{1,0:T(8,128)(2,1)} fusion(bf16[1280,2048]{1,0:T(8,128)(2,1)} %bitcast.13, s32[1024]{0:T(1024)S(1)} %broadcast_clamp_fusion), kind=kCustom, calls=%fused_computation.1 | custom fusion | bytes 8392704 | tf_op jit(solution)/shard_map/gather | solution.py:81
  356.2 0.0 copy-start.2
  356.2 7.4 %fusion = bf16[128,2048]{1,0:T(8,128)(2,1)} fusion(bf16[1024,2048]{1,0:T(8,128)(2,1)} %gather_fusion.1, f32[128,8]{1,0:T(8,128)S(1)} %copy.26), kind=kLoop, calls=%fused_computation.4 | loop fusion | flops 6029312 | bytes 4722688 | tf_op jit(solution)/shard_map/reduce_sum | solution.py:82
  363.6 0.0 copy-start.6
  363.6 0.0 all-reduce.5.cloned.1.call-update
  363.6 0.0 all-reduce.7.cloned.1.call-start
  363.6 143.9 %all-gather = bf16[128,1,3200]{2,1,0:T(2,128)(2,1)S(1)} all-gather(bf16[1,1,3200]{2,1,0:T(2,128)(2,1)S(1)} %fusion.80), channel_id=1, replica_groups=mesh['pp'=4,'ep'=32,'tp'=4] {'ep','tp'}, dimensions={0}, use_global_device_ids=true | all-gather | bytes 825600 | tf_op jit(solution)/shard_map/all_gather | solution.py:88
  507.6 3.7 fusion.19
  511.3 0.0 all-reduce.7.cloned.1.call-update
  511.3 1.3 dynamic-slice
  512.6 0.0 all-reduce.5.cloned.1.call-done
  512.6 0.0 copy-done.2
  512.6 1.2 fusion.22
  513.8 2.6 collective-permute-start
  516.4 195.3 %all-reduce.7.cloned.1.call-done = f32[128,3200]{1,0:T(8,128)} async-done(((f32[128,3200]{1,0:T(8,128)}), f32[128,3200]{1,0:T(8,128)}) %all-reduce.7.cloned.1.call-update) | async-done | bytes 1638416
  711.7 0.0 copy-done.6
  711.7 1.6 convert_bitcast_fusion
  713.3 4.3 collective-permute-start.1
  717.6 0.8 collective-permute-done.1
  718.4 0.0 collective-permute-done
  718.4 0.8 copy.42
  719.2 0.6 copy.43
  (14 shorter events, 0.2 us)
Async XLA Ops:
  7.2 173.7 %copy-start = (bf16[1,1,192,2048]{3,2,1,0:T(8,128)(2,1)S(1)}, bf16[1,1,192,2048]{3,2,1,0:T(8,128)(2,1)}, u32[]{:S(2)}) copy-start(bf16[1,1,192,2048]{3,2,1,0:T(8,128)(2,1)} %param.18) | copy-start | bytes 2359300
  31.7 147.3 %copy-start.7 = (bf16[1,1,2048,192]{2,3,1,0:T(8,128)(2,1)S(1)}, bf16[1,1,2048,192]{2,3,1,0:T(8,128)(2,1)}, u32[]{:S(2)}) copy-start(bf16[1,1,2048,192]{2,3,1,0:T(8,128)(2,1)} %param.16) | copy-start | bytes 2359300
  176.6 2.3 copy-start.1
  176.6 4.2 copy-start.8
  189.3 8.4 %copy-start.4 = (f32[1,128,8]{1,2,0:T(8,128)S(1)}, f32[1,128,8]{1,2,0:T(8,128)}, u32[]{:S(2)}) copy-start(f32[1,128,8]{1,2,0:T(8,128)} %param.14) | copy-start | bytes 12292
  189.3 8.5 %copy-start.3 = (bf16[1,1,3200]{2,1,0:T(2,128)(2,1)S(1)}, bf16[1,1,3200]{2,1,0:T(2,128)(2,1)}, u32[]{:S(2)}) copy-start(bf16[1,1,3200]{2,1,0:T(2,128)(2,1)} %param.19) | copy-start | bytes 19204
  189.3 9.9 %copy-start.5 = (f32[1,3200]{1,0:T(1,128)S(1)}, f32[1,3200]{1,0:T(1,128)}, u32[]{:S(2)}) copy-start(f32[1,3200]{1,0:T(1,128)} %param.20) | copy-start | bytes 38404
  189.3 154.8 %all-to-all-start.1 = ((bf16[32,40,2048]{2,1,0:T(8,128)(2,1)}), bf16[32,40,2048]{2,1,0:T(8,128)(2,1)}, u32[]{:S(2)}, u32[]{:S(2)}) async-start(bf16[32,40,2048]{2,1,0:T(8,128)(2,1)} %bitcast.79), calls=%async_computation.1 | async-start | bytes 10485760 | tf_op jit(solution)/shard_map/all_to_all | solution.py:69
  197.5 315.1 %all-reduce.5.cloned.1.call-start = ((), (), s32[]{:S(2)}) async-start(), calls=%async_computation.2 | async-start | bytes 1048576 | tf_op jit(solution)/shard_map/psum | solution.py:83
  356.2 156.4 %copy-start.2 = (bf16[1,128,2048]{2,1,0:T(8,128)(2,1)S(1)}, bf16[1,128,2048]{2,1,0:T(8,128)(2,1)}, u32[]{:S(2)}) copy-start(bf16[1,128,2048]{2,1,0:T(8,128)(2,1)} %param.12) | copy-start | bytes 1572868
  363.6 348.1 %copy-start.6 = (f32[1,3200]{1,0:T(1,128)S(1)}, f32[1,3200]{1,0:T(1,128)}, u32[]{:S(2)}) copy-start(f32[1,3200]{1,0:T(1,128)} %param.23) | copy-start | bytes 38404
  363.6 348.1 %all-reduce.7.cloned.1.call-start = ((), (), s32[]{:S(2)}) async-start(), calls=%async_computation.3 | async-start | bytes 3276800
  513.8 204.6 %collective-permute-start = (bf16[1,128,2048]{2,1,0:T(8,128)(2,1)S(1)}, bf16[1,128,2048]{2,1,0:T(8,128)(2,1)S(1)}, u32[]{:S(2)}, u32[]{:S(2)}) collective-permute-start(bf16[1,128,2048]{2,1,0:T(8,128)(2,1)S(1)} %fusion.22), channel_id=1, source_target_pairs={{0,128},{128,256},{256,384},{384,0},{1,129},{129,257},{257,385},{3... | collective-permute-start | bytes 1572872 | tf_op jit(solution)/shard_map/ppermute | solution.py:10
  713.3 5.1 collective-permute-start.1
Sparse Core Ops, SparseCore 0:
  363.7 62.0 all-reduce.4
  511.5 200.1 all-reduce.6
where the time goes:
time: 729 us; the launch traced here: 727 us
  waiting for transfers between devices  341 us (47%)
  blocking collectives  289 us (40%)
  local copies, waits for them, and re-layouts  29.2 us (4%)
  other arithmetic  23.2 us (3%)
  starting transfers between devices  15.4 us (2%)
  between operations  14.9 us (2%)
  matrix products  14.1 us (2%)
    unnamed x3, waiting for transfers between devices  195 us
    all_to_all x1, blocking collectives, body(): lax.all_to_all(slots, 'ep', split_axis=0, concat_axis=0, tiled=True)  145 us
    all_to_all x1, waiting for transfers between devices, body(): lax.all_to_all(expert_partial(lax.all_to_all(slots, 'ep', split_axis=0, c...  145 us
    all_gather x1, blocking collectives, body(): all_rows = lax.all_gather(image_normed, ('ep', 'tp'), axis=0, tiled=True)  144 us
  transfers between devices with their start and end apart: 5, of which 3 were waited for; matrix products, arithmetic and copies ran while one was open for 1% of the time, Pallas kernels for 0%

commit v1 on v0

v1 whole, which is shorter than its diff:
```python
import jax
import jax.numpy as jnp
import numpy as np
from jax import lax
from jax.experimental import pallas as pl
from jax.experimental.pallas import tpu as pltpu
from jax.sharding import Mesh, PartitionSpec as P

BF16 = jnp.bfloat16
F32 = jnp.float32
VM = pl.BlockSpec(memory_space=pltpu.VMEM)
SM = pl.BlockSpec(memory_space=pltpu.SMEM)
CAP = 40
LIMIT = 48 * 1024 * 1024


def call(kernel, outs, scalars=0, flops=0, moved=0):
    def run(*operands):
        specs = [SM] * scalars + [VM] * (len(operands) - scalars)
        return pl.pallas_call(
            kernel,
            out_shape=outs,
            in_specs=specs,
            out_specs=jax.tree.map(lambda _: VM, outs),
            compiler_params=pltpu.CompilerParams(vmem_limit_bytes=LIMIT),
            cost_estimate=pl.CostEstimate(flops=flops, bytes_accessed=moved, transcendentals=0),
        )(*operands)

    return run


def shaped(dims, kind=BF16):
    return jax.ShapeDtypeStruct(dims, kind)


def nt(a, b):
    return lax.dot_general(a, b, (((1,), (1,)), ((), ())), preferred_element_type=F32)


def table_kernel(where, meta, pick, high, low):
    rows, toks = pick.shape
    group = rows // CAP
    topk = meta.shape[0] // 2
    first = where[0] * group
    wanted = (lax.broadcasted_iota(jnp.int32, (group, toks), 0) + first).astype(F32)
    scores = meta[topk:, :]
    total = jnp.sum(scores, axis=0, keepdims=True)
    member = jnp.zeros((group, toks), F32)
    weight = jnp.zeros((group, toks), F32)
    for k in range(topk):
        same = meta[k : k + 1, :] == wanted
        member = jnp.where(same, 1.0, member)
        weight = jnp.where(same, meta[topk + k : topk + k + 1, :] / total, weight)
    earlier = lax.broadcasted_iota(jnp.int32, (toks, toks), 0) < lax.broadcasted_iota(jnp.int32, (toks, toks), 1)
    rank = jnp.dot(member.astype(BF16), earlier.astype(F32).astype(BF16), preferred_element_type=F32)
    rank = jnp.where(member > 0.5, rank, -1.0)
    slots = lax.broadcasted_iota(jnp.int32, (group, CAP, toks), 1).astype(F32)
    hit = jnp.where(rank[:, None, :] == slots, 1.0, 0.0)
    pick[...] = hit.reshape(rows, toks).astype(BF16)
    scaled = (hit * weight[:, None, :]).reshape(rows, toks).T
    top = scaled.astype(BF16)
    high[...] = top
    low[...] = (scaled - top.astype(F32)).astype(BF16)


def pack_kernel(pick, toks, gain, rows):
    wide = toks[...].astype(F32)
    scale = lax.rsqrt(jnp.mean(wide * wide, axis=-1, keepdims=True) + 1e-06)
    normed = (wide * scale * gain[...]).astype(BF16)
    rows[...] = jnp.dot(pick[...], normed, preferred_element_type=F32).astype(BF16)


def expert_kernel(*refs):
    rows, out = refs[0], refs[-1]
    flat = rows[...]
    total = None
    for s in range(4):
        gate_w, up_w, down_w = refs[1 + 3 * s : 4 + 3 * s]
        gate = nt(flat, gate_w[...])
        upval = nt(flat, up_w[...])
        hidden = (gate * jax.nn.sigmoid(gate) * upval).astype(BF16)
        made = jnp.dot(hidden, down_w[...], preferred_element_type=F32)
        total = made if total is None else total + made
    out[...] = total.astype(BF16)


def combine_kernel(where, high, low, made, *pieces):
    n = len(pieces)
    cols = made.shape[1] // n
    for k in range(n):
        q = lax.rem(where[0] + k, n)
        part = made[:, pl.ds(pl.multiple_of(q * cols, cols), cols)]
        summed = jnp.dot(high[...], part, preferred_element_type=F32)
        summed += jnp.dot(low[...], part, preferred_element_type=F32)
        pieces[k][...] = summed.astype(BF16)


def layer_kernel(where, toks, *refs):
    pieces, out = refs[:-1], refs[-1]
    cols = out.shape[1]
    total = toks[:, pl.ds(pl.multiple_of(where[1] * cols, cols), cols)].astype(F32)
    for piece in pieces:
        total += piece[...].astype(F32)
    out[...] = total.astype(BF16)


def join_kernel(where, own, across, other, other_across, out):
    cols = own.shape[1]
    t = where[1]
    yl, core = t // 2, lax.rem(t, 2)
    for ref, quarter in (
        (own, t),
        (across, (1 - yl) * 2 + core),
        (other, yl * 2 + 1 - core),
        (other_across, (1 - yl) * 2 + 1 - core),
    ):
        out[:, pl.ds(pl.multiple_of(quarter * cols, cols), cols)] = ref[...]


def rms_scale(values, gain):
    wide = values.astype(F32)
    return wide * lax.rsqrt(jnp.mean(wide * wide, axis=-1, keepdims=True) + 1e-06) * gain


def body(
    trunk_in,
    expert_ids,
    gate_scores,
    trunk_gain,
    w_gate,
    w_up,
    w_down,
    image_in,
    image_gain,
    fc_in,
    fc_out,
    layer_scale,
):
    n_pp, n_yh, n_z = (lax.axis_size(a) for a in ("pp", "yh", "z"))
    n_tp = 4
    square = ("yh", "yl", "core")
    where = jnp.stack([lax.axis_index("yh"), lax.axis_index(("yl", "core"))]).astype(jnp.int32)

    def swapped(value):
        return lax.ppermute(value, square, [(a * n_tp + b, b * n_tp + a) for a in range(n_yh) for b in range(n_tp)])

    def flipped(value, axis):
        return lax.ppermute(value, axis, [(0, 1), (1, 0)])

    tokens = trunk_in[0]
    width = tokens.shape[1]
    toks = tokens.shape[0]
    meta = jnp.concatenate([expert_ids[0].T.astype(F32), gate_scores[0].T], axis=0)
    meta = swapped(meta)
    sent = swapped(tokens)

    own = [w_gate[0, 0].T, w_up[0, 0].T, w_down[0, 0]]
    across = [flipped(w, "yl") for w in own]
    other = [flipped(w, "core") for w in own]

    n_rows = n_z * CAP
    pick, high, low = call(
        table_kernel,
        (shaped((n_rows, toks)), shaped((toks, n_rows)), shaped((toks, n_rows))),
        scalars=1,
    )(where, meta)
    rows = call(pack_kernel, shaped((n_rows, width)), flops=2 * n_rows * toks * width, moved=2 * n_rows * width)(
        pick, sent, trunk_gain
    )

    image = image_in[0]
    image_normed = rms_scale(image, image_gain[0]).astype(BF16)
    column = lax.all_gather(image_normed, "z", axis=0, tiled=True)
    all_rows = lax.all_gather(column, square, axis=0, tiled=True)

    def over_z(value):
        return lax.all_to_all(value.reshape(n_z, CAP, width), "z", split_axis=0, concat_axis=0, tiled=True).reshape(
            n_rows, width
        )

    arrived = over_z(rows)
    other_across = [flipped(w, "core") for w in across]
    made = call(
        expert_kernel,
        shaped((n_rows, width)),
        flops=6 * n_rows * width * 768,
        moved=12 * 192 * width * 2,
    )(arrived, *own, *across, *other, *other_across)
    returned = over_z(made)

    hidden = jax.nn.gelu(jnp.dot(all_rows, fc_in[0], preferred_element_type=F32), approximate=False).astype(BF16)
    part = jnp.dot(hidden, fc_out[0], preferred_element_type=F32).astype(BF16)
    part = part.reshape(n_yh * n_tp, n_z, part.shape[1])
    column_sum = lax.psum_scatter(part, square, scatter_dimension=0, tiled=True)[0]
    spread = lax.all_to_all(column_sum.astype(F32)[:, None, :], "z", split_axis=0, concat_axis=0, tiled=True)
    summed = jnp.sum(spread, axis=0)
    encoded = (image.astype(F32) + layer_scale[0] * summed).astype(BF16)
    image_out = lax.ppermute(encoded[None], "pp", [(s, (s - 1) % n_pp) for s in range(n_pp)])

    quarter = width // n_tp
    pieces = call(combine_kernel, tuple(shaped((toks, quarter)) for _ in range(n_tp)), scalars=1, flops=4 * n_rows * toks * width)(
        where, high, low, returned
    )
    pieces = [
        lax.ppermute(
            piece,
            square,
            [(a * n_tp + b, b * n_tp + (a + k) % n_tp) for a in range(n_yh) for b in range(n_tp)],
        )
        for k, piece in enumerate(pieces)
    ]
    layer = call(layer_kernel, shaped((toks, quarter)), scalars=1)(where, tokens, *pieces)
    here = lax.ppermute(layer, "pp", [(s, (s + 1) % n_pp) for s in range(n_pp)])
    there = lax.ppermute(
        layer, ("pp", "yl"), [(s * 2 + y, ((s + 1) % n_pp) * 2 + 1 - y) for s in range(n_pp) for y in range(2)]
    )
    here_other, there_other = flipped(here, "core"), flipped(there, "core")
    trunk_out = call(join_kernel, shaped((toks, width)), scalars=1)(where, here, there, here_other, there_other)
    return (trunk_out[None], image_out)


def solution(mesh):
    n_pp, n_ep, n_tp = (mesh.shape[a] for a in ("pp", "ep", "tp"))
    fine = Mesh(
        np.asarray(mesh.devices).reshape(n_pp, n_tp, n_ep // n_tp, n_tp // 2, 2),
        ("pp", "yh", "z", "yl", "core"),
    )
    ep, tp = ("yh", "z"), ("yl", "core")
    return jax.shard_map(
        body,
        mesh=fine,
        in_specs=(
            P("pp", ep, None),
            P("pp", ep, None),
            P("pp", ep, None),
            P("pp", None),
            P("pp", ep, None, tp),
            P("pp", ep, None, tp),
            P("pp", ep, tp, None),
            P("pp", ep + tp, None),
            P("pp", None),
            P("pp", None, ep + tp),
            P("pp", ep + tp, None),
            P("pp", None),
        ),
        out_specs=(P("pp", ep, None), P("pp", ep + tp, None)),
        check_vma=False,
    )
```

time: 729 us -> 294 us (0.40)
  waiting for transfers between devices: 341 us -> 56.5 us
  blocking collectives: 289 us -> 70.9 us
  starting transfers between devices: 15.4 us -> 126 us
  local copies, waits for them, and re-layouts: 29.2 us -> 4.1 us
  other arithmetic: 23.2 us -> 3.02 us
  Pallas kernels: 0 us -> 14.5 us
  matrix products: 14.1 us -> 3.28 us
    unnamed x3 -> x2, waiting for transfers between devices: 195 us -> 43.8 us
    all_to_all x1 -> x0, blocking collectives: 145 us -> none  [body(): lax.all_to_all(slots, 'ep', split_axis=0, concat_axis=0, tiled=True)]
    all_to_all x1 -> x3, waiting for transfers between devices: 145 us -> 1.91 us  [the longest x1 1.91 us: body(): lax.all_to_all(column_sum.astype(F32)[:, None, :], 'z', split_axis=0, con...]
    ppermute x2 -> x20, starting transfers between devices: 6.96 us -> 102 us  [the longest x11 72.3 us: flipped(): return lax.ppermute(value, axis, [(0, 1), (1, 0)])]
    all_gather x1 -> x2, blocking collectives: 144 us -> 70.9 us  [the longest x1 44.1 us: body(): column = lax.all_gather(image_normed, 'z', axis=0, tiled=True)]
    gather x2 -> x0, local copies, waits for them, and re-layouts: 18.2 us -> none  [the longest x1 12 us: body(): picked = returned.reshape(-1, width)[slot].reshape(tok_rows, topk, width)]
    all_to_all x1 -> x3, starting transfers between devices: 8.15 us -> 23.4 us  [the longest x2 16.9 us: over_z(): lax.all_to_all(value.reshape(n_z, CAP, width), 'z', split_axis=0, concat_...]
    pallas_call x0 -> x6, Pallas kernels: none -> 14.5 us  [run(): pl.pallas_call(kernel, out_shape=outs, in_specs=specs, out_specs=jax.tree...]
  transfers between devices with their start and end apart: 5 -> 24, of which waited for: 3 -> 8; matrix products, arithmetic and copies ran while one was open for 1% -> 2% of each run, Pallas kernels for 0% -> 1%
where the time goes in v1:
time: 294 us; the launch traced here: 293 us
  starting transfers between devices  126 us (43%)
  blocking collectives  70.9 us (24%)
  waiting for transfers between devices  56.5 us (19%)
  between operations  15.1 us (5%)
  Pallas kernels  14.5 us (5%)
  local copies, waits for them, and re-layouts  4.1 us (1%)
  matrix products  3.28 us (1%)
  other arithmetic  3.02 us (1%)
    ppermute x11, starting transfers between devices, flipped(): return lax.ppermute(value, axis, [(0, 1), (1, 0)])  72.3 us
    all_gather x1, blocking collectives, body(): column = lax.all_gather(image_normed, 'z', axis=0, tiled=True)  44.1 us
    unnamed x2, waiting for transfers between devices  43.8 us
    all_gather x1, blocking collectives, body(): all_rows = lax.all_gather(column, square, axis=0, tiled=True)  26.8 us
    all_to_all x2, starting transfers between devices, over_z(): lax.all_to_all(value.reshape(n_z, CAP, width), 'z', split_axis=0, concat_...  16.9 us
    ppermute x4, starting transfers between devices, body(): lax.ppermute(piece, square, [(a * n_tp + b, b * n_tp + (a + k) % n_tp) fo...  14.9 us
    pallas_call x6, Pallas kernels, run(): pl.pallas_call(kernel, out_shape=outs, in_specs=specs, out_specs=jax.tree...  14.5 us
    ppermute x2, starting transfers between devices, swapped(): lax.ppermute(value, square, [(a * n_tp + b, b * n_tp + a) for a in range(...  7.65 us
  transfers between devices with their start and end apart: 24, of which 8 were waited for; matrix products, arithmetic and copies ran while one was open for 2% of the time, Pallas kernels for 1%

profile of v1, /device:TPU:1, one launch (start us, length us, event | category | flops | bytes accessed | tf_op | source)
XLA Modules:
  0.0 293.0 jit_solution(17850228393251924423)
XLA Ops:
  7.2 0.0 copy-start
  7.2 5.7 %collective-permute-start.1 = (bf16[128,2048]{1,0:T(8,128)(2,1)}, bf16[128,2048]{1,0:T(8,128)(2,1)S(1)}, u32[]{:S(2)}, u32[]{:S(2)}) collective-permute-start(bf16[128,2048]{1,0:T(8,128)(2,1)} %bitcast.61), channel_id=1, source_target_pairs={{0,0},{1,32},{2,64},{3,96},{32,1},{33,33},{34,65},{35,97},{64,2},{... | collective-permute-start | bytes 1572872 | tf_op jit(solution)/shard_map/ppermute | solution.py:145
  12.9 0.7 convert_bitcast_fusion
  13.6 0.7 pad_maximum_fusion
  14.3 1.9 collective-permute-start
  16.2 0.1 pad_add_fusion.where
  16.3 5.3 %collective-permute-done.meta = f32[16,128]{1,0:T(8,128)S(1)} collective-permute-done((f32[16,128]{1,0:T(8,128)S(1)}, f32[16,128]{1,0:T(8,128)S(1)}, u32[]{:S(2)}, u32[]{:S(2)}) %collective-permute-start) | collective-permute-done | bytes 8224 | tf_op jit(solution)/shard_map/ppermute | solution.py:145
  21.6 0.8 shard_map.131
  22.5 0.0 collective-permute-done.1.toks
  22.5 0.0 copy-start.7
  22.5 0.7 copy-done.7
  23.2 1.7 shard_map.132
  24.9 10.2 %all-to-all-start = ((bf16[8,40,2048]{2,1,0:T(8,128)(2,1)}), bf16[8,40,2048]{2,1,0:T(8,128)(2,1)}, u32[]{:S(2)}, u32[]{:S(2)}) async-start(bf16[8,40,2048]{2,1,0:T(8,128)(2,1)} %bitcast.7), calls=%async_computation | async-start | bytes 2621440 | tf_op jit(solution)/shard_map/all_to_all | solution.py:177
  35.1 9.5 %collective-permute-start.2 = (bf16[192,2048]{1,0:T(8,128)(2,1)S(1)}, bf16[192,2048]{1,0:T(8,128)(2,1)}, u32[]{:S(2)}, u32[]{:S(2)}) collective-permute-start(bf16[192,2048]{1,0:T(8,128)(2,1)S(1)} %bitcast.52), channel_id=1, source_target_pairs={{0,2},{2,0},{1,3},{3,1},{4,6},{6,4},{5,7},{7,5},{8,10},{10,8},{9,1... | collective-permute-start | bytes 2359304 | tf_op jit(solution)/shard_map/ppermute | solution.py:148
  44.6 1.9 collective-permute-start.3
  46.6 3.4 %collective-permute-start.4 = (bf16[192,2048]{1,0:T(8,128)(2,1)S(1)}, bf16[192,2048]{1,0:T(8,128)(2,1)}, u32[]{:S(2)}, u32[]{:S(2)}) collective-permute-start(bf16[192,2048]{1,0:T(8,128)(2,1)S(1)} %bitcast.58), channel_id=1, source_target_pairs={{0,2},{2,0},{1,3},{3,1},{4,6},{6,4},{5,7},{7,5},{8,10},{10,8},{9,1... | collective-permute-start | bytes 2359304 | tf_op jit(solution)/shard_map/ppermute | solution.py:148
  49.9 9.3 %collective-permute-start.5 = (bf16[192,2048]{1,0:T(8,128)(2,1)S(1)}, bf16[192,2048]{1,0:T(8,128)(2,1)S(1)}, u32[]{:S(2)}, u32[]{:S(2)}) collective-permute-start(bf16[192,2048]{1,0:T(8,128)(2,1)S(1)} %bitcast.53), channel_id=1, source_target_pairs={{0,1},{1,0},{2,3},{3,2},{4,5},{5,4},{6,7},{7,6},{8,9},{9,8},{10,11... | collective-permute-start | bytes 2359304 | tf_op jit(solution)/shard_map/ppermute | solution.py:148
  59.3 1.9 collective-permute-start.6
  61.2 0.0 collective-permute-done.2.refs_4_
  61.2 10.7 %collective-permute-start.7 = (bf16[192,2048]{1,0:T(8,128)(2,1)S(1)}, bf16[192,2048]{1,0:T(8,128)(2,1)}, u32[]{:S(2)}, u32[]{:S(2)}) collective-permute-start(bf16[192,2048]{1,0:T(8,128)(2,1)S(1)} %bitcast.59), channel_id=1, source_target_pairs={{0,1},{1,0},{2,3},{3,2},{4,5},{5,4},{6,7},{7,6},{8,9},{9,8},{10,11... | collective-permute-start | bytes 2359304 | tf_op jit(solution)/shard_map/ppermute | solution.py:148
  72.0 0.9 collective-permute-done.3.refs_5_
  72.8 16.0 %collective-permute-start.8 = (bf16[192,2048]{1,0:T(8,128)(2,1)}, bf16[192,2048]{1,0:T(8,128)(2,1)}, u32[]{:S(2)}, u32[]{:S(2)}) collective-permute-start(bf16[192,2048]{1,0:T(8,128)(2,1)} %collective-permute-done.2.refs_4_), channel_id=1, source_target_pairs={{0,1},{1,0},{2,3},{3,2},{4,5},{5,4},{6,7},{7,6},{8,9},{9,8},{10,11... | collective-permute-start | bytes 2359304 | tf_op jit(solution)/shard_map/ppermute | solution.py:148
  88.8 0.9 collective-permute-done.4.refs_6_
  89.7 9.1 %collective-permute-start.9 = (bf16[192,2048]{1,0:T(8,128)(2,1)}, bf16[192,2048]{1,0:T(8,128)(2,1)}, u32[]{:S(2)}, u32[]{:S(2)}) collective-permute-start(bf16[192,2048]{1,0:T(8,128)(2,1)} %collective-permute-done.3.refs_5_), channel_id=1, source_target_pairs={{0,1},{1,0},{2,3},{3,2},{4,5},{5,4},{6,7},{7,6},{8,9},{9,8},{10,11... | collective-permute-start | bytes 2359304 | tf_op jit(solution)/shard_map/ppermute | solution.py:148
  98.8 0.0 collective-permute-done.5.refs_7_
  98.8 0.9 copy-done.4
  99.7 1.9 collective-permute-start.10
  101.7 0.6 fusion.48
  103.0 0.0 collective-permute-done.7.refs_9_
  103.0 0.0 collective-permute-done.8.refs_10_
  103.0 1.2 collective-permute-done.10.refs_12_
  104.2 0.0 all-to-all-done
  104.2 1.1 copy-done.5
  105.4 8.7 %shard_map.133 = bf16[320,2048]{1,0:T(8,128)(2,1)} custom-call(bf16[320,2048]{1,0:T(8,128)(2,1)} %bitcast.8.refs_0_, bf16[192,2048]{1,0:T(8,128)(2,1)S(1)} %bitcast.54, bf16[192,2048]{1,0:T(8,128)(2,1)S(1)} %bitcast.57, bf16[192,2048]{1,0:T(8,128)(2,1)S(1)} %bitcast.60, bf16[192,2048]{1,0:T(8,128)(2,1)} %collective-permute-done.2.refs_4_, ...), custom_call_target="tpu_custom_call" | custom-call | flops 3019898880 | bytes 9437184 | tf_op jit(solution)/shard_map/pallas_call | solution.py:20
  114.1 6.8 %all-to-all-start.1 = ((bf16[8,40,2048]{2,1,0:T(8,128)(2,1)}), bf16[8,40,2048]{2,1,0:T(8,128)(2,1)S(1)}, u32[]{:S(2)}, u32[]{:S(2)}) async-start(bf16[8,40,2048]{2,1,0:T(8,128)(2,1)} %bitcast.63), calls=%async_computation.1 | async-start | bytes 2621440 | tf_op jit(solution)/shard_map/all_to_all | solution.py:177
  120.8 0.0 reduce-scatter.4.cloned.1.call-start
  120.9 44.1 %all-gather = bf16[8,1,3200]{2,1,0:T(2,128)(2,1)S(1)} all-gather(bf16[1,1,3200]{2,1,0:T(2,128)(2,1)S(1)} %fusion.51), channel_id=1, replica_groups=mesh['pp'=4,'yh'=4,'z'=8,'yl'=2,'core'=2] {'z'}, dimensions={0}, use_global_device_ids=true | all-gather | bytes 57600 | tf_op jit(solution)/shard_map/all_gather | solution.py:173
  165.1 26.8 %all_gather.7 = bf16[128,3200]{1,0:T(8,128)(2,1)S(1)} all-gather(bf16[8,3200]{1,0:T(8,128)(2,1)S(1)} %bitcast.65), channel_id=1, replica_groups=mesh['pp'=4,'yh'=4,'z'=8,'yl'=2,'core'=2] {'yh','yl','core'}, dimensions={0}, use_global_device_ids=true | all-gather | bytes 870400 | tf_op jit(solution)/shard_map/all_gather | solution.py:174
  191.8 3.3 %fusion = bf16[16,8,3200]{2,1,0:T(8,128)(2,1)} fusion(bf16[1,100,3200]{2,1,0:T(8,128)(2,1)S(1)} %copy-done, bf16[128,3200]{1,0:T(8,128)(2,1)S(1)} %all_gather.7, bf16[1,3200,100]{1,2,0:T(8,128)(2,1)} %param.21), kind=kOutput, calls=%fused_computation.1 | convolution fusion | flops 165081600 | bytes 2918400 | tf_op jit(solution)/shard_map/dot_general | solution.py:192
  195.1 0.0 reduce-scatter.4.cloned.1.call-update
  195.2 1.3 shard_map.134
  196.4 0.0 copy-start.10
  196.4 3.1 %collective-permute-start.11 = (bf16[128,512]{1,0:T(8,128)(2,1)S(1)}, bf16[128,512]{1,0:T(8,128)(2,1)S(1)}, u32[]{:S(2)}, u32[]{:S(2)}) collective-permute-start(bf16[128,512]{1,0:T(8,128)(2,1)S(1)} %get-tuple-element.12), channel_id=1, source_target_pairs={{0,0},{1,32},{2,64},{3,96},{32,1},{33,33},{34,65},{35,97},{64,2},{... | collective-permute-start | bytes 393224 | tf_op jit(solution)/shard_map/ppermute | solution.py:205
  199.6 1.9 collective-permute-start.12
  201.5 5.7 %collective-permute-start.13 = (bf16[128,512]{1,0:T(8,128)(2,1)S(1)}, bf16[128,512]{1,0:T(8,128)(2,1)S(1)}, u32[]{:S(2)}, u32[]{:S(2)}) collective-permute-start(bf16[128,512]{1,0:T(8,128)(2,1)S(1)} %get-tuple-element.14), channel_id=1, source_target_pairs={{0,2},{1,34},{2,66},{3,98},{32,3},{33,35},{34,67},{35,99},{64,0},{... | collective-permute-start | bytes 393224 | tf_op jit(solution)/shard_map/ppermute | solution.py:205
  207.3 4.1 %collective-permute-start.14 = (bf16[128,512]{1,0:T(8,128)(2,1)S(1)}, bf16[128,512]{1,0:T(8,128)(2,1)S(1)}, u32[]{:S(2)}, u32[]{:S(2)}) collective-permute-start(bf16[128,512]{1,0:T(8,128)(2,1)S(1)} %get-tuple-element.15), channel_id=1, source_target_pairs={{0,3},{1,35},{2,67},{3,99},{32,0},{33,32},{34,64},{35,96},{64,1},{... | collective-permute-start | bytes 393224 | tf_op jit(solution)/shard_map/ppermute | solution.py:205
  211.4 43.8 %reduce-scatter.4.cloned.1.call-done = bf16[1,8,3200]{2,1,0:T(8,128)(2,1)} async-done(((bf16[16,8,3200]{2,1,0:T(8,128)(2,1)}), bf16[1,8,3200]{2,1,0:T(8,128)(2,1)}) %reduce-scatter.4.cloned.1.call-update) | async-done | bytes 51216
  255.2 0.8 bitcast_convert_fusion
  256.0 0.7 copy.14
  256.8 6.5 %all-to-all-start.2 = ((f32[8,1,3200]{2,1,0:T(1,128)}), f32[8,1,3200]{2,1,0:T(1,128)S(1)}, u32[]{:S(2)}, u32[]{:S(2)}) async-start(f32[8,1,3200]{2,1,0:T(1,128)} %copy.14), calls=%async_computation.2 | async-start | bytes 204800 | tf_op jit(solution)/shard_map/all_to_all | solution.py:195
  263.3 0.0 collective-permute-done.12.refs_1_
  263.3 0.0 collective-permute-done.13.refs_2_
  263.3 0.6 shard_map.135
  263.9 3.1 %collective-permute-start.15 = (bf16[128,512]{1,0:T(8,128)(2,1)S(1)}, bf16[128,512]{1,0:T(8,128)(2,1)S(1)}, u32[]{:S(2)}, u32[]{:S(2)}) collective-permute-start(bf16[128,512]{1,0:T(8,128)(2,1)S(1)} %shard_map.135), channel_id=1, source_target_pairs={{0,128},{128,256},{256,384},{384,0},{1,129},{129,257},{257,385},{3... | collective-permute-start | bytes 393224 | tf_op jit(solution)/shard_map/ppermute | solution.py:213
  267.0 1.9 collective-permute-start.16
  269.0 1.9 all-to-all-done.2
  270.9 0.1 reduce_sum.21
  271.0 0.2 collective-permute-done.15.own
  271.1 4.4 %collective-permute-start.17 = (bf16[128,512]{1,0:T(8,128)(2,1)S(1)}, bf16[128,512]{1,0:T(8,128)(2,1)S(1)}, u32[]{:S(2)}, u32[]{:S(2)}) collective-permute-start(bf16[128,512]{1,0:T(8,128)(2,1)S(1)} %collective-permute-done.15.own), channel_id=1, source_target_pairs={{0,1},{1,0},{2,3},{3,2},{4,5},{5,4},{6,7},{7,6},{8,9},{9,8},{10,11... | collective-permute-start | bytes 393224 | tf_op jit(solution)/shard_map/ppermute | solution.py:148
  275.5 4.1 %collective-permute-start.18 = (bf16[128,512]{1,0:T(8,128)(2,1)S(1)}, bf16[128,512]{1,0:T(8,128)(2,1)S(1)}, u32[]{:S(2)}, u32[]{:S(2)}) collective-permute-start(bf16[128,512]{1,0:T(8,128)(2,1)S(1)} %collective-permute-done.16.across), channel_id=1, source_target_pairs={{0,1},{1,0},{2,3},{3,2},{4,5},{5,4},{6,7},{7,6},{8,9},{9,8},{10,11... | collective-permute-start | bytes 393224 | tf_op jit(solution)/shard_map/ppermute | solution.py:148
  279.7 2.2 collective-permute-start.19
  281.9 2.2 collective-permute-done.19
  284.2 1.4 shard_map.136
  285.6 0.6 copy.19
  (27 shorter events, 0.1 us)
Async XLA Ops:
  7.2 184.7 %copy-start = (bf16[1,100,3200]{2,1,0:T(8,128)(2,1)S(1)}, bf16[1,100,3200]{2,1,0:T(8,128)(2,1)}, u32[]{:S(2)}) copy-start(bf16[1,100,3200]{2,1,0:T(8,128)(2,1)} %param.22) | copy-start | bytes 1920004
  7.2 15.3 %collective-permute-start.1 = (bf16[128,2048]{1,0:T(8,128)(2,1)}, bf16[128,2048]{1,0:T(8,128)(2,1)S(1)}, u32[]{:S(2)}, u32[]{:S(2)}) collective-permute-start(bf16[128,2048]{1,0:T(8,128)(2,1)} %bitcast.61), channel_id=1, source_target_pairs={{0,0},{1,32},{2,64},{3,96},{32,1},{33,33},{34,65},{35,97},{64,2},{... | collective-permute-start | bytes 1572872 | tf_op jit(solution)/shard_map/ppermute | solution.py:145
  14.3 7.3 %collective-permute-start = (f32[16,128]{1,0:T(8,128)S(1)}, f32[16,128]{1,0:T(8,128)S(1)}, u32[]{:S(2)}, u32[]{:S(2)}) collective-permute-start(f32[16,128]{1,0:T(8,128)S(1)} %pad_maximum_fusion), channel_id=1, source_target_pairs={{0,0},{1,32},{2,64},{3,96},{32,1},{33,33},{34,65},{35,97},{64,2},{... | collective-permute-start | bytes 24584 | tf_op jit(solution)/shard_map/ppermute | solution.py:145
  22.5 0.7 copy-start.7
  24.9 10.2 %copy-start.1 = (bf16[1,1,2048,192]{2,3,1,0:T(8,128)(2,1)S(1)}, bf16[1,1,2048,192]{2,3,1,0:T(8,128)(2,1)}, u32[]{:S(2)}) copy-start(bf16[1,1,2048,192]{2,3,1,0:T(8,128)(2,1)} %param.16) | copy-start | bytes 2359300
  24.9 19.7 %copy-start.2 = (bf16[1,1,2048,192]{2,3,1,0:T(8,128)(2,1)S(1)}, bf16[1,1,2048,192]{2,3,1,0:T(8,128)(2,1)}, u32[]{:S(2)}) copy-start(bf16[1,1,2048,192]{2,3,1,0:T(8,128)(2,1)} %param.17) | copy-start | bytes 2359300
  24.9 21.7 %copy-start.3 = (bf16[1,1,192,2048]{3,2,1,0:T(8,128)(2,1)S(1)}, bf16[1,1,192,2048]{3,2,1,0:T(8,128)(2,1)}, u32[]{:S(2)}) copy-start(bf16[1,1,192,2048]{3,2,1,0:T(8,128)(2,1)} %param.18) | copy-start | bytes 2359300
  24.9 76.7 %copy-start.8 = (bf16[1,1,3200]{2,1,0:T(2,128)(2,1)S(1)}, bf16[1,1,3200]{2,1,0:T(2,128)(2,1)}, u32[]{:S(2)}) copy-start(bf16[1,1,3200]{2,1,0:T(2,128)(2,1)} %param.19) | copy-start | bytes 19204
  24.9 79.3 %all-to-all-start = ((bf16[8,40,2048]{2,1,0:T(8,128)(2,1)}), bf16[8,40,2048]{2,1,0:T(8,128)(2,1)}, u32[]{:S(2)}, u32[]{:S(2)}) async-start(bf16[8,40,2048]{2,1,0:T(8,128)(2,1)} %bitcast.7), calls=%async_computation | async-start | bytes 2621440 | tf_op jit(solution)/shard_map/all_to_all | solution.py:177
  35.1 26.1 %collective-permute-start.2 = (bf16[192,2048]{1,0:T(8,128)(2,1)S(1)}, bf16[192,2048]{1,0:T(8,128)(2,1)}, u32[]{:S(2)}, u32[]{:S(2)}) collective-permute-start(bf16[192,2048]{1,0:T(8,128)(2,1)S(1)} %bitcast.52), channel_id=1, source_target_pairs={{0,2},{2,0},{1,3},{3,1},{4,6},{6,4},{5,7},{7,5},{8,10},{10,8},{9,1... | collective-permute-start | bytes 2359304 | tf_op jit(solution)/shard_map/ppermute | solution.py:148
  44.6 28.2 %collective-permute-start.3 = (bf16[192,2048]{1,0:T(8,128)(2,1)S(1)}, bf16[192,2048]{1,0:T(8,128)(2,1)}, u32[]{:S(2)}, u32[]{:S(2)}) collective-permute-start(bf16[192,2048]{1,0:T(8,128)(2,1)S(1)} %bitcast.55), channel_id=1, source_target_pairs={{0,2},{2,0},{1,3},{3,1},{4,6},{6,4},{5,7},{7,5},{8,10},{10,8},{9,1... | collective-permute-start | bytes 2359304 | tf_op jit(solution)/shard_map/ppermute | solution.py:148
  46.6 43.1 %collective-permute-start.4 = (bf16[192,2048]{1,0:T(8,128)(2,1)S(1)}, bf16[192,2048]{1,0:T(8,128)(2,1)}, u32[]{:S(2)}, u32[]{:S(2)}) collective-permute-start(bf16[192,2048]{1,0:T(8,128)(2,1)S(1)} %bitcast.58), channel_id=1, source_target_pairs={{0,2},{2,0},{1,3},{3,1},{4,6},{6,4},{5,7},{7,5},{8,10},{10,8},{9,1... | collective-permute-start | bytes 2359304 | tf_op jit(solution)/shard_map/ppermute | solution.py:148
  49.9 48.9 %collective-permute-start.5 = (bf16[192,2048]{1,0:T(8,128)(2,1)S(1)}, bf16[192,2048]{1,0:T(8,128)(2,1)S(1)}, u32[]{:S(2)}, u32[]{:S(2)}) collective-permute-start(bf16[192,2048]{1,0:T(8,128)(2,1)S(1)} %bitcast.53), channel_id=1, source_target_pairs={{0,1},{1,0},{2,3},{3,2},{4,5},{5,4},{6,7},{7,6},{8,9},{9,8},{10,11... | collective-permute-start | bytes 2359304 | tf_op jit(solution)/shard_map/ppermute | solution.py:148
  59.3 43.7 %collective-permute-start.6 = (bf16[192,2048]{1,0:T(8,128)(2,1)S(1)}, bf16[192,2048]{1,0:T(8,128)(2,1)}, u32[]{:S(2)}, u32[]{:S(2)}) collective-permute-start(bf16[192,2048]{1,0:T(8,128)(2,1)S(1)} %bitcast.56), channel_id=1, source_target_pairs={{0,1},{1,0},{2,3},{3,2},{4,5},{5,4},{6,7},{7,6},{8,9},{9,8},{10,11... | collective-permute-start | bytes 2359304 | tf_op jit(solution)/shard_map/ppermute | solution.py:148
  61.2 41.7 %collective-permute-start.7 = (bf16[192,2048]{1,0:T(8,128)(2,1)S(1)}, bf16[192,2048]{1,0:T(8,128)(2,1)}, u32[]{:S(2)}, u32[]{:S(2)}) collective-permute-start(bf16[192,2048]{1,0:T(8,128)(2,1)S(1)} %bitcast.59), channel_id=1, source_target_pairs={{0,1},{1,0},{2,3},{3,2},{4,5},{5,4},{6,7},{7,6},{8,9},{9,8},{10,11... | collective-permute-start | bytes 2359304 | tf_op jit(solution)/shard_map/ppermute | solution.py:148
  72.8 30.2 %collective-permute-start.8 = (bf16[192,2048]{1,0:T(8,128)(2,1)}, bf16[192,2048]{1,0:T(8,128)(2,1)}, u32[]{:S(2)}, u32[]{:S(2)}) collective-permute-start(bf16[192,2048]{1,0:T(8,128)(2,1)} %collective-permute-done.2.refs_4_), channel_id=1, source_target_pairs={{0,1},{1,0},{2,3},{3,2},{4,5},{5,4},{6,7},{7,6},{8,9},{9,8},{10,11... | collective-permute-start | bytes 2359304 | tf_op jit(solution)/shard_map/ppermute | solution.py:148
  89.7 13.3 %collective-permute-start.9 = (bf16[192,2048]{1,0:T(8,128)(2,1)}, bf16[192,2048]{1,0:T(8,128)(2,1)}, u32[]{:S(2)}, u32[]{:S(2)}) collective-permute-start(bf16[192,2048]{1,0:T(8,128)(2,1)} %collective-permute-done.3.refs_5_), channel_id=1, source_target_pairs={{0,1},{1,0},{2,3},{3,2},{4,5},{5,4},{6,7},{7,6},{8,9},{9,8},{10,11... | collective-permute-start | bytes 2359304 | tf_op jit(solution)/shard_map/ppermute | solution.py:148
  98.8 0.9 copy-start.4
  99.7 4.5 %collective-permute-start.10 = (bf16[192,2048]{1,0:T(8,128)(2,1)}, bf16[192,2048]{1,0:T(8,128)(2,1)}, u32[]{:S(2)}, u32[]{:S(2)}) collective-permute-start(bf16[192,2048]{1,0:T(8,128)(2,1)} %collective-permute-done.4.refs_6_), channel_id=1, source_target_pairs={{0,1},{1,0},{2,3},{3,2},{4,5},{5,4},{6,7},{7,6},{8,9},{9,8},{10,11... | collective-permute-start | bytes 2359304 | tf_op jit(solution)/shard_map/ppermute | solution.py:148
  104.2 1.1 copy-start.5
  114.1 6.8 %copy-start.9 = (f32[1,3200]{1,0:T(1,128)S(1)}, f32[1,3200]{1,0:T(1,128)}, u32[]{:S(2)}) copy-start(f32[1,3200]{1,0:T(1,128)} %param.20) | copy-start | bytes 38404
  114.1 81.1 %all-to-all-start.1 = ((bf16[8,40,2048]{2,1,0:T(8,128)(2,1)}), bf16[8,40,2048]{2,1,0:T(8,128)(2,1)S(1)}, u32[]{:S(2)}, u32[]{:S(2)}) async-start(bf16[8,40,2048]{2,1,0:T(8,128)(2,1)} %bitcast.63), calls=%async_computation.1 | async-start | bytes 2621440 | tf_op jit(solution)/shard_map/all_to_all | solution.py:177
  120.8 134.4 %reduce-scatter.4.cloned.1.call-start = ((), (), s32[]{:S(2)}) async-start(), calls=%async_computation.4 | async-start | bytes 870400
  195.1 68.2 %copy-start.6 = (bf16[1,128,2048]{2,1,0:T(8,128)(2,1)S(1)}, bf16[1,128,2048]{2,1,0:T(8,128)(2,1)}, u32[]{:S(2)}) copy-start(bf16[1,128,2048]{2,1,0:T(8,128)(2,1)} %param.12) | copy-start | bytes 1572868
  196.4 83.3 %copy-start.10 = (f32[1,3200]{1,0:T(1,128)S(1)}, f32[1,3200]{1,0:T(1,128)}, u32[]{:S(2)}) copy-start(f32[1,3200]{1,0:T(1,128)} %param.23) | copy-start | bytes 38404
  196.4 66.8 %collective-permute-start.11 = (bf16[128,512]{1,0:T(8,128)(2,1)S(1)}, bf16[128,512]{1,0:T(8,128)(2,1)S(1)}, u32[]{:S(2)}, u32[]{:S(2)}) collective-permute-start(bf16[128,512]{1,0:T(8,128)(2,1)S(1)} %get-tuple-element.12), channel_id=1, source_target_pairs={{0,0},{1,32},{2,64},{3,96},{32,1},{33,33},{34,65},{35,97},{64,2},{... | collective-permute-start | bytes 393224 | tf_op jit(solution)/shard_map/ppermute | solution.py:205
  199.6 63.7 %collective-permute-start.12 = (bf16[128,512]{1,0:T(8,128)(2,1)S(1)}, bf16[128,512]{1,0:T(8,128)(2,1)S(1)}, u32[]{:S(2)}, u32[]{:S(2)}) collective-permute-start(bf16[128,512]{1,0:T(8,128)(2,1)S(1)} %get-tuple-element.13), channel_id=1, source_target_pairs={{0,1},{1,33},{2,65},{3,97},{32,2},{33,34},{34,66},{35,98},{64,3},{... | collective-permute-start | bytes 393224 | tf_op jit(solution)/shard_map/ppermute | solution.py:205
  201.5 61.8 %collective-permute-start.13 = (bf16[128,512]{1,0:T(8,128)(2,1)S(1)}, bf16[128,512]{1,0:T(8,128)(2,1)S(1)}, u32[]{:S(2)}, u32[]{:S(2)}) collective-permute-start(bf16[128,512]{1,0:T(8,128)(2,1)S(1)} %get-tuple-element.14), channel_id=1, source_target_pairs={{0,2},{1,34},{2,66},{3,98},{32,3},{33,35},{34,67},{35,99},{64,0},{... | collective-permute-start | bytes 393224 | tf_op jit(solution)/shard_map/ppermute | solution.py:205
  207.3 56.0 %collective-permute-start.14 = (bf16[128,512]{1,0:T(8,128)(2,1)S(1)}, bf16[128,512]{1,0:T(8,128)(2,1)S(1)}, u32[]{:S(2)}, u32[]{:S(2)}) collective-permute-start(bf16[128,512]{1,0:T(8,128)(2,1)S(1)} %get-tuple-element.15), channel_id=1, source_target_pairs={{0,3},{1,35},{2,67},{3,99},{32,0},{33,32},{34,64},{35,96},{64,1},{... | collective-permute-start | bytes 393224 | tf_op jit(solution)/shard_map/ppermute | solution.py:205
  256.8 14.1 %all-to-all-start.2 = ((f32[8,1,3200]{2,1,0:T(1,128)}), f32[8,1,3200]{2,1,0:T(1,128)S(1)}, u32[]{:S(2)}, u32[]{:S(2)}) async-start(f32[8,1,3200]{2,1,0:T(1,128)} %copy.14), calls=%async_computation.2 | async-start | bytes 204800 | tf_op jit(solution)/shard_map/all_to_all | solution.py:195
  263.9 7.2 %collective-permute-start.15 = (bf16[128,512]{1,0:T(8,128)(2,1)S(1)}, bf16[128,512]{1,0:T(8,128)(2,1)S(1)}, u32[]{:S(2)}, u32[]{:S(2)}) collective-permute-start(bf16[128,512]{1,0:T(8,128)(2,1)S(1)} %shard_map.135), channel_id=1, source_target_pairs={{0,128},{128,256},{256,384},{384,0},{1,129},{129,257},{257,385},{3... | collective-permute-start | bytes 393224 | tf_op jit(solution)/shard_map/ppermute | solution.py:213
  267.0 8.5 %collective-permute-start.16 = (bf16[128,512]{1,0:T(8,128)(2,1)S(1)}, bf16[128,512]{1,0:T(8,128)(2,1)S(1)}, u32[]{:S(2)}, u32[]{:S(2)}) collective-permute-start(bf16[128,512]{1,0:T(8,128)(2,1)S(1)} %shard_map.135), channel_id=1, source_target_pairs={{0,130},{2,128},{128,258},{130,256},{256,386},{258,384},{384,2},{3... | collective-permute-start | bytes 393224 | tf_op jit(solution)/shard_map/ppermute | solution.py:214
  271.1 13.0 %collective-permute-start.17 = (bf16[128,512]{1,0:T(8,128)(2,1)S(1)}, bf16[128,512]{1,0:T(8,128)(2,1)S(1)}, u32[]{:S(2)}, u32[]{:S(2)}) collective-permute-start(bf16[128,512]{1,0:T(8,128)(2,1)S(1)} %collective-permute-done.15.own), channel_id=1, source_target_pairs={{0,1},{1,0},{2,3},{3,2},{4,5},{5,4},{6,7},{7,6},{8,9},{9,8},{10,11... | collective-permute-start | bytes 393224 | tf_op jit(solution)/shard_map/ppermute | solution.py:148
  275.5 8.6 %collective-permute-start.18 = (bf16[128,512]{1,0:T(8,128)(2,1)S(1)}, bf16[128,512]{1,0:T(8,128)(2,1)S(1)}, u32[]{:S(2)}, u32[]{:S(2)}) collective-permute-start(bf16[128,512]{1,0:T(8,128)(2,1)S(1)} %collective-permute-done.16.across), channel_id=1, source_target_pairs={{0,1},{1,0},{2,3},{3,2},{4,5},{5,4},{6,7},{7,6},{8,9},{9,8},{10,11... | collective-permute-start | bytes 393224 | tf_op jit(solution)/shard_map/ppermute | solution.py:148
  279.7 4.4 %collective-permute-start.19 = (bf16[1,1,3200]{2,1,0:T(2,128)(2,1)S(1)}, bf16[1,1,3200]{2,1,0:T(2,128)(2,1)S(1)}, u32[]{:S(2)}, u32[]{:S(2)}) collective-permute-start(bf16[1,1,3200]{2,1,0:T(2,128)(2,1)S(1)} %fusion.53), channel_id=1, source_target_pairs={{0,384},{128,0},{256,128},{384,256},{1,385},{129,1},{257,129},{385... | collective-permute-start | bytes 19208 | tf_op jit(solution)/shard_map/ppermute | solution.py:198
Sparse Core Ops, SparseCore 0:
  195.3 59.9 reduce-scatter.3

commit v2 on v1

--- a/solution.py
+++ b/solution.py
@@ -1,3 +1,5 @@
+import functools
+
 import jax
 import jax.numpy as jnp
 import numpy as np
@@ -70,41 +72,43 @@
     rows[...] = jnp.dot(pick[...], normed, preferred_element_type=F32).astype(BF16)
 
 
-def expert_kernel(*refs):
-    rows, out = refs[0], refs[-1]
+def expert_kernel(rows, *refs):
+    weights, out = refs[:-1], refs[-1]
     flat = rows[...]
     total = None
-    for s in range(4):
-        gate_w, up_w, down_w = refs[1 + 3 * s : 4 + 3 * s]
-        gate = nt(flat, gate_w[...])
-        upval = nt(flat, up_w[...])
+    for ref in weights:
+        n = ref.shape[0] // 3
+        gate = nt(flat, ref[:n, :])
+        upval = nt(flat, ref[n : 2 * n, :])
         hidden = (gate * jax.nn.sigmoid(gate) * upval).astype(BF16)
-        made = jnp.dot(hidden, down_w[...], preferred_element_type=F32)
+        made = jnp.dot(hidden, ref[2 * n :, :], preferred_element_type=F32)
         total = made if total is None else total + made
     out[...] = total.astype(BF16)
 
 
-def combine_kernel(where, high, low, made, *pieces):
+def combine_kernel(where, toks, high, low, made, *pieces):
     n = len(pieces)
     cols = made.shape[1] // n
     for k in range(n):
         q = lax.rem(where[0] + k, n)
-        part = made[:, pl.ds(pl.multiple_of(q * cols, cols), cols)]
+        block = pl.ds(pl.multiple_of(q * cols, cols), cols)
+        part = made[:, block]
         summed = jnp.dot(high[...], part, preferred_element_type=F32)
         summed += jnp.dot(low[...], part, preferred_element_type=F32)
+        if k == 0:
+            summed += toks[:, block].astype(F32)
         pieces[k][...] = summed.astype(BF16)
 
 
-def layer_kernel(where, toks, *refs):
+def layer_kernel(*refs):
     pieces, out = refs[:-1], refs[-1]
-    cols = out.shape[1]
-    total = toks[:, pl.ds(pl.multiple_of(where[1] * cols, cols), cols)].astype(F32)
-    for piece in pieces:
+    total = pieces[0][...].astype(F32)
+    for piece in pieces[1:]:
         total += piece[...].astype(F32)
     out[...] = total.astype(BF16)
 
 
-def join_kernel(where, own, across, other, other_across, out):
+def join_kernel(where, own, across, other, both, out):
     cols = own.shape[1]
     t = where[1]
     yl, core = t // 2, lax.rem(t, 2)
@@ -112,14 +116,26 @@
         (own, t),
         (across, (1 - yl) * 2 + core),
         (other, yl * 2 + 1 - core),
-        (other_across, (1 - yl) * 2 + 1 - core),
+        (both, (1 - yl) * 2 + 1 - core),
     ):
         out[:, pl.ds(pl.multiple_of(quarter * cols, cols), cols)] = ref[...]
 
 
-def rms_scale(values, gain):
-    wide = values.astype(F32)
-    return wide * lax.rsqrt(jnp.mean(wide * wide, axis=-1, keepdims=True) + 1e-06) * gain
+def image_kernel(n_z, where, rows, gain, first, second, mine, theirs):
+    n, dv = rows.shape[0], gain.shape[1]
+    wide = rows[:, :dv].astype(F32)
+    scale = lax.rsqrt(jnp.mean(wide * wide, axis=-1, keepdims=True) + 1e-06)
+    normed = (wide * scale * gain[...]).astype(BF16)
+    made = nt(normed, first[...])
+    hidden = (0.5 * made * (1.0 + lax.erf(made * np.float32(0.5**0.5)))).astype(BF16)
+    core = lax.rem(where[1], 2)
+    at = lax.broadcasted_iota(jnp.int32, (n // 2, n), 0)
+    column = lax.broadcasted_iota(jnp.int32, (n // 2, n), 1)
+    for out, side in ((mine, core), (theirs, 1 - core)):
+        source = lax.rem(at, n_z) * (n // n_z) + at // n_z * 2 + side
+        order = jnp.where(column == source, 1.0, 0.0).astype(BF16)
+        half = jnp.dot(order, hidden, preferred_element_type=F32).astype(BF16)
+        out[...] = jnp.dot(half, second[...], preferred_element_type=F32).astype(out.dtype)
 
 
 def body(
@@ -137,7 +153,8 @@
     layer_scale,
 ):
     n_pp, n_yh, n_z = (lax.axis_size(a) for a in ("pp", "yh", "z"))
-    n_tp = 4
+    n_tp = lax.axis_size("yl") * lax.axis_size("core")
+    n_square = n_yh * n_tp
     square = ("yh", "yl", "core")
     where = jnp.stack([lax.axis_index("yh"), lax.axis_index(("yl", "core"))]).astype(jnp.int32)
 
@@ -145,18 +162,28 @@
         return lax.ppermute(value, square, [(a * n_tp + b, b * n_tp + a) for a in range(n_yh) for b in range(n_tp)])
 
     def flipped(value, axis):
-        return lax.ppermute(value, axis, [(0, 1), (1, 0)])
+        n = lax.axis_size(axis)
+        return lax.ppermute(value, axis, [(i, n - 1 - i) for i in range(n)])
+
+    def exchanged(value, axis):
+        return lax.all_to_all(value, axis, split_axis=0, concat_axis=0, tiled=True)
+
+    own = jnp.concatenate([w_gate[0, 0].T, w_up[0, 0].T, w_down[0, 0]], axis=0)
+    across = flipped(own, "yl")
+    other = flipped(own, "core")
 
     tokens = trunk_in[0]
-    width = tokens.shape[1]
-    toks = tokens.shape[0]
-    meta = jnp.concatenate([expert_ids[0].T.astype(F32), gate_scores[0].T], axis=0)
-    meta = swapped(meta)
+    toks, width = tokens.shape
     sent = swapped(tokens)
-
-    own = [w_gate[0, 0].T, w_up[0, 0].T, w_down[0, 0]]
-    across = [flipped(w, "yl") for w in own]
-    other = [flipped(w, "core") for w in own]
+    meta = swapped(jnp.concatenate([expert_ids[0].T.astype(F32), gate_scores[0].T], axis=0))
+
+    image = image_in[0]
+    dv = image.shape[1]
+    image_wide, meta = lax.optimization_barrier((image.astype(F32), meta))
+    ring = exchanged(jnp.broadcast_to(image_wide[None], (n_square, 1, dv)), square)
+    ring, sent = lax.optimization_barrier((ring, sent))
+    ring = jnp.pad(ring.reshape(n_square, dv).astype(BF16), ((0, 0), (0, -dv % 1024)))
+    all_rows = lax.all_gather(ring, "z", axis=0, tiled=True)
 
     n_rows = n_z * CAP
     pick, high, low = call(
@@ -167,55 +194,54 @@
     rows = call(pack_kernel, shaped((n_rows, width)), flops=2 * n_rows * toks * width, moved=2 * n_rows * width)(
         pick, sent, trunk_gain
     )
-
-    image = image_in[0]
-    image_normed = rms_scale(image, image_gain[0]).astype(BF16)
-    column = lax.all_gather(image_normed, "z", axis=0, tiled=True)
-    all_rows = lax.all_gather(column, square, axis=0, tiled=True)
-
-    def over_z(value):
-        return lax.all_to_all(value.reshape(n_z, CAP, width), "z", split_axis=0, concat_axis=0, tiled=True).reshape(
-            n_rows, width
-        )
-
-    arrived = over_z(rows)
-    other_across = [flipped(w, "core") for w in across]
+    arrived = exchanged(rows.reshape(n_z, CAP, width), "z").reshape(n_rows, width)
+    n_image = n_z * n_square
+    mine, theirs = call(
+        functools.partial(image_kernel, n_z),
+        (shaped((n_image // 2, dv), F32), shaped((n_image // 2, dv))),
+        scalars=1,
+        flops=4 * n_image * dv * 100,
+        moved=4 * n_image * dv,
+    )(where, all_rows, image_gain, fc_in[0].T, fc_out[0])
+    across, arrived, theirs = lax.optimization_barrier((across, arrived, theirs))
+    both = flipped(across, "core")
+    chip = (mine + flipped(theirs, "core").astype(F32)).reshape(n_square // 2, n_z, dv)
+    both, chip = lax.optimization_barrier((both, chip))
+    column = lax.psum_scatter(chip, ("yh", "yl"), scatter_dimension=0, tiled=True)[0]
     made = call(
         expert_kernel,
         shaped((n_rows, width)),
         flops=6 * n_rows * width * 768,
         moved=12 * 192 * width * 2,
-    )(arrived, *own, *across, *other, *other_across)
-    returned = over_z(made)
-
-    hidden = jax.nn.gelu(jnp.dot(all_rows, fc_in[0], preferred_element_type=F32), approximate=False).astype(BF16)
-    part = jnp.dot(hidden, fc_out[0], preferred_element_type=F32).astype(BF16)
-    part = part.reshape(n_yh * n_tp, n_z, part.shape[1])
-    column_sum = lax.psum_scatter(part, square, scatter_dimension=0, tiled=True)[0]
-    spread = lax.all_to_all(column_sum.astype(F32)[:, None, :], "z", split_axis=0, concat_axis=0, tiled=True)
-    summed = jnp.sum(spread, axis=0)
-    encoded = (image.astype(F32) + layer_scale[0] * summed).astype(BF16)
-    image_out = lax.ppermute(encoded[None], "pp", [(s, (s - 1) % n_pp) for s in range(n_pp)])
+    )(arrived, own, other, across, both)
+    returned = exchanged(made.reshape(n_z, CAP, width), "z").reshape(n_rows, width)
 
     quarter = width // n_tp
     pieces = call(combine_kernel, tuple(shaped((toks, quarter)) for _ in range(n_tp)), scalars=1, flops=4 * n_rows * toks * width)(
-        where, high, low, returned
+        where, sent, high, low, returned
     )
     pieces = [
         lax.ppermute(
             piece,
-            square,
-            [(a * n_tp + b, b * n_tp + (a + k) % n_tp) for a in range(n_yh) for b in range(n_tp)],
+            ("pp",) + square,
+            [
+                (s * n_square + a * n_tp + b, (s + 1) % n_pp * n_square + b * n_tp + (a + k) % n_tp)
+                for s in range(n_pp)
+                for a in range(n_yh)
+                for b in range(n_tp)
+            ],
         )
         for k, piece in enumerate(pieces)
     ]
-    layer = call(layer_kernel, shaped((toks, quarter)), scalars=1)(where, tokens, *pieces)
-    here = lax.ppermute(layer, "pp", [(s, (s + 1) % n_pp) for s in range(n_pp)])
-    there = lax.ppermute(
-        layer, ("pp", "yl"), [(s * 2 + y, ((s + 1) % n_pp) * 2 + 1 - y) for s in range(n_pp) for y in range(2)]
-    )
-    here_other, there_other = flipped(here, "core"), flipped(there, "core")
-    trunk_out = call(join_kernel, shaped((toks, width)), scalars=1)(where, here, there, here_other, there_other)
+    column, pieces = lax.optimization_barrier((column, pieces))
+    summed = jnp.sum(exchanged(column[:, None, :], "z"), axis=0)
+    encoded = (image.astype(F32) + layer_scale[0] * summed).astype(BF16)
+    image_out = lax.ppermute(encoded[None], "pp", [(s, (s - 1) % n_pp) for s in range(n_pp)])
+
+    layer = call(layer_kernel, shaped((toks, quarter)))(*pieces)
+    trunk_out = call(join_kernel, shaped((toks, width)), scalars=1)(
+        where, layer, flipped(layer, "yl"), flipped(layer, "core"), flipped(layer, ("yl", "core"))
+    )
     return (trunk_out[None], image_out)
 
 

time: 294 us -> 227 us (0.77)
  blocking collectives: 70.9 us -> 0 us
  starting transfers between devices: 126 us -> 77.5 us
  waiting for transfers between devices: 56.5 us -> 95.9 us
  local copies, waits for them, and re-layouts: 4.1 us -> 16.4 us
  other arithmetic: 3.02 us -> 7.52 us
  matrix products: 3.28 us -> 0 us
    all_gather x2 -> x0, blocking collectives: 70.9 us -> none  [the longest x1 44.1 us: body(): column = lax.all_gather(image_normed, 'z', axis=0, tiled=True)]
    ppermute x17 -> x11, starting transfers between devices: 92.3 us -> 39.7 us  [the longest x7 21.2 us: flipped(): return lax.ppermute(value, axis, [(i, n - 1 - i) for i in range(n)])]
    all_gather x0 -> x1, waiting for transfers between devices: none -> 46.6 us  [body(): all_rows = lax.all_gather(ring, 'z', axis=0, tiled=True)]
    unnamed x2 -> x3, waiting for transfers between devices: 43.8 us -> 0.73 us
    all_to_all x3 -> x4, waiting for transfers between devices: 1.91 us -> 34.7 us  [exchanged(): return lax.all_to_all(value, axis, split_axis=0, concat_axis=0, tiled=True)]
    ppermute x17 -> x11, waiting for transfers between devices: 3.2 us -> 13.9 us  [the longest x4 8.3 us: body(): lax.ppermute(piece, ('pp',) + square, [(s * n_square + a * n_tp + b, (s +...]
    unnamed x24 -> x36, local copies, waits for them, and re-layouts: 3.35 us -> 11.7 us
    ppermute x2, waiting for transfers between devices: 5.33 us -> 0.01 us  [swapped(): lax.ppermute(value, square, [(a * n_tp + b, b * n_tp + a) for a in range(...]
  transfers between devices with their start and end apart: 24 -> 20, of which waited for: 8 -> 6; matrix products, arithmetic and copies ran while one was open for 2% -> 4% of each run, Pallas kernels for 1% -> 3%
where the time goes in v2:
time: 227 us; the launch traced here: 226 us
  waiting for transfers between devices  95.9 us (42%)
  starting transfers between devices  77.5 us (34%)
  local copies, waits for them, and re-layouts  16.4 us (7%)
  between operations  14.4 us (6%)
  Pallas kernels  14.2 us (6%)
  other arithmetic  7.52 us (3%)
    all_gather x1, waiting for transfers between devices, body(): all_rows = lax.all_gather(ring, 'z', axis=0, tiled=True)  46.6 us
    all_to_all x4, waiting for transfers between devices, exchanged(): return lax.all_to_all(value, axis, split_axis=0, concat_axis=0, tiled=True)  34.7 us
    all_to_all x4, starting transfers between devices, exchanged(): return lax.all_to_all(value, axis, split_axis=0, concat_axis=0, tiled=True)  27.7 us
    ppermute x7, starting transfers between devices, flipped(): return lax.ppermute(value, axis, [(i, n - 1 - i) for i in range(n)])  21.2 us
    ppermute x4, starting transfers between devices, body(): lax.ppermute(piece, ('pp',) + square, [(s * n_square + a * n_tp + b, (s +...  18.6 us
    pallas_call x7, Pallas kernels, run(): pl.pallas_call(kernel, out_shape=outs, in_specs=specs, out_specs=jax.tree...  14.2 us
    unnamed x36, local copies, waits for them, and re-layouts  11.7 us
    ppermute x4, waiting for transfers between devices, body(): lax.ppermute(piece, ('pp',) + square, [(s * n_square + a * n_tp + b, (s +...  8.3 us
  transfers between devices with their start and end apart: 20, of which 6 were waited for; matrix products, arithmetic and copies ran while one was open for 4% of the time, Pallas kernels for 3%

profile of v2, /device:TPU:1, one launch (start us, length us, event | category | flops | bytes accessed | tf_op | source)
XLA Modules:
  0.0 225.9 jit_solution(11645419139624633664)
XLA Ops:
  7.2 0.7 convert_bitcast_fusion.1
  7.9 0.7 pad_maximum_fusion.1
  8.5 5.6 %collective-permute-start.1 = (f32[16,128]{1,0:T(8,128)S(1)}, f32[16,128]{1,0:T(8,128)S(1)}, u32[]{:S(2)}, u32[]{:S(2)}) collective-permute-start(f32[16,128]{1,0:T(8,128)S(1)} %pad_maximum_fusion.1), channel_id=1, source_target_pairs={{0,0},{1,32},{2,64},{3,96},{32,1},{33,33},{34,65},{35,97},{64,2},{... | collective-permute-start | bytes 24584 | tf_op jit(solution)/shard_map/ppermute | solution.py:162
  14.1 1.9 collective-permute-start.2
  16.1 0.7 bitcast_convert_fusion
  16.9 0.1 broadcast_in_dim.18
  17.0 0.5 broadcast.4
  17.5 1.2 reduce.2
  18.7 0.8 reshape.48
  19.6 9.9 %all-to-all-start = ((bf16[16,2,1600]{2,1,0:T(2,128)(2,1)}), bf16[16,2,1600]{2,1,0:T(2,128)(2,1)S(1)}, u32[]{:S(2)}, u32[]{:S(2)}) async-start(bf16[16,2,1600]{2,1,0:T(2,128)(2,1)} %reshape.48), calls=%async_computation | async-start | bytes 212992 | tf_op jit(solution)/shard_map/all_to_all | solution.py:169
  29.5 1.8 pad_maximum_fusion.refs_0_
  31.3 3.3 %collective-permute-start = (bf16[576,2048]{1,0:T(8,128)(2,1)S(1)}, bf16[576,2048]{1,0:T(8,128)(2,1)}, u32[]{:S(2)}, u32[]{:S(2)}) collective-permute-start(bf16[576,2048]{1,0:T(8,128)(2,1)S(1)} %pad_maximum_fusion.refs_0_), channel_id=1, source_target_pairs={{0,2},{2,0},{1,3},{3,1},{4,6},{6,4},{5,7},{7,5},{8,10},{10,8},{9,1... | collective-permute-start | bytes 7077896 | tf_op jit(solution)/shard_map/ppermute | solution.py:166
  34.6 0.1 pad_add_fusion.where
  34.6 0.8 shard_map.131
  35.5 0.6 copy-done.6
  36.1 0.6 copy-done.8
  36.7 0.6 copy-done.10
  37.4 0.7 all-to-all-done
  38.1 0.8 reshape.49
  38.9 0.9 copy-done.11
  39.8 0.7 copy-done.13
  40.5 0.7 shard_map.132
  41.2 1.1 copy-done.1
  42.2 10.0 %all-to-all-start.1 = ((bf16[8,40,2048]{2,1,0:T(8,128)(2,1)}), bf16[8,40,2048]{2,1,0:T(8,128)(2,1)}, u32[]{:S(2)}, u32[]{:S(2)}) async-start(bf16[8,40,2048]{2,1,0:T(8,128)(2,1)} %bitcast.42), calls=%async_computation.1 | async-start | bytes 2621440 | tf_op jit(solution)/shard_map/all_to_all | solution.py:169
  52.3 0.0 all-gather.2.cloned.1.call-start
  52.3 0.9 copy.19
  53.3 0.7 pad.4
  53.9 0.0 all-gather.2.cloned.1.call-update
  54.0 46.6 %all-gather.2.cloned.1.call-done.rows = bf16[128,4096]{1,0:T(8,128)(2,1)} async-done(((bf16[16,4096]{1,0:T(8,128)(2,1)}), bf16[128,4096]{1,0:T(8,128)(2,1)}) %all-gather.2.cloned.1.call-update) | async-done | bytes 1048592 | tf_op jit(solution)/shard_map/all_gather | solution.py:186
  100.6 1.2 copy-done.2
  101.8 1.1 copy-done.5
  102.9 0.7 copy-done.12
  103.6 2.1 shard_map.133
  105.7 0.9 copy-done.3
  106.6 0.7 copy-done.14
  107.3 6.0 %collective-permute-start.3 = (bf16[576,2048]{1,0:T(8,128)(2,1)}, bf16[576,2048]{1,0:T(8,128)(2,1)}, u32[]{:S(2)}, u32[]{:S(2)}) collective-permute-start(bf16[576,2048]{1,0:T(8,128)(2,1)} %collective-permute-done.refs_2_), channel_id=1, source_target_pairs={{0,1},{1,0},{2,3},{3,2},{4,5},{5,4},{6,7},{7,6},{8,9},{9,8},{10,11... | collective-permute-start | bytes 7077896 | tf_op jit(solution)/shard_map/ppermute | solution.py:166
  113.3 1.9 collective-permute-start.5
  115.2 2.4 %collective-permute-start.4 = (bf16[64,3200]{1,0:T(8,128)(2,1)}, bf16[64,3200]{1,0:T(8,128)(2,1)S(1)}, u32[]{:S(2)}, u32[]{:S(2)}) collective-permute-start(bf16[64,3200]{1,0:T(8,128)(2,1)} %copy-done.14), channel_id=1, source_target_pairs={{0,1},{1,0},{2,3},{3,2},{4,5},{5,4},{6,7},{7,6},{8,9},{9,8},{10,11... | collective-permute-start | bytes 1228808 | tf_op jit(solution)/shard_map/ppermute | solution.py:166
  117.6 4.0 %collective-permute-done.4 = bf16[64,3200]{1,0:T(8,128)(2,1)S(1)} collective-permute-done((bf16[64,3200]{1,0:T(8,128)(2,1)}, bf16[64,3200]{1,0:T(8,128)(2,1)S(1)}, u32[]{:S(2)}, u32[]{:S(2)}) %collective-permute-start.4) | collective-permute-done | bytes 409632 | tf_op jit(solution)/shard_map/ppermute | solution.py:166
  121.6 2.2 add_bitcast_fusion
  123.8 7.9 %shard_map.134 = bf16[320,2048]{1,0:T(8,128)(2,1)S(1)} custom-call(bf16[320,2048]{1,0:T(8,128)(2,1)} %bitcast.14.rows, bf16[576,2048]{1,0:T(8,128)(2,1)S(1)} %pad_maximum_fusion.refs_0_, bf16[576,2048]{1,0:T(8,128)(2,1)} %collective-permute-done.5.refs_1_, bf16[576,2048]{1,0:T(8,128)(2,1)} %collective-permute-done.refs_2_, ...), custom_call_target="tpu_custom_call" | custom-call | flops 3019898880 | bytes 9437184 | tf_op jit(solution)/shard_map/pallas_call | solution.py:22
  131.7 1.1 copy-done
  132.8 4.3 %all-to-all-start.2 = ((bf16[8,40,2048]{2,1,0:T(8,128)(2,1)}), bf16[8,40,2048]{2,1,0:T(8,128)(2,1)S(1)}, u32[]{:S(2)}, u32[]{:S(2)}) async-start(bf16[8,40,2048]{2,1,0:T(8,128)(2,1)} %bitcast.41), calls=%async_computation.2 | async-start | bytes 2621440 | tf_op jit(solution)/shard_map/all_to_all | solution.py:169
  137.1 0.0 reduce-scatter.4.cloned.1.call-start
  137.2 0.7 reduce-scatter.4.cloned.1.call-update
  137.9 34.0 %all-to-all-done.2 = bf16[8,40,2048]{2,1,0:T(8,128)(2,1)S(1)} async-done(((bf16[8,40,2048]{2,1,0:T(8,128)(2,1)}), bf16[8,40,2048]{2,1,0:T(8,128)(2,1)S(1)}, u32[]{:S(2)}, u32[]{:S(2)}) %all-to-all-start.2) | async-done | bytes 1310752 | tf_op jit(solution)/shard_map/all_to_all | solution.py:169
  171.9 1.3 shard_map.135
  173.2 5.5 %collective-permute-start.6 = (bf16[128,512]{1,0:T(8,128)(2,1)S(1)}, bf16[128,512]{1,0:T(8,128)(2,1)S(1)}, u32[]{:S(2)}, u32[]{:S(2)}) collective-permute-start(bf16[128,512]{1,0:T(8,128)(2,1)S(1)} %get-tuple-element.39), channel_id=1, source_target_pairs={{0,128},{1,160},{2,192},{3,224},{32,129},{33,161},{34,193},{35,225... | collective-permute-start | bytes 393224 | tf_op jit(solution)/shard_map/ppermute | solution.py:224
  178.7 2.5 %collective-permute-start.7 = (bf16[128,512]{1,0:T(8,128)(2,1)S(1)}, bf16[128,512]{1,0:T(8,128)(2,1)S(1)}, u32[]{:S(2)}, u32[]{:S(2)}) collective-permute-start(bf16[128,512]{1,0:T(8,128)(2,1)S(1)} %get-tuple-element.40), channel_id=1, source_target_pairs={{0,129},{1,161},{2,193},{3,225},{32,130},{33,162},{34,194},{35,226... | collective-permute-start | bytes 393224 | tf_op jit(solution)/shard_map/ppermute | solution.py:224
  181.2 6.0 %collective-permute-start.8 = (bf16[128,512]{1,0:T(8,128)(2,1)S(1)}, bf16[128,512]{1,0:T(8,128)(2,1)S(1)}, u32[]{:S(2)}, u32[]{:S(2)}) collective-permute-start(bf16[128,512]{1,0:T(8,128)(2,1)S(1)} %get-tuple-element.41), channel_id=1, source_target_pairs={{0,130},{1,162},{2,194},{3,226},{32,131},{33,163},{34,195},{35,227... | collective-permute-start | bytes 393224 | tf_op jit(solution)/shard_map/ppermute | solution.py:224
  187.3 4.5 %collective-permute-start.9 = (bf16[128,512]{1,0:T(8,128)(2,1)S(1)}, bf16[128,512]{1,0:T(8,128)(2,1)S(1)}, u32[]{:S(2)}, u32[]{:S(2)}) collective-permute-start(bf16[128,512]{1,0:T(8,128)(2,1)S(1)} %get-tuple-element.42), channel_id=1, source_target_pairs={{0,131},{1,163},{2,195},{3,227},{32,128},{33,160},{34,192},{35,224... | collective-permute-start | bytes 393224 | tf_op jit(solution)/shard_map/ppermute | solution.py:224
  191.8 0.0 reduce-scatter.4.cloned.1.call-done
  191.9 8.3 %collective-permute-done.9.refs_3_ = bf16[128,512]{1,0:T(8,128)(2,1)S(1)} collective-permute-done((bf16[128,512]{1,0:T(8,128)(2,1)S(1)}, bf16[128,512]{1,0:T(8,128)(2,1)S(1)}, u32[]{:S(2)}, u32[]{:S(2)}) %collective-permute-start.9) | collective-permute-done | bytes 131104 | tf_op jit(solution)/shard_map/ppermute | solution.py:224
  200.2 1.6 copy.15
  201.8 3.4 %all-to-all-start.3 = ((f32[8,1,3200]{2,1,0:T(1,128)}), f32[8,1,3200]{2,1,0:T(1,128)S(1)}, u32[]{:S(2)}, u32[]{:S(2)}) async-start(f32[8,1,3200]{2,1,0:T(1,128)} %copy.15), calls=%async_computation.3 | async-start | bytes 204800 | tf_op jit(solution)/shard_map/all_to_all | solution.py:169
  205.2 0.1 shard_map.136.own
  205.2 2.3 %collective-permute-start.10 = (bf16[128,512]{1,0:T(8,128)(2,1)S(1)}, bf16[128,512]{1,0:T(8,128)(2,1)S(1)}, u32[]{:S(2)}, u32[]{:S(2)}) collective-permute-start(bf16[128,512]{1,0:T(8,128)(2,1)S(1)} %shard_map.136.own), channel_id=1, source_target_pairs={{0,2},{2,0},{1,3},{3,1},{4,6},{6,4},{5,7},{7,5},{8,10},{10,8},{9,1... | collective-permute-start | bytes 393224 | tf_op jit(solution)/shard_map/ppermute | solution.py:166
  207.6 1.9 collective-permute-start.11
  209.5 3.4 %collective-permute-start.12 = (bf16[128,512]{1,0:T(8,128)(2,1)S(1)}, bf16[128,512]{1,0:T(8,128)(2,1)S(1)}, u32[]{:S(2)}, u32[]{:S(2)}) collective-permute-start(bf16[128,512]{1,0:T(8,128)(2,1)S(1)} %shard_map.136.own), channel_id=1, source_target_pairs={{0,3},{1,2},{2,1},{3,0},{4,7},{5,6},{6,5},{7,4},{8,11},{9,10},{10,... | collective-permute-start | bytes 393224 | tf_op jit(solution)/shard_map/ppermute | solution.py:166
  212.9 0.1 reduce_sum.11
  213.0 2.5 %collective-permute-start.13 = (bf16[1,1,3200]{2,1,0:T(2,128)(2,1)S(1)}, bf16[1,1,3200]{2,1,0:T(2,128)(2,1)S(1)}, u32[]{:S(2)}, u32[]{:S(2)}) collective-permute-start(bf16[1,1,3200]{2,1,0:T(2,128)(2,1)S(1)} %convert_bitcast_fusion), channel_id=1, source_target_pairs={{0,384},{128,0},{256,128},{384,256},{1,385},{129,1},{257,129},{385... | collective-permute-start | bytes 19208 | tf_op jit(solution)/shard_map/ppermute | solution.py:239
  215.5 1.6 collective-permute-done.12.both
  217.1 1.4 shard_map.137
  218.5 0.6 copy.21
  (37 shorter events, 0.2 us)
Async XLA Ops:
  8.5 8.3 %collective-permute-start.1 = (f32[16,128]{1,0:T(8,128)S(1)}, f32[16,128]{1,0:T(8,128)S(1)}, u32[]{:S(2)}, u32[]{:S(2)}) collective-permute-start(f32[16,128]{1,0:T(8,128)S(1)} %pad_maximum_fusion.1), channel_id=1, source_target_pairs={{0,0},{1,32},{2,64},{3,96},{32,1},{33,33},{34,65},{35,97},{64,2},{... | collective-permute-start | bytes 24584 | tf_op jit(solution)/shard_map/ppermute | solution.py:162
  14.1 24.8 %collective-permute-start.2 = (bf16[128,2048]{1,0:T(8,128)(2,1)}, bf16[128,2048]{1,0:T(8,128)(2,1)S(1)}, u32[]{:S(2)}, u32[]{:S(2)}) collective-permute-start(bf16[128,2048]{1,0:T(8,128)(2,1)} %bitcast.53), channel_id=1, source_target_pairs={{0,0},{1,32},{2,64},{3,96},{32,1},{33,33},{34,65},{35,97},{64,2},{... | collective-permute-start | bytes 1572872 | tf_op jit(solution)/shard_map/ppermute | solution.py:162
  19.6 18.5 %all-to-all-start = ((bf16[16,2,1600]{2,1,0:T(2,128)(2,1)}), bf16[16,2,1600]{2,1,0:T(2,128)(2,1)S(1)}, u32[]{:S(2)}, u32[]{:S(2)}) async-start(bf16[16,2,1600]{2,1,0:T(2,128)(2,1)} %reshape.48), calls=%async_computation | async-start | bytes 212992 | tf_op jit(solution)/shard_map/all_to_all | solution.py:169
  31.3 76.0 %collective-permute-start = (bf16[576,2048]{1,0:T(8,128)(2,1)S(1)}, bf16[576,2048]{1,0:T(8,128)(2,1)}, u32[]{:S(2)}, u32[]{:S(2)}) collective-permute-start(bf16[576,2048]{1,0:T(8,128)(2,1)S(1)} %pad_maximum_fusion.refs_0_), channel_id=1, source_target_pairs={{0,2},{2,0},{1,3},{3,1},{4,6},{6,4},{5,7},{7,5},{8,10},{10,8},{9,1... | collective-permute-start | bytes 7077896 | tf_op jit(solution)/shard_map/ppermute | solution.py:166
  35.5 0.6 copy-start.6
  36.1 0.6 copy-start.8
  36.7 0.6 copy-start.10
  38.9 0.9 copy-start.11
  39.8 0.7 copy-start.13
  40.5 60.1 %copy-start.4 = (bf16[1,3200,100]{1,2,0:T(8,128)(2,1)S(1)}, bf16[1,3200,100]{1,2,0:T(8,128)(2,1)}, u32[]{:S(2)}) copy-start(bf16[1,3200,100]{1,2,0:T(8,128)(2,1)} %param.21) | copy-start | bytes 1920004
  41.2 1.1 copy-start.1
  42.2 65.1 %all-to-all-start.1 = ((bf16[8,40,2048]{2,1,0:T(8,128)(2,1)}), bf16[8,40,2048]{2,1,0:T(8,128)(2,1)}, u32[]{:S(2)}, u32[]{:S(2)}) async-start(bf16[8,40,2048]{2,1,0:T(8,128)(2,1)} %bitcast.42), calls=%async_computation.1 | async-start | bytes 2621440 | tf_op jit(solution)/shard_map/all_to_all | solution.py:169
  52.3 48.3 %all-gather.2.cloned.1.call-start = ((), (), s32[]{:S(2)}) async-start(), calls=%async_computation.5 | async-start | bytes 1179648 | tf_op jit(solution)/shard_map/all_gather | solution.py:186
  100.6 1.2 copy-start.2
  101.8 1.1 copy-start.5
  102.9 0.7 copy-start.12
  105.7 0.9 copy-start.3
  106.5 0.8 copy-start.14
  107.3 16.4 %collective-permute-start.3 = (bf16[576,2048]{1,0:T(8,128)(2,1)}, bf16[576,2048]{1,0:T(8,128)(2,1)}, u32[]{:S(2)}, u32[]{:S(2)}) collective-permute-start(bf16[576,2048]{1,0:T(8,128)(2,1)} %collective-permute-done.refs_2_), channel_id=1, source_target_pairs={{0,1},{1,0},{2,3},{3,2},{4,5},{5,4},{6,7},{7,6},{8,9},{9,8},{10,11... | collective-permute-start | bytes 7077896 | tf_op jit(solution)/shard_map/ppermute | solution.py:166
  113.3 10.5 %collective-permute-start.5 = (bf16[576,2048]{1,0:T(8,128)(2,1)S(1)}, bf16[576,2048]{1,0:T(8,128)(2,1)}, u32[]{:S(2)}, u32[]{:S(2)}) collective-permute-start(bf16[576,2048]{1,0:T(8,128)(2,1)S(1)} %pad_maximum_fusion.refs_0_), channel_id=1, source_target_pairs={{0,1},{1,0},{2,3},{3,2},{4,5},{5,4},{6,7},{7,6},{8,9},{9,8},{10,11... | collective-permute-start | bytes 7077896 | tf_op jit(solution)/shard_map/ppermute | solution.py:166
  115.2 6.4 %collective-permute-start.4 = (bf16[64,3200]{1,0:T(8,128)(2,1)}, bf16[64,3200]{1,0:T(8,128)(2,1)S(1)}, u32[]{:S(2)}, u32[]{:S(2)}) collective-permute-start(bf16[64,3200]{1,0:T(8,128)(2,1)} %copy-done.14), channel_id=1, source_target_pairs={{0,1},{1,0},{2,3},{3,2},{4,5},{5,4},{6,7},{7,6},{8,9},{9,8},{10,11... | collective-permute-start | bytes 1228808 | tf_op jit(solution)/shard_map/ppermute | solution.py:166
  131.7 1.1 copy-start
  132.8 39.2 %copy-start.7 = (bf16[128,320]{1,0:T(8,128)(2,1)S(1)}, bf16[128,320]{1,0:T(8,128)(2,1)}, u32[]{:S(2)}) copy-start(bf16[128,320]{1,0:T(8,128)(2,1)} %copy-done.6) | copy-start | bytes 245764
  132.8 39.2 %copy-start.9 = (bf16[128,320]{1,0:T(8,128)(2,1)S(1)}, bf16[128,320]{1,0:T(8,128)(2,1)}, u32[]{:S(2)}) copy-start(bf16[128,320]{1,0:T(8,128)(2,1)} %copy-done.8) | copy-start | bytes 245764
  132.8 39.2 %all-to-all-start.2 = ((bf16[8,40,2048]{2,1,0:T(8,128)(2,1)}), bf16[8,40,2048]{2,1,0:T(8,128)(2,1)S(1)}, u32[]{:S(2)}, u32[]{:S(2)}) async-start(bf16[8,40,2048]{2,1,0:T(8,128)(2,1)} %bitcast.41), calls=%async_computation.2 | async-start | bytes 2621440 | tf_op jit(solution)/shard_map/all_to_all | solution.py:169
  137.1 75.8 %copy-start.15 = (bf16[1,1,3200]{2,1,0:T(2,128)(2,1)S(1)}, bf16[1,1,3200]{2,1,0:T(2,128)(2,1)}, u32[]{:S(2)}) copy-start(bf16[1,1,3200]{2,1,0:T(2,128)(2,1)} %param.19) | copy-start | bytes 19204
  137.1 75.8 %copy-start.16 = (f32[1,3200]{1,0:T(1,128)S(1)}, f32[1,3200]{1,0:T(1,128)}, u32[]{:S(2)}) copy-start(f32[1,3200]{1,0:T(1,128)} %param.23) | copy-start | bytes 38404
  137.1 54.7 %reduce-scatter.4.cloned.1.call-start = ((), (), s32[]{:S(2)}) async-start(), calls=%async_computation.6 | async-start | bytes 921600
  173.2 18.6 %collective-permute-start.6 = (bf16[128,512]{1,0:T(8,128)(2,1)S(1)}, bf16[128,512]{1,0:T(8,128)(2,1)S(1)}, u32[]{:S(2)}, u32[]{:S(2)}) collective-permute-start(bf16[128,512]{1,0:T(8,128)(2,1)S(1)} %get-tuple-element.39), channel_id=1, source_target_pairs={{0,128},{1,160},{2,192},{3,224},{32,129},{33,161},{34,193},{35,225... | collective-permute-start | bytes 393224 | tf_op jit(solution)/shard_map/ppermute | solution.py:224
  178.7 13.1 %collective-permute-start.7 = (bf16[128,512]{1,0:T(8,128)(2,1)S(1)}, bf16[128,512]{1,0:T(8,128)(2,1)S(1)}, u32[]{:S(2)}, u32[]{:S(2)}) collective-permute-start(bf16[128,512]{1,0:T(8,128)(2,1)S(1)} %get-tuple-element.40), channel_id=1, source_target_pairs={{0,129},{1,161},{2,193},{3,225},{32,130},{33,162},{34,194},{35,226... | collective-permute-start | bytes 393224 | tf_op jit(solution)/shard_map/ppermute | solution.py:224
  181.2 10.6 %collective-permute-start.8 = (bf16[128,512]{1,0:T(8,128)(2,1)S(1)}, bf16[128,512]{1,0:T(8,128)(2,1)S(1)}, u32[]{:S(2)}, u32[]{:S(2)}) collective-permute-start(bf16[128,512]{1,0:T(8,128)(2,1)S(1)} %get-tuple-element.41), channel_id=1, source_target_pairs={{0,130},{1,162},{2,194},{3,226},{32,131},{33,163},{34,195},{35,227... | collective-permute-start | bytes 393224 | tf_op jit(solution)/shard_map/ppermute | solution.py:224
  187.3 12.9 %collective-permute-start.9 = (bf16[128,512]{1,0:T(8,128)(2,1)S(1)}, bf16[128,512]{1,0:T(8,128)(2,1)S(1)}, u32[]{:S(2)}, u32[]{:S(2)}) collective-permute-start(bf16[128,512]{1,0:T(8,128)(2,1)S(1)} %get-tuple-element.42), channel_id=1, source_target_pairs={{0,131},{1,163},{2,195},{3,227},{32,128},{33,160},{34,192},{35,224... | collective-permute-start | bytes 393224 | tf_op jit(solution)/shard_map/ppermute | solution.py:224
  201.8 11.1 %all-to-all-start.3 = ((f32[8,1,3200]{2,1,0:T(1,128)}), f32[8,1,3200]{2,1,0:T(1,128)S(1)}, u32[]{:S(2)}, u32[]{:S(2)}) async-start(f32[8,1,3200]{2,1,0:T(1,128)} %copy.15), calls=%async_computation.3 | async-start | bytes 204800 | tf_op jit(solution)/shard_map/all_to_all | solution.py:169
  205.2 10.3 %collective-permute-start.10 = (bf16[128,512]{1,0:T(8,128)(2,1)S(1)}, bf16[128,512]{1,0:T(8,128)(2,1)S(1)}, u32[]{:S(2)}, u32[]{:S(2)}) collective-permute-start(bf16[128,512]{1,0:T(8,128)(2,1)S(1)} %shard_map.136.own), channel_id=1, source_target_pairs={{0,2},{2,0},{1,3},{3,1},{4,6},{6,4},{5,7},{7,5},{8,10},{10,8},{9,1... | collective-permute-start | bytes 393224 | tf_op jit(solution)/shard_map/ppermute | solution.py:166
  207.6 7.9 %collective-permute-start.11 = (bf16[128,512]{1,0:T(8,128)(2,1)S(1)}, bf16[128,512]{1,0:T(8,128)(2,1)S(1)}, u32[]{:S(2)}, u32[]{:S(2)}) collective-permute-start(bf16[128,512]{1,0:T(8,128)(2,1)S(1)} %shard_map.136.own), channel_id=1, source_target_pairs={{0,1},{1,0},{2,3},{3,2},{4,5},{5,4},{6,7},{7,6},{8,9},{9,8},{10,11... | collective-permute-start | bytes 393224 | tf_op jit(solution)/shard_map/ppermute | solution.py:166
  209.5 7.6 %collective-permute-start.12 = (bf16[128,512]{1,0:T(8,128)(2,1)S(1)}, bf16[128,512]{1,0:T(8,128)(2,1)S(1)}, u32[]{:S(2)}, u32[]{:S(2)}) collective-permute-start(bf16[128,512]{1,0:T(8,128)(2,1)S(1)} %shard_map.136.own), channel_id=1, source_target_pairs={{0,3},{1,2},{2,1},{3,0},{4,7},{5,6},{6,5},{7,4},{8,11},{9,10},{10,... | collective-permute-start | bytes 393224 | tf_op jit(solution)/shard_map/ppermute | solution.py:166
  213.0 5.5 %collective-permute-start.13 = (bf16[1,1,3200]{2,1,0:T(2,128)(2,1)S(1)}, bf16[1,1,3200]{2,1,0:T(2,128)(2,1)S(1)}, u32[]{:S(2)}, u32[]{:S(2)}) collective-permute-start(bf16[1,1,3200]{2,1,0:T(2,128)(2,1)S(1)} %convert_bitcast_fusion), channel_id=1, source_target_pairs={{0,384},{128,0},{256,128},{384,256},{1,385},{129,1},{257,129},{385... | collective-permute-start | bytes 19208 | tf_op jit(solution)/shard_map/ppermute | solution.py:239
Sparse Core Ops, SparseCore 0:
  55.8 44.7 all-gather.1
  140.8 36.6 reduce-scatter.3

commit v3 on v2

v3 whole, which is shorter than its diff:
```python
import functools

import jax
import jax.numpy as jnp
import numpy as np
from jax import lax
from jax.experimental import pallas as pl
from jax.experimental.pallas import tpu as pltpu
from jax.sharding import Mesh, PartitionSpec as P

BF16 = jnp.bfloat16
F32 = jnp.float32
VM = pl.BlockSpec(memory_space=pltpu.VMEM)
SM = pl.BlockSpec(memory_space=pltpu.SMEM)
CAP = 40
LIMIT = 48 * 1024 * 1024


def call(kernel, outs, scalars=0, flops=0, moved=0):
    def run(*operands):
        specs = [SM] * scalars + [VM] * (len(operands) - scalars)
        return pl.pallas_call(
            kernel,
            out_shape=outs,
            in_specs=specs,
            out_specs=jax.tree.map(lambda _: VM, outs),
            compiler_params=pltpu.CompilerParams(vmem_limit_bytes=LIMIT),
            cost_estimate=pl.CostEstimate(flops=flops, bytes_accessed=moved, transcendentals=0),
        )(*operands)

    return run


def shaped(dims, kind=BF16):
    return jax.ShapeDtypeStruct(dims, kind)


def nt(a, b):
    return lax.dot_general(a, b, (((1,), (1,)), ((), ())), preferred_element_type=F32)


def table_kernel(where, meta, pick, high, low):
    rows, toks = pick.shape
    group = rows // CAP
    topk = meta.shape[0] // 2
    first = where[0] * group
    wanted = (lax.broadcasted_iota(jnp.int32, (group, toks), 0) + first).astype(F32)
    scores = meta[topk:, :]
    total = jnp.sum(scores, axis=0, keepdims=True)
    member = jnp.zeros((group, toks), F32)
    weight = jnp.zeros((group, toks), F32)
    for k in range(topk):
        same = meta[k : k + 1, :] == wanted
        member = jnp.where(same, 1.0, member)
        weight = jnp.where(same, meta[topk + k : topk + k + 1, :] / total, weight)
    earlier = lax.broadcasted_iota(jnp.int32, (toks, toks), 0) < lax.broadcasted_iota(jnp.int32, (toks, toks), 1)
    rank = jnp.dot(member.astype(BF16), earlier.astype(F32).astype(BF16), preferred_element_type=F32)
    rank = jnp.where(member > 0.5, rank, -1.0)
    slots = lax.broadcasted_iota(jnp.int32, (group, CAP, toks), 1).astype(F32)
    hit = jnp.where(rank[:, None, :] == slots, 1.0, 0.0)
    pick[...] = hit.reshape(rows, toks).astype(BF16)
    scaled = (hit * weight[:, None, :]).reshape(rows, toks).T
    top = scaled.astype(BF16)
    high[...] = top
    low[...] = (scaled - top.astype(F32)).astype(BF16)


def pack_kernel(pick, toks, gain, rows):
    wide = toks[...].astype(F32)
    scale = lax.rsqrt(jnp.mean(wide * wide, axis=-1, keepdims=True) + 1e-06)
    normed = (wide * scale * gain[...]).astype(BF16)
    rows[...] = jnp.dot(pick[...], normed, preferred_element_type=F32).astype(BF16)


def expert_kernel(rows, *refs):
    shards, out = refs[:4], refs[4]
    rows_v, gate_v, up_v, down_v, hidden_v, out_v, row_sem, in_sem, out_sem = refs[5:]
    count = shards[0].shape[0] // 3
    row_copy = pltpu.make_async_copy(rows, rows_v, row_sem)
    row_copy.start()
    copies = []
    for s, shard in enumerate(shards):
        for p, held in enumerate((gate_v, up_v, down_v)):
            copies.append(
                pltpu.make_async_copy(
                    shard.at[pl.ds(p * count, count)], held.at[pl.ds(s * count, count)], in_sem.at[3 * s + p]
                )
            )
    for p in (0, 1, 2):
        for s in range(4):
            copies[3 * s + p].start() if p < 2 else None
    for s in range(4):
        copies[3 * s + 2].start()
    row_copy.wait()
    flat = rows_v[...]
    step = 256
    seen = 0
    for c in range(4 * count // step):
        while seen * count < (c + 1) * step:
            copies[3 * seen].wait()
            copies[3 * seen + 1].wait()
            seen += 1
        block = slice(c * step, (c + 1) * step)
        gate = nt(flat, gate_v[block, :])
        upval = nt(flat, up_v[block, :])
        hidden_v[:, block] = (gate * jax.nn.sigmoid(gate) * upval).astype(BF16)
    for s in range(4):
        copies[3 * s + 2].wait()
    cols = out_v.shape[1] // 4
    leaving = []
    for j in range(4):
        block = slice(j * cols, (j + 1) * cols)
        out_v[:, block] = jnp.dot(hidden_v[...], down_v[:, block], preferred_element_type=F32).astype(BF16)
        copy = pltpu.make_async_copy(
            out_v.at[:, pl.ds(j * cols, cols)], out.at[:, pl.ds(j * cols, cols)], out_sem.at[j]
        )
        copy.start()
        leaving.append(copy)
    for copy in leaving:
        copy.wait()


def experts(rows, shards):
    n, width = rows.shape
    count = shards[0].shape[0] // 3 * 4
    anywhere = pl.BlockSpec(memory_space=pl.ANY)
    return pl.pallas_call(
        expert_kernel,
        out_shape=shaped((n, width)),
        in_specs=[anywhere] * 5,
        out_specs=pl.BlockSpec(memory_space=pltpu.HBM),
        scratch_shapes=[
            pltpu.VMEM((n, width), BF16),
            pltpu.VMEM((count, width), BF16),
            pltpu.VMEM((count, width), BF16),
            pltpu.VMEM((count, width), BF16),
            pltpu.VMEM((n, count), BF16),
            pltpu.VMEM((n, width), BF16),
            pltpu.SemaphoreType.DMA,
            pltpu.SemaphoreType.DMA((12,)),
            pltpu.SemaphoreType.DMA((4,)),
        ],
        compiler_params=pltpu.CompilerParams(vmem_limit_bytes=LIMIT),
        cost_estimate=pl.CostEstimate(flops=6 * n * width * count, bytes_accessed=6 * count * width, transcendentals=0),
    )(rows, *shards)


def combine_kernel(where, toks, high, low, made, kept, given):
    half = made.shape[1] // 2
    a = where[0]
    for out, h in ((kept, a // 2), (given, 1 - a // 2)):
        block = pl.ds(pl.multiple_of(h * half, half), half)
        part = made[:, block]
        summed = jnp.dot(high[...], part, preferred_element_type=F32)
        summed += jnp.dot(low[...], part, preferred_element_type=F32)
        if out is kept:
            summed += jnp.where(lax.rem(a, 2) == 0, toks[:, block].astype(F32), 0.0)
        out[...] = summed.astype(BF16)


def add_kernel(left, right, out):
    out[...] = (left[...].astype(F32) + right[...].astype(F32)).astype(out.dtype)


def join_kernel(where, own, across, out):
    cols = own.shape[1]
    yl = where[1] // 2
    for ref, half in ((own, yl), (across, 1 - yl)):
        out[:, pl.ds(pl.multiple_of(half * cols, cols), cols)] = ref[...]


def spread_kernel(row, out):
    wide = row[...].astype(F32)
    for i in range(out.shape[0]):
        out[i] = wide


def ring_kernel(ring, out):
    out[...] = jnp.concatenate([ring[i] for i in range(ring.shape[0])], axis=0).astype(BF16)


def pair_kernel(own, other, out):
    n = own.shape[0]
    out[:n, :] = own[...]
    out[n:, :] = other[...]


def image_kernel(sizes, where, *refs):
    groups, (gain, first, second, mine, theirs) = refs[:-5], refs[-5:]
    n_yh, n_z = sizes
    wide = jnp.concatenate([group[...] for group in groups], axis=0).astype(F32)
    n = wide.shape[0]
    scale = lax.rsqrt(jnp.mean(wide * wide, axis=-1, keepdims=True) + 1e-06)
    normed = (wide * scale * gain[...]).astype(BF16)
    made = nt(normed, first[...])
    hidden = (0.5 * made * (1.0 + lax.erf(made * np.float32(0.5**0.5)))).astype(BF16)
    yh, yl, core, z_here = where[0], where[1] // 2, lax.rem(where[1], 2), where[2]
    at = lax.broadcasted_iota(jnp.int32, (n // 2, n), 0)
    column = lax.broadcasted_iota(jnp.int32, (n // 2, n), 1)
    z = lax.rem(at, n_z)
    high = lax.rem(at // n_z + yh, n_yh)
    low = lax.rem(at // (n_z * n_yh) + yl, 2)
    apart = lax.rem(z // 2 - z_here // 2 + n_z // 2, n_z // 2)
    group = jnp.where(apart == 0, 0, jnp.where(apart == 3, 1, apart + 1))
    block = group * 2 + lax.rem(z + z_here, 2)
    for out, side in ((mine, core), (theirs, 1 - core)):
        source = ((block * n_yh + high) * 2 + low) * 2 + side
        order = jnp.where(column == source, 1.0, 0.0).astype(BF16)
        half = jnp.dot(order, hidden, preferred_element_type=F32).astype(BF16)
        out[...] = jnp.dot(half, second[...], preferred_element_type=F32).astype(out.dtype)


def fold_kernel(held, came, keep, *sends):
    total = held[...] + came[...].astype(F32)
    n = keep.shape[0]
    keep[...] = total[:n]
    for i, send in enumerate(sends):
        send[...] = total[n + i * send.shape[0] : n + (i + 1) * send.shape[0]].astype(BF16)


def column_kernel(held, *refs):
    out = refs[-1]
    total = held[...]
    for came in refs[:-1]:
        total += came[...].astype(F32)
    for i in range(out.shape[0]):
        out[i] = total[i : i + 1]


def encoded_kernel(spread, image, scale, out):
    total = spread[0]
    for i in range(1, spread.shape[0]):
        total += spread[i]
    out[...] = (image[...].astype(F32) + scale[...] * total).astype(BF16)


def body(
    trunk_in,
    expert_ids,
    gate_scores,
    trunk_gain,
    w_gate,
    w_up,
    w_down,
    image_in,
    image_gain,
    fc_in,
    fc_out,
    layer_scale,
):
    n_pp, n_yh, n_z = (lax.axis_size(a) for a in ("pp", "yh", "z"))
    n_tp = lax.axis_size("yl") * lax.axis_size("core")
    n_square = n_yh * n_tp
    square = ("yh", "yl", "core")
    where = jnp.stack([lax.axis_index("yh"), lax.axis_index(("yl", "core")), lax.axis_index("z")]).astype(jnp.int32)

    def swapped(value):
        return lax.ppermute(value, square, [(a * n_tp + b, b * n_tp + a) for a in range(n_yh) for b in range(n_tp)])

    def shifted(value, axis, by):
        n = lax.axis_size(axis)
        return lax.ppermute(value, axis, [(i, (i + by) % n) for i in range(n)])

    def exchanged(value, axis):
        return lax.all_to_all(value, axis, split_axis=0, concat_axis=0, tiled=True)

    own = jnp.concatenate([w_gate[0, 0].T, w_up[0, 0].T, w_down[0, 0]], axis=0)
    across = shifted(own, "yl", 1)
    other = shifted(own, "core", 1)

    tokens = trunk_in[0]
    toks, width = tokens.shape
    sent = swapped(tokens)
    meta = swapped(jnp.concatenate([expert_ids[0].T.astype(F32), gate_scores[0].T], axis=0))

    image = image_in[0]
    dv = image.shape[1]
    ring = exchanged(call(spread_kernel, shaped((n_square, 1, dv), F32))(image), square)
    ring = call(ring_kernel, shaped((n_square, dv)))(ring)
    ring, sent = lax.optimization_barrier((ring, sent))
    ring_beside = lax.ppermute(ring, "z", [(i, i ^ 1) for i in range(n_z)])
    pair = call(pair_kernel, shaped((2 * n_square, dv)))(ring, ring_beside)
    below, above = shifted(pair, "z", 2), shifted(pair, "z", -2)
    far = shifted(below, "z", 2)

    n_rows = n_z * CAP
    pick, high, low = call(
        table_kernel,
        (shaped((n_rows, toks)), shaped((toks, n_rows)), shaped((toks, n_rows))),
        scalars=1,
    )(where, meta)
    rows = call(pack_kernel, shaped((n_rows, width)), flops=2 * n_rows * toks * width, moved=2 * n_rows * width)(
        pick, sent, trunk_gain
    )
    arrived = exchanged(rows.reshape(n_z, CAP, width), "z").reshape(n_rows, width)
    across, arrived, above, far = lax.optimization_barrier((across, arrived, above, far))
    both = shifted(across, "core", 1)
    made = experts(arrived, (own, other, across, both))
    returned = exchanged(made.reshape(n_z, CAP, width), "z").reshape(n_rows, width)

    n_image = n_z * n_square
    mine, theirs = call(
        functools.partial(image_kernel, (n_yh, n_z)),
        (shaped((n_image // 2, dv), F32), shaped((n_image // 2, dv))),
        scalars=1,
        flops=4 * n_image * dv * 100,
        moved=4 * n_image * dv,
    )(where, pair, below, above, far, image_gain, fc_in[0].T, fc_out[0])
    mine, theirs = call(fold_kernel, (shaped((n_image // 4, dv), F32), shaped((n_image // 4, dv))))(
        mine, shifted(theirs, "core", 1)
    )
    mine, *theirs = call(
        fold_kernel, (shaped((n_z, dv), F32),) + tuple(shaped((n_z, dv)) for _ in range(n_yh - 1))
    )(mine, shifted(theirs, "yl", 1))
    column = call(column_kernel, shaped((n_z, 1, dv), F32))(
        mine, *[shifted(part, "yh", k + 1) for k, part in enumerate(theirs)]
    )

    column, returned = lax.optimization_barrier((column, returned))
    half = width // 2
    pieces = call(combine_kernel, (shaped((toks, half)), shaped((toks, half))), scalars=1, flops=4 * n_rows * toks * width)(
        where, sent, high, low, returned
    )
    pieces = [
        lax.ppermute(
            piece,
            ("pp",) + square,
            [
                (s * n_square + a * n_tp + b, (s + 1) % n_pp * n_square + b * n_tp + (a ^ flip))
                for s in range(n_pp)
                for a in range(n_yh)
                for b in range(n_tp)
            ],
        )
        for flip, piece in zip((0, 2), pieces)
    ]
    spread, pieces = lax.optimization_barrier((exchanged(column, "z"), pieces))
    part = call(add_kernel, shaped((toks, half)))(*pieces)
    layer = call(add_kernel, shaped((toks, half)))(part, shifted(part, "core", 1))
    trunk_out = call(join_kernel, shaped((toks, width)), scalars=1)(where, layer, shifted(layer, "yl", 1))

    encoded = call(encoded_kernel, shaped((1, dv)))(spread, image, layer_scale)
    image_out = shifted(encoded[None], "pp", -1)
    return (trunk_out[None], image_out)


def solution(mesh):
    n_pp, n_ep, n_tp = (mesh.shape[a] for a in ("pp", "ep", "tp"))
    fine = Mesh(
        np.asarray(mesh.devices).reshape(n_pp, n_tp, n_ep // n_tp, n_tp // 2, 2),
        ("pp", "yh", "z", "yl", "core"),
    )
    ep, tp = ("yh", "z"), ("yl", "core")
    return jax.shard_map(
        body,
        mesh=fine,
        in_specs=(
            P("pp", ep, None),
            P("pp", ep, None),
            P("pp", ep, None),
            P("pp", None),
            P("pp", ep, None, tp),
            P("pp", ep, None, tp),
            P("pp", ep, tp, None),
            P("pp", ep + tp, None),
            P("pp", None),
            P("pp", None, ep + tp),
            P("pp", ep + tp, None),
            P("pp", None),
        ),
        out_specs=(P("pp", ep, None), P("pp", ep + tp, None)),
        check_vma=False,
    )
```

time: 227 us -> 204 us (0.90)
  waiting for transfers between devices: 95.9 us -> 60.6 us
  starting transfers between devices: 77.5 us -> 104 us
  between operations: 14.4 us -> 1.01 us
  blocking collectives: 0 us -> 11.1 us
  local copies, waits for them, and re-layouts: 16.4 us -> 8.88 us
  other arithmetic: 7.52 us -> 3.22 us
    ppermute x8 -> x15, waiting for transfers between devices: 5.56 us -> 53.3 us  [the longest x1 29.4 us: body(): ring_beside = lax.ppermute(ring, 'z', [(i, i ^ 1) for i in range(n_z)])]
    all_gather x1 -> x0, waiting for transfers between devices: 46.6 us -> none  [body(): all_rows = lax.all_gather(ring, 'z', axis=0, tiled=True)]
    ppermute x8 -> x15, starting transfers between devices: 23.6 us -> 57.3 us  [the longest x14 54 us: shifted(): return lax.ppermute(value, axis, [(i, (i + by) % n) for i in range(n)])]
    all_to_all x4 -> x3, waiting for transfers between devices: 34.7 us -> 6.06 us  [exchanged(): return lax.all_to_all(value, axis, split_axis=0, concat_axis=0, tiled=True)]
    all_to_all x0 -> x1, blocking collectives: none -> 11.1 us  [exchanged(): return lax.all_to_all(value, axis, split_axis=0, concat_axis=0, tiled=True)]
    ppermute x4 -> x2, starting transfers between devices: 18.6 us -> 10.2 us  [body(): lax.ppermute(piece, ('pp',) + square, [(s * n_square + a * n_tp + b, (s +...]
    ppermute x4 -> x2, waiting for transfers between devices: 8.3 us -> 1.29 us  [body(): lax.ppermute(piece, ('pp',) + square, [(s * n_square + a * n_tp + b, (s +...]
    pallas_call x7 -> x14, Pallas kernels: 14.2 us -> 7.23 us  [run(): pl.pallas_call(kernel, out_shape=outs, in_specs=specs, out_specs=jax.tree...]
  transfers between devices with their start and end apart: 20 -> 22, of which waited for: 6 -> 13; matrix products, arithmetic and copies ran while one was open for 4% -> 2% of each run, Pallas kernels for 3% -> 2%
where the time goes in v3:
time: 204 us; the launch traced here: 203 us
  starting transfers between devices  104 us (51%)
  waiting for transfers between devices  60.6 us (30%)
  Pallas kernels  14.1 us (7%)
  blocking collectives  11.1 us (5%)
  local copies, waits for them, and re-layouts  8.88 us (4%)
  other arithmetic  3.22 us (2%)
    ppermute x14, starting transfers between devices, shifted(): return lax.ppermute(value, axis, [(i, (i + by) % n) for i in range(n)])  54 us
    ppermute x1, waiting for transfers between devices, body(): ring_beside = lax.ppermute(ring, 'z', [(i, i ^ 1) for i in range(n_z)])  29.4 us
    all_to_all x3, starting transfers between devices, exchanged(): return lax.all_to_all(value, axis, split_axis=0, concat_axis=0, tiled=True)  28.9 us
    ppermute x14, waiting for transfers between devices, shifted(): return lax.ppermute(value, axis, [(i, (i + by) % n) for i in range(n)])  23.9 us
    all_to_all x1, blocking collectives, exchanged(): return lax.all_to_all(value, axis, split_axis=0, concat_axis=0, tiled=True)  11.1 us
    ppermute x2, starting transfers between devices, body(): lax.ppermute(piece, ('pp',) + square, [(s * n_square + a * n_tp + b, (s +...  10.2 us
    unnamed x33, local copies, waits for them, and re-layouts  8.88 us
    ppermute x2, starting transfers between devices, swapped(): lax.ppermute(value, square, [(a * n_tp + b, b * n_tp + a) for a in range(...  7.52 us
  transfers between devices with their start and end apart: 22, of which 13 were waited for; matrix products, arithmetic and copies ran while one was open for 2% of the time, Pallas kernels for 2%

profile of v3, /device:TPU:1, one launch (start us, length us, event | category | flops | bytes accessed | tf_op | source)
XLA Modules:
  0.0 203.0 jit_solution(9319129865465384185)
XLA Ops:
  0.6 5.6 %collective-permute-start = (bf16[128,2048]{1,0:T(8,128)(2,1)}, bf16[128,2048]{1,0:T(8,128)(2,1)S(1)}, u32[]{:S(2)}, u32[]{:S(2)}) collective-permute-start(bf16[128,2048]{1,0:T(8,128)(2,1)} %bitcast.42), channel_id=1, source_target_pairs={{0,0},{1,32},{2,64},{3,96},{32,1},{33,33},{34,65},{35,97},{64,2},{... | collective-permute-start | bytes 1572872 | tf_op jit(solution)/shard_map/ppermute | solution.py:258
  6.2 0.7 convert_bitcast_fusion
  6.9 0.7 pad_maximum_fusion.1
  7.6 1.9 collective-permute-start.4
  9.5 0.0 copy-start.10
  9.6 0.7 copy-done.10
  10.3 0.7 shard_map.131
  11.0 9.9 %all-to-all-start = ((f32[16,1,3200]{2,1,0:T(1,128)}), f32[16,1,3200]{2,1,0:T(1,128)S(1)}, u32[]{:S(2)}, u32[]{:S(2)}) async-start(f32[16,1,3200]{2,1,0:T(1,128)} %shard_map.131), calls=%async_computation | async-start | bytes 409600 | tf_op jit(solution)/shard_map/all_to_all | solution.py:265
  20.9 1.8 pad_maximum_fusion.refs_0_
  22.7 3.3 %collective-permute-start.3 = (bf16[576,2048]{1,0:T(8,128)(2,1)S(1)}, bf16[576,2048]{1,0:T(8,128)(2,1)}, u32[]{:S(2)}, u32[]{:S(2)}) collective-permute-start(bf16[576,2048]{1,0:T(8,128)(2,1)S(1)} %pad_maximum_fusion.refs_0_), channel_id=1, source_target_pairs={{0,2},{2,0},{1,3},{3,1},{4,6},{6,4},{5,7},{7,5},{8,10},{10,8},{9,1... | collective-permute-start | bytes 7077896 | tf_op jit(solution)/shard_map/ppermute | solution.py:262
  26.0 0.1 pad_add_fusion.where
  26.1 0.8 shard_map.134
  26.9 0.6 copy-done.6
  27.5 0.6 copy-done.8
  28.2 2.8 %all-to-all-done.ring = f32[16,1,3200]{2,1,0:T(1,128)S(1)} async-done(((f32[16,1,3200]{2,1,0:T(1,128)}), f32[16,1,3200]{2,1,0:T(1,128)S(1)}, u32[]{:S(2)}, u32[]{:S(2)}) %all-to-all-start) | async-done | bytes 204832 | tf_op jit(solution)/shard_map/all_to_all | solution.py:265
  31.0 0.1 shard_map.132.own
  31.1 0.7 shard_map.135
  31.8 1.1 copy-done.1
  32.9 10.0 %all-to-all-start.1 = ((bf16[8,40,2048]{2,1,0:T(8,128)(2,1)}), bf16[8,40,2048]{2,1,0:T(8,128)(2,1)}, u32[]{:S(2)}, u32[]{:S(2)}) async-start(bf16[8,40,2048]{2,1,0:T(8,128)(2,1)} %bitcast.31), calls=%async_computation.1 | async-start | bytes 2621440 | tf_op jit(solution)/shard_map/all_to_all | solution.py:265
  42.9 3.4 %collective-permute-start.1 = (bf16[16,3200]{1,0:T(8,128)(2,1)S(1)}, bf16[16,3200]{1,0:T(8,128)(2,1)S(1)}, u32[]{:S(2)}, u32[]{:S(2)}) collective-permute-start(bf16[16,3200]{1,0:T(8,128)(2,1)S(1)} %shard_map.132.own), channel_id=1, source_target_pairs={{0,4},{4,0},{8,12},{12,8},{16,20},{20,16},{24,28},{28,24},{1,5},{5... | collective-permute-start | bytes 307208 | tf_op jit(solution)/shard_map/ppermute | solution.py:281
  46.3 29.4 %collective-permute-done.1.other = bf16[16,3200]{1,0:T(8,128)(2,1)S(1)} collective-permute-done((bf16[16,3200]{1,0:T(8,128)(2,1)S(1)}, bf16[16,3200]{1,0:T(8,128)(2,1)S(1)}, u32[]{:S(2)}, u32[]{:S(2)}) %collective-permute-start.1) | collective-permute-done | bytes 102432 | tf_op jit(solution)/shard_map/ppermute | solution.py:281
  75.7 2.6 %collective-permute-start.2 = (bf16[32,3200]{1,0:T(8,128)(2,1)S(1)}, bf16[32,3200]{1,0:T(8,128)(2,1)S(1)}, u32[]{:S(2)}, u32[]{:S(2)}) collective-permute-start(bf16[32,3200]{1,0:T(8,128)(2,1)S(1)} %shard_map.133.refs_0_), channel_id=1, source_target_pairs={{0,8},{4,12},{8,16},{12,20},{16,24},{20,28},{24,0},{28,4},{1,9},{5... | collective-permute-start | bytes 614408 | tf_op jit(solution)/shard_map/ppermute | solution.py:262
  78.2 4.8 %collective-permute-start.5 = (bf16[32,3200]{1,0:T(8,128)(2,1)S(1)}, bf16[32,3200]{1,0:T(8,128)(2,1)S(1)}, u32[]{:S(2)}, u32[]{:S(2)}) collective-permute-start(bf16[32,3200]{1,0:T(8,128)(2,1)S(1)} %shard_map.133.refs_0_), channel_id=1, source_target_pairs={{0,24},{4,28},{8,0},{12,4},{16,8},{20,12},{24,16},{28,20},{1,25},{... | collective-permute-start | bytes 614408 | tf_op jit(solution)/shard_map/ppermute | solution.py:262
  83.1 2.8 %collective-permute-done.2.refs_1_ = bf16[32,3200]{1,0:T(8,128)(2,1)S(1)} collective-permute-done((bf16[32,3200]{1,0:T(8,128)(2,1)S(1)}, bf16[32,3200]{1,0:T(8,128)(2,1)S(1)}, u32[]{:S(2)}, u32[]{:S(2)}) %collective-permute-start.2) | collective-permute-done | bytes 204832 | tf_op jit(solution)/shard_map/ppermute | solution.py:262
  85.9 7.0 %collective-permute-start.6 = (bf16[32,3200]{1,0:T(8,128)(2,1)S(1)}, bf16[32,3200]{1,0:T(8,128)(2,1)S(1)}, u32[]{:S(2)}, u32[]{:S(2)}) collective-permute-start(bf16[32,3200]{1,0:T(8,128)(2,1)S(1)} %collective-permute-done.2.refs_1_), channel_id=1, source_target_pairs={{0,8},{4,12},{8,16},{12,20},{16,24},{20,28},{24,0},{28,4},{1,9},{5... | collective-permute-start | bytes 614408 | tf_op jit(solution)/shard_map/ppermute | solution.py:262
  92.9 2.7 %collective-permute-start.12 = (bf16[576,2048]{1,0:T(8,128)(2,1)S(1)}, bf16[576,2048]{1,0:T(8,128)(2,1)}, u32[]{:S(2)}, u32[]{:S(2)}) collective-permute-start(bf16[576,2048]{1,0:T(8,128)(2,1)S(1)} %pad_maximum_fusion.refs_0_), channel_id=1, source_target_pairs={{0,1},{1,0},{2,3},{3,2},{4,5},{5,4},{6,7},{7,6},{8,9},{9,8},{10,11... | collective-permute-start | bytes 7077896 | tf_op jit(solution)/shard_map/ppermute | solution.py:262
  95.6 2.0 %collective-permute-done.6.refs_3_ = bf16[32,3200]{1,0:T(8,128)(2,1)S(1)} collective-permute-done((bf16[32,3200]{1,0:T(8,128)(2,1)S(1)}, bf16[32,3200]{1,0:T(8,128)(2,1)S(1)}, u32[]{:S(2)}, u32[]{:S(2)}) %collective-permute-start.6) | collective-permute-done | bytes 204832 | tf_op jit(solution)/shard_map/ppermute | solution.py:262
  97.7 0.7 copy-done.4
  98.3 6.8 %collective-permute-start.13 = (bf16[576,2048]{1,0:T(8,128)(2,1)}, bf16[576,2048]{1,0:T(8,128)(2,1)S(1)}, u32[]{:S(2)}, u32[]{:S(2)}) collective-permute-start(bf16[576,2048]{1,0:T(8,128)(2,1)} %collective-permute-done.3.refs_2_), channel_id=1, source_target_pairs={{0,1},{1,0},{2,3},{3,2},{4,5},{5,4},{6,7},{7,6},{8,9},{9,8},{10,11... | collective-permute-start | bytes 7077896 | tf_op jit(solution)/shard_map/ppermute | solution.py:262
  105.2 4.3 %collective-permute-done.13.refs_3_ = bf16[576,2048]{1,0:T(8,128)(2,1)S(1)} collective-permute-done((bf16[576,2048]{1,0:T(8,128)(2,1)}, bf16[576,2048]{1,0:T(8,128)(2,1)S(1)}, u32[]{:S(2)}, u32[]{:S(2)}) %collective-permute-start.13) | collective-permute-done | bytes 2359328 | tf_op jit(solution)/shard_map/ppermute | solution.py:262
  109.5 1.4 copy-done.15
  111.0 6.9 %shard_map.140 = bf16[320,2048]{1,0:T(8,128)(2,1)S(1)} custom-call(bf16[320,2048]{1,0:T(8,128)(2,1)} %bitcast.15.rows, bf16[576,2048]{1,0:T(8,128)(2,1)S(1)} %pad_maximum_fusion.refs_0_, bf16[576,2048]{1,0:T(8,128)(2,1)} %collective-permute-done.12.refs_1_, bf16[576,2048]{1,0:T(8,128)(2,1)} %collective-permute-done.3.refs_2_, bf16[576,2048]{1,0:T(8,128)(2,1)} %copy-done.15), custom_call_target="tpu_custom_call" | custom-call | flops 3019898880 | bytes 9437184 | tf_op jit(solution)/shard_map/pallas_call | solution.py:127
  117.9 1.1 copy-done
  119.0 8.9 %all-to-all-start.2 = ((bf16[8,40,2048]{2,1,0:T(8,128)(2,1)}), bf16[8,40,2048]{2,1,0:T(8,128)(2,1)S(1)}, u32[]{:S(2)}, u32[]{:S(2)}) async-start(bf16[8,40,2048]{2,1,0:T(8,128)(2,1)} %bitcast.29), calls=%async_computation.2 | async-start | bytes 2621440 | tf_op jit(solution)/shard_map/all_to_all | solution.py:265
  128.0 0.0 copy-start.3
  128.0 1.1 copy-done.3
  129.1 2.0 shard_map.136
  131.0 2.6 %collective-permute-start.7 = (bf16[64,3200]{1,0:T(8,128)(2,1)S(1)}, bf16[64,3200]{1,0:T(8,128)(2,1)S(1)}, u32[]{:S(2)}, u32[]{:S(2)}) collective-permute-start(bf16[64,3200]{1,0:T(8,128)(2,1)S(1)} %get-tuple-element.32), channel_id=1, source_target_pairs={{0,1},{1,0},{2,3},{3,2},{4,5},{5,4},{6,7},{7,6},{8,9},{9,8},{10,11... | collective-permute-start | bytes 1228808 | tf_op jit(solution)/shard_map/ppermute | solution.py:262
  133.6 1.4 collective-permute-done.7.came
  135.0 0.1 shard_map.137
  135.0 2.0 collective-permute-start.8
  137.1 6.1 %collective-permute-done.8.came = bf16[32,3200]{1,0:T(8,128)(2,1)S(1)} collective-permute-done((bf16[32,3200]{1,0:T(8,128)(2,1)S(1)}, bf16[32,3200]{1,0:T(8,128)(2,1)S(1)}, u32[]{:S(2)}, u32[]{:S(2)}) %collective-permute-start.8) | collective-permute-done | bytes 204832 | tf_op jit(solution)/shard_map/ppermute | solution.py:262
  143.2 0.1 shard_map.138
  143.3 3.5 %collective-permute-start.9 = (bf16[8,3200]{1,0:T(8,128)(2,1)S(1)}, bf16[8,3200]{1,0:T(8,128)(2,1)S(1)}, u32[]{:S(2)}, u32[]{:S(2)}) collective-permute-start(bf16[8,3200]{1,0:T(8,128)(2,1)S(1)} %get-tuple-element.36), channel_id=1, source_target_pairs={{0,32},{32,64},{64,96},{96,0},{1,33},{33,65},{65,97},{97,1},{2,34}... | collective-permute-start | bytes 153608 | tf_op jit(solution)/shard_map/ppermute | solution.py:262
  146.8 5.9 %collective-permute-start.10 = (bf16[8,3200]{1,0:T(8,128)(2,1)S(1)}, bf16[8,3200]{1,0:T(8,128)(2,1)S(1)}, u32[]{:S(2)}, u32[]{:S(2)}) collective-permute-start(bf16[8,3200]{1,0:T(8,128)(2,1)S(1)} %get-tuple-element.37), channel_id=1, source_target_pairs={{0,64},{32,96},{64,0},{96,32},{1,65},{33,97},{65,1},{97,33},{2,66}... | collective-permute-start | bytes 153608 | tf_op jit(solution)/shard_map/ppermute | solution.py:262
  152.7 3.9 %collective-permute-start.11 = (bf16[8,3200]{1,0:T(8,128)(2,1)S(1)}, bf16[8,3200]{1,0:T(8,128)(2,1)S(1)}, u32[]{:S(2)}, u32[]{:S(2)}) collective-permute-start(bf16[8,3200]{1,0:T(8,128)(2,1)S(1)} %get-tuple-element.38), channel_id=1, source_target_pairs={{0,96},{32,0},{64,32},{96,64},{1,97},{33,1},{65,33},{97,65},{2,98}... | collective-permute-start | bytes 153608 | tf_op jit(solution)/shard_map/ppermute | solution.py:262
  156.6 2.8 %collective-permute-done.11.refs_2_ = bf16[8,3200]{1,0:T(8,128)(2,1)S(1)} collective-permute-done((bf16[8,3200]{1,0:T(8,128)(2,1)S(1)}, bf16[8,3200]{1,0:T(8,128)(2,1)S(1)}, u32[]{:S(2)}, u32[]{:S(2)}) %collective-permute-start.11) | collective-permute-done | bytes 51232 | tf_op jit(solution)/shard_map/ppermute | solution.py:262
  159.5 3.2 %all-to-all-done.2 = bf16[8,40,2048]{2,1,0:T(8,128)(2,1)S(1)} async-done(((bf16[8,40,2048]{2,1,0:T(8,128)(2,1)}), bf16[8,40,2048]{2,1,0:T(8,128)(2,1)S(1)}, u32[]{:S(2)}, u32[]{:S(2)}) %all-to-all-start.2) | async-done | bytes 1310752 | tf_op jit(solution)/shard_map/all_to_all | solution.py:265
  162.8 0.9 copy-done.9
  163.6 1.3 shard_map.141
  164.9 4.8 %collective-permute-start.14 = (bf16[128,1024]{1,0:T(8,128)(2,1)S(1)}, bf16[128,1024]{1,0:T(8,128)(2,1)S(1)}, u32[]{:S(2)}, u32[]{:S(2)}) collective-permute-start(bf16[128,1024]{1,0:T(8,128)(2,1)S(1)} %get-tuple-element.45), channel_id=1, source_target_pairs={{0,128},{1,160},{2,192},{3,224},{32,129},{33,161},{34,193},{35,225... | collective-permute-start | bytes 786440 | tf_op jit(solution)/shard_map/ppermute | solution.py:325
  169.8 5.4 %collective-permute-start.15 = (bf16[128,1024]{1,0:T(8,128)(2,1)S(1)}, bf16[128,1024]{1,0:T(8,128)(2,1)S(1)}, u32[]{:S(2)}, u32[]{:S(2)}) collective-permute-start(bf16[128,1024]{1,0:T(8,128)(2,1)S(1)} %get-tuple-element.46), channel_id=1, source_target_pairs={{0,130},{1,162},{2,194},{3,226},{32,131},{33,163},{34,195},{35,227... | collective-permute-start | bytes 786440 | tf_op jit(solution)/shard_map/ppermute | solution.py:325
  175.2 11.1 %all_to_all.20.spread = f32[8,1,3200]{2,1,0:T(1,128)S(1)} all-to-all(f32[8,1,3200]{2,1,0:T(1,128)S(1)} %shard_map.139), channel_id=1, replica_groups=mesh['pp'=4,'yh'=4,'z'=8,'yl'=2,'core'=2] {'z'}, dimensions={0} | all-to-all | bytes 204800 | tf_op jit(solution)/shard_map/all_to_all | solution.py:265
  186.3 1.3 collective-permute-done.15.right
  187.6 0.1 shard_map.142.left
  187.6 2.8 %collective-permute-start.16 = (bf16[128,1024]{1,0:T(8,128)(2,1)S(1)}, bf16[128,1024]{1,0:T(8,128)(2,1)S(1)}, u32[]{:S(2)}, u32[]{:S(2)}) collective-permute-start(bf16[128,1024]{1,0:T(8,128)(2,1)S(1)} %shard_map.142.left), channel_id=1, source_target_pairs={{0,1},{1,0},{2,3},{3,2},{4,5},{5,4},{6,7},{7,6},{8,9},{9,8},{10,11... | collective-permute-start | bytes 786440 | tf_op jit(solution)/shard_map/ppermute | solution.py:262
  190.4 1.1 collective-permute-done.16.right
  191.5 0.1 shard_map.143.own
  191.6 3.0 %collective-permute-start.17 = (bf16[128,1024]{1,0:T(8,128)(2,1)S(1)}, bf16[128,1024]{1,0:T(8,128)(2,1)S(1)}, u32[]{:S(2)}, u32[]{:S(2)}) collective-permute-start(bf16[128,1024]{1,0:T(8,128)(2,1)S(1)} %shard_map.143.own), channel_id=1, source_target_pairs={{0,2},{2,0},{1,3},{3,1},{4,6},{6,4},{5,7},{7,5},{8,10},{10,8},{9,1... | collective-permute-start | bytes 786440 | tf_op jit(solution)/shard_map/ppermute | solution.py:262
  194.6 3.1 %collective-permute-start.18 = (bf16[1,1,3200]{2,1,0:T(2,128)(2,1)S(1)}, bf16[1,1,3200]{2,1,0:T(2,128)(2,1)S(1)}, u32[]{:S(2)}, u32[]{:S(2)}) collective-permute-start(bf16[1,1,3200]{2,1,0:T(2,128)(2,1)S(1)} %bitcast.36), channel_id=1, source_target_pairs={{0,384},{128,0},{256,128},{384,256},{1,385},{129,1},{257,129},{385... | collective-permute-start | bytes 19208 | tf_op jit(solution)/shard_map/ppermute | solution.py:262
  197.8 1.6 collective-permute-done.18
  199.4 1.7 collective-permute-done.17.across
  201.0 1.4 shard_map.144
  202.4 0.6 copy.15
  (33 shorter events, 0.2 us)
Async XLA Ops:
  0.6 30.4 %collective-permute-start = (bf16[128,2048]{1,0:T(8,128)(2,1)}, bf16[128,2048]{1,0:T(8,128)(2,1)S(1)}, u32[]{:S(2)}, u32[]{:S(2)}) collective-permute-start(bf16[128,2048]{1,0:T(8,128)(2,1)} %bitcast.42), channel_id=1, source_target_pairs={{0,0},{1,32},{2,64},{3,96},{32,1},{33,33},{34,65},{35,97},{64,2},{... | collective-permute-start | bytes 1572872 | tf_op jit(solution)/shard_map/ppermute | solution.py:258
  7.6 18.4 %collective-permute-start.4 = (f32[16,128]{1,0:T(8,128)S(1)}, f32[16,128]{1,0:T(8,128)S(1)}, u32[]{:S(2)}, u32[]{:S(2)}) collective-permute-start(f32[16,128]{1,0:T(8,128)S(1)} %pad_maximum_fusion.1), channel_id=1, source_target_pairs={{0,0},{1,32},{2,64},{3,96},{32,1},{33,33},{34,65},{35,97},{64,2},{... | collective-permute-start | bytes 24584 | tf_op jit(solution)/shard_map/ppermute | solution.py:258
  9.5 0.7 copy-start.10
  11.0 20.0 %all-to-all-start = ((f32[16,1,3200]{2,1,0:T(1,128)}), f32[16,1,3200]{2,1,0:T(1,128)S(1)}, u32[]{:S(2)}, u32[]{:S(2)}) async-start(f32[16,1,3200]{2,1,0:T(1,128)} %shard_map.131), calls=%async_computation | async-start | bytes 409600 | tf_op jit(solution)/shard_map/all_to_all | solution.py:265
  20.9 10.2 %copy-start.14 = (f32[1,2048]{1,0:T(1,128)S(1)}, f32[1,2048]{1,0:T(1,128)}, u32[]{:S(2)}) copy-start(f32[1,2048]{1,0:T(1,128)} %gain.1) | copy-start | bytes 24580
  22.7 75.7 %collective-permute-start.3 = (bf16[576,2048]{1,0:T(8,128)(2,1)S(1)}, bf16[576,2048]{1,0:T(8,128)(2,1)}, u32[]{:S(2)}, u32[]{:S(2)}) collective-permute-start(bf16[576,2048]{1,0:T(8,128)(2,1)S(1)} %pad_maximum_fusion.refs_0_), channel_id=1, source_target_pairs={{0,2},{2,0},{1,3},{3,1},{4,6},{6,4},{5,7},{7,5},{8,10},{10,8},{9,1... | collective-permute-start | bytes 7077896 | tf_op jit(solution)/shard_map/ppermute | solution.py:262
  26.9 0.6 copy-start.6
  27.5 0.6 copy-start.8
  31.8 1.1 copy-start.1
  32.9 65.5 %all-to-all-start.1 = ((bf16[8,40,2048]{2,1,0:T(8,128)(2,1)}), bf16[8,40,2048]{2,1,0:T(8,128)(2,1)}, u32[]{:S(2)}, u32[]{:S(2)}) async-start(bf16[8,40,2048]{2,1,0:T(8,128)(2,1)} %bitcast.31), calls=%async_computation.1 | async-start | bytes 2621440 | tf_op jit(solution)/shard_map/all_to_all | solution.py:265
  42.9 32.7 %collective-permute-start.1 = (bf16[16,3200]{1,0:T(8,128)(2,1)S(1)}, bf16[16,3200]{1,0:T(8,128)(2,1)S(1)}, u32[]{:S(2)}, u32[]{:S(2)}) collective-permute-start(bf16[16,3200]{1,0:T(8,128)(2,1)S(1)} %shard_map.132.own), channel_id=1, source_target_pairs={{0,4},{4,0},{8,12},{12,8},{16,20},{20,16},{24,28},{28,24},{1,5},{5... | collective-permute-start | bytes 307208 | tf_op jit(solution)/shard_map/ppermute | solution.py:281
  75.7 10.2 %collective-permute-start.2 = (bf16[32,3200]{1,0:T(8,128)(2,1)S(1)}, bf16[32,3200]{1,0:T(8,128)(2,1)S(1)}, u32[]{:S(2)}, u32[]{:S(2)}) collective-permute-start(bf16[32,3200]{1,0:T(8,128)(2,1)S(1)} %shard_map.133.refs_0_), channel_id=1, source_target_pairs={{0,8},{4,12},{8,16},{12,20},{16,24},{20,28},{24,0},{28,4},{1,9},{5... | collective-permute-start | bytes 614408 | tf_op jit(solution)/shard_map/ppermute | solution.py:262
  78.2 17.4 %collective-permute-start.5 = (bf16[32,3200]{1,0:T(8,128)(2,1)S(1)}, bf16[32,3200]{1,0:T(8,128)(2,1)S(1)}, u32[]{:S(2)}, u32[]{:S(2)}) collective-permute-start(bf16[32,3200]{1,0:T(8,128)(2,1)S(1)} %shard_map.133.refs_0_), channel_id=1, source_target_pairs={{0,24},{4,28},{8,0},{12,4},{16,8},{20,12},{24,16},{28,20},{1,25},{... | collective-permute-start | bytes 614408 | tf_op jit(solution)/shard_map/ppermute | solution.py:262
  85.9 11.8 %collective-permute-start.6 = (bf16[32,3200]{1,0:T(8,128)(2,1)S(1)}, bf16[32,3200]{1,0:T(8,128)(2,1)S(1)}, u32[]{:S(2)}, u32[]{:S(2)}) collective-permute-start(bf16[32,3200]{1,0:T(8,128)(2,1)S(1)} %collective-permute-done.2.refs_1_), channel_id=1, source_target_pairs={{0,8},{4,12},{8,16},{12,20},{16,24},{20,28},{24,0},{28,4},{1,9},{5... | collective-permute-start | bytes 614408 | tf_op jit(solution)/shard_map/ppermute | solution.py:262
  92.9 12.3 %collective-permute-start.12 = (bf16[576,2048]{1,0:T(8,128)(2,1)S(1)}, bf16[576,2048]{1,0:T(8,128)(2,1)}, u32[]{:S(2)}, u32[]{:S(2)}) collective-permute-start(bf16[576,2048]{1,0:T(8,128)(2,1)S(1)} %pad_maximum_fusion.refs_0_), channel_id=1, source_target_pairs={{0,1},{1,0},{2,3},{3,2},{4,5},{5,4},{6,7},{7,6},{8,9},{9,8},{10,11... | collective-permute-start | bytes 7077896 | tf_op jit(solution)/shard_map/ppermute | solution.py:262
  97.7 0.7 copy-start.4
  98.3 11.2 %collective-permute-start.13 = (bf16[576,2048]{1,0:T(8,128)(2,1)}, bf16[576,2048]{1,0:T(8,128)(2,1)S(1)}, u32[]{:S(2)}, u32[]{:S(2)}) collective-permute-start(bf16[576,2048]{1,0:T(8,128)(2,1)} %collective-permute-done.3.refs_2_), channel_id=1, source_target_pairs={{0,1},{1,0},{2,3},{3,2},{4,5},{5,4},{6,7},{7,6},{8,9},{9,8},{10,11... | collective-permute-start | bytes 7077896 | tf_op jit(solution)/shard_map/ppermute | solution.py:262
  109.5 1.4 copy-start.15
  117.9 1.1 copy-start
  119.0 9.0 %copy-start.2 = (bf16[1,3200,100]{1,2,0:T(8,128)(2,1)S(1)}, bf16[1,3200,100]{1,2,0:T(8,128)(2,1)}, u32[]{:S(2)}) copy-start(bf16[1,3200,100]{1,2,0:T(8,128)(2,1)} %param.21) | copy-start | bytes 1920004
  119.0 9.0 %copy-start.5 = (bf16[32,3200]{1,0:T(8,128)(2,1)S(1)}, bf16[32,3200]{1,0:T(8,128)(2,1)}, u32[]{:S(2)}) copy-start(bf16[32,3200]{1,0:T(8,128)(2,1)} %copy-done.4) | copy-start | bytes 614404
  119.0 9.0 %copy-start.13 = (f32[1,3200]{1,0:T(1,128)S(1)}, f32[1,3200]{1,0:T(1,128)}, u32[]{:S(2)}) copy-start(f32[1,3200]{1,0:T(1,128)} %refs_4_.1) | copy-start | bytes 38404
  119.0 43.8 %copy-start.7 = (bf16[128,320]{1,0:T(8,128)(2,1)S(1)}, bf16[128,320]{1,0:T(8,128)(2,1)}, u32[]{:S(2)}) copy-start(bf16[128,320]{1,0:T(8,128)(2,1)} %copy-done.6) | copy-start | bytes 245764
  119.0 43.7 %all-to-all-start.2 = ((bf16[8,40,2048]{2,1,0:T(8,128)(2,1)}), bf16[8,40,2048]{2,1,0:T(8,128)(2,1)S(1)}, u32[]{:S(2)}, u32[]{:S(2)}) async-start(bf16[8,40,2048]{2,1,0:T(8,128)(2,1)} %bitcast.29), calls=%async_computation.2 | async-start | bytes 2621440 | tf_op jit(solution)/shard_map/all_to_all | solution.py:265
  128.0 1.1 copy-start.3
  131.0 3.9 %collective-permute-start.7 = (bf16[64,3200]{1,0:T(8,128)(2,1)S(1)}, bf16[64,3200]{1,0:T(8,128)(2,1)S(1)}, u32[]{:S(2)}, u32[]{:S(2)}) collective-permute-start(bf16[64,3200]{1,0:T(8,128)(2,1)S(1)} %get-tuple-element.32), channel_id=1, source_target_pairs={{0,1},{1,0},{2,3},{3,2},{4,5},{5,4},{6,7},{7,6},{8,9},{9,8},{10,11... | collective-permute-start | bytes 1228808 | tf_op jit(solution)/shard_map/ppermute | solution.py:262
  135.0 8.2 %collective-permute-start.8 = (bf16[32,3200]{1,0:T(8,128)(2,1)S(1)}, bf16[32,3200]{1,0:T(8,128)(2,1)S(1)}, u32[]{:S(2)}, u32[]{:S(2)}) collective-permute-start(bf16[32,3200]{1,0:T(8,128)(2,1)S(1)} %get-tuple-element.34), channel_id=1, source_target_pairs={{0,2},{2,0},{1,3},{3,1},{4,6},{6,4},{5,7},{7,5},{8,10},{10,8},{9,1... | collective-permute-start | bytes 614408 | tf_op jit(solution)/shard_map/ppermute | solution.py:262
  143.2 51.3 %copy-start.11 = (bf16[1,1,3200]{2,1,0:T(2,128)(2,1)S(1)}, bf16[1,1,3200]{2,1,0:T(2,128)(2,1)}, u32[]{:S(2)}) copy-start(bf16[1,1,3200]{2,1,0:T(2,128)(2,1)} %param.19) | copy-start | bytes 19204
  143.2 51.4 %copy-start.12 = (f32[1,3200]{1,0:T(1,128)S(1)}, f32[1,3200]{1,0:T(1,128)}, u32[]{:S(2)}) copy-start(f32[1,3200]{1,0:T(1,128)} %scale.1) | copy-start | bytes 38404
  143.3 13.3 %collective-permute-start.9 = (bf16[8,3200]{1,0:T(8,128)(2,1)S(1)}, bf16[8,3200]{1,0:T(8,128)(2,1)S(1)}, u32[]{:S(2)}, u32[]{:S(2)}) collective-permute-start(bf16[8,3200]{1,0:T(8,128)(2,1)S(1)} %get-tuple-element.36), channel_id=1, source_target_pairs={{0,32},{32,64},{64,96},{96,0},{1,33},{33,65},{65,97},{97,1},{2,34}... | collective-permute-start | bytes 153608 | tf_op jit(solution)/shard_map/ppermute | solution.py:262
  146.8 9.8 %collective-permute-start.10 = (bf16[8,3200]{1,0:T(8,128)(2,1)S(1)}, bf16[8,3200]{1,0:T(8,128)(2,1)S(1)}, u32[]{:S(2)}, u32[]{:S(2)}) collective-permute-start(bf16[8,3200]{1,0:T(8,128)(2,1)S(1)} %get-tuple-element.37), channel_id=1, source_target_pairs={{0,64},{32,96},{64,0},{96,32},{1,65},{33,97},{65,1},{97,33},{2,66}... | collective-permute-start | bytes 153608 | tf_op jit(solution)/shard_map/ppermute | solution.py:262
  152.7 6.7 %collective-permute-start.11 = (bf16[8,3200]{1,0:T(8,128)(2,1)S(1)}, bf16[8,3200]{1,0:T(8,128)(2,1)S(1)}, u32[]{:S(2)}, u32[]{:S(2)}) collective-permute-start(bf16[8,3200]{1,0:T(8,128)(2,1)S(1)} %get-tuple-element.38), channel_id=1, source_target_pairs={{0,96},{32,0},{64,32},{96,64},{1,97},{33,1},{65,33},{97,65},{2,98}... | collective-permute-start | bytes 153608 | tf_op jit(solution)/shard_map/ppermute | solution.py:262
  162.8 0.9 copy-start.9
  164.9 21.4 %collective-permute-start.14 = (bf16[128,1024]{1,0:T(8,128)(2,1)S(1)}, bf16[128,1024]{1,0:T(8,128)(2,1)S(1)}, u32[]{:S(2)}, u32[]{:S(2)}) collective-permute-start(bf16[128,1024]{1,0:T(8,128)(2,1)S(1)} %get-tuple-element.45), channel_id=1, source_target_pairs={{0,128},{1,160},{2,192},{3,224},{32,129},{33,161},{34,193},{35,225... | collective-permute-start | bytes 786440 | tf_op jit(solution)/shard_map/ppermute | solution.py:325
  169.8 17.8 %collective-permute-start.15 = (bf16[128,1024]{1,0:T(8,128)(2,1)S(1)}, bf16[128,1024]{1,0:T(8,128)(2,1)S(1)}, u32[]{:S(2)}, u32[]{:S(2)}) collective-permute-start(bf16[128,1024]{1,0:T(8,128)(2,1)S(1)} %get-tuple-element.46), channel_id=1, source_target_pairs={{0,130},{1,162},{2,194},{3,226},{32,131},{33,163},{34,195},{35,227... | collective-permute-start | bytes 786440 | tf_op jit(solution)/shard_map/ppermute | solution.py:325
  187.6 3.9 %collective-permute-start.16 = (bf16[128,1024]{1,0:T(8,128)(2,1)S(1)}, bf16[128,1024]{1,0:T(8,128)(2,1)S(1)}, u32[]{:S(2)}, u32[]{:S(2)}) collective-permute-start(bf16[128,1024]{1,0:T(8,128)(2,1)S(1)} %shard_map.142.left), channel_id=1, source_target_pairs={{0,1},{1,0},{2,3},{3,2},{4,5},{5,4},{6,7},{7,6},{8,9},{9,8},{10,11... | collective-permute-start | bytes 786440 | tf_op jit(solution)/shard_map/ppermute | solution.py:262
  191.6 9.4 %collective-permute-start.17 = (bf16[128,1024]{1,0:T(8,128)(2,1)S(1)}, bf16[128,1024]{1,0:T(8,128)(2,1)S(1)}, u32[]{:S(2)}, u32[]{:S(2)}) collective-permute-start(bf16[128,1024]{1,0:T(8,128)(2,1)S(1)} %shard_map.143.own), channel_id=1, source_target_pairs={{0,2},{2,0},{1,3},{3,1},{4,6},{6,4},{5,7},{7,5},{8,10},{10,8},{9,1... | collective-permute-start | bytes 786440 | tf_op jit(solution)/shard_map/ppermute | solution.py:262
  194.6 4.7 %collective-permute-start.18 = (bf16[1,1,3200]{2,1,0:T(2,128)(2,1)S(1)}, bf16[1,1,3200]{2,1,0:T(2,128)(2,1)S(1)}, u32[]{:S(2)}, u32[]{:S(2)}) collective-permute-start(bf16[1,1,3200]{2,1,0:T(2,128)(2,1)S(1)} %bitcast.36), channel_id=1, source_target_pairs={{0,384},{128,0},{256,128},{384,256},{1,385},{129,1},{257,129},{385... | collective-permute-start | bytes 19208 | tf_op jit(solution)/shard_map/ppermute | solution.py:262

commit v4 on v3

--- a/solution.py
+++ b/solution.py
@@ -13,7 +13,8 @@
 VM = pl.BlockSpec(memory_space=pltpu.VMEM)
 SM = pl.BlockSpec(memory_space=pltpu.SMEM)
 CAP = 40
-LIMIT = 48 * 1024 * 1024
+SMALL = 12 * 1024 * 1024
+LARGE = 24 * 1024 * 1024
 
 
 def call(kernel, outs, scalars=0, flops=0, moved=0):
@@ -24,7 +25,7 @@
             out_shape=outs,
             in_specs=specs,
             out_specs=jax.tree.map(lambda _: VM, outs),
-            compiler_params=pltpu.CompilerParams(vmem_limit_bytes=LIMIT),
+            compiler_params=pltpu.CompilerParams(vmem_limit_bytes=SMALL),
             cost_estimate=pl.CostEstimate(flops=flops, bytes_accessed=moved, transcendentals=0),
         )(*operands)
 
@@ -86,9 +87,9 @@
                     shard.at[pl.ds(p * count, count)], held.at[pl.ds(s * count, count)], in_sem.at[3 * s + p]
                 )
             )
-    for p in (0, 1, 2):
-        for s in range(4):
-            copies[3 * s + p].start() if p < 2 else None
+    for s in range(4):
+        copies[3 * s].start()
+        copies[3 * s + 1].start()
     for s in range(4):
         copies[3 * s + 2].start()
     row_copy.wait()
@@ -126,9 +127,9 @@
     anywhere = pl.BlockSpec(memory_space=pl.ANY)
     return pl.pallas_call(
         expert_kernel,
-        out_shape=shaped((n, width)),
+        out_shape=pltpu.HBM((n, width), BF16),
         in_specs=[anywhere] * 5,
-        out_specs=pl.BlockSpec(memory_space=pltpu.HBM),
+        out_specs=anywhere,
         scratch_shapes=[
             pltpu.VMEM((n, width), BF16),
             pltpu.VMEM((count, width), BF16),
@@ -140,7 +141,7 @@
             pltpu.SemaphoreType.DMA((12,)),
             pltpu.SemaphoreType.DMA((4,)),
         ],
-        compiler_params=pltpu.CompilerParams(vmem_limit_bytes=LIMIT),
+        compiler_params=pltpu.CompilerParams(vmem_limit_bytes=LARGE),
         cost_estimate=pl.CostEstimate(flops=6 * n * width * count, bytes_accessed=6 * count * width, transcendentals=0),
     )(rows, *shards)
 
@@ -175,39 +176,33 @@
         out[i] = wide
 
 
-def ring_kernel(ring, out):
-    out[...] = jnp.concatenate([ring[i] for i in range(ring.shape[0])], axis=0).astype(BF16)
+def rows_kernel(spread, out):
+    out[...] = jnp.concatenate([spread[i] for i in range(spread.shape[0])], axis=0).astype(BF16)
 
 
 def pair_kernel(own, other, out):
-    n = own.shape[0]
-    out[:n, :] = own[...]
-    out[n:, :] = other[...]
-
-
-def image_kernel(sizes, where, *refs):
+    out[...] = jnp.concatenate([own[...].astype(F32), other[...].astype(F32)], axis=0).astype(BF16)
+
+
+def image_kernel(n_z, *refs):
     groups, (gain, first, second, mine, theirs) = refs[:-5], refs[-5:]
-    n_yh, n_z = sizes
-    wide = jnp.concatenate([group[...] for group in groups], axis=0).astype(F32)
-    n = wide.shape[0]
+    wide = [group[...].astype(F32) for group in groups]
+    n_yh = len(wide)
+    blocks = []
+    for core in range(2):
+        for low in range(2):
+            for ahead in range(n_yh):
+                at = (low * 2 + core) * n_z
+                blocks.append(wide[(n_yh - ahead) % n_yh][at : at + n_z, :])
+    wide = jnp.concatenate(blocks, axis=0)
     scale = lax.rsqrt(jnp.mean(wide * wide, axis=-1, keepdims=True) + 1e-06)
     normed = (wide * scale * gain[...]).astype(BF16)
     made = nt(normed, first[...])
     hidden = (0.5 * made * (1.0 + lax.erf(made * np.float32(0.5**0.5)))).astype(BF16)
-    yh, yl, core, z_here = where[0], where[1] // 2, lax.rem(where[1], 2), where[2]
-    at = lax.broadcasted_iota(jnp.int32, (n // 2, n), 0)
-    column = lax.broadcasted_iota(jnp.int32, (n // 2, n), 1)
-    z = lax.rem(at, n_z)
-    high = lax.rem(at // n_z + yh, n_yh)
-    low = lax.rem(at // (n_z * n_yh) + yl, 2)
-    apart = lax.rem(z // 2 - z_here // 2 + n_z // 2, n_z // 2)
-    group = jnp.where(apart == 0, 0, jnp.where(apart == 3, 1, apart + 1))
-    block = group * 2 + lax.rem(z + z_here, 2)
-    for out, side in ((mine, core), (theirs, 1 - core)):
-        source = ((block * n_yh + high) * 2 + low) * 2 + side
-        order = jnp.where(column == source, 1.0, 0.0).astype(BF16)
-        half = jnp.dot(order, hidden, preferred_element_type=F32).astype(BF16)
-        out[...] = jnp.dot(half, second[...], preferred_element_type=F32).astype(out.dtype)
+    whole = jnp.dot(hidden, second[...], preferred_element_type=F32)
+    half = mine.shape[0]
+    mine[...] = whole[:half]
+    theirs[...] = whole[half:].astype(BF16)
 
 
 def fold_kernel(held, came, keep, *sends):
@@ -252,7 +247,7 @@
     n_tp = lax.axis_size("yl") * lax.axis_size("core")
     n_square = n_yh * n_tp
     square = ("yh", "yl", "core")
-    where = jnp.stack([lax.axis_index("yh"), lax.axis_index(("yl", "core")), lax.axis_index("z")]).astype(jnp.int32)
+    where = jnp.stack([lax.axis_index("yh"), lax.axis_index(("yl", "core"))]).astype(jnp.int32)
 
     def swapped(value):
         return lax.ppermute(value, square, [(a * n_tp + b, b * n_tp + a) for a in range(n_yh) for b in range(n_tp)])
@@ -275,13 +270,11 @@
 
     image = image_in[0]
     dv = image.shape[1]
-    ring = exchanged(call(spread_kernel, shaped((n_square, 1, dv), F32))(image), square)
-    ring = call(ring_kernel, shaped((n_square, dv)))(ring)
-    ring, sent = lax.optimization_barrier((ring, sent))
-    ring_beside = lax.ppermute(ring, "z", [(i, i ^ 1) for i in range(n_z)])
-    pair = call(pair_kernel, shaped((2 * n_square, dv)))(ring, ring_beside)
-    below, above = shifted(pair, "z", 2), shifted(pair, "z", -2)
-    far = shifted(below, "z", 2)
+    column = exchanged(call(spread_kernel, shaped((n_z, 1, dv), F32))(image), "z")
+    column = call(rows_kernel, shaped((n_z, dv)))(column)
+    column, sent = lax.optimization_barrier((column, sent))
+    chip = call(pair_kernel, shaped((2 * n_z, dv)))(column, shifted(column, "core", 1))
+    chips = call(pair_kernel, shaped((4 * n_z, dv)))(chip, shifted(chip, "yl", 1))
 
     n_rows = n_z * CAP
     pick, high, low = call(
@@ -289,23 +282,24 @@
         (shaped((n_rows, toks)), shaped((toks, n_rows)), shaped((toks, n_rows))),
         scalars=1,
     )(where, meta)
-    rows = call(pack_kernel, shaped((n_rows, width)), flops=2 * n_rows * toks * width, moved=2 * n_rows * width)(
+    rows = call(pack_kernel, pltpu.HBM((n_rows, width), BF16), flops=2 * n_rows * toks * width, moved=2 * n_rows * width)(
         pick, sent, trunk_gain
     )
     arrived = exchanged(rows.reshape(n_z, CAP, width), "z").reshape(n_rows, width)
-    across, arrived, above, far = lax.optimization_barrier((across, arrived, above, far))
+    across, arrived, chips = lax.optimization_barrier((across, arrived, chips))
     both = shifted(across, "core", 1)
+    others = [shifted(chips, "yh", k) for k in range(1, n_yh)]
     made = experts(arrived, (own, other, across, both))
+    made, others = lax.optimization_barrier((made, others))
     returned = exchanged(made.reshape(n_z, CAP, width), "z").reshape(n_rows, width)
 
     n_image = n_z * n_square
     mine, theirs = call(
-        functools.partial(image_kernel, (n_yh, n_z)),
+        functools.partial(image_kernel, n_z),
         (shaped((n_image // 2, dv), F32), shaped((n_image // 2, dv))),
-        scalars=1,
         flops=4 * n_image * dv * 100,
         moved=4 * n_image * dv,
-    )(where, pair, below, above, far, image_gain, fc_in[0].T, fc_out[0])
+    )(chips, *others, image_gain, fc_in[0].T, fc_out[0])
     mine, theirs = call(fold_kernel, (shaped((n_image // 4, dv), F32), shaped((n_image // 4, dv))))(
         mine, shifted(theirs, "core", 1)
     )

time: 204 us -> 216 us (1.059)
  waiting for transfers between devices: 60.6 us -> 83.9 us
  starting transfers between devices: 104 us -> 98.6 us
  local copies, waits for them, and re-layouts: 8.88 us -> 4.59 us
    ppermute x2, waiting for transfers between devices: 0.01 us -> 41.7 us  [swapped(): lax.ppermute(value, square, [(a * n_tp + b, b * n_tp + a) for a in range(...]
    ppermute x1 -> x0, waiting for transfers between devices: 29.4 us -> none  [body(): ring_beside = lax.ppermute(ring, 'z', [(i, i ^ 1) for i in range(n_z)])]
    all_to_all x3, waiting for transfers between devices: 6.06 us -> 13.7 us  [exchanged(): return lax.all_to_all(value, axis, split_axis=0, concat_axis=0, tiled=True)]
    all_to_all x3, starting transfers between devices: 28.9 us -> 23.8 us  [exchanged(): return lax.all_to_all(value, axis, split_axis=0, concat_axis=0, tiled=True)]
    unnamed x33 -> x29, local copies, waits for them, and re-layouts: 8.88 us -> 4.59 us
    ppermute x1 -> x0, starting transfers between devices: 3.36 us -> none  [body(): ring_beside = lax.ppermute(ring, 'z', [(i, i ^ 1) for i in range(n_z)])]
    ppermute x14 -> x16, waiting for transfers between devices: 23.9 us -> 27.1 us  [shifted(): return lax.ppermute(value, axis, [(i, (i + by) % n) for i in range(n)])]
    ppermute x14 -> x16, starting transfers between devices: 54 us -> 57 us  [shifted(): return lax.ppermute(value, axis, [(i, (i + by) % n) for i in range(n)])]
  transfers between devices with their start and end apart: 22 -> 23, of which waited for: 13 -> 14; matrix products, arithmetic and copies ran while one was open for 2% -> 1% of each run, Pallas kernels for 2% -> 5%
where the time goes in v4:
time: 216 us; the launch traced here: 214 us
  starting transfers between devices  98.6 us (46%)
  waiting for transfers between devices  83.9 us (39%)
  Pallas kernels  14.1 us (7%)
  blocking collectives  9.87 us (5%)
  local copies, waits for them, and re-layouts  4.59 us (2%)
    ppermute x16, starting transfers between devices, shifted(): return lax.ppermute(value, axis, [(i, (i + by) % n) for i in range(n)])  57 us
    ppermute x2, waiting for transfers between devices, swapped(): lax.ppermute(value, square, [(a * n_tp + b, b * n_tp + a) for a in range(...  41.7 us
    ppermute x16, waiting for transfers between devices, shifted(): return lax.ppermute(value, axis, [(i, (i + by) % n) for i in range(n)])  27.1 us
    all_to_all x3, starting transfers between devices, exchanged(): return lax.all_to_all(value, axis, split_axis=0, concat_axis=0, tiled=True)  23.8 us
    all_to_all x3, waiting for transfers between devices, exchanged(): return lax.all_to_all(value, axis, split_axis=0, concat_axis=0, tiled=True)  13.7 us
    all_to_all x1, blocking collectives, exchanged(): return lax.all_to_all(value, axis, split_axis=0, concat_axis=0, tiled=True)  9.87 us
    ppermute x2, starting transfers between devices, body(): lax.ppermute(piece, ('pp',) + square, [(s * n_square + a * n_tp + b, (s +...  9.08 us
    ppermute x2, starting transfers between devices, swapped(): lax.ppermute(value, square, [(a * n_tp + b, b * n_tp + a) for a in range(...  8.75 us
  transfers between devices with their start and end apart: 23, of which 14 were waited for; matrix products, arithmetic and copies ran while one was open for 1% of the time, Pallas kernels for 5%

profile of v4, /device:TPU:1, one launch (start us, length us, event | category | flops | bytes accessed | tf_op | source)
XLA Modules:
  0.0 214.0 jit_solution(1732197014847683161)
XLA Ops:
  0.6 5.6 %collective-permute-start.2 = (bf16[128,2048]{1,0:T(8,128)(2,1)}, bf16[128,2048]{1,0:T(8,128)(2,1)S(1)}, u32[]{:S(2)}, u32[]{:S(2)}) collective-permute-start(bf16[128,2048]{1,0:T(8,128)(2,1)} %bitcast.41), channel_id=1, source_target_pairs={{0,0},{1,32},{2,64},{3,96},{32,1},{33,33},{34,65},{35,97},{64,2},{... | collective-permute-start | bytes 1572872 | tf_op jit(solution)/shard_map/ppermute | solution.py:253
  6.3 1.8 pad_maximum_fusion.refs_0_
  8.1 4.8 %collective-permute-start = (bf16[576,2048]{1,0:T(8,128)(2,1)S(1)}, bf16[576,2048]{1,0:T(8,128)(2,1)}, u32[]{:S(2)}, u32[]{:S(2)}) collective-permute-start(bf16[576,2048]{1,0:T(8,128)(2,1)S(1)} %pad_maximum_fusion.refs_0_), channel_id=1, source_target_pairs={{0,2},{2,0},{1,3},{3,1},{4,6},{6,4},{5,7},{7,5},{8,10},{10,8},{9,1... | collective-permute-start | bytes 7077896 | tf_op jit(solution)/shard_map/ppermute | solution.py:257
  12.9 0.7 shard_map.132
  13.5 10.0 %all-to-all-start = ((f32[8,1,3200]{2,1,0:T(1,128)}), f32[8,1,3200]{2,1,0:T(1,128)S(1)}, u32[]{:S(2)}, u32[]{:S(2)}) async-start(f32[8,1,3200]{2,1,0:T(1,128)} %shard_map.132), calls=%async_computation | async-start | bytes 204800 | tf_op jit(solution)/shard_map/all_to_all | solution.py:260
  23.6 3.1 %collective-permute-start.1 = (f32[16,128]{1,0:T(8,128)S(1)}, f32[16,128]{1,0:T(8,128)S(1)}, u32[]{:S(2)}, u32[]{:S(2)}) collective-permute-start(f32[16,128]{1,0:T(8,128)S(1)} %pad_maximum_fusion.1), channel_id=1, source_target_pairs={{0,0},{1,32},{2,64},{3,96},{32,1},{33,33},{34,65},{35,97},{64,2},{... | collective-permute-start | bytes 24584 | tf_op jit(solution)/shard_map/ppermute | solution.py:253
  26.7 0.1 pad_add_fusion.where
  26.8 41.7 %collective-permute-done.1.meta = f32[16,128]{1,0:T(8,128)S(1)} collective-permute-done((f32[16,128]{1,0:T(8,128)S(1)}, f32[16,128]{1,0:T(8,128)S(1)}, u32[]{:S(2)}, u32[]{:S(2)}) %collective-permute-start.1) | collective-permute-done | bytes 8224 | tf_op jit(solution)/shard_map/ppermute | solution.py:253
  68.5 0.8 shard_map.131
  69.3 0.6 copy-done.4
  70.0 0.6 copy-done.6
  70.6 0.0 all-to-all-done.spread
  70.7 1.7 shard_map.134
  72.4 10.0 %all-to-all-start.1 = ((bf16[8,40,2048]{2,1,0:T(8,128)(2,1)}), bf16[8,40,2048]{2,1,0:T(8,128)(2,1)}, u32[]{:S(2)}, u32[]{:S(2)}) async-start(bf16[8,40,2048]{2,1,0:T(8,128)(2,1)} %bitcast.35), calls=%async_computation.1 | async-start | bytes 2621440 | tf_op jit(solution)/shard_map/all_to_all | solution.py:260
  82.5 1.9 collective-permute-start.3
  84.4 1.2 collective-permute-done.3.other
  85.6 6.2 %collective-permute-start.4 = (bf16[16,3200]{1,0:T(8,128)(2,1)S(1)}, bf16[16,3200]{1,0:T(8,128)(2,1)S(1)}, u32[]{:S(2)}, u32[]{:S(2)}) collective-permute-start(bf16[16,3200]{1,0:T(8,128)(2,1)S(1)} %shard_map.135.own), channel_id=1, source_target_pairs={{0,2},{2,0},{1,3},{3,1},{4,6},{6,4},{5,7},{7,5},{8,10},{10,8},{9,1... | collective-permute-start | bytes 307208 | tf_op jit(solution)/shard_map/ppermute | solution.py:257
  91.8 2.4 %collective-permute-start.5 = (bf16[576,2048]{1,0:T(8,128)(2,1)S(1)}, bf16[576,2048]{1,0:T(8,128)(2,1)}, u32[]{:S(2)}, u32[]{:S(2)}) collective-permute-start(bf16[576,2048]{1,0:T(8,128)(2,1)S(1)} %pad_maximum_fusion.refs_0_), channel_id=1, source_target_pairs={{0,1},{1,0},{2,3},{3,2},{4,5},{5,4},{6,7},{7,6},{8,9},{9,8},{10,11... | collective-permute-start | bytes 7077896 | tf_op jit(solution)/shard_map/ppermute | solution.py:257
  94.2 0.7 collective-permute-done.4.other
  95.0 0.0 collective-permute-done.refs_2_
  95.0 8.2 %all-to-all-done.1 = bf16[8,40,2048]{2,1,0:T(8,128)(2,1)} async-done(((bf16[8,40,2048]{2,1,0:T(8,128)(2,1)}), bf16[8,40,2048]{2,1,0:T(8,128)(2,1)}, u32[]{:S(2)}, u32[]{:S(2)}) %all-to-all-start.1) | async-done | bytes 1310752 | tf_op jit(solution)/shard_map/all_to_all | solution.py:260
  103.1 1.9 collective-permute-start.6
  105.1 6.9 %collective-permute-start.7 = (bf16[32,3200]{1,0:T(8,128)(2,1)S(1)}, bf16[32,3200]{1,0:T(8,128)(2,1)S(1)}, u32[]{:S(2)}, u32[]{:S(2)}) collective-permute-start(bf16[32,3200]{1,0:T(8,128)(2,1)S(1)} %shard_map.136.refs_0_), channel_id=1, source_target_pairs={{0,32},{32,64},{64,96},{96,0},{1,33},{33,65},{65,97},{97,1},{2,34}... | collective-permute-start | bytes 614408 | tf_op jit(solution)/shard_map/ppermute | solution.py:257
  111.9 5.7 %collective-permute-start.8 = (bf16[32,3200]{1,0:T(8,128)(2,1)S(1)}, bf16[32,3200]{1,0:T(8,128)(2,1)S(1)}, u32[]{:S(2)}, u32[]{:S(2)}) collective-permute-start(bf16[32,3200]{1,0:T(8,128)(2,1)S(1)} %shard_map.136.refs_0_), channel_id=1, source_target_pairs={{0,64},{32,96},{64,0},{96,32},{1,65},{33,97},{65,1},{97,33},{2,66}... | collective-permute-start | bytes 614408 | tf_op jit(solution)/shard_map/ppermute | solution.py:257
  117.7 1.9 collective-permute-start.9
  119.6 0.0 collective-permute-done.5.refs_1_
  119.6 6.5 %shard_map.137 = bf16[320,2048]{1,0:T(8,128)(2,1)} custom-call(bf16[320,2048]{1,0:T(8,128)(2,1)} %bitcast.14.rows, bf16[576,2048]{1,0:T(8,128)(2,1)S(1)} %pad_maximum_fusion.refs_0_, bf16[576,2048]{1,0:T(8,128)(2,1)} %collective-permute-done.5.refs_1_, bf16[576,2048]{1,0:T(8,128)(2,1)} %collective-permute-done.refs_2_, ...), custom_call_target="tpu_custom_call" | custom-call | flops 3019898880 | bytes 9437184 | tf_op jit(solution)/shard_map/pallas_call | solution.py:128
  126.2 0.0 copy-start
  126.2 0.0 copy-start.9
  126.2 8.0 %collective-permute-done.8.refs_2_ = bf16[32,3200]{1,0:T(8,128)(2,1)S(1)} collective-permute-done((bf16[32,3200]{1,0:T(8,128)(2,1)S(1)}, bf16[32,3200]{1,0:T(8,128)(2,1)S(1)}, u32[]{:S(2)}, u32[]{:S(2)}) %collective-permute-start.8) | collective-permute-done | bytes 204832 | tf_op jit(solution)/shard_map/ppermute | solution.py:257
  134.3 2.8 %collective-permute-done.9.refs_3_ = bf16[32,3200]{1,0:T(8,128)(2,1)S(1)} collective-permute-done((bf16[32,3200]{1,0:T(8,128)(2,1)S(1)}, bf16[32,3200]{1,0:T(8,128)(2,1)S(1)}, u32[]{:S(2)}, u32[]{:S(2)}) %collective-permute-start.9) | collective-permute-done | bytes 204832 | tf_op jit(solution)/shard_map/ppermute | solution.py:257
  137.1 0.7 copy-done.2
  137.8 3.7 %all-to-all-start.2 = ((bf16[8,40,2048]{2,1,0:T(8,128)(2,1)}), bf16[8,40,2048]{2,1,0:T(8,128)(2,1)S(1)}, u32[]{:S(2)}, u32[]{:S(2)}) async-start(bf16[8,40,2048]{2,1,0:T(8,128)(2,1)} %bitcast.34), calls=%async_computation.2 | async-start | bytes 2621440 | tf_op jit(solution)/shard_map/all_to_all | solution.py:260
  141.5 0.0 copy-start.1
  141.5 1.1 copy-done.1
  142.6 1.3 shard_map.138
  143.9 2.4 %collective-permute-start.10 = (bf16[64,3200]{1,0:T(8,128)(2,1)S(1)}, bf16[64,3200]{1,0:T(8,128)(2,1)S(1)}, u32[]{:S(2)}, u32[]{:S(2)}) collective-permute-start(bf16[64,3200]{1,0:T(8,128)(2,1)S(1)} %get-tuple-element.39), channel_id=1, source_target_pairs={{0,1},{1,0},{2,3},{3,2},{4,5},{5,4},{6,7},{7,6},{8,9},{9,8},{10,11... | collective-permute-start | bytes 1228808 | tf_op jit(solution)/shard_map/ppermute | solution.py:257
  146.3 1.4 collective-permute-done.10.came
  147.7 0.1 shard_map.139
  147.7 1.9 collective-permute-start.11
  149.7 6.3 %collective-permute-done.11.came = bf16[32,3200]{1,0:T(8,128)(2,1)S(1)} collective-permute-done((bf16[32,3200]{1,0:T(8,128)(2,1)S(1)}, bf16[32,3200]{1,0:T(8,128)(2,1)S(1)}, u32[]{:S(2)}, u32[]{:S(2)}) %collective-permute-start.11) | collective-permute-done | bytes 204832 | tf_op jit(solution)/shard_map/ppermute | solution.py:257
  155.9 0.1 shard_map.140
  156.0 2.1 collective-permute-start.12
  158.1 5.9 %collective-permute-start.13 = (bf16[8,3200]{1,0:T(8,128)(2,1)S(1)}, bf16[8,3200]{1,0:T(8,128)(2,1)S(1)}, u32[]{:S(2)}, u32[]{:S(2)}) collective-permute-start(bf16[8,3200]{1,0:T(8,128)(2,1)S(1)} %get-tuple-element.44), channel_id=1, source_target_pairs={{0,64},{32,96},{64,0},{96,32},{1,65},{33,97},{65,1},{97,33},{2,66}... | collective-permute-start | bytes 153608 | tf_op jit(solution)/shard_map/ppermute | solution.py:257
  164.0 4.1 %collective-permute-start.14 = (bf16[8,3200]{1,0:T(8,128)(2,1)S(1)}, bf16[8,3200]{1,0:T(8,128)(2,1)S(1)}, u32[]{:S(2)}, u32[]{:S(2)}) collective-permute-start(bf16[8,3200]{1,0:T(8,128)(2,1)S(1)} %get-tuple-element.45), channel_id=1, source_target_pairs={{0,96},{32,0},{64,32},{96,64},{1,97},{33,1},{65,33},{97,65},{2,98}... | collective-permute-start | bytes 153608 | tf_op jit(solution)/shard_map/ppermute | solution.py:257
  168.1 0.0 collective-permute-done.12.refs_0_
  168.2 2.4 %collective-permute-done.14.refs_2_ = bf16[8,3200]{1,0:T(8,128)(2,1)S(1)} collective-permute-done((bf16[8,3200]{1,0:T(8,128)(2,1)S(1)}, bf16[8,3200]{1,0:T(8,128)(2,1)S(1)}, u32[]{:S(2)}, u32[]{:S(2)}) %collective-permute-start.14) | collective-permute-done | bytes 51232 | tf_op jit(solution)/shard_map/ppermute | solution.py:257
  170.7 5.6 %all-to-all-done.2 = bf16[8,40,2048]{2,1,0:T(8,128)(2,1)S(1)} async-done(((bf16[8,40,2048]{2,1,0:T(8,128)(2,1)}), bf16[8,40,2048]{2,1,0:T(8,128)(2,1)S(1)}, u32[]{:S(2)}, u32[]{:S(2)}) %all-to-all-start.2) | async-done | bytes 1310752 | tf_op jit(solution)/shard_map/all_to_all | solution.py:260
  176.2 0.9 copy-done.7
  177.1 1.3 shard_map.142
  178.4 3.4 %collective-permute-start.15 = (bf16[128,1024]{1,0:T(8,128)(2,1)S(1)}, bf16[128,1024]{1,0:T(8,128)(2,1)S(1)}, u32[]{:S(2)}, u32[]{:S(2)}) collective-permute-start(bf16[128,1024]{1,0:T(8,128)(2,1)S(1)} %get-tuple-element.51), channel_id=1, source_target_pairs={{0,128},{1,160},{2,192},{3,224},{32,129},{33,161},{34,193},{35,225... | collective-permute-start | bytes 786440 | tf_op jit(solution)/shard_map/ppermute | solution.py:319
  181.8 5.7 %collective-permute-start.16 = (bf16[128,1024]{1,0:T(8,128)(2,1)S(1)}, bf16[128,1024]{1,0:T(8,128)(2,1)S(1)}, u32[]{:S(2)}, u32[]{:S(2)}) collective-permute-start(bf16[128,1024]{1,0:T(8,128)(2,1)S(1)} %get-tuple-element.52), channel_id=1, source_target_pairs={{0,130},{1,162},{2,194},{3,226},{32,131},{33,163},{34,195},{35,227... | collective-permute-start | bytes 786440 | tf_op jit(solution)/shard_map/ppermute | solution.py:319
  187.5 9.9 %all_to_all.20.spread = f32[8,1,3200]{2,1,0:T(1,128)S(1)} all-to-all(f32[8,1,3200]{2,1,0:T(1,128)S(1)} %shard_map.141), channel_id=1, replica_groups=mesh['pp'=4,'yh'=4,'z'=8,'yl'=2,'core'=2] {'z'}, dimensions={0} | all-to-all | bytes 204800 | tf_op jit(solution)/shard_map/all_to_all | solution.py:260
  197.4 1.3 collective-permute-done.16.right
  198.7 0.1 shard_map.143.left
  198.8 2.6 %collective-permute-start.17 = (bf16[128,1024]{1,0:T(8,128)(2,1)S(1)}, bf16[128,1024]{1,0:T(8,128)(2,1)S(1)}, u32[]{:S(2)}, u32[]{:S(2)}) collective-permute-start(bf16[128,1024]{1,0:T(8,128)(2,1)S(1)} %shard_map.143.left), channel_id=1, source_target_pairs={{0,1},{1,0},{2,3},{3,2},{4,5},{5,4},{6,7},{7,6},{8,9},{9,8},{10,11... | collective-permute-start | bytes 786440 | tf_op jit(solution)/shard_map/ppermute | solution.py:257
  201.4 1.1 collective-permute-done.17.right
  202.5 0.1 shard_map.144.own
  202.6 3.3 %collective-permute-start.18 = (bf16[128,1024]{1,0:T(8,128)(2,1)S(1)}, bf16[128,1024]{1,0:T(8,128)(2,1)S(1)}, u32[]{:S(2)}, u32[]{:S(2)}) collective-permute-start(bf16[128,1024]{1,0:T(8,128)(2,1)S(1)} %shard_map.144.own), channel_id=1, source_target_pairs={{0,2},{2,0},{1,3},{3,1},{4,6},{6,4},{5,7},{7,5},{8,10},{10,8},{9,1... | collective-permute-start | bytes 786440 | tf_op jit(solution)/shard_map/ppermute | solution.py:257
  205.9 2.9 %collective-permute-start.19 = (bf16[1,1,3200]{2,1,0:T(2,128)(2,1)S(1)}, bf16[1,1,3200]{2,1,0:T(2,128)(2,1)S(1)}, u32[]{:S(2)}, u32[]{:S(2)}) collective-permute-start(bf16[1,1,3200]{2,1,0:T(2,128)(2,1)S(1)} %bitcast.33), channel_id=1, source_target_pairs={{0,384},{128,0},{256,128},{384,256},{1,385},{129,1},{257,129},{385... | collective-permute-start | bytes 19208 | tf_op jit(solution)/shard_map/ppermute | solution.py:257
  208.9 1.8 collective-permute-done.19
  210.7 1.3 collective-permute-done.18.across
  212.0 1.4 shard_map.145
  213.4 0.6 copy.15
  (32 shorter events, 0.2 us)
Async XLA Ops:
  0.6 70.0 %collective-permute-start.2 = (bf16[128,2048]{1,0:T(8,128)(2,1)}, bf16[128,2048]{1,0:T(8,128)(2,1)S(1)}, u32[]{:S(2)}, u32[]{:S(2)}) collective-permute-start(bf16[128,2048]{1,0:T(8,128)(2,1)} %bitcast.41), channel_id=1, source_target_pairs={{0,0},{1,32},{2,64},{3,96},{32,1},{33,33},{34,65},{35,97},{64,2},{... | collective-permute-start | bytes 1572872 | tf_op jit(solution)/shard_map/ppermute | solution.py:253
  6.2 6.6 %copy-start.8 = (bf16[1,1,3200]{2,1,0:T(2,128)(2,1)S(1)}, bf16[1,1,3200]{2,1,0:T(2,128)(2,1)}, u32[]{:S(2)}) copy-start(bf16[1,1,3200]{2,1,0:T(2,128)(2,1)} %param.19) | copy-start | bytes 19204
  6.3 17.3 %copy-start.12 = (s32[1,128,8]{1,2,0:T(8,128)S(1)}, s32[1,128,8]{1,2,0:T(8,128)}, u32[]{:S(2)}) copy-start(s32[1,128,8]{1,2,0:T(8,128)} %param.13) | copy-start | bytes 12292
  6.3 17.3 %copy-start.13 = (f32[1,128,8]{1,2,0:T(8,128)S(1)}, f32[1,128,8]{1,2,0:T(8,128)}, u32[]{:S(2)}) copy-start(f32[1,128,8]{1,2,0:T(8,128)} %param.14) | copy-start | bytes 12292
  6.3 64.4 %copy-start.11 = (f32[1,2048]{1,0:T(1,128)S(1)}, f32[1,2048]{1,0:T(1,128)}, u32[]{:S(2)}) copy-start(f32[1,2048]{1,0:T(1,128)} %gain.1) | copy-start | bytes 24580
  8.1 86.9 %collective-permute-start = (bf16[576,2048]{1,0:T(8,128)(2,1)S(1)}, bf16[576,2048]{1,0:T(8,128)(2,1)}, u32[]{:S(2)}, u32[]{:S(2)}) collective-permute-start(bf16[576,2048]{1,0:T(8,128)(2,1)S(1)} %pad_maximum_fusion.refs_0_), channel_id=1, source_target_pairs={{0,2},{2,0},{1,3},{3,1},{4,6},{6,4},{5,7},{7,5},{8,10},{10,8},{9,1... | collective-permute-start | bytes 7077896 | tf_op jit(solution)/shard_map/ppermute | solution.py:257
  13.5 57.1 %all-to-all-start = ((f32[8,1,3200]{2,1,0:T(1,128)}), f32[8,1,3200]{2,1,0:T(1,128)S(1)}, u32[]{:S(2)}, u32[]{:S(2)}) async-start(f32[8,1,3200]{2,1,0:T(1,128)} %shard_map.132), calls=%async_computation | async-start | bytes 204800 | tf_op jit(solution)/shard_map/all_to_all | solution.py:260
  23.6 44.9 %collective-permute-start.1 = (f32[16,128]{1,0:T(8,128)S(1)}, f32[16,128]{1,0:T(8,128)S(1)}, u32[]{:S(2)}, u32[]{:S(2)}) collective-permute-start(f32[16,128]{1,0:T(8,128)S(1)} %pad_maximum_fusion.1), channel_id=1, source_target_pairs={{0,0},{1,32},{2,64},{3,96},{32,1},{33,33},{34,65},{35,97},{64,2},{... | collective-permute-start | bytes 24584 | tf_op jit(solution)/shard_map/ppermute | solution.py:253
  69.3 0.7 copy-start.4
  70.0 0.6 copy-start.6
  72.4 30.7 %all-to-all-start.1 = ((bf16[8,40,2048]{2,1,0:T(8,128)(2,1)}), bf16[8,40,2048]{2,1,0:T(8,128)(2,1)}, u32[]{:S(2)}, u32[]{:S(2)}) async-start(bf16[8,40,2048]{2,1,0:T(8,128)(2,1)} %bitcast.35), calls=%async_computation.1 | async-start | bytes 2621440 | tf_op jit(solution)/shard_map/all_to_all | solution.py:260
  82.5 3.1 %collective-permute-start.3 = (bf16[8,3200]{1,0:T(8,128)(2,1)S(1)}, bf16[8,3200]{1,0:T(8,128)(2,1)S(1)}, u32[]{:S(2)}, u32[]{:S(2)}) collective-permute-start(bf16[8,3200]{1,0:T(8,128)(2,1)S(1)} %shard_map.133.own), channel_id=1, source_target_pairs={{0,1},{1,0},{2,3},{3,2},{4,5},{5,4},{6,7},{7,6},{8,9},{9,8},{10,11... | collective-permute-start | bytes 153608 | tf_op jit(solution)/shard_map/ppermute | solution.py:257
  85.6 9.3 %collective-permute-start.4 = (bf16[16,3200]{1,0:T(8,128)(2,1)S(1)}, bf16[16,3200]{1,0:T(8,128)(2,1)S(1)}, u32[]{:S(2)}, u32[]{:S(2)}) collective-permute-start(bf16[16,3200]{1,0:T(8,128)(2,1)S(1)} %shard_map.135.own), channel_id=1, source_target_pairs={{0,2},{2,0},{1,3},{3,1},{4,6},{6,4},{5,7},{7,5},{8,10},{10,8},{9,1... | collective-permute-start | bytes 307208 | tf_op jit(solution)/shard_map/ppermute | solution.py:257
  91.8 27.8 %collective-permute-start.5 = (bf16[576,2048]{1,0:T(8,128)(2,1)S(1)}, bf16[576,2048]{1,0:T(8,128)(2,1)}, u32[]{:S(2)}, u32[]{:S(2)}) collective-permute-start(bf16[576,2048]{1,0:T(8,128)(2,1)S(1)} %pad_maximum_fusion.refs_0_), channel_id=1, source_target_pairs={{0,1},{1,0},{2,3},{3,2},{4,5},{5,4},{6,7},{7,6},{8,9},{9,8},{10,11... | collective-permute-start | bytes 7077896 | tf_op jit(solution)/shard_map/ppermute | solution.py:257
  103.1 16.5 %collective-permute-start.6 = (bf16[576,2048]{1,0:T(8,128)(2,1)}, bf16[576,2048]{1,0:T(8,128)(2,1)S(1)}, u32[]{:S(2)}, u32[]{:S(2)}) collective-permute-start(bf16[576,2048]{1,0:T(8,128)(2,1)} %collective-permute-done.refs_2_), channel_id=1, source_target_pairs={{0,1},{1,0},{2,3},{3,2},{4,5},{5,4},{6,7},{7,6},{8,9},{9,8},{10,11... | collective-permute-start | bytes 7077896 | tf_op jit(solution)/shard_map/ppermute | solution.py:257
  105.1 21.2 %collective-permute-start.7 = (bf16[32,3200]{1,0:T(8,128)(2,1)S(1)}, bf16[32,3200]{1,0:T(8,128)(2,1)S(1)}, u32[]{:S(2)}, u32[]{:S(2)}) collective-permute-start(bf16[32,3200]{1,0:T(8,128)(2,1)S(1)} %shard_map.136.refs_0_), channel_id=1, source_target_pairs={{0,32},{32,64},{64,96},{96,0},{1,33},{33,65},{65,97},{97,1},{2,34}... | collective-permute-start | bytes 614408 | tf_op jit(solution)/shard_map/ppermute | solution.py:257
  111.9 22.3 %collective-permute-start.8 = (bf16[32,3200]{1,0:T(8,128)(2,1)S(1)}, bf16[32,3200]{1,0:T(8,128)(2,1)S(1)}, u32[]{:S(2)}, u32[]{:S(2)}) collective-permute-start(bf16[32,3200]{1,0:T(8,128)(2,1)S(1)} %shard_map.136.refs_0_), channel_id=1, source_target_pairs={{0,64},{32,96},{64,0},{96,32},{1,65},{33,97},{65,1},{97,33},{2,66}... | collective-permute-start | bytes 614408 | tf_op jit(solution)/shard_map/ppermute | solution.py:257
  117.7 19.4 %collective-permute-start.9 = (bf16[32,3200]{1,0:T(8,128)(2,1)S(1)}, bf16[32,3200]{1,0:T(8,128)(2,1)S(1)}, u32[]{:S(2)}, u32[]{:S(2)}) collective-permute-start(bf16[32,3200]{1,0:T(8,128)(2,1)S(1)} %shard_map.136.refs_0_), channel_id=1, source_target_pairs={{0,96},{32,0},{64,32},{96,64},{1,97},{33,1},{65,33},{97,65},{2,98}... | collective-permute-start | bytes 614408 | tf_op jit(solution)/shard_map/ppermute | solution.py:257
  126.2 15.3 %copy-start = (bf16[1,3200,100]{1,2,0:T(8,128)(2,1)S(1)}, bf16[1,3200,100]{1,2,0:T(8,128)(2,1)}, u32[]{:S(2)}) copy-start(bf16[1,3200,100]{1,2,0:T(8,128)(2,1)} %param.21) | copy-start | bytes 1920004
  126.2 15.3 %copy-start.9 = (f32[1,3200]{1,0:T(1,128)S(1)}, f32[1,3200]{1,0:T(1,128)}, u32[]{:S(2)}) copy-start(f32[1,3200]{1,0:T(1,128)} %refs_4_.1) | copy-start | bytes 38404
  137.1 0.7 copy-start.2
  137.8 3.7 %copy-start.3 = (bf16[32,3200]{1,0:T(8,128)(2,1)S(1)}, bf16[32,3200]{1,0:T(8,128)(2,1)}, u32[]{:S(2)}) copy-start(bf16[32,3200]{1,0:T(8,128)(2,1)} %copy-done.2) | copy-start | bytes 614404
  137.8 38.4 %copy-start.5 = (bf16[128,320]{1,0:T(8,128)(2,1)S(1)}, bf16[128,320]{1,0:T(8,128)(2,1)}, u32[]{:S(2)}) copy-start(bf16[128,320]{1,0:T(8,128)(2,1)} %copy-done.4) | copy-start | bytes 245764
  137.8 38.4 %all-to-all-start.2 = ((bf16[8,40,2048]{2,1,0:T(8,128)(2,1)}), bf16[8,40,2048]{2,1,0:T(8,128)(2,1)S(1)}, u32[]{:S(2)}, u32[]{:S(2)}) async-start(bf16[8,40,2048]{2,1,0:T(8,128)(2,1)} %bitcast.34), calls=%async_computation.2 | async-start | bytes 2621440 | tf_op jit(solution)/shard_map/all_to_all | solution.py:260
  141.5 1.1 copy-start.1
  143.9 3.8 %collective-permute-start.10 = (bf16[64,3200]{1,0:T(8,128)(2,1)S(1)}, bf16[64,3200]{1,0:T(8,128)(2,1)S(1)}, u32[]{:S(2)}, u32[]{:S(2)}) collective-permute-start(bf16[64,3200]{1,0:T(8,128)(2,1)S(1)} %get-tuple-element.39), channel_id=1, source_target_pairs={{0,1},{1,0},{2,3},{3,2},{4,5},{5,4},{6,7},{7,6},{8,9},{9,8},{10,11... | collective-permute-start | bytes 1228808 | tf_op jit(solution)/shard_map/ppermute | solution.py:257
  147.7 8.2 %collective-permute-start.11 = (bf16[32,3200]{1,0:T(8,128)(2,1)S(1)}, bf16[32,3200]{1,0:T(8,128)(2,1)S(1)}, u32[]{:S(2)}, u32[]{:S(2)}) collective-permute-start(bf16[32,3200]{1,0:T(8,128)(2,1)S(1)} %get-tuple-element.41), channel_id=1, source_target_pairs={{0,2},{2,0},{1,3},{3,1},{4,6},{6,4},{5,7},{7,5},{8,10},{10,8},{9,1... | collective-permute-start | bytes 614408 | tf_op jit(solution)/shard_map/ppermute | solution.py:257
  155.9 50.0 %copy-start.10 = (f32[1,3200]{1,0:T(1,128)S(1)}, f32[1,3200]{1,0:T(1,128)}, u32[]{:S(2)}) copy-start(f32[1,3200]{1,0:T(1,128)} %scale.1) | copy-start | bytes 38404
  156.0 12.2 %collective-permute-start.12 = (bf16[8,3200]{1,0:T(8,128)(2,1)S(1)}, bf16[8,3200]{1,0:T(8,128)(2,1)S(1)}, u32[]{:S(2)}, u32[]{:S(2)}) collective-permute-start(bf16[8,3200]{1,0:T(8,128)(2,1)S(1)} %get-tuple-element.43), channel_id=1, source_target_pairs={{0,32},{32,64},{64,96},{96,0},{1,33},{33,65},{65,97},{97,1},{2,34}... | collective-permute-start | bytes 153608 | tf_op jit(solution)/shard_map/ppermute | solution.py:257
  158.1 10.1 %collective-permute-start.13 = (bf16[8,3200]{1,0:T(8,128)(2,1)S(1)}, bf16[8,3200]{1,0:T(8,128)(2,1)S(1)}, u32[]{:S(2)}, u32[]{:S(2)}) collective-permute-start(bf16[8,3200]{1,0:T(8,128)(2,1)S(1)} %get-tuple-element.44), channel_id=1, source_target_pairs={{0,64},{32,96},{64,0},{96,32},{1,65},{33,97},{65,1},{97,33},{2,66}... | collective-permute-start | bytes 153608 | tf_op jit(solution)/shard_map/ppermute | solution.py:257
  164.0 6.6 %collective-permute-start.14 = (bf16[8,3200]{1,0:T(8,128)(2,1)S(1)}, bf16[8,3200]{1,0:T(8,128)(2,1)S(1)}, u32[]{:S(2)}, u32[]{:S(2)}) collective-permute-start(bf16[8,3200]{1,0:T(8,128)(2,1)S(1)} %get-tuple-element.45), channel_id=1, source_target_pairs={{0,96},{32,0},{64,32},{96,64},{1,97},{33,1},{65,33},{97,65},{2,98}... | collective-permute-start | bytes 153608 | tf_op jit(solution)/shard_map/ppermute | solution.py:257
  176.2 0.9 copy-start.7
  178.4 19.0 %collective-permute-start.15 = (bf16[128,1024]{1,0:T(8,128)(2,1)S(1)}, bf16[128,1024]{1,0:T(8,128)(2,1)S(1)}, u32[]{:S(2)}, u32[]{:S(2)}) collective-permute-start(bf16[128,1024]{1,0:T(8,128)(2,1)S(1)} %get-tuple-element.51), channel_id=1, source_target_pairs={{0,128},{1,160},{2,192},{3,224},{32,129},{33,161},{34,193},{35,225... | collective-permute-start | bytes 786440 | tf_op jit(solution)/shard_map/ppermute | solution.py:319
  181.8 16.9 %collective-permute-start.16 = (bf16[128,1024]{1,0:T(8,128)(2,1)S(1)}, bf16[128,1024]{1,0:T(8,128)(2,1)S(1)}, u32[]{:S(2)}, u32[]{:S(2)}) collective-permute-start(bf16[128,1024]{1,0:T(8,128)(2,1)S(1)} %get-tuple-element.52), channel_id=1, source_target_pairs={{0,130},{1,162},{2,194},{3,226},{32,131},{33,163},{34,195},{35,227... | collective-permute-start | bytes 786440 | tf_op jit(solution)/shard_map/ppermute | solution.py:319
  198.8 3.8 %collective-permute-start.17 = (bf16[128,1024]{1,0:T(8,128)(2,1)S(1)}, bf16[128,1024]{1,0:T(8,128)(2,1)S(1)}, u32[]{:S(2)}, u32[]{:S(2)}) collective-permute-start(bf16[128,1024]{1,0:T(8,128)(2,1)S(1)} %shard_map.143.left), channel_id=1, source_target_pairs={{0,1},{1,0},{2,3},{3,2},{4,5},{5,4},{6,7},{7,6},{8,9},{9,8},{10,11... | collective-permute-start | bytes 786440 | tf_op jit(solution)/shard_map/ppermute | solution.py:257
  202.6 9.4 %collective-permute-start.18 = (bf16[128,1024]{1,0:T(8,128)(2,1)S(1)}, bf16[128,1024]{1,0:T(8,128)(2,1)S(1)}, u32[]{:S(2)}, u32[]{:S(2)}) collective-permute-start(bf16[128,1024]{1,0:T(8,128)(2,1)S(1)} %shard_map.144.own), channel_id=1, source_target_pairs={{0,2},{2,0},{1,3},{3,1},{4,6},{6,4},{5,7},{7,5},{8,10},{10,8},{9,1... | collective-permute-start | bytes 786440 | tf_op jit(solution)/shard_map/ppermute | solution.py:257
  205.9 4.7 %collective-permute-start.19 = (bf16[1,1,3200]{2,1,0:T(2,128)(2,1)S(1)}, bf16[1,1,3200]{2,1,0:T(2,128)(2,1)S(1)}, u32[]{:S(2)}, u32[]{:S(2)}) collective-permute-start(bf16[1,1,3200]{2,1,0:T(2,128)(2,1)S(1)} %bitcast.33), channel_id=1, source_target_pairs={{0,384},{128,0},{256,128},{384,256},{1,385},{129,1},{257,129},{385... | collective-permute-start | bytes 19208 | tf_op jit(solution)/shard_map/ppermute | solution.py:257

commit v5 on v4

--- a/solution.py
+++ b/solution.py
@@ -40,78 +40,100 @@
     return lax.dot_general(a, b, (((1,), (1,)), ((), ())), preferred_element_type=F32)
 
 
-def table_kernel(where, meta, pick, high, low):
-    rows, toks = pick.shape
-    group = rows // CAP
-    topk = meta.shape[0] // 2
-    first = where[0] * group
+def send_kernel(ids, scores, toks, out):
+    topk, count = ids.shape
+    width = toks.shape[1]
+    given = scores[...]
+    weights = given / jnp.sum(given, axis=0, keepdims=True)
+    top = weights.astype(BF16).astype(F32)
+    parts = [ids[...].astype(F32), top, weights - top, jnp.zeros((out.shape[1] - width - 3 * topk, count), F32)]
+    out[:, :width] = toks[...]
+    out[:, width:] = jnp.concatenate(parts, axis=0).T.astype(BF16)
+
+
+def table(group, first, meta, topk):
+    meta = meta.astype(F32).T
+    toks = meta.shape[1]
     wanted = (lax.broadcasted_iota(jnp.int32, (group, toks), 0) + first).astype(F32)
-    scores = meta[topk:, :]
-    total = jnp.sum(scores, axis=0, keepdims=True)
     member = jnp.zeros((group, toks), F32)
     weight = jnp.zeros((group, toks), F32)
     for k in range(topk):
         same = meta[k : k + 1, :] == wanted
         member = jnp.where(same, 1.0, member)
-        weight = jnp.where(same, meta[topk + k : topk + k + 1, :] / total, weight)
+        weight = jnp.where(same, meta[topk + k : topk + k + 1, :] + meta[2 * topk + k : 2 * topk + k + 1, :], weight)
     earlier = lax.broadcasted_iota(jnp.int32, (toks, toks), 0) < lax.broadcasted_iota(jnp.int32, (toks, toks), 1)
     rank = jnp.dot(member.astype(BF16), earlier.astype(F32).astype(BF16), preferred_element_type=F32)
     rank = jnp.where(member > 0.5, rank, -1.0)
     slots = lax.broadcasted_iota(jnp.int32, (group, CAP, toks), 1).astype(F32)
-    hit = jnp.where(rank[:, None, :] == slots, 1.0, 0.0)
-    pick[...] = hit.reshape(rows, toks).astype(BF16)
-    scaled = (hit * weight[:, None, :]).reshape(rows, toks).T
+    return jnp.where(rank[:, None, :] == slots, 1.0, 0.0), weight
+
+
+def pack_kernel(topk, where, sent, gain, rows):
+    n, width = rows.shape
+    group = n // CAP
+    hit, _ = table(group, where[0] * group, sent[:, width:], topk)
+    wide = sent[:, :width].astype(F32)
+    scale = lax.rsqrt(jnp.mean(wide * wide, axis=-1, keepdims=True) + 1e-06)
+    normed = (wide * scale * gain[...]).astype(BF16)
+    pick = hit.reshape(n, hit.shape[2]).astype(BF16)
+    rows[...] = jnp.dot(pick, normed, preferred_element_type=F32).astype(BF16)
+
+
+def weigh_kernel(topk, where, meta, high, low):
+    toks, n = high.shape
+    group = n // CAP
+    hit, weight = table(group, where[0] * group, meta[...], topk)
+    scaled = (hit * weight[:, None, :]).reshape(n, toks).T
     top = scaled.astype(BF16)
     high[...] = top
     low[...] = (scaled - top.astype(F32)).astype(BF16)
 
 
-def pack_kernel(pick, toks, gain, rows):
-    wide = toks[...].astype(F32)
-    scale = lax.rsqrt(jnp.mean(wide * wide, axis=-1, keepdims=True) + 1e-06)
-    normed = (wide * scale * gain[...]).astype(BF16)
-    rows[...] = jnp.dot(pick[...], normed, preferred_element_type=F32).astype(BF16)
-
-
-def expert_kernel(rows, *refs):
+def hidden_kernel(rows, *refs):
     shards, out = refs[:4], refs[4]
-    rows_v, gate_v, up_v, down_v, hidden_v, out_v, row_sem, in_sem, out_sem = refs[5:]
-    count = shards[0].shape[0] // 3
+    rows_v, gate_v, up_v, row_sem, in_sem = refs[5:]
+    count = shards[0].shape[0] // 2
     row_copy = pltpu.make_async_copy(rows, rows_v, row_sem)
     row_copy.start()
     copies = []
     for s, shard in enumerate(shards):
-        for p, held in enumerate((gate_v, up_v, down_v)):
-            copies.append(
-                pltpu.make_async_copy(
-                    shard.at[pl.ds(p * count, count)], held.at[pl.ds(s * count, count)], in_sem.at[3 * s + p]
-                )
-            )
-    for s in range(4):
-        copies[3 * s].start()
-        copies[3 * s + 1].start()
-    for s in range(4):
-        copies[3 * s + 2].start()
+        place = pl.ds(s * count, count)
+        copies.append(pltpu.make_async_copy(shard.at[pl.ds(0, count)], gate_v.at[place], in_sem.at[2 * s]))
+        copies.append(pltpu.make_async_copy(shard.at[pl.ds(count, count)], up_v.at[place], in_sem.at[2 * s + 1]))
+    for copy in copies:
+        copy.start()
     row_copy.wait()
     flat = rows_v[...]
     step = 256
     seen = 0
     for c in range(4 * count // step):
         while seen * count < (c + 1) * step:
-            copies[3 * seen].wait()
-            copies[3 * seen + 1].wait()
+            copies[2 * seen].wait()
+            copies[2 * seen + 1].wait()
             seen += 1
         block = slice(c * step, (c + 1) * step)
         gate = nt(flat, gate_v[block, :])
         upval = nt(flat, up_v[block, :])
-        hidden_v[:, block] = (gate * jax.nn.sigmoid(gate) * upval).astype(BF16)
-    for s in range(4):
-        copies[3 * s + 2].wait()
+        out[:, block] = (gate * jax.nn.sigmoid(gate) * upval).astype(BF16)
+
+
+def down_kernel(hidden, *refs):
+    shards, out = refs[:4], refs[4]
+    down_v, out_v, in_sem, out_sem = refs[5:]
+    count = shards[0].shape[0]
+    copies = [
+        pltpu.make_async_copy(shard, down_v.at[pl.ds(s * count, count)], in_sem.at[s])
+        for s, shard in enumerate(shards)
+    ]
+    for copy in copies:
+        copy.start()
+    for copy in copies:
+        copy.wait()
     cols = out_v.shape[1] // 4
     leaving = []
     for j in range(4):
         block = slice(j * cols, (j + 1) * cols)
-        out_v[:, block] = jnp.dot(hidden_v[...], down_v[:, block], preferred_element_type=F32).astype(BF16)
+        out_v[:, block] = jnp.dot(hidden[...], down_v[:, block], preferred_element_type=F32).astype(BF16)
         copy = pltpu.make_async_copy(
             out_v.at[:, pl.ds(j * cols, cols)], out.at[:, pl.ds(j * cols, cols)], out_sem.at[j]
         )
@@ -121,29 +143,46 @@
         copy.wait()
 
 
-def experts(rows, shards):
+ANYWHERE = pl.BlockSpec(memory_space=pl.ANY)
+
+
+def hidden_units(rows, shards):
     n, width = rows.shape
-    count = shards[0].shape[0] // 3 * 4
-    anywhere = pl.BlockSpec(memory_space=pl.ANY)
+    count = shards[0].shape[0] * 2
     return pl.pallas_call(
-        expert_kernel,
-        out_shape=pltpu.HBM((n, width), BF16),
-        in_specs=[anywhere] * 5,
-        out_specs=anywhere,
+        hidden_kernel,
+        out_shape=shaped((n, count)),
+        in_specs=[ANYWHERE] * 5,
+        out_specs=VM,
         scratch_shapes=[
             pltpu.VMEM((n, width), BF16),
             pltpu.VMEM((count, width), BF16),
             pltpu.VMEM((count, width), BF16),
+            pltpu.SemaphoreType.DMA,
+            pltpu.SemaphoreType.DMA((8,)),
+        ],
+        compiler_params=pltpu.CompilerParams(vmem_limit_bytes=LARGE),
+        cost_estimate=pl.CostEstimate(flops=4 * n * width * count, bytes_accessed=4 * count * width, transcendentals=0),
+    )(rows, *shards)
+
+
+def expert_rows(hidden, shards):
+    n, count = hidden.shape
+    width = shards[0].shape[1]
+    return pl.pallas_call(
+        down_kernel,
+        out_shape=pltpu.HBM((n, width), BF16),
+        in_specs=[VM] + [ANYWHERE] * 4,
+        out_specs=ANYWHERE,
+        scratch_shapes=[
             pltpu.VMEM((count, width), BF16),
-            pltpu.VMEM((n, count), BF16),
             pltpu.VMEM((n, width), BF16),
-            pltpu.SemaphoreType.DMA,
-            pltpu.SemaphoreType.DMA((12,)),
+            pltpu.SemaphoreType.DMA((4,)),
             pltpu.SemaphoreType.DMA((4,)),
         ],
-        compiler_params=pltpu.CompilerParams(vmem_limit_bytes=LARGE),
-        cost_estimate=pl.CostEstimate(flops=6 * n * width * count, bytes_accessed=6 * count * width, transcendentals=0),
-    )(rows, *shards)
+        compiler_params=pltpu.CompilerParams(vmem_limit_bytes=SMALL),
+        cost_estimate=pl.CostEstimate(flops=2 * n * width * count, bytes_accessed=2 * count * width, transcendentals=0),
+    )(hidden, *shards)
 
 
 def combine_kernel(where, toks, high, low, made, kept, given):
@@ -181,19 +220,22 @@
 
 
 def pair_kernel(own, other, out):
-    out[...] = jnp.concatenate([own[...].astype(F32), other[...].astype(F32)], axis=0).astype(BF16)
-
-
-def image_kernel(n_z, *refs):
-    groups, (gain, first, second, mine, theirs) = refs[:-5], refs[-5:]
-    wide = [group[...].astype(F32) for group in groups]
-    n_yh = len(wide)
+    both = jnp.concatenate([own[...].astype(F32), other[...].astype(F32)], axis=0).astype(BF16)
+    dv = both.shape[1]
+    out[:, :dv] = both
+    if out.shape[1] > dv:
+        out[:, dv:] = jnp.zeros((out.shape[0], out.shape[1] - dv), BF16)
+
+
+def image_kernel(n_yh, rows, gain, first, second, mine, theirs):
+    wide = rows[:, : gain.shape[1]].astype(F32)
+    n_z = wide.shape[0] // (4 * n_yh)
     blocks = []
     for core in range(2):
         for low in range(2):
-            for ahead in range(n_yh):
-                at = (low * 2 + core) * n_z
-                blocks.append(wide[(n_yh - ahead) % n_yh][at : at + n_z, :])
+            for high in range(n_yh):
+                at = ((high * 2 + low) * 2 + core) * n_z
+                blocks.append(wide[at : at + n_z, :])
     wide = jnp.concatenate(blocks, axis=0)
     scale = lax.rsqrt(jnp.mean(wide * wide, axis=-1, keepdims=True) + 1e-06)
     normed = (wide * scale * gain[...]).astype(BF16)
@@ -209,15 +251,12 @@
     total = held[...] + came[...].astype(F32)
     n = keep.shape[0]
     keep[...] = total[:n]
-    for i, send in enumerate(sends):
-        send[...] = total[n + i * send.shape[0] : n + (i + 1) * send.shape[0]].astype(BF16)
-
-
-def column_kernel(held, *refs):
-    out = refs[-1]
+    for send in sends:
+        send[...] = total[n:].astype(BF16)
+
+
+def column_kernel(held, out):
     total = held[...]
-    for came in refs[:-1]:
-        total += came[...].astype(F32)
     for i in range(out.shape[0]):
         out[i] = total[i : i + 1]
 
@@ -259,58 +298,62 @@
     def exchanged(value, axis):
         return lax.all_to_all(value, axis, split_axis=0, concat_axis=0, tiled=True)
 
-    own = jnp.concatenate([w_gate[0, 0].T, w_up[0, 0].T, w_down[0, 0]], axis=0)
-    across = shifted(own, "yl", 1)
-    other = shifted(own, "core", 1)
-
     tokens = trunk_in[0]
     toks, width = tokens.shape
-    sent = swapped(tokens)
-    meta = swapped(jnp.concatenate([expert_ids[0].T.astype(F32), gate_scores[0].T], axis=0))
+    topk = expert_ids.shape[2]
+    packed = call(send_kernel, shaped((toks, width + 128)))(expert_ids[0].T, gate_scores[0].T, tokens)
+
+    own = jnp.concatenate([w_gate[0, 0].T, w_up[0, 0].T], axis=0)
+    sent = swapped(packed)
+    own, sent = lax.optimization_barrier((own, sent))
+    across = shifted(own, "yl", 1)
+    own_down = w_down[0, 0]
+    across_down = shifted(own_down, "yl", 1)
+    other = shifted(own, "core", 1)
+    other_down = shifted(own_down, "core", 1)
+    both = shifted(across, "core", 1)
 
     image = image_in[0]
     dv = image.shape[1]
     column = exchanged(call(spread_kernel, shaped((n_z, 1, dv), F32))(image), "z")
     column = call(rows_kernel, shaped((n_z, dv)))(column)
     column, sent = lax.optimization_barrier((column, sent))
+
+    n_rows = n_z * CAP
+    rows = call(functools.partial(pack_kernel, topk), pltpu.HBM((n_rows, width), BF16), scalars=1)(
+        where, sent, trunk_gain
+    )
+    arrived = exchanged(rows.reshape(n_z, CAP, width), "z").reshape(n_rows, width)
+
     chip = call(pair_kernel, shaped((2 * n_z, dv)))(column, shifted(column, "core", 1))
-    chips = call(pair_kernel, shaped((4 * n_z, dv)))(chip, shifted(chip, "yl", 1))
-
-    n_rows = n_z * CAP
-    pick, high, low = call(
-        table_kernel,
-        (shaped((n_rows, toks)), shaped((toks, n_rows)), shaped((toks, n_rows))),
-        scalars=1,
-    )(where, meta)
-    rows = call(pack_kernel, pltpu.HBM((n_rows, width), BF16), flops=2 * n_rows * toks * width, moved=2 * n_rows * width)(
-        pick, sent, trunk_gain
-    )
-    arrived = exchanged(rows.reshape(n_z, CAP, width), "z").reshape(n_rows, width)
-    across, arrived, chips = lax.optimization_barrier((across, arrived, chips))
-    both = shifted(across, "core", 1)
-    others = [shifted(chips, "yh", k) for k in range(1, n_yh)]
-    made = experts(arrived, (own, other, across, both))
-    made, others = lax.optimization_barrier((made, others))
+    arrived, chip = lax.optimization_barrier((arrived, chip))
+
+    hidden = hidden_units(arrived, (own, other, across, both))
+    hidden, across_down = lax.optimization_barrier((hidden, across_down))
+    both_down = shifted(across_down, "core", 1)
+    chips = call(pair_kernel, shaped((4 * n_z, dv + -dv % 1024)))(chip, shifted(chip, "yl", 1))
+    all_rows = lax.all_gather(chips, "yh", axis=0, tiled=True)
+    made = expert_rows(hidden, (own_down, other_down, across_down, both_down))
+    made, chips, meta = lax.optimization_barrier((made, chips, sent[:, width:]))
     returned = exchanged(made.reshape(n_z, CAP, width), "z").reshape(n_rows, width)
+    high, low = call(functools.partial(weigh_kernel, topk), (shaped((toks, n_rows)), shaped((toks, n_rows))), scalars=1)(
+        where, meta
+    )
 
     n_image = n_z * n_square
     mine, theirs = call(
-        functools.partial(image_kernel, n_z),
+        functools.partial(image_kernel, n_yh),
         (shaped((n_image // 2, dv), F32), shaped((n_image // 2, dv))),
         flops=4 * n_image * dv * 100,
         moved=4 * n_image * dv,
-    )(chips, *others, image_gain, fc_in[0].T, fc_out[0])
+    )(all_rows, image_gain, fc_in[0].T, fc_out[0])
     mine, theirs = call(fold_kernel, (shaped((n_image // 4, dv), F32), shaped((n_image // 4, dv))))(
         mine, shifted(theirs, "core", 1)
     )
-    mine, *theirs = call(
-        fold_kernel, (shaped((n_z, dv), F32),) + tuple(shaped((n_z, dv)) for _ in range(n_yh - 1))
-    )(mine, shifted(theirs, "yl", 1))
-    column = call(column_kernel, shaped((n_z, 1, dv), F32))(
-        mine, *[shifted(part, "yh", k + 1) for k, part in enumerate(theirs)]
-    )
-
-    column, returned = lax.optimization_barrier((column, returned))
+    mine = call(fold_kernel, shaped((n_image // 4, dv), F32))(mine, shifted(theirs, "yl", 1))
+    column = lax.psum_scatter(mine.reshape(n_yh, n_z, dv), "yh", scatter_dimension=0, tiled=True)[0]
+    column = call(column_kernel, shaped((n_z, 1, dv), F32))(column)
+
     half = width // 2
     pieces = call(combine_kernel, (shaped((toks, half)), shaped((toks, half))), scalars=1, flops=4 * n_rows * toks * width)(
         where, sent, high, low, returned

time: 216 us -> 234 us (1.083)
  between operations: 1.08 us -> 14.5 us
  starting transfers between devices: 98.6 us -> 89.5 us
  blocking collectives: 9.87 us -> 14.2 us
  local copies, waits for them, and re-layouts: 4.59 us -> 8.91 us
  Pallas kernels: 14.1 us -> 17.5 us
  waiting for transfers between devices: 83.9 us -> 86.5 us
    ppermute x2 -> x1, waiting for transfers between devices: 41.7 us -> 7.62 us  [swapped(): lax.ppermute(value, square, [(a * n_tp + b, b * n_tp + a) for a in range(...]
    all_gather x0 -> x1, waiting for transfers between devices: none -> 27.8 us  [body(): all_rows = lax.all_gather(chips, 'yh', axis=0, tiled=True)]
    unnamed x0 -> x3, waiting for transfers between devices: none -> 20.7 us
    ppermute x16 -> x13, waiting for transfers between devices: 27.1 us -> 15.5 us  [shifted(): return lax.ppermute(value, axis, [(i, (i + by) % n) for i in range(n)])]
    all_to_all x3, starting transfers between devices: 23.8 us -> 18.7 us  [exchanged(): return lax.all_to_all(value, axis, split_axis=0, concat_axis=0, tiled=True)]
    unnamed x29 -> x37, local copies, waits for them, and re-layouts: 4.59 us -> 8.91 us
    all_to_all x1, blocking collectives: 9.87 us -> 14.2 us  [exchanged(): return lax.all_to_all(value, axis, split_axis=0, concat_axis=0, tiled=True)]
    ppermute x2 -> x1, starting transfers between devices: 8.75 us -> 5.74 us  [swapped(): lax.ppermute(value, square, [(a * n_tp + b, b * n_tp + a) for a in range(...]
  transfers between devices with their start and end apart: 23 -> 21, of which waited for: 14 -> 12; matrix products, arithmetic and copies ran while one was open for 1% -> 1% of each run, Pallas kernels for 5% -> 7%
where the time goes in v5:
time: 234 us; the launch traced here: 232 us
  starting transfers between devices  89.5 us (38%)
  waiting for transfers between devices  86.5 us (37%)
  Pallas kernels  17.5 us (7%)
  between operations  14.5 us (6%)
  blocking collectives  14.2 us (6%)
  local copies, waits for them, and re-layouts  8.91 us (4%)
    ppermute x13, starting transfers between devices, shifted(): return lax.ppermute(value, axis, [(i, (i + by) % n) for i in range(n)])  57.3 us
    all_gather x1, waiting for transfers between devices, body(): all_rows = lax.all_gather(chips, 'yh', axis=0, tiled=True)  27.8 us
    unnamed x3, waiting for transfers between devices  20.7 us
    all_to_all x3, starting transfers between devices, exchanged(): return lax.all_to_all(value, axis, split_axis=0, concat_axis=0, tiled=True)  18.7 us
    ppermute x13, waiting for transfers between devices, shifted(): return lax.ppermute(value, axis, [(i, (i + by) % n) for i in range(n)])  15.5 us
    all_to_all x3, waiting for transfers between devices, exchanged(): return lax.all_to_all(value, axis, split_axis=0, concat_axis=0, tiled=True)  14.9 us
    all_to_all x1, blocking collectives, exchanged(): return lax.all_to_all(value, axis, split_axis=0, concat_axis=0, tiled=True)  14.2 us
    pallas_call x16, Pallas kernels, run(): pl.pallas_call(kernel, out_shape=outs, in_specs=specs, out_specs=jax.tree...  9.74 us
  transfers between devices with their start and end apart: 21, of which 12 were waited for; matrix products, arithmetic and copies ran while one was open for 1% of the time, Pallas kernels for 7%

profile of v5, /device:TPU:1, one launch (start us, length us, event | category | flops | bytes accessed | tf_op | source)
XLA Modules:
  0.0 232.5 jit_solution(5978233978984007862)
XLA Ops:
  7.2 1.0 copy-done.6
  8.2 0.7 copy-done.15
  8.9 0.7 copy-done.16
  9.6 0.1 shard_map.133
  9.7 5.7 %collective-permute-start = (bf16[128,2176]{1,0:T(8,128)(2,1)S(1)}, bf16[128,2176]{1,0:T(8,128)(2,1)S(1)}, u32[]{:S(2)}, u32[]{:S(2)}) collective-permute-start(bf16[128,2176]{1,0:T(8,128)(2,1)S(1)} %shard_map.133), channel_id=1, source_target_pairs={{0,0},{1,32},{2,64},{3,96},{32,1},{33,33},{34,65},{35,97},{64,2},{... | collective-permute-start | bytes 1671176 | tf_op jit(solution)/shard_map/ppermute | solution.py:292
  15.5 0.0 copy-start.10
  15.5 1.3 pad_maximum_fusion.refs_0_
  16.8 7.6 %collective-permute-done.sent.toks = bf16[128,2176]{1,0:T(8,128)(2,1)S(1)} collective-permute-done((bf16[128,2176]{1,0:T(8,128)(2,1)S(1)}, bf16[128,2176]{1,0:T(8,128)(2,1)S(1)}, u32[]{:S(2)}, u32[]{:S(2)}) %collective-permute-start) | collective-permute-done | bytes 557088 | tf_op jit(solution)/shard_map/ppermute | solution.py:292
  24.4 9.6 %collective-permute-start.6 = (bf16[384,2048]{1,0:T(8,128)(2,1)S(1)}, bf16[384,2048]{1,0:T(8,128)(2,1)}, u32[]{:S(2)}, u32[]{:S(2)}) collective-permute-start(bf16[384,2048]{1,0:T(8,128)(2,1)S(1)} %pad_maximum_fusion.refs_0_), channel_id=1, source_target_pairs={{0,2},{2,0},{1,3},{3,1},{4,6},{6,4},{5,7},{7,5},{8,10},{10,8},{9,1... | collective-permute-start | bytes 4718600 | tf_op jit(solution)/shard_map/ppermute | solution.py:296
  34.0 0.7 shard_map.131
  34.7 10.0 %all-to-all-start = ((f32[8,1,3200]{2,1,0:T(1,128)}), f32[8,1,3200]{2,1,0:T(1,128)S(1)}, u32[]{:S(2)}, u32[]{:S(2)}) async-start(f32[8,1,3200]{2,1,0:T(1,128)} %shard_map.131), calls=%async_computation | async-start | bytes 204800 | tf_op jit(solution)/shard_map/all_to_all | solution.py:299
  44.7 0.1 pad_add_fusion.where
  44.8 7.5 %all-to-all-done.spread = f32[8,1,3200]{2,1,0:T(1,128)S(1)} async-done(((f32[8,1,3200]{2,1,0:T(1,128)}), f32[8,1,3200]{2,1,0:T(1,128)S(1)}, u32[]{:S(2)}, u32[]{:S(2)}) %all-to-all-start) | async-done | bytes 102432 | tf_op jit(solution)/shard_map/all_to_all | solution.py:299
  52.4 0.0 copy-start.7
  52.4 2.4 %shard_map.134 = bf16[320,2048]{1,0:T(8,128)(2,1)} custom-call(s32[2]{0:T(128)S(1)} %pad_add_fusion.where, bf16[128,2176]{1,0:T(8,128)(2,1)S(1)} %collective-permute-done.sent.toks, f32[1,2048]{1,0:T(1,128)S(1)} %copy-done.14), custom_call_target="tpu_custom_call" | custom-call | tf_op jit(solution)/shard_map/pallas_call | solution.py:23
  54.7 3.6 %all-to-all-start.1 = ((bf16[8,40,2048]{2,1,0:T(8,128)(2,1)}), bf16[8,40,2048]{2,1,0:T(8,128)(2,1)S(1)}, u32[]{:S(2)}, u32[]{:S(2)}) async-start(bf16[8,40,2048]{2,1,0:T(8,128)(2,1)} %bitcast.44), calls=%async_computation.1 | async-start | bytes 2621440 | tf_op jit(solution)/shard_map/all_to_all | solution.py:299
  58.3 0.0 all-gather.2.cloned.1.call-start
  58.4 10.2 %collective-permute-start.5 = (bf16[384,2048]{1,0:T(8,128)(2,1)S(1)}, bf16[384,2048]{1,0:T(8,128)(2,1)}, u32[]{:S(2)}, u32[]{:S(2)}) collective-permute-start(bf16[384,2048]{1,0:T(8,128)(2,1)S(1)} %pad_maximum_fusion.refs_0_), channel_id=1, source_target_pairs={{0,1},{1,0},{2,3},{3,2},{4,5},{5,4},{6,7},{7,6},{8,9},{9,8},{10,11... | collective-permute-start | bytes 4718600 | tf_op jit(solution)/shard_map/ppermute | solution.py:296
  68.6 2.7 %collective-permute-start.7 = (bf16[384,2048]{1,0:T(8,128)(2,1)}, bf16[384,2048]{1,0:T(8,128)(2,1)}, u32[]{:S(2)}, u32[]{:S(2)}) collective-permute-start(bf16[384,2048]{1,0:T(8,128)(2,1)} %collective-permute-done.6.refs_2_), channel_id=1, source_target_pairs={{0,1},{1,0},{2,3},{3,2},{4,5},{5,4},{6,7},{7,6},{8,9},{9,8},{10,11... | collective-permute-start | bytes 4718600 | tf_op jit(solution)/shard_map/ppermute | solution.py:296
  71.3 3.4 %collective-permute-start.8 = (bf16[192,2048]{1,0:T(8,128)(2,1)}, bf16[192,2048]{1,0:T(8,128)(2,1)}, u32[]{:S(2)}, u32[]{:S(2)}) collective-permute-start(bf16[192,2048]{1,0:T(8,128)(2,1)} %bitcast.32), channel_id=1, source_target_pairs={{0,2},{2,0},{1,3},{3,1},{4,6},{6,4},{5,7},{7,5},{8,10},{10,8},{9,1... | collective-permute-start | bytes 2359304 | tf_op jit(solution)/shard_map/ppermute | solution.py:296
  74.7 2.2 collective-permute-start.1
  76.9 2.1 collective-permute-start.9
  79.1 0.8 copy-done.8
  79.9 7.3 %all-to-all-done.1 = bf16[8,40,2048]{2,1,0:T(8,128)(2,1)S(1)} async-done(((bf16[8,40,2048]{2,1,0:T(8,128)(2,1)}), bf16[8,40,2048]{2,1,0:T(8,128)(2,1)S(1)}, u32[]{:S(2)}, u32[]{:S(2)}) %all-to-all-start.1) | async-done | bytes 1310752 | tf_op jit(solution)/shard_map/all_to_all | solution.py:299
  87.2 4.3 %shard_map.141.hidden = bf16[320,768]{1,0:T(8,128)(2,1)S(1)} custom-call(bf16[320,2048]{1,0:T(8,128)(2,1)S(1)} %bitcast.31, bf16[384,2048]{1,0:T(8,128)(2,1)S(1)} %pad_maximum_fusion.refs_0_, bf16[384,2048]{1,0:T(8,128)(2,1)} %collective-permute-done.5.refs_1_, bf16[384,2048]{1,0:T(8,128)(2,1)} %collective-permute-done.6.refs_2_, ...), custom_call_target="tpu_custom_call" | custom-call | flops 2013265920 | bytes 6291456 | tf_op jit(solution)/shard_map/pallas_call | solution.py:152
  91.6 0.8 copy-done
  92.3 0.4 collective-permute-done.8.refs_2_
  92.7 7.8 %collective-permute-start.10 = (bf16[192,2048]{1,0:T(8,128)(2,1)}, bf16[192,2048]{1,0:T(8,128)(2,1)S(1)}, u32[]{:S(2)}, u32[]{:S(2)}) collective-permute-start(bf16[192,2048]{1,0:T(8,128)(2,1)} %collective-permute-done.8.refs_2_), channel_id=1, source_target_pairs={{0,1},{1,0},{2,3},{3,2},{4,5},{5,4},{6,7},{7,6},{8,9},{9,8},{10,11... | collective-permute-start | bytes 2359304 | tf_op jit(solution)/shard_map/ppermute | solution.py:296
  100.5 1.9 collective-permute-start.2
  102.5 4.5 %collective-permute-done.2.other = bf16[16,3200]{1,0:T(8,128)(2,1)S(1)} collective-permute-done((bf16[16,3200]{1,0:T(8,128)(2,1)S(1)}, bf16[16,3200]{1,0:T(8,128)(2,1)S(1)}, u32[]{:S(2)}, u32[]{:S(2)}) %collective-permute-start.2) | collective-permute-done | bytes 102432 | tf_op jit(solution)/shard_map/ppermute | solution.py:296
  106.9 0.7 shard_map.136
  107.7 0.0 all-gather.2.cloned.1.call-update
  107.7 1.0 copy-done.1
  108.8 1.1 copy-done.3
  109.9 3.5 %shard_map.142 = bf16[320,2048]{1,0:T(8,128)(2,1)} custom-call(bf16[320,768]{1,0:T(8,128)(2,1)S(1)} %copy-done.1, bf16[192,2048]{1,0:T(8,128)(2,1)S(1)} %bitcast.34, bf16[192,2048]{1,0:T(8,128)(2,1)} %collective-permute-done.9.refs_1_, bf16[192,2048]{1,0:T(8,128)(2,1)} %collective-permute-done.8.refs_2_, bf16[192,2048]{1,0:T(8,128)(2,1)S(1)} %collective-permute-done.10.refs_3_), custom_call_target="tpu_custom_call" | custom-call | flops 1006632960 | bytes 3145728 | tf_op jit(solution)/shard_map/pallas_call | solution.py:172
  113.4 5.1 %all-to-all-start.3 = ((bf16[8,40,2048]{2,1,0:T(8,128)(2,1)}), bf16[8,40,2048]{2,1,0:T(8,128)(2,1)S(1)}, u32[]{:S(2)}, u32[]{:S(2)}) async-start(bf16[8,40,2048]{2,1,0:T(8,128)(2,1)} %bitcast.45), calls=%async_computation.3 | async-start | bytes 2621440 | tf_op jit(solution)/shard_map/all_to_all | solution.py:299
  118.5 0.0 reduce-scatter.4.cloned.1.call-start
  118.5 27.8 %all-gather.2.cloned.1.call-done.rows = bf16[128,4096]{1,0:T(8,128)(2,1)} async-done(((bf16[32,4096]{1,0:T(8,128)(2,1)}), bf16[128,4096]{1,0:T(8,128)(2,1)}) %all-gather.2.cloned.1.call-update) | async-done | bytes 1048592 | tf_op jit(solution)/shard_map/all_gather | solution.py:335
  146.4 1.2 copy-done.2
  147.6 1.3 shard_map.137
  148.9 2.8 %collective-permute-start.3 = (bf16[64,3200]{1,0:T(8,128)(2,1)S(1)}, bf16[64,3200]{1,0:T(8,128)(2,1)S(1)}, u32[]{:S(2)}, u32[]{:S(2)}) collective-permute-start(bf16[64,3200]{1,0:T(8,128)(2,1)S(1)} %get-tuple-element.28), channel_id=1, source_target_pairs={{0,1},{1,0},{2,3},{3,2},{4,5},{5,4},{6,7},{7,6},{8,9},{9,8},{10,11... | collective-permute-start | bytes 1228808 | tf_op jit(solution)/shard_map/ppermute | solution.py:296
  151.6 1.4 collective-permute-done.3.came
  153.0 0.1 shard_map.138
  153.1 1.9 collective-permute-start.4
  155.0 6.3 %collective-permute-done.4.came = bf16[32,3200]{1,0:T(8,128)(2,1)S(1)} collective-permute-done((bf16[32,3200]{1,0:T(8,128)(2,1)S(1)}, bf16[32,3200]{1,0:T(8,128)(2,1)S(1)}, u32[]{:S(2)}, u32[]{:S(2)}) %collective-permute-start.4) | collective-permute-done | bytes 204832 | tf_op jit(solution)/shard_map/ppermute | solution.py:296
  161.2 0.8 shard_map.139
  162.0 0.0 reduce-scatter.4.cloned.1.call-update
  162.1 0.9 shard_map.143
  163.0 1.3 shard_map.144
  164.2 5.4 %collective-permute-start.11 = (bf16[128,1024]{1,0:T(8,128)(2,1)S(1)}, bf16[128,1024]{1,0:T(8,128)(2,1)S(1)}, u32[]{:S(2)}, u32[]{:S(2)}) collective-permute-start(bf16[128,1024]{1,0:T(8,128)(2,1)S(1)} %get-tuple-element.39), channel_id=1, source_target_pairs={{0,128},{1,160},{2,192},{3,224},{32,129},{33,161},{34,193},{35,225... | collective-permute-start | bytes 786440 | tf_op jit(solution)/shard_map/ppermute | solution.py:362
  169.7 2.4 %collective-permute-start.12 = (bf16[128,1024]{1,0:T(8,128)(2,1)S(1)}, bf16[128,1024]{1,0:T(8,128)(2,1)S(1)}, u32[]{:S(2)}, u32[]{:S(2)}) collective-permute-start(bf16[128,1024]{1,0:T(8,128)(2,1)S(1)} %get-tuple-element.40), channel_id=1, source_target_pairs={{0,130},{1,162},{2,194},{3,226},{32,131},{33,163},{34,195},{35,227... | collective-permute-start | bytes 786440 | tf_op jit(solution)/shard_map/ppermute | solution.py:362
  172.1 20.6 %reduce-scatter.4.cloned.1.call-done = f32[1,8,3200]{2,1,0:T(8,128)} async-done(((f32[4,8,3200]{2,1,0:T(8,128)}), f32[1,8,3200]{2,1,0:T(8,128)}) %reduce-scatter.4.cloned.1.call-update) | async-done | bytes 102416
  192.7 0.9 copy-done.9
  193.6 14.2 %all_to_all.20.spread = f32[8,1,3200]{2,1,0:T(1,128)S(1)} all-to-all(f32[8,1,3200]{2,1,0:T(1,128)S(1)} %shard_map.140), channel_id=1, replica_groups=mesh['pp'=4,'yh'=4,'z'=8,'yl'=2,'core'=2] {'z'}, dimensions={0} | all-to-all | bytes 204800 | tf_op jit(solution)/shard_map/all_to_all | solution.py:299
  207.8 0.1 shard_map.145.left
  207.8 4.7 %collective-permute-start.13 = (bf16[128,1024]{1,0:T(8,128)(2,1)S(1)}, bf16[128,1024]{1,0:T(8,128)(2,1)S(1)}, u32[]{:S(2)}, u32[]{:S(2)}) collective-permute-start(bf16[128,1024]{1,0:T(8,128)(2,1)S(1)} %shard_map.145.left), channel_id=1, source_target_pairs={{0,1},{1,0},{2,3},{3,2},{4,5},{5,4},{6,7},{7,6},{8,9},{9,8},{10,11... | collective-permute-start | bytes 786440 | tf_op jit(solution)/shard_map/ppermute | solution.py:296
  212.5 1.1 collective-permute-done.13.right
  213.7 0.1 shard_map.146.own
  213.7 3.6 %collective-permute-start.14 = (bf16[128,1024]{1,0:T(8,128)(2,1)S(1)}, bf16[128,1024]{1,0:T(8,128)(2,1)S(1)}, u32[]{:S(2)}, u32[]{:S(2)}) collective-permute-start(bf16[128,1024]{1,0:T(8,128)(2,1)S(1)} %shard_map.146.own), channel_id=1, source_target_pairs={{0,2},{2,0},{1,3},{3,1},{4,6},{6,4},{5,7},{7,5},{8,10},{10,8},{9,1... | collective-permute-start | bytes 786440 | tf_op jit(solution)/shard_map/ppermute | solution.py:296
  217.4 4.4 %collective-permute-start.15 = (bf16[1,1,3200]{2,1,0:T(2,128)(2,1)S(1)}, bf16[1,1,3200]{2,1,0:T(2,128)(2,1)S(1)}, u32[]{:S(2)}, u32[]{:S(2)}) collective-permute-start(bf16[1,1,3200]{2,1,0:T(2,128)(2,1)S(1)} %bitcast.41), channel_id=1, source_target_pairs={{0,384},{128,0},{256,128},{384,256},{1,385},{129,1},{257,129},{385... | collective-permute-start | bytes 19208 | tf_op jit(solution)/shard_map/ppermute | solution.py:296
  221.8 0.8 collective-permute-done.15
  222.6 1.0 collective-permute-done.14.across
  223.6 1.4 shard_map.147
  225.0 0.6 copy.15
  (39 shorter events, 0.2 us)
Async XLA Ops:
  7.2 1.0 copy-start.6
  8.2 0.7 copy-start.15
  8.9 0.7 copy-start.16
  9.6 5.9 %copy-start.17 = (bf16[1,1,2048,192]{2,3,1,0:T(8,128)(2,1)S(1)}, bf16[1,1,2048,192]{2,3,1,0:T(8,128)(2,1)}, u32[]{:S(2)}) copy-start(bf16[1,1,2048,192]{2,3,1,0:T(8,128)(2,1)} %param.17) | copy-start | bytes 2359300
  9.7 14.7 %collective-permute-start = (bf16[128,2176]{1,0:T(8,128)(2,1)S(1)}, bf16[128,2176]{1,0:T(8,128)(2,1)S(1)}, u32[]{:S(2)}, u32[]{:S(2)}) collective-permute-start(bf16[128,2176]{1,0:T(8,128)(2,1)S(1)} %shard_map.133), channel_id=1, source_target_pairs={{0,0},{1,32},{2,64},{3,96},{32,1},{33,33},{34,65},{35,97},{64,2},{... | collective-permute-start | bytes 1671176 | tf_op jit(solution)/shard_map/ppermute | solution.py:292
  15.5 18.5 %copy-start.10 = (bf16[1,1,3200]{2,1,0:T(2,128)(2,1)S(1)}, bf16[1,1,3200]{2,1,0:T(2,128)(2,1)}, u32[]{:S(2)}) copy-start(bf16[1,1,3200]{2,1,0:T(2,128)(2,1)} %param.19) | copy-start | bytes 19204
  15.5 36.9 %copy-start.14 = (f32[1,2048]{1,0:T(1,128)S(1)}, f32[1,2048]{1,0:T(1,128)}, u32[]{:S(2)}) copy-start(f32[1,2048]{1,0:T(1,128)} %gain.2) | copy-start | bytes 24580
  24.4 44.1 %collective-permute-start.6 = (bf16[384,2048]{1,0:T(8,128)(2,1)S(1)}, bf16[384,2048]{1,0:T(8,128)(2,1)}, u32[]{:S(2)}, u32[]{:S(2)}) collective-permute-start(bf16[384,2048]{1,0:T(8,128)(2,1)S(1)} %pad_maximum_fusion.refs_0_), channel_id=1, source_target_pairs={{0,2},{2,0},{1,3},{3,1},{4,6},{6,4},{5,7},{7,5},{8,10},{10,8},{9,1... | collective-permute-start | bytes 4718600 | tf_op jit(solution)/shard_map/ppermute | solution.py:296
  34.7 17.7 %all-to-all-start = ((f32[8,1,3200]{2,1,0:T(1,128)}), f32[8,1,3200]{2,1,0:T(1,128)S(1)}, u32[]{:S(2)}, u32[]{:S(2)}) async-start(f32[8,1,3200]{2,1,0:T(1,128)} %shard_map.131), calls=%async_computation | async-start | bytes 204800 | tf_op jit(solution)/shard_map/all_to_all | solution.py:299
  52.4 22.3 %copy-start.7 = (bf16[8,3200]{1,0:T(8,128)(2,1)}, bf16[8,3200]{1,0:T(8,128)(2,1)S(1)}, u32[]{:S(2)}) copy-start(bf16[8,3200]{1,0:T(8,128)(2,1)S(1)} %shard_map.132.own) | copy-start | bytes 153604
  54.7 32.5 %all-to-all-start.1 = ((bf16[8,40,2048]{2,1,0:T(8,128)(2,1)}), bf16[8,40,2048]{2,1,0:T(8,128)(2,1)S(1)}, u32[]{:S(2)}, u32[]{:S(2)}) async-start(bf16[8,40,2048]{2,1,0:T(8,128)(2,1)} %bitcast.44), calls=%async_computation.1 | async-start | bytes 2621440 | tf_op jit(solution)/shard_map/all_to_all | solution.py:299
  58.3 88.0 %all-gather.2.cloned.1.call-start = ((), (), s32[]{:S(2)}) async-start(), calls=%async_computation.5 | async-start | bytes 1310720 | tf_op jit(solution)/shard_map/all_gather | solution.py:335
  58.4 28.9 %collective-permute-start.5 = (bf16[384,2048]{1,0:T(8,128)(2,1)S(1)}, bf16[384,2048]{1,0:T(8,128)(2,1)}, u32[]{:S(2)}, u32[]{:S(2)}) collective-permute-start(bf16[384,2048]{1,0:T(8,128)(2,1)S(1)} %pad_maximum_fusion.refs_0_), channel_id=1, source_target_pairs={{0,1},{1,0},{2,3},{3,2},{4,5},{5,4},{6,7},{7,6},{8,9},{9,8},{10,11... | collective-permute-start | bytes 4718600 | tf_op jit(solution)/shard_map/ppermute | solution.py:296
  68.6 18.7 %collective-permute-start.7 = (bf16[384,2048]{1,0:T(8,128)(2,1)}, bf16[384,2048]{1,0:T(8,128)(2,1)}, u32[]{:S(2)}, u32[]{:S(2)}) collective-permute-start(bf16[384,2048]{1,0:T(8,128)(2,1)} %collective-permute-done.6.refs_2_), channel_id=1, source_target_pairs={{0,1},{1,0},{2,3},{3,2},{4,5},{5,4},{6,7},{7,6},{8,9},{9,8},{10,11... | collective-permute-start | bytes 4718600 | tf_op jit(solution)/shard_map/ppermute | solution.py:296
  71.3 21.4 %collective-permute-start.8 = (bf16[192,2048]{1,0:T(8,128)(2,1)}, bf16[192,2048]{1,0:T(8,128)(2,1)}, u32[]{:S(2)}, u32[]{:S(2)}) collective-permute-start(bf16[192,2048]{1,0:T(8,128)(2,1)} %bitcast.32), channel_id=1, source_target_pairs={{0,2},{2,0},{1,3},{3,1},{4,6},{6,4},{5,7},{7,5},{8,10},{10,8},{9,1... | collective-permute-start | bytes 2359304 | tf_op jit(solution)/shard_map/ppermute | solution.py:296
  74.7 4.3 %collective-permute-start.1 = (bf16[8,3200]{1,0:T(8,128)(2,1)S(1)}, bf16[8,3200]{1,0:T(8,128)(2,1)S(1)}, u32[]{:S(2)}, u32[]{:S(2)}) collective-permute-start(bf16[8,3200]{1,0:T(8,128)(2,1)S(1)} %shard_map.132.own), channel_id=1, source_target_pairs={{0,1},{1,0},{2,3},{3,2},{4,5},{5,4},{6,7},{7,6},{8,9},{9,8},{10,11... | collective-permute-start | bytes 153608 | tf_op jit(solution)/shard_map/ppermute | solution.py:296
  76.9 30.8 %collective-permute-start.9 = (bf16[192,2048]{1,0:T(8,128)(2,1)}, bf16[192,2048]{1,0:T(8,128)(2,1)}, u32[]{:S(2)}, u32[]{:S(2)}) collective-permute-start(bf16[192,2048]{1,0:T(8,128)(2,1)} %bitcast.33), channel_id=1, source_target_pairs={{0,1},{1,0},{2,3},{3,2},{4,5},{5,4},{6,7},{7,6},{8,9},{9,8},{10,11... | collective-permute-start | bytes 2359304 | tf_op jit(solution)/shard_map/ppermute | solution.py:296
  79.1 0.8 copy-start.8
  91.5 0.8 copy-start
  92.7 15.0 %collective-permute-start.10 = (bf16[192,2048]{1,0:T(8,128)(2,1)}, bf16[192,2048]{1,0:T(8,128)(2,1)S(1)}, u32[]{:S(2)}, u32[]{:S(2)}) collective-permute-start(bf16[192,2048]{1,0:T(8,128)(2,1)} %collective-permute-done.8.refs_2_), channel_id=1, source_target_pairs={{0,1},{1,0},{2,3},{3,2},{4,5},{5,4},{6,7},{7,6},{8,9},{9,8},{10,11... | collective-permute-start | bytes 2359304 | tf_op jit(solution)/shard_map/ppermute | solution.py:296
  100.5 6.4 %collective-permute-start.2 = (bf16[16,3200]{1,0:T(8,128)(2,1)S(1)}, bf16[16,3200]{1,0:T(8,128)(2,1)S(1)}, u32[]{:S(2)}, u32[]{:S(2)}) collective-permute-start(bf16[16,3200]{1,0:T(8,128)(2,1)S(1)} %shard_map.135.own), channel_id=1, source_target_pairs={{0,2},{2,0},{1,3},{3,1},{4,6},{6,4},{5,7},{7,5},{8,10},{10,8},{9,1... | collective-permute-start | bytes 307208 | tf_op jit(solution)/shard_map/ppermute | solution.py:296
  107.7 1.0 copy-start.1
  108.8 1.1 copy-start.3
  113.4 33.0 %copy-start.4 = (bf16[1,3200,100]{1,2,0:T(8,128)(2,1)S(1)}, bf16[1,3200,100]{1,2,0:T(8,128)(2,1)}, u32[]{:S(2)}) copy-start(bf16[1,3200,100]{1,2,0:T(8,128)(2,1)} %param.21) | copy-start | bytes 1920004
  113.4 33.0 %copy-start.5 = (bf16[1,100,3200]{2,1,0:T(8,128)(2,1)S(1)}, bf16[1,100,3200]{2,1,0:T(8,128)(2,1)}, u32[]{:S(2)}) copy-start(bf16[1,100,3200]{2,1,0:T(8,128)(2,1)} %param.22) | copy-start | bytes 1920004
  113.4 32.9 %copy-start.13 = (f32[1,3200]{1,0:T(1,128)S(1)}, f32[1,3200]{1,0:T(1,128)}, u32[]{:S(2)}) copy-start(f32[1,3200]{1,0:T(1,128)} %gain.3) | copy-start | bytes 38404
  113.4 49.5 %all-to-all-start.3 = ((bf16[8,40,2048]{2,1,0:T(8,128)(2,1)}), bf16[8,40,2048]{2,1,0:T(8,128)(2,1)S(1)}, u32[]{:S(2)}, u32[]{:S(2)}) async-start(bf16[8,40,2048]{2,1,0:T(8,128)(2,1)} %bitcast.45), calls=%async_computation.3 | async-start | bytes 2621440 | tf_op jit(solution)/shard_map/all_to_all | solution.py:299
  118.5 74.2 %reduce-scatter.4.cloned.1.call-start = ((), (), s32[]{:S(2)}) async-start(), calls=%async_computation.6 | async-start | bytes 512000
  146.4 1.2 copy-start.2
  148.9 4.1 %collective-permute-start.3 = (bf16[64,3200]{1,0:T(8,128)(2,1)S(1)}, bf16[64,3200]{1,0:T(8,128)(2,1)S(1)}, u32[]{:S(2)}, u32[]{:S(2)}) collective-permute-start(bf16[64,3200]{1,0:T(8,128)(2,1)S(1)} %get-tuple-element.28), channel_id=1, source_target_pairs={{0,1},{1,0},{2,3},{3,2},{4,5},{5,4},{6,7},{7,6},{8,9},{9,8},{10,11... | collective-permute-start | bytes 1228808 | tf_op jit(solution)/shard_map/ppermute | solution.py:296
  153.1 8.2 %collective-permute-start.4 = (bf16[32,3200]{1,0:T(8,128)(2,1)S(1)}, bf16[32,3200]{1,0:T(8,128)(2,1)S(1)}, u32[]{:S(2)}, u32[]{:S(2)}) collective-permute-start(bf16[32,3200]{1,0:T(8,128)(2,1)S(1)} %get-tuple-element.30), channel_id=1, source_target_pairs={{0,2},{2,0},{1,3},{3,1},{4,6},{6,4},{5,7},{7,5},{8,10},{10,8},{9,1... | collective-permute-start | bytes 614408 | tf_op jit(solution)/shard_map/ppermute | solution.py:296
  162.9 54.4 %copy-start.11 = (bf16[1,1,3200]{2,1,0:T(2,128)(2,1)S(1)}, bf16[1,1,3200]{2,1,0:T(2,128)(2,1)}, u32[]{:S(2)}) copy-start(bf16[1,1,3200]{2,1,0:T(2,128)(2,1)} %param.19) | copy-start | bytes 19204
  163.0 54.4 %copy-start.12 = (f32[1,3200]{1,0:T(1,128)S(1)}, f32[1,3200]{1,0:T(1,128)}, u32[]{:S(2)}) copy-start(f32[1,3200]{1,0:T(1,128)} %scale.1) | copy-start | bytes 38404
  164.2 43.5 %collective-permute-start.11 = (bf16[128,1024]{1,0:T(8,128)(2,1)S(1)}, bf16[128,1024]{1,0:T(8,128)(2,1)S(1)}, u32[]{:S(2)}, u32[]{:S(2)}) collective-permute-start(bf16[128,1024]{1,0:T(8,128)(2,1)S(1)} %get-tuple-element.39), channel_id=1, source_target_pairs={{0,128},{1,160},{2,192},{3,224},{32,129},{33,161},{34,193},{35,225... | collective-permute-start | bytes 786440 | tf_op jit(solution)/shard_map/ppermute | solution.py:362
  169.7 38.1 %collective-permute-start.12 = (bf16[128,1024]{1,0:T(8,128)(2,1)S(1)}, bf16[128,1024]{1,0:T(8,128)(2,1)S(1)}, u32[]{:S(2)}, u32[]{:S(2)}) collective-permute-start(bf16[128,1024]{1,0:T(8,128)(2,1)S(1)} %get-tuple-element.40), channel_id=1, source_target_pairs={{0,130},{1,162},{2,194},{3,226},{32,131},{33,163},{34,195},{35,227... | collective-permute-start | bytes 786440 | tf_op jit(solution)/shard_map/ppermute | solution.py:362
  192.7 0.9 copy-start.9
  207.8 5.8 %collective-permute-start.13 = (bf16[128,1024]{1,0:T(8,128)(2,1)S(1)}, bf16[128,1024]{1,0:T(8,128)(2,1)S(1)}, u32[]{:S(2)}, u32[]{:S(2)}) collective-permute-start(bf16[128,1024]{1,0:T(8,128)(2,1)S(1)} %shard_map.145.left), channel_id=1, source_target_pairs={{0,1},{1,0},{2,3},{3,2},{4,5},{5,4},{6,7},{7,6},{8,9},{9,8},{10,11... | collective-permute-start | bytes 786440 | tf_op jit(solution)/shard_map/ppermute | solution.py:296
  213.7 9.9 %collective-permute-start.14 = (bf16[128,1024]{1,0:T(8,128)(2,1)S(1)}, bf16[128,1024]{1,0:T(8,128)(2,1)S(1)}, u32[]{:S(2)}, u32[]{:S(2)}) collective-permute-start(bf16[128,1024]{1,0:T(8,128)(2,1)S(1)} %shard_map.146.own), channel_id=1, source_target_pairs={{0,2},{2,0},{1,3},{3,1},{4,6},{6,4},{5,7},{7,5},{8,10},{10,8},{9,1... | collective-permute-start | bytes 786440 | tf_op jit(solution)/shard_map/ppermute | solution.py:296
  217.4 5.2 %collective-permute-start.15 = (bf16[1,1,3200]{2,1,0:T(2,128)(2,1)S(1)}, bf16[1,1,3200]{2,1,0:T(2,128)(2,1)S(1)}, u32[]{:S(2)}, u32[]{:S(2)}) collective-permute-start(bf16[1,1,3200]{2,1,0:T(2,128)(2,1)S(1)} %bitcast.41), channel_id=1, source_target_pairs={{0,384},{128,0},{256,128},{384,256},{1,385},{129,1},{257,129},{385... | collective-permute-start | bytes 19208 | tf_op jit(solution)/shard_map/ppermute | solution.py:296
Sparse Core Ops, SparseCore 0:
  107.8 38.4 all-gather.1
  162.2 30.4 reduce-scatter.3

commit v6 on v4

--- a/solution.py
+++ b/solution.py
@@ -13,6 +13,7 @@
 VM = pl.BlockSpec(memory_space=pltpu.VMEM)
 SM = pl.BlockSpec(memory_space=pltpu.SMEM)
 CAP = 40
+ROWS = 48
 SMALL = 12 * 1024 * 1024
 LARGE = 24 * 1024 * 1024
 
@@ -40,11 +41,9 @@
     return lax.dot_general(a, b, (((1,), (1,)), ((), ())), preferred_element_type=F32)
 
 
-def table_kernel(where, meta, pick, high, low):
-    rows, toks = pick.shape
-    group = rows // CAP
+def table(group, slots, first, meta):
+    toks = meta.shape[1]
     topk = meta.shape[0] // 2
-    first = where[0] * group
     wanted = (lax.broadcasted_iota(jnp.int32, (group, toks), 0) + first).astype(F32)
     scores = meta[topk:, :]
     total = jnp.sum(scores, axis=0, keepdims=True)
@@ -57,20 +56,35 @@
     earlier = lax.broadcasted_iota(jnp.int32, (toks, toks), 0) < lax.broadcasted_iota(jnp.int32, (toks, toks), 1)
     rank = jnp.dot(member.astype(BF16), earlier.astype(F32).astype(BF16), preferred_element_type=F32)
     rank = jnp.where(member > 0.5, rank, -1.0)
-    slots = lax.broadcasted_iota(jnp.int32, (group, CAP, toks), 1).astype(F32)
-    hit = jnp.where(rank[:, None, :] == slots, 1.0, 0.0)
-    pick[...] = hit.reshape(rows, toks).astype(BF16)
-    scaled = (hit * weight[:, None, :]).reshape(rows, toks).T
+    slot = lax.broadcasted_iota(jnp.int32, (group, slots, toks), 1).astype(F32)
+    return jnp.where(rank[:, None, :] == slot, 1.0, 0.0), weight
+
+
+def pack_kernel(where, meta, toks, gain, image, rows):
+    n, width = rows.shape
+    group = n // ROWS
+    hit, _ = table(group, ROWS, where[0] * group, meta[...])
+    wide = toks[...].astype(F32)
+    scale = lax.rsqrt(jnp.mean(wide * wide, axis=-1, keepdims=True) + 1e-06)
+    normed = (wide * scale * gain[...]).astype(BF16)
+    dv = image.shape[1]
+    picture = image[...].astype(F32)
+    spare = jnp.zeros((1, 2 * width - dv), F32)
+    picture = jnp.concatenate([picture[:, :width], jnp.concatenate([picture[:, width:], spare], axis=1)], axis=0)
+    picture = jnp.concatenate([picture, jnp.zeros((ROWS - CAP - 2, width), F32)], axis=0)
+    empty = jnp.zeros((CAP, width), F32)
+    made = jnp.dot(hit.reshape(n, hit.shape[2]).astype(BF16), normed, preferred_element_type=F32)
+    rows[...] = (made + jnp.concatenate([empty, picture] * group, axis=0)).astype(BF16)
+
+
+def weigh_kernel(where, meta, high, low):
+    toks, n = high.shape
+    group = n // CAP
+    hit, weight = table(group, CAP, where[0] * group, meta[...])
+    scaled = (hit * weight[:, None, :]).reshape(n, toks).T
     top = scaled.astype(BF16)
     high[...] = top
     low[...] = (scaled - top.astype(F32)).astype(BF16)
-
-
-def pack_kernel(pick, toks, gain, rows):
-    wide = toks[...].astype(F32)
-    scale = lax.rsqrt(jnp.mean(wide * wide, axis=-1, keepdims=True) + 1e-06)
-    normed = (wide * scale * gain[...]).astype(BF16)
-    rows[...] = jnp.dot(pick[...], normed, preferred_element_type=F32).astype(BF16)
 
 
 def expert_kernel(rows, *refs):
@@ -102,8 +116,8 @@
             copies[3 * seen + 1].wait()
             seen += 1
         block = slice(c * step, (c + 1) * step)
-        gate = nt(flat, gate_v[block, :])
-        upval = nt(flat, up_v[block, :])
+        gate = nt(flat, gate_v[block, :]).reshape(-1, ROWS, step)[:, :CAP].reshape(-1, step)
+        upval = nt(flat, up_v[block, :]).reshape(-1, ROWS, step)[:, :CAP].reshape(-1, step)
         hidden_v[:, block] = (gate * jax.nn.sigmoid(gate) * upval).astype(BF16)
     for s in range(4):
         copies[3 * s + 2].wait()
@@ -122,7 +136,8 @@
 
 
 def experts(rows, shards):
-    n, width = rows.shape
+    given, width = rows.shape
+    n = given // ROWS * CAP
     count = shards[0].shape[0] // 3 * 4
     anywhere = pl.BlockSpec(memory_space=pl.ANY)
     return pl.pallas_call(
@@ -131,7 +146,7 @@
         in_specs=[anywhere] * 5,
         out_specs=anywhere,
         scratch_shapes=[
-            pltpu.VMEM((n, width), BF16),
+            pltpu.VMEM((given, width), BF16),
             pltpu.VMEM((count, width), BF16),
             pltpu.VMEM((count, width), BF16),
             pltpu.VMEM((count, width), BF16),
@@ -170,39 +185,25 @@
         out[:, pl.ds(pl.multiple_of(half * cols, cols), cols)] = ref[...]
 
 
-def spread_kernel(row, out):
-    wide = row[...].astype(F32)
-    for i in range(out.shape[0]):
-        out[i] = wide
-
-
-def rows_kernel(spread, out):
-    out[...] = jnp.concatenate([spread[i] for i in range(spread.shape[0])], axis=0).astype(BF16)
-
-
-def pair_kernel(own, other, out):
-    out[...] = jnp.concatenate([own[...].astype(F32), other[...].astype(F32)], axis=0).astype(BF16)
-
-
-def image_kernel(n_z, *refs):
-    groups, (gain, first, second, mine, theirs) = refs[:-5], refs[-5:]
-    wide = [group[...].astype(F32) for group in groups]
-    n_yh = len(wide)
-    blocks = []
-    for core in range(2):
-        for low in range(2):
-            for ahead in range(n_yh):
-                at = (low * 2 + core) * n_z
-                blocks.append(wide[(n_yh - ahead) % n_yh][at : at + n_z, :])
-    wide = jnp.concatenate(blocks, axis=0)
+def image_kernel(sizes, where, own, other, gain, first, second, mine, theirs):
+    n_yh, n_z = sizes
+    wide = jnp.concatenate([own[...].astype(F32), other[...].astype(F32)], axis=0)
+    n = wide.shape[0]
     scale = lax.rsqrt(jnp.mean(wide * wide, axis=-1, keepdims=True) + 1e-06)
     normed = (wide * scale * gain[...]).astype(BF16)
     made = nt(normed, first[...])
     hidden = (0.5 * made * (1.0 + lax.erf(made * np.float32(0.5**0.5)))).astype(BF16)
-    whole = jnp.dot(hidden, second[...], preferred_element_type=F32)
-    half = mine.shape[0]
-    mine[...] = whole[:half]
-    theirs[...] = whole[half:].astype(BF16)
+    yh, yl = where[0], where[1] // 2
+    at = lax.broadcasted_iota(jnp.int32, (n, n), 0)
+    z = lax.rem(at, n_z)
+    high = lax.rem(at // n_z + yh, n_yh)
+    low = lax.rem(at // (n_z * n_yh) + yl, 2)
+    source = ((at // (2 * n_z * n_yh) * n_yh + high) * 2 + low) * n_z + z
+    order = jnp.where(lax.broadcasted_iota(jnp.int32, (n, n), 1) == source, 1.0, 0.0).astype(BF16)
+    turned = jnp.dot(order, hidden, preferred_element_type=F32).astype(BF16)
+    whole = jnp.dot(turned, second[...], preferred_element_type=F32)
+    mine[...] = whole[: n // 2]
+    theirs[...] = whole[n // 2 :].astype(BF16)
 
 
 def fold_kernel(held, came, keep, *sends):
@@ -259,47 +260,39 @@
     def exchanged(value, axis):
         return lax.all_to_all(value, axis, split_axis=0, concat_axis=0, tiled=True)
 
-    own = jnp.concatenate([w_gate[0, 0].T, w_up[0, 0].T, w_down[0, 0]], axis=0)
-    across = shifted(own, "yl", 1)
-    other = shifted(own, "core", 1)
-
     tokens = trunk_in[0]
     toks, width = tokens.shape
     sent = swapped(tokens)
     meta = swapped(jnp.concatenate([expert_ids[0].T.astype(F32), gate_scores[0].T], axis=0))
+    own = jnp.concatenate([w_gate[0, 0].T, w_up[0, 0].T, w_down[0, 0]], axis=0)
+    own, sent, meta = lax.optimization_barrier((own, sent, meta))
+    across = shifted(own, "yl", 1)
+    other = shifted(own, "core", 1)
+    both = shifted(across, "core", 1)
 
     image = image_in[0]
     dv = image.shape[1]
-    column = exchanged(call(spread_kernel, shaped((n_z, 1, dv), F32))(image), "z")
-    column = call(rows_kernel, shaped((n_z, dv)))(column)
-    column, sent = lax.optimization_barrier((column, sent))
-    chip = call(pair_kernel, shaped((2 * n_z, dv)))(column, shifted(column, "core", 1))
-    chips = call(pair_kernel, shaped((4 * n_z, dv)))(chip, shifted(chip, "yl", 1))
-
+    rows = call(pack_kernel, pltpu.HBM((n_z * ROWS, width), BF16), scalars=1)(where, meta, sent, trunk_gain, image)
+    arrived = exchanged(rows.reshape(n_z, ROWS, width), "z")
+
+    column = arrived[:, CAP : CAP + 2, :].reshape(n_z, 2 * width)[:, :dv]
+    spread = jnp.broadcast_to(column[None], (n_yh * 2, n_z, dv))
+    image_own = exchanged(spread, ("yh", "yl")).reshape(-1, dv)
+
+    made = experts(arrived.reshape(-1, width), (own, other, across, both))
+    made, meta = lax.optimization_barrier((made, meta))
     n_rows = n_z * CAP
-    pick, high, low = call(
-        table_kernel,
-        (shaped((n_rows, toks)), shaped((toks, n_rows)), shaped((toks, n_rows))),
-        scalars=1,
-    )(where, meta)
-    rows = call(pack_kernel, pltpu.HBM((n_rows, width), BF16), flops=2 * n_rows * toks * width, moved=2 * n_rows * width)(
-        pick, sent, trunk_gain
-    )
-    arrived = exchanged(rows.reshape(n_z, CAP, width), "z").reshape(n_rows, width)
-    across, arrived, chips = lax.optimization_barrier((across, arrived, chips))
-    both = shifted(across, "core", 1)
-    others = [shifted(chips, "yh", k) for k in range(1, n_yh)]
-    made = experts(arrived, (own, other, across, both))
-    made, others = lax.optimization_barrier((made, others))
     returned = exchanged(made.reshape(n_z, CAP, width), "z").reshape(n_rows, width)
+    high, low = call(weigh_kernel, (shaped((toks, n_rows)), shaped((toks, n_rows))), scalars=1)(where, meta)
 
     n_image = n_z * n_square
     mine, theirs = call(
-        functools.partial(image_kernel, n_z),
+        functools.partial(image_kernel, (n_yh, n_z)),
         (shaped((n_image // 2, dv), F32), shaped((n_image // 2, dv))),
+        scalars=1,
         flops=4 * n_image * dv * 100,
         moved=4 * n_image * dv,
-    )(chips, *others, image_gain, fc_in[0].T, fc_out[0])
+    )(where, image_own, shifted(image_own, "core", 1), image_gain, fc_in[0].T, fc_out[0])
     mine, theirs = call(fold_kernel, (shaped((n_image // 4, dv), F32), shaped((n_image // 4, dv))))(
         mine, shifted(theirs, "core", 1)
     )

time: 216 us -> 192 us (0.89)
  waiting for transfers between devices: 83.9 us -> 55.1 us
  blocking collectives: 9.87 us -> 14.4 us
    ppermute x2, waiting for transfers between devices: 41.7 us -> 3.61 us  [swapped(): lax.ppermute(value, square, [(a * n_tp + b, b * n_tp + a) for a in range(...]
    ppermute x16 -> x12, waiting for transfers between devices: 27.1 us -> 42.6 us  [shifted(): return lax.ppermute(value, axis, [(i, (i + by) % n) for i in range(n)])]
    all_to_all x3, waiting for transfers between devices: 13.7 us -> 8.89 us  [exchanged(): return lax.all_to_all(value, axis, split_axis=0, concat_axis=0, tiled=True)]
    all_to_all x1, blocking collectives: 9.87 us -> 14.4 us  [exchanged(): return lax.all_to_all(value, axis, split_axis=0, concat_axis=0, tiled=True)]
    all_to_all x3, starting transfers between devices: 23.8 us -> 27.9 us  [exchanged(): return lax.all_to_all(value, axis, split_axis=0, concat_axis=0, tiled=True)]
    ppermute x16 -> x12, starting transfers between devices: 57 us -> 53.3 us  [shifted(): return lax.ppermute(value, axis, [(i, (i + by) % n) for i in range(n)])]
    unnamed x29 -> x15, local copies, waits for them, and re-layouts: 4.59 us -> 2.73 us
    pallas_call x15 -> x11, Pallas kernels: 7.52 us -> 8.17 us  [run(): pl.pallas_call(kernel, out_shape=outs, in_specs=specs, out_specs=jax.tree...]
  transfers between devices with their start and end apart: 23 -> 19, of which waited for: 14 -> 12; matrix products, arithmetic and copies ran while one was open for 1% -> 3% of each run, Pallas kernels for 5% -> 7%
where the time goes in v6:
time: 192 us; the launch traced here: 191 us
  starting transfers between devices  98.4 us (51%)
  waiting for transfers between devices  55.1 us (29%)
  Pallas kernels  15.2 us (8%)
  blocking collectives  14.4 us (8%)
  local copies, waits for them, and re-layouts  3.52 us (2%)
  other arithmetic  3.23 us (2%)
    ppermute x12, starting transfers between devices, shifted(): return lax.ppermute(value, axis, [(i, (i + by) % n) for i in range(n)])  53.3 us
    ppermute x12, waiting for transfers between devices, shifted(): return lax.ppermute(value, axis, [(i, (i + by) % n) for i in range(n)])  42.6 us
    all_to_all x3, starting transfers between devices, exchanged(): return lax.all_to_all(value, axis, split_axis=0, concat_axis=0, tiled=True)  27.9 us
    all_to_all x1, blocking collectives, exchanged(): return lax.all_to_all(value, axis, split_axis=0, concat_axis=0, tiled=True)  14.4 us
    ppermute x2, starting transfers between devices, body(): lax.ppermute(piece, ('pp',) + square, [(s * n_square + a * n_tp + b, (s +...  9.7 us
    all_to_all x3, waiting for transfers between devices, exchanged(): return lax.all_to_all(value, axis, split_axis=0, concat_axis=0, tiled=True)  8.89 us
    pallas_call x11, Pallas kernels, run(): pl.pallas_call(kernel, out_shape=outs, in_specs=specs, out_specs=jax.tree...  8.17 us
    ppermute x2, starting transfers between devices, swapped(): lax.ppermute(value, square, [(a * n_tp + b, b * n_tp + a) for a in range(...  7.52 us
  transfers between devices with their start and end apart: 19, of which 12 were waited for; matrix products, arithmetic and copies ran while one was open for 3% of the time, Pallas kernels for 7%

profile of v6, /device:TPU:1, one launch (start us, length us, event | category | flops | bytes accessed | tf_op | source)
XLA Modules:
  0.0 190.9 jit_solution(1537961603480939990)
XLA Ops:
  0.6 5.6 %collective-permute-start = (bf16[128,2048]{1,0:T(8,128)(2,1)}, bf16[128,2048]{1,0:T(8,128)(2,1)S(1)}, u32[]{:S(2)}, u32[]{:S(2)}) collective-permute-start(bf16[128,2048]{1,0:T(8,128)(2,1)} %bitcast.48), channel_id=1, source_target_pairs={{0,0},{1,32},{2,64},{3,96},{32,1},{33,33},{34,65},{35,97},{64,2},{... | collective-permute-start | bytes 1572872 | tf_op jit(solution)/shard_map/ppermute | solution.py:254
  6.2 0.7 convert_bitcast_fusion
  6.9 0.7 pad_maximum_fusion.1
  7.6 1.9 collective-permute-start.1
  9.5 0.0 copy-start.2
  9.6 0.0 copy-start.5
  9.6 1.8 pad_maximum_fusion.refs_0_
  11.3 3.6 %collective-permute-done.1.meta = f32[16,128]{1,0:T(8,128)S(1)} collective-permute-done((f32[16,128]{1,0:T(8,128)S(1)}, f32[16,128]{1,0:T(8,128)S(1)}, u32[]{:S(2)}, u32[]{:S(2)}) %collective-permute-start.1) | collective-permute-done | bytes 8224 | tf_op jit(solution)/shard_map/ppermute | solution.py:254
  14.9 0.0 collective-permute-done.toks
  15.0 9.5 %collective-permute-start.9 = (bf16[576,2048]{1,0:T(8,128)(2,1)S(1)}, bf16[576,2048]{1,0:T(8,128)(2,1)}, u32[]{:S(2)}, u32[]{:S(2)}) collective-permute-start(bf16[576,2048]{1,0:T(8,128)(2,1)S(1)} %pad_maximum_fusion.refs_0_), channel_id=1, source_target_pairs={{0,2},{2,0},{1,3},{3,1},{4,6},{6,4},{5,7},{7,5},{8,10},{10,8},{9,1... | collective-permute-start | bytes 7077896 | tf_op jit(solution)/shard_map/ppermute | solution.py:258
  24.5 0.1 pad_add_fusion.where
  24.6 0.0 copy-done.2
  24.6 0.0 copy-done.5
  24.6 2.4 %shard_map.131 = bf16[384,2048]{1,0:T(8,128)(2,1)} custom-call(s32[2]{0:T(128)S(1)} %pad_add_fusion.where, f32[16,128]{1,0:T(8,128)S(1)} %collective-permute-done.1.meta, bf16[128,2048]{1,0:T(8,128)(2,1)S(1)} %collective-permute-done.toks, f32[1,2048]{1,0:T(1,128)S(1)} %copy-done.5, bf16[1,3200]{1,0:T(2,128)(2,1)S(1)} %bitcast.37), custom_call_target="tpu_custom_call" | custom-call | tf_op jit(solution)/shard_map/pallas_call | solution.py:24
  27.0 10.0 %all-to-all-start = ((bf16[8,48,2048]{2,1,0:T(8,128)(2,1)}), bf16[8,48,2048]{2,1,0:T(8,128)(2,1)}, u32[]{:S(2)}, u32[]{:S(2)}) async-start(bf16[8,48,2048]{2,1,0:T(8,128)(2,1)} %bitcast.40), calls=%async_computation | async-start | bytes 3145728 | tf_op jit(solution)/shard_map/all_to_all | solution.py:261
  37.0 8.8 %collective-permute-start.8 = (bf16[576,2048]{1,0:T(8,128)(2,1)S(1)}, bf16[576,2048]{1,0:T(8,128)(2,1)}, u32[]{:S(2)}, u32[]{:S(2)}) collective-permute-start(bf16[576,2048]{1,0:T(8,128)(2,1)S(1)} %pad_maximum_fusion.refs_0_), channel_id=1, source_target_pairs={{0,1},{1,0},{2,3},{3,2},{4,5},{5,4},{6,7},{7,6},{8,9},{9,8},{10,11... | collective-permute-start | bytes 7077896 | tf_op jit(solution)/shard_map/ppermute | solution.py:258
  45.8 24.0 %collective-permute-done.9.refs_2_ = bf16[576,2048]{1,0:T(8,128)(2,1)} collective-permute-done((bf16[576,2048]{1,0:T(8,128)(2,1)S(1)}, bf16[576,2048]{1,0:T(8,128)(2,1)}, u32[]{:S(2)}, u32[]{:S(2)}) %collective-permute-start.9) | collective-permute-done | bytes 2359328 | tf_op jit(solution)/shard_map/ppermute | solution.py:258
  69.8 8.9 %collective-permute-start.10 = (bf16[576,2048]{1,0:T(8,128)(2,1)}, bf16[576,2048]{1,0:T(8,128)(2,1)}, u32[]{:S(2)}, u32[]{:S(2)}) collective-permute-start(bf16[576,2048]{1,0:T(8,128)(2,1)} %collective-permute-done.9.refs_2_), channel_id=1, source_target_pairs={{0,1},{1,0},{2,3},{3,2},{4,5},{5,4},{6,7},{7,6},{8,9},{9,8},{10,11... | collective-permute-start | bytes 7077896 | tf_op jit(solution)/shard_map/ppermute | solution.py:258
  78.7 0.0 all-to-all-done
  78.7 1.0 slice_bitcast_fusion
  79.7 0.8 broadcast_in_dim.12
  80.5 8.1 %all-to-all-start.1 = ((bf16[8,8,3200]{2,1,0:T(8,128)(2,1)}), bf16[8,8,3200]{2,1,0:T(8,128)(2,1)S(1)}, u32[]{:S(2)}, u32[]{:S(2)}) async-start(bf16[8,8,3200]{2,1,0:T(8,128)(2,1)} %broadcast_in_dim.12), calls=%async_computation.1 | async-start | bytes 819200 | tf_op jit(solution)/shard_map/all_to_all | solution.py:261
  88.6 0.0 collective-permute-done.8.refs_1_
  88.6 0.0 collective-permute-done.10.refs_3_
  88.6 7.0 %shard_map.136 = bf16[320,2048]{1,0:T(8,128)(2,1)} custom-call(bf16[384,2048]{1,0:T(8,128)(2,1)} %bitcast.18.rows, bf16[576,2048]{1,0:T(8,128)(2,1)S(1)} %pad_maximum_fusion.refs_0_, bf16[576,2048]{1,0:T(8,128)(2,1)} %collective-permute-done.8.refs_1_, bf16[576,2048]{1,0:T(8,128)(2,1)} %collective-permute-done.9.refs_2_, ...), custom_call_target="tpu_custom_call" | custom-call | flops 3019898880 | bytes 9437184 | tf_op jit(solution)/shard_map/pallas_call | solution.py:143
  95.7 0.0 copy-start
  95.7 0.0 copy-start.4
  95.7 8.4 %all-to-all-done.1 = bf16[8,8,3200]{2,1,0:T(8,128)(2,1)S(1)} async-done(((bf16[8,8,3200]{2,1,0:T(8,128)(2,1)}), bf16[8,8,3200]{2,1,0:T(8,128)(2,1)S(1)}, u32[]{:S(2)}, u32[]{:S(2)}) %all-to-all-start.1) | async-done | bytes 409632 | tf_op jit(solution)/shard_map/all_to_all | solution.py:261
  104.1 9.7 %all-to-all-start.2 = ((bf16[8,40,2048]{2,1,0:T(8,128)(2,1)}), bf16[8,40,2048]{2,1,0:T(8,128)(2,1)S(1)}, u32[]{:S(2)}, u32[]{:S(2)}) async-start(bf16[8,40,2048]{2,1,0:T(8,128)(2,1)} %bitcast.41), calls=%async_computation.2 | async-start | bytes 2621440 | tf_op jit(solution)/shard_map/all_to_all | solution.py:261
  113.8 2.7 %collective-permute-start.2 = (bf16[64,3200]{1,0:T(8,128)(2,1)S(1)}, bf16[64,3200]{1,0:T(8,128)(2,1)S(1)}, u32[]{:S(2)}, u32[]{:S(2)}) collective-permute-start(bf16[64,3200]{1,0:T(8,128)(2,1)S(1)} %bitcast.33), channel_id=1, source_target_pairs={{0,1},{1,0},{2,3},{3,2},{4,5},{5,4},{6,7},{7,6},{8,9},{9,8},{10,11... | collective-permute-start | bytes 1228808 | tf_op jit(solution)/shard_map/ppermute | solution.py:258
  116.5 1.4 collective-permute-done.2.other
  117.9 0.0 copy-done
  117.9 1.1 copy-done.1
  119.0 1.9 %shard_map.132 = (f32[64,3200]{1,0:T(8,128)S(1)}, bf16[64,3200]{1,0:T(8,128)(2,1)S(1)}) custom-call(s32[2]{0:T(128)S(1)} %pad_add_fusion.where, bf16[64,3200]{1,0:T(8,128)(2,1)S(1)} %bitcast.34, bf16[64,3200]{1,0:T(8,128)(2,1)S(1)} %collective-permute-done.2.other, f32[1,3200]{1,0:T(1,128)S(1)} %copy-done.4, bf16[100,3200]{1,0:T(8,128)(2,1)S(1)} %bitcast.35, ...), custom_call_target="tpu_custom_call" | custom-call | flops 163840000 | bytes 1638400 | tf_op jit(solution)/shard_map/pallas_call | solution.py:24
  120.9 2.3 %collective-permute-start.3 = (bf16[64,3200]{1,0:T(8,128)(2,1)S(1)}, bf16[64,3200]{1,0:T(8,128)(2,1)S(1)}, u32[]{:S(2)}, u32[]{:S(2)}) collective-permute-start(bf16[64,3200]{1,0:T(8,128)(2,1)S(1)} %get-tuple-element.27), channel_id=1, source_target_pairs={{0,1},{1,0},{2,3},{3,2},{4,5},{5,4},{6,7},{7,6},{8,9},{9,8},{10,11... | collective-permute-start | bytes 1228808 | tf_op jit(solution)/shard_map/ppermute | solution.py:258
  123.2 1.4 collective-permute-done.3.came
  124.6 0.1 shard_map.133
  124.6 2.2 %collective-permute-start.4 = (bf16[32,3200]{1,0:T(8,128)(2,1)S(1)}, bf16[32,3200]{1,0:T(8,128)(2,1)S(1)}, u32[]{:S(2)}, u32[]{:S(2)}) collective-permute-start(bf16[32,3200]{1,0:T(8,128)(2,1)S(1)} %get-tuple-element.29), channel_id=1, source_target_pairs={{0,2},{2,0},{1,3},{3,1},{4,6},{6,4},{5,7},{7,5},{8,10},{10,8},{9,1... | collective-permute-start | bytes 614408 | tf_op jit(solution)/shard_map/ppermute | solution.py:258
  126.9 6.0 %collective-permute-done.4.came = bf16[32,3200]{1,0:T(8,128)(2,1)S(1)} collective-permute-done((bf16[32,3200]{1,0:T(8,128)(2,1)S(1)}, bf16[32,3200]{1,0:T(8,128)(2,1)S(1)}, u32[]{:S(2)}, u32[]{:S(2)}) %collective-permute-start.4) | collective-permute-done | bytes 204832 | tf_op jit(solution)/shard_map/ppermute | solution.py:258
  132.8 0.1 shard_map.134
  132.9 1.9 %collective-permute-start.5 = (bf16[8,3200]{1,0:T(8,128)(2,1)S(1)}, bf16[8,3200]{1,0:T(8,128)(2,1)S(1)}, u32[]{:S(2)}, u32[]{:S(2)}) collective-permute-start(bf16[8,3200]{1,0:T(8,128)(2,1)S(1)} %get-tuple-element.31), channel_id=1, source_target_pairs={{0,32},{32,64},{64,96},{96,0},{1,33},{33,65},{65,97},{97,1},{2,34}... | collective-permute-start | bytes 153608 | tf_op jit(solution)/shard_map/ppermute | solution.py:258
  134.8 4.0 %collective-permute-start.6 = (bf16[8,3200]{1,0:T(8,128)(2,1)S(1)}, bf16[8,3200]{1,0:T(8,128)(2,1)S(1)}, u32[]{:S(2)}, u32[]{:S(2)}) collective-permute-start(bf16[8,3200]{1,0:T(8,128)(2,1)S(1)} %get-tuple-element.32), channel_id=1, source_target_pairs={{0,64},{32,96},{64,0},{96,32},{1,65},{33,97},{65,1},{97,33},{2,66}... | collective-permute-start | bytes 153608 | tf_op jit(solution)/shard_map/ppermute | solution.py:258
  138.9 3.6 %collective-permute-start.7 = (bf16[8,3200]{1,0:T(8,128)(2,1)S(1)}, bf16[8,3200]{1,0:T(8,128)(2,1)S(1)}, u32[]{:S(2)}, u32[]{:S(2)}) collective-permute-start(bf16[8,3200]{1,0:T(8,128)(2,1)S(1)} %get-tuple-element.33), channel_id=1, source_target_pairs={{0,96},{32,0},{64,32},{96,64},{1,97},{33,1},{65,33},{97,65},{2,98}... | collective-permute-start | bytes 153608 | tf_op jit(solution)/shard_map/ppermute | solution.py:258
  142.5 0.0 collective-permute-done.5.refs_0_
  142.5 1.4 collective-permute-done.6.refs_1_
  143.9 3.4 %collective-permute-done.7.refs_2_ = bf16[8,3200]{1,0:T(8,128)(2,1)S(1)} collective-permute-done((bf16[8,3200]{1,0:T(8,128)(2,1)S(1)}, bf16[8,3200]{1,0:T(8,128)(2,1)S(1)}, u32[]{:S(2)}, u32[]{:S(2)}) %collective-permute-start.7) | collective-permute-done | bytes 51232 | tf_op jit(solution)/shard_map/ppermute | solution.py:258
  147.3 0.8 shard_map.137
  148.1 0.5 all-to-all-done.2
  148.6 1.3 shard_map.138
  149.9 7.8 %collective-permute-start.11 = (bf16[128,1024]{1,0:T(8,128)(2,1)S(1)}, bf16[128,1024]{1,0:T(8,128)(2,1)S(1)}, u32[]{:S(2)}, u32[]{:S(2)}) collective-permute-start(bf16[128,1024]{1,0:T(8,128)(2,1)S(1)} %get-tuple-element.41), channel_id=1, source_target_pairs={{0,128},{1,160},{2,192},{3,224},{32,129},{33,161},{34,193},{35,225... | collective-permute-start | bytes 786440 | tf_op jit(solution)/shard_map/ppermute | solution.py:312
  157.7 1.9 %collective-permute-start.12 = (bf16[128,1024]{1,0:T(8,128)(2,1)S(1)}, bf16[128,1024]{1,0:T(8,128)(2,1)S(1)}, u32[]{:S(2)}, u32[]{:S(2)}) collective-permute-start(bf16[128,1024]{1,0:T(8,128)(2,1)S(1)} %get-tuple-element.42), channel_id=1, source_target_pairs={{0,130},{1,162},{2,194},{3,226},{32,131},{33,163},{34,195},{35,227... | collective-permute-start | bytes 786440 | tf_op jit(solution)/shard_map/ppermute | solution.py:312
  159.6 14.4 %all_to_all.20.spread = f32[8,1,3200]{2,1,0:T(1,128)S(1)} all-to-all(f32[8,1,3200]{2,1,0:T(1,128)S(1)} %shard_map.135), channel_id=1, replica_groups=mesh['pp'=4,'yh'=4,'z'=8,'yl'=2,'core'=2] {'z'}, dimensions={0} | all-to-all | bytes 204800 | tf_op jit(solution)/shard_map/all_to_all | solution.py:261
  174.1 0.0 collective-permute-done.11.left
  174.1 0.0 collective-permute-done.12.right
  174.1 0.1 shard_map.139.left
  174.1 4.1 %collective-permute-start.13 = (bf16[128,1024]{1,0:T(8,128)(2,1)S(1)}, bf16[128,1024]{1,0:T(8,128)(2,1)S(1)}, u32[]{:S(2)}, u32[]{:S(2)}) collective-permute-start(bf16[128,1024]{1,0:T(8,128)(2,1)S(1)} %shard_map.139.left), channel_id=1, source_target_pairs={{0,1},{1,0},{2,3},{3,2},{4,5},{5,4},{6,7},{7,6},{8,9},{9,8},{10,11... | collective-permute-start | bytes 786440 | tf_op jit(solution)/shard_map/ppermute | solution.py:258
  178.3 1.1 collective-permute-done.13.right
  179.4 0.1 shard_map.140.own
  179.5 1.9 %collective-permute-start.14 = (bf16[128,1024]{1,0:T(8,128)(2,1)S(1)}, bf16[128,1024]{1,0:T(8,128)(2,1)S(1)}, u32[]{:S(2)}, u32[]{:S(2)}) collective-permute-start(bf16[128,1024]{1,0:T(8,128)(2,1)S(1)} %shard_map.140.own), channel_id=1, source_target_pairs={{0,2},{2,0},{1,3},{3,1},{4,6},{6,4},{5,7},{7,5},{8,10},{10,8},{9,1... | collective-permute-start | bytes 786440 | tf_op jit(solution)/shard_map/ppermute | solution.py:258
  181.4 3.4 %collective-permute-start.15 = (bf16[1,1,3200]{2,1,0:T(2,128)(2,1)S(1)}, bf16[1,1,3200]{2,1,0:T(2,128)(2,1)S(1)}, u32[]{:S(2)}, u32[]{:S(2)}) collective-permute-start(bf16[1,1,3200]{2,1,0:T(2,128)(2,1)S(1)} %bitcast.39), channel_id=1, source_target_pairs={{0,384},{128,0},{256,128},{384,256},{1,385},{129,1},{257,129},{385... | collective-permute-start | bytes 19208 | tf_op jit(solution)/shard_map/ppermute | solution.py:258
  184.8 1.4 collective-permute-done.15
  186.2 2.7 %collective-permute-done.14.across = bf16[128,1024]{1,0:T(8,128)(2,1)S(1)} collective-permute-done((bf16[128,1024]{1,0:T(8,128)(2,1)S(1)}, bf16[128,1024]{1,0:T(8,128)(2,1)S(1)}, u32[]{:S(2)}, u32[]{:S(2)}) %collective-permute-start.14) | collective-permute-done | bytes 262176 | tf_op jit(solution)/shard_map/ppermute | solution.py:258
  188.9 1.4 shard_map.141
  190.3 0.6 copy.16
  (8 shorter events, 0.1 us)
Async XLA Ops:
  0.6 14.3 %collective-permute-start = (bf16[128,2048]{1,0:T(8,128)(2,1)}, bf16[128,2048]{1,0:T(8,128)(2,1)S(1)}, u32[]{:S(2)}, u32[]{:S(2)}) collective-permute-start(bf16[128,2048]{1,0:T(8,128)(2,1)} %bitcast.48), channel_id=1, source_target_pairs={{0,0},{1,32},{2,64},{3,96},{32,1},{33,33},{34,65},{35,97},{64,2},{... | collective-permute-start | bytes 1572872 | tf_op jit(solution)/shard_map/ppermute | solution.py:254
  7.6 7.3 %collective-permute-start.1 = (f32[16,128]{1,0:T(8,128)S(1)}, f32[16,128]{1,0:T(8,128)S(1)}, u32[]{:S(2)}, u32[]{:S(2)}) collective-permute-start(f32[16,128]{1,0:T(8,128)S(1)} %pad_maximum_fusion.1), channel_id=1, source_target_pairs={{0,0},{1,32},{2,64},{3,96},{32,1},{33,33},{34,65},{35,97},{64,2},{... | collective-permute-start | bytes 24584 | tf_op jit(solution)/shard_map/ppermute | solution.py:254
  9.5 15.0 %copy-start.2 = (bf16[1,1,3200]{2,1,0:T(2,128)(2,1)S(1)}, bf16[1,1,3200]{2,1,0:T(2,128)(2,1)}, u32[]{:S(2)}) copy-start(bf16[1,1,3200]{2,1,0:T(2,128)(2,1)} %param.19) | copy-start | bytes 19204
  9.6 15.0 %copy-start.5 = (f32[1,2048]{1,0:T(1,128)S(1)}, f32[1,2048]{1,0:T(1,128)}, u32[]{:S(2)}) copy-start(f32[1,2048]{1,0:T(1,128)} %gain.2) | copy-start | bytes 24580
  15.0 54.9 %collective-permute-start.9 = (bf16[576,2048]{1,0:T(8,128)(2,1)S(1)}, bf16[576,2048]{1,0:T(8,128)(2,1)}, u32[]{:S(2)}, u32[]{:S(2)}) collective-permute-start(bf16[576,2048]{1,0:T(8,128)(2,1)S(1)} %pad_maximum_fusion.refs_0_), channel_id=1, source_target_pairs={{0,2},{2,0},{1,3},{3,1},{4,6},{6,4},{5,7},{7,5},{8,10},{10,8},{9,1... | collective-permute-start | bytes 7077896 | tf_op jit(solution)/shard_map/ppermute | solution.py:258
  27.0 51.7 %all-to-all-start = ((bf16[8,48,2048]{2,1,0:T(8,128)(2,1)}), bf16[8,48,2048]{2,1,0:T(8,128)(2,1)}, u32[]{:S(2)}, u32[]{:S(2)}) async-start(bf16[8,48,2048]{2,1,0:T(8,128)(2,1)} %bitcast.40), calls=%async_computation | async-start | bytes 3145728 | tf_op jit(solution)/shard_map/all_to_all | solution.py:261
  37.0 51.6 %collective-permute-start.8 = (bf16[576,2048]{1,0:T(8,128)(2,1)S(1)}, bf16[576,2048]{1,0:T(8,128)(2,1)}, u32[]{:S(2)}, u32[]{:S(2)}) collective-permute-start(bf16[576,2048]{1,0:T(8,128)(2,1)S(1)} %pad_maximum_fusion.refs_0_), channel_id=1, source_target_pairs={{0,1},{1,0},{2,3},{3,2},{4,5},{5,4},{6,7},{7,6},{8,9},{9,8},{10,11... | collective-permute-start | bytes 7077896 | tf_op jit(solution)/shard_map/ppermute | solution.py:258
  69.8 18.8 %collective-permute-start.10 = (bf16[576,2048]{1,0:T(8,128)(2,1)}, bf16[576,2048]{1,0:T(8,128)(2,1)}, u32[]{:S(2)}, u32[]{:S(2)}) collective-permute-start(bf16[576,2048]{1,0:T(8,128)(2,1)} %collective-permute-done.9.refs_2_), channel_id=1, source_target_pairs={{0,1},{1,0},{2,3},{3,2},{4,5},{5,4},{6,7},{7,6},{8,9},{9,8},{10,11... | collective-permute-start | bytes 7077896 | tf_op jit(solution)/shard_map/ppermute | solution.py:258
  80.5 23.6 %all-to-all-start.1 = ((bf16[8,8,3200]{2,1,0:T(8,128)(2,1)}), bf16[8,8,3200]{2,1,0:T(8,128)(2,1)S(1)}, u32[]{:S(2)}, u32[]{:S(2)}) async-start(bf16[8,8,3200]{2,1,0:T(8,128)(2,1)} %broadcast_in_dim.12), calls=%async_computation.1 | async-start | bytes 819200 | tf_op jit(solution)/shard_map/all_to_all | solution.py:261
  95.7 22.2 %copy-start = (bf16[1,3200,100]{1,2,0:T(8,128)(2,1)S(1)}, bf16[1,3200,100]{1,2,0:T(8,128)(2,1)}, u32[]{:S(2)}) copy-start(bf16[1,3200,100]{1,2,0:T(8,128)(2,1)} %param.21) | copy-start | bytes 1920004
  95.7 22.2 %copy-start.4 = (f32[1,3200]{1,0:T(1,128)S(1)}, f32[1,3200]{1,0:T(1,128)}, u32[]{:S(2)}) copy-start(f32[1,3200]{1,0:T(1,128)} %gain.3) | copy-start | bytes 38404
  104.1 44.6 %all-to-all-start.2 = ((bf16[8,40,2048]{2,1,0:T(8,128)(2,1)}), bf16[8,40,2048]{2,1,0:T(8,128)(2,1)S(1)}, u32[]{:S(2)}, u32[]{:S(2)}) async-start(bf16[8,40,2048]{2,1,0:T(8,128)(2,1)} %bitcast.41), calls=%async_computation.2 | async-start | bytes 2621440 | tf_op jit(solution)/shard_map/all_to_all | solution.py:261
  113.8 4.1 %collective-permute-start.2 = (bf16[64,3200]{1,0:T(8,128)(2,1)S(1)}, bf16[64,3200]{1,0:T(8,128)(2,1)S(1)}, u32[]{:S(2)}, u32[]{:S(2)}) collective-permute-start(bf16[64,3200]{1,0:T(8,128)(2,1)S(1)} %bitcast.33), channel_id=1, source_target_pairs={{0,1},{1,0},{2,3},{3,2},{4,5},{5,4},{6,7},{7,6},{8,9},{9,8},{10,11... | collective-permute-start | bytes 1228808 | tf_op jit(solution)/shard_map/ppermute | solution.py:258
  117.9 1.1 copy-start.1
  120.9 3.6 %collective-permute-start.3 = (bf16[64,3200]{1,0:T(8,128)(2,1)S(1)}, bf16[64,3200]{1,0:T(8,128)(2,1)S(1)}, u32[]{:S(2)}, u32[]{:S(2)}) collective-permute-start(bf16[64,3200]{1,0:T(8,128)(2,1)S(1)} %get-tuple-element.27), channel_id=1, source_target_pairs={{0,1},{1,0},{2,3},{3,2},{4,5},{5,4},{6,7},{7,6},{8,9},{9,8},{10,11... | collective-permute-start | bytes 1228808 | tf_op jit(solution)/shard_map/ppermute | solution.py:258
  124.6 8.2 %collective-permute-start.4 = (bf16[32,3200]{1,0:T(8,128)(2,1)S(1)}, bf16[32,3200]{1,0:T(8,128)(2,1)S(1)}, u32[]{:S(2)}, u32[]{:S(2)}) collective-permute-start(bf16[32,3200]{1,0:T(8,128)(2,1)S(1)} %get-tuple-element.29), channel_id=1, source_target_pairs={{0,2},{2,0},{1,3},{3,1},{4,6},{6,4},{5,7},{7,5},{8,10},{10,8},{9,1... | collective-permute-start | bytes 614408 | tf_op jit(solution)/shard_map/ppermute | solution.py:258
  132.8 48.6 %copy-start.3 = (f32[1,3200]{1,0:T(1,128)S(1)}, f32[1,3200]{1,0:T(1,128)}, u32[]{:S(2)}) copy-start(f32[1,3200]{1,0:T(1,128)} %scale.1) | copy-start | bytes 38404
  132.9 9.6 %collective-permute-start.5 = (bf16[8,3200]{1,0:T(8,128)(2,1)S(1)}, bf16[8,3200]{1,0:T(8,128)(2,1)S(1)}, u32[]{:S(2)}, u32[]{:S(2)}) collective-permute-start(bf16[8,3200]{1,0:T(8,128)(2,1)S(1)} %get-tuple-element.31), channel_id=1, source_target_pairs={{0,32},{32,64},{64,96},{96,0},{1,33},{33,65},{65,97},{97,1},{2,34}... | collective-permute-start | bytes 153608 | tf_op jit(solution)/shard_map/ppermute | solution.py:258
  134.8 9.1 %collective-permute-start.6 = (bf16[8,3200]{1,0:T(8,128)(2,1)S(1)}, bf16[8,3200]{1,0:T(8,128)(2,1)S(1)}, u32[]{:S(2)}, u32[]{:S(2)}) collective-permute-start(bf16[8,3200]{1,0:T(8,128)(2,1)S(1)} %get-tuple-element.32), channel_id=1, source_target_pairs={{0,64},{32,96},{64,0},{96,32},{1,65},{33,97},{65,1},{97,33},{2,66}... | collective-permute-start | bytes 153608 | tf_op jit(solution)/shard_map/ppermute | solution.py:258
  138.9 8.4 %collective-permute-start.7 = (bf16[8,3200]{1,0:T(8,128)(2,1)S(1)}, bf16[8,3200]{1,0:T(8,128)(2,1)S(1)}, u32[]{:S(2)}, u32[]{:S(2)}) collective-permute-start(bf16[8,3200]{1,0:T(8,128)(2,1)S(1)} %get-tuple-element.33), channel_id=1, source_target_pairs={{0,96},{32,0},{64,32},{96,64},{1,97},{33,1},{65,33},{97,65},{2,98}... | collective-permute-start | bytes 153608 | tf_op jit(solution)/shard_map/ppermute | solution.py:258
  149.9 24.2 %collective-permute-start.11 = (bf16[128,1024]{1,0:T(8,128)(2,1)S(1)}, bf16[128,1024]{1,0:T(8,128)(2,1)S(1)}, u32[]{:S(2)}, u32[]{:S(2)}) collective-permute-start(bf16[128,1024]{1,0:T(8,128)(2,1)S(1)} %get-tuple-element.41), channel_id=1, source_target_pairs={{0,128},{1,160},{2,192},{3,224},{32,129},{33,161},{34,193},{35,225... | collective-permute-start | bytes 786440 | tf_op jit(solution)/shard_map/ppermute | solution.py:312
  157.7 16.4 %collective-permute-start.12 = (bf16[128,1024]{1,0:T(8,128)(2,1)S(1)}, bf16[128,1024]{1,0:T(8,128)(2,1)S(1)}, u32[]{:S(2)}, u32[]{:S(2)}) collective-permute-start(bf16[128,1024]{1,0:T(8,128)(2,1)S(1)} %get-tuple-element.42), channel_id=1, source_target_pairs={{0,130},{1,162},{2,194},{3,226},{32,131},{33,163},{34,195},{35,227... | collective-permute-start | bytes 786440 | tf_op jit(solution)/shard_map/ppermute | solution.py:312
  174.1 5.3 %collective-permute-start.13 = (bf16[128,1024]{1,0:T(8,128)(2,1)S(1)}, bf16[128,1024]{1,0:T(8,128)(2,1)S(1)}, u32[]{:S(2)}, u32[]{:S(2)}) collective-permute-start(bf16[128,1024]{1,0:T(8,128)(2,1)S(1)} %shard_map.139.left), channel_id=1, source_target_pairs={{0,1},{1,0},{2,3},{3,2},{4,5},{5,4},{6,7},{7,6},{8,9},{9,8},{10,11... | collective-permute-start | bytes 786440 | tf_op jit(solution)/shard_map/ppermute | solution.py:258
  179.5 9.4 %collective-permute-start.14 = (bf16[128,1024]{1,0:T(8,128)(2,1)S(1)}, bf16[128,1024]{1,0:T(8,128)(2,1)S(1)}, u32[]{:S(2)}, u32[]{:S(2)}) collective-permute-start(bf16[128,1024]{1,0:T(8,128)(2,1)S(1)} %shard_map.140.own), channel_id=1, source_target_pairs={{0,2},{2,0},{1,3},{3,1},{4,6},{6,4},{5,7},{7,5},{8,10},{10,8},{9,1... | collective-permute-start | bytes 786440 | tf_op jit(solution)/shard_map/ppermute | solution.py:258
  181.4 4.7 %collective-permute-start.15 = (bf16[1,1,3200]{2,1,0:T(2,128)(2,1)S(1)}, bf16[1,1,3200]{2,1,0:T(2,128)(2,1)S(1)}, u32[]{:S(2)}, u32[]{:S(2)}) collective-permute-start(bf16[1,1,3200]{2,1,0:T(2,128)(2,1)S(1)} %bitcast.39), channel_id=1, source_target_pairs={{0,384},{128,0},{256,128},{384,256},{1,385},{129,1},{257,129},{385... | collective-permute-start | bytes 19208 | tf_op jit(solution)/shard_map/ppermute | solution.py:258

commit v7 on v6

--- a/solution.py
+++ b/solution.py
@@ -13,7 +13,21 @@
 VM = pl.BlockSpec(memory_space=pltpu.VMEM)
 SM = pl.BlockSpec(memory_space=pltpu.SMEM)
 CAP = 40
-ROWS = 48
+ROWS = 56
+
+
+def served(n):
+    table = {}
+    for a in range(n):
+        for t, c in enumerate((a - 1, a + 2 if a % 2 == 0 else a, a + 1, a if a % 2 == 0 else a + 2)):
+            c %= n
+            apart = (a - c) % n
+            if apart % 2 == 1:
+                copy = 2 if apart == 1 else 0
+            else:
+                copy = 3 if (apart == 2) == (c % 2 == 0) else 1
+            table[a, t] = (c, copy)
+    return table
 SMALL = 12 * 1024 * 1024
 LARGE = 24 * 1024 * 1024
 
@@ -60,21 +74,20 @@
     return jnp.where(rank[:, None, :] == slot, 1.0, 0.0), weight
 
 
-def pack_kernel(where, meta, toks, gain, image, rows):
+def pack_kernel(where, meta, toks, gain, ring, rows):
     n, width = rows.shape
     group = n // ROWS
     hit, _ = table(group, ROWS, where[0] * group, meta[...])
     wide = toks[...].astype(F32)
     scale = lax.rsqrt(jnp.mean(wide * wide, axis=-1, keepdims=True) + 1e-06)
     normed = (wide * scale * gain[...]).astype(BF16)
-    dv = image.shape[1]
-    picture = image[...].astype(F32)
-    spare = jnp.zeros((1, 2 * width - dv), F32)
-    picture = jnp.concatenate([picture[:, :width], jnp.concatenate([picture[:, width:], spare], axis=1)], axis=0)
-    picture = jnp.concatenate([picture, jnp.zeros((ROWS - CAP - 2, width), F32)], axis=0)
+    images = jnp.concatenate([ring[i] for i in range(ring.shape[0])], axis=0)
+    count, dv = images.shape
+    spare = jnp.zeros((count, 2 * width - dv), F32)
     empty = jnp.zeros((CAP, width), F32)
+    added = jnp.concatenate([empty, images[:, :width], jnp.concatenate([images[:, width:], spare], axis=1)], axis=0)
     made = jnp.dot(hit.reshape(n, hit.shape[2]).astype(BF16), normed, preferred_element_type=F32)
-    rows[...] = (made + jnp.concatenate([empty, picture] * group, axis=0)).astype(BF16)
+    rows[...] = (made + jnp.concatenate([added] * group, axis=0)).astype(BF16)
 
 
 def weigh_kernel(where, meta, high, low):
@@ -163,14 +176,14 @@
 
 def combine_kernel(where, toks, high, low, made, kept, given):
     half = made.shape[1] // 2
-    a = where[0]
-    for out, h in ((kept, a // 2), (given, 1 - a // 2)):
+    low_side, core = where[2] // 2, lax.rem(where[2], 2)
+    for out, h in ((kept, low_side), (given, 1 - low_side)):
         block = pl.ds(pl.multiple_of(h * half, half), half)
         part = made[:, block]
         summed = jnp.dot(high[...], part, preferred_element_type=F32)
         summed += jnp.dot(low[...], part, preferred_element_type=F32)
         if out is kept:
-            summed += jnp.where(lax.rem(a, 2) == 0, toks[:, block].astype(F32), 0.0)
+            summed += jnp.where(core == 0, toks[:, block].astype(F32), 0.0)
         out[...] = summed.astype(BF16)
 
 
@@ -185,23 +198,36 @@
         out[:, pl.ds(pl.multiple_of(half * cols, cols), cols)] = ref[...]
 
 
-def image_kernel(sizes, where, own, other, gain, first, second, mine, theirs):
+def spread_kernel(row, out):
+    wide = row[...].astype(F32)
+    for i in range(out.shape[0]):
+        out[i] = wide
+
+
+def image_kernel(sizes, where, rows, gain, weigh, first, first_other, second, second_other, mine, theirs):
     n_yh, n_z = sizes
-    wide = jnp.concatenate([own[...].astype(F32), other[...].astype(F32)], axis=0)
-    n = wide.shape[0]
+    n = rows.shape[0]
+    wide = rows[...].astype(F32)
     scale = lax.rsqrt(jnp.mean(wide * wide, axis=-1, keepdims=True) + 1e-06)
     normed = (wide * scale * gain[...]).astype(BF16)
-    made = nt(normed, first[...])
-    hidden = (0.5 * made * (1.0 + lax.erf(made * np.float32(0.5**0.5)))).astype(BF16)
     yh, yl = where[0], where[1] // 2
     at = lax.broadcasted_iota(jnp.int32, (n, n), 0)
     z = lax.rem(at, n_z)
     high = lax.rem(at // n_z + yh, n_yh)
     low = lax.rem(at // (n_z * n_yh) + yl, 2)
-    source = ((at // (2 * n_z * n_yh) * n_yh + high) * 2 + low) * n_z + z
+    source = (z * n_yh + high) * 2 + low
     order = jnp.where(lax.broadcasted_iota(jnp.int32, (n, n), 1) == source, 1.0, 0.0).astype(BF16)
-    turned = jnp.dot(order, hidden, preferred_element_type=F32).astype(BF16)
-    whole = jnp.dot(turned, second[...], preferred_element_type=F32)
+    whole = None
+    for w_in, w_out in ((first, second), (first_other, second_other)):
+        made = nt(normed, w_in[...])
+        hidden = (0.5 * made * (1.0 + lax.erf(made * np.float32(0.5**0.5)))).astype(BF16)
+        turned = jnp.dot(order, hidden, preferred_element_type=F32).astype(BF16)
+        part = jnp.dot(turned, w_out[...], preferred_element_type=F32)
+        whole = part if whole is None else whole + part
+    whole = whole * weigh[...]
+    images = jnp.dot(order, rows[...], preferred_element_type=F32)
+    mark = lax.broadcasted_iota(jnp.int32, (n, 1), 0) == where[3]
+    whole = whole + jnp.where(mark, images, 0.0)
     mine[...] = whole[: n // 2]
     theirs[...] = whole[n // 2 :].astype(BF16)
 
@@ -223,11 +249,11 @@
         out[i] = total[i : i + 1]
 
 
-def encoded_kernel(spread, image, scale, out):
+def encoded_kernel(spread, out):
     total = spread[0]
     for i in range(1, spread.shape[0]):
         total += spread[i]
-    out[...] = (image[...].astype(F32) + scale[...] * total).astype(BF16)
+    out[...] = total.astype(BF16)
 
 
 def body(
@@ -248,10 +274,14 @@
     n_tp = lax.axis_size("yl") * lax.axis_size("core")
     n_square = n_yh * n_tp
     square = ("yh", "yl", "core")
-    where = jnp.stack([lax.axis_index("yh"), lax.axis_index(("yl", "core"))]).astype(jnp.int32)
-
-    def swapped(value):
-        return lax.ppermute(value, square, [(a * n_tp + b, b * n_tp + a) for a in range(n_yh) for b in range(n_tp)])
+    serve = served(n_yh)
+    copies = np.array([serve[a, t][1] for a in range(n_yh) for t in range(n_tp)], np.int32)
+    yh, t = lax.axis_index("yh"), lax.axis_index(("yl", "core"))
+    where = jnp.stack([yh, t, jnp.asarray(copies)[yh * n_tp + t], lax.axis_index("z")]).astype(jnp.int32)
+
+    def fetched(value):
+        pairs = [(c * n_tp + copy, a * n_tp + t) for (a, t), (c, copy) in serve.items()]
+        return lax.ppermute(value, square, pairs)
 
     def shifted(value, axis, by):
         n = lax.axis_size(axis)
@@ -262,22 +292,22 @@
 
     tokens = trunk_in[0]
     toks, width = tokens.shape
-    sent = swapped(tokens)
-    meta = swapped(jnp.concatenate([expert_ids[0].T.astype(F32), gate_scores[0].T], axis=0))
+    sent = fetched(tokens)
+    meta = fetched(jnp.concatenate([expert_ids[0].T.astype(F32), gate_scores[0].T], axis=0))
     own = jnp.concatenate([w_gate[0, 0].T, w_up[0, 0].T, w_down[0, 0]], axis=0)
-    own, sent, meta = lax.optimization_barrier((own, sent, meta))
+    image = image_in[0]
+    dv = image.shape[1]
+    ring = exchanged(call(spread_kernel, shaped((n_yh * 2, 1, dv), F32))(image), ("yh", "yl"))
+    own, sent, meta, ring = lax.optimization_barrier((own, sent, meta, ring))
     across = shifted(own, "yl", 1)
     other = shifted(own, "core", 1)
+    first, second = fc_in[0].T, fc_out[0]
+    first_other, second_other = shifted(first, "core", 1), shifted(second, "core", 1)
+    across, first_other, second_other = lax.optimization_barrier((across, first_other, second_other))
     both = shifted(across, "core", 1)
 
-    image = image_in[0]
-    dv = image.shape[1]
-    rows = call(pack_kernel, pltpu.HBM((n_z * ROWS, width), BF16), scalars=1)(where, meta, sent, trunk_gain, image)
+    rows = call(pack_kernel, pltpu.HBM((n_z * ROWS, width), BF16), scalars=1)(where, meta, sent, trunk_gain, ring)
     arrived = exchanged(rows.reshape(n_z, ROWS, width), "z")
-
-    column = arrived[:, CAP : CAP + 2, :].reshape(n_z, 2 * width)[:, :dv]
-    spread = jnp.broadcast_to(column[None], (n_yh * 2, n_z, dv))
-    image_own = exchanged(spread, ("yh", "yl")).reshape(-1, dv)
 
     made = experts(arrived.reshape(-1, width), (own, other, across, both))
     made, meta = lax.optimization_barrier((made, meta))
@@ -285,23 +315,28 @@
     returned = exchanged(made.reshape(n_z, CAP, width), "z").reshape(n_rows, width)
     high, low = call(weigh_kernel, (shaped((toks, n_rows)), shaped((toks, n_rows))), scalars=1)(where, meta)
 
-    n_image = n_z * n_square
+    images = [arrived[:, CAP : CAP + 8, :], arrived[:, CAP + 8 : CAP + 16, : dv - width]]
+    images = jnp.concatenate(images, axis=2).reshape(-1, dv)
+    n_image = images.shape[0]
     mine, theirs = call(
         functools.partial(image_kernel, (n_yh, n_z)),
         (shaped((n_image // 2, dv), F32), shaped((n_image // 2, dv))),
         scalars=1,
-        flops=4 * n_image * dv * 100,
-        moved=4 * n_image * dv,
-    )(where, image_own, shifted(image_own, "core", 1), image_gain, fc_in[0].T, fc_out[0])
-    mine, theirs = call(fold_kernel, (shaped((n_image // 4, dv), F32), shaped((n_image // 4, dv))))(
-        mine, shifted(theirs, "core", 1)
-    )
+        flops=8 * n_image * dv * 100,
+        moved=8 * 100 * dv,
+    )(where, images, image_gain, layer_scale, first, first_other, second, second_other)
     mine, *theirs = call(
         fold_kernel, (shaped((n_z, dv), F32),) + tuple(shaped((n_z, dv)) for _ in range(n_yh - 1))
     )(mine, shifted(theirs, "yl", 1))
-    column = call(column_kernel, shaped((n_z, 1, dv), F32))(
-        mine, *[shifted(part, "yh", k + 1) for k, part in enumerate(theirs)]
-    )
+    parts = [
+        lax.ppermute(
+            part,
+            ("pp", "yh"),
+            [(s * n_yh + h, (s - 1) % n_pp * n_yh + (h + k) % n_yh) for s in range(n_pp) for h in range(n_yh)],
+        )
+        for k, part in enumerate([mine, *theirs])
+    ]
+    column = call(column_kernel, shaped((n_z, 1, dv), F32))(*parts)
 
     column, returned = lax.optimization_barrier((column, returned))
     half = width // 2
@@ -313,10 +348,9 @@
             piece,
             ("pp",) + square,
             [
-                (s * n_square + a * n_tp + b, (s + 1) % n_pp * n_square + b * n_tp + (a ^ flip))
+                (s * n_square + a * n_tp + t, (s + 1) % n_pp * n_square + c * n_tp + (copy ^ flip))
                 for s in range(n_pp)
-                for a in range(n_yh)
-                for b in range(n_tp)
+                for (a, t), (c, copy) in serve.items()
             ],
         )
         for flip, piece in zip((0, 2), pieces)
@@ -326,8 +360,7 @@
     layer = call(add_kernel, shaped((toks, half)))(part, shifted(part, "core", 1))
     trunk_out = call(join_kernel, shaped((toks, width)), scalars=1)(where, layer, shifted(layer, "yl", 1))
 
-    encoded = call(encoded_kernel, shaped((1, dv)))(spread, image, layer_scale)
-    image_out = shifted(encoded[None], "pp", -1)
+    image_out = call(encoded_kernel, shaped((1, dv)))(spread)[None]
     return (trunk_out[None], image_out)
 
 

time: 192 us -> 186 us (0.969)
  starting transfers between devices: 98.4 us -> 89 us
  local copies, waits for them, and re-layouts: 3.52 us -> 12.1 us
  waiting for transfers between devices: 55.1 us -> 47 us
    ppermute x12 -> x8, starting transfers between devices: 53.3 us -> 31.6 us  [shifted(): return lax.ppermute(value, axis, [(i, (i + by) % n) for i in range(n)])]
    ppermute x4 -> x8, starting transfers between devices: 17.2 us -> 33.8 us  [the longest x4 15.2 us: body(): lax.ppermute(part, ('pp', 'yh'), [(s * n_yh + h, (s - 1) % n_pp * n_yh +...]
    unnamed x15 -> x30, local copies, waits for them, and re-layouts: 2.73 us -> 9.5 us
    ppermute x12 -> x8, waiting for transfers between devices: 42.6 us -> 35.9 us  [shifted(): return lax.ppermute(value, axis, [(i, (i + by) % n) for i in range(n)])]
    all_to_all x3, starting transfers between devices: 27.9 us -> 23.6 us  [exchanged(): return lax.all_to_all(value, axis, split_axis=0, concat_axis=0, tiled=True)]
    all_to_all x3, waiting for transfers between devices: 8.89 us -> 6.17 us  [exchanged(): return lax.all_to_all(value, axis, split_axis=0, concat_axis=0, tiled=True)]
    ppermute x4 -> x8, waiting for transfers between devices: 3.62 us -> 4.93 us  [the longest x4 4.84 us: body(): lax.ppermute(part, ('pp', 'yh'), [(s * n_yh + h, (s - 1) % n_pp * n_yh +...]
  transfers between devices with their start and end apart: 19 -> 19, of which waited for: 12 -> 10; matrix products, arithmetic and copies ran while one was open for 3% -> 4% of each run, Pallas kernels for 7% -> 4%
where the time goes in v7:
time: 186 us; the launch traced here: 184 us
  starting transfers between devices  89 us (48%)
  waiting for transfers between devices  47 us (25%)
  Pallas kernels  17 us (9%)
  blocking collectives  13.7 us (7%)
  local copies, waits for them, and re-layouts  12.1 us (7%)
  other arithmetic  3.94 us (2%)
    ppermute x8, waiting for transfers between devices, shifted(): return lax.ppermute(value, axis, [(i, (i + by) % n) for i in range(n)])  35.9 us
    ppermute x8, starting transfers between devices, shifted(): return lax.ppermute(value, axis, [(i, (i + by) % n) for i in range(n)])  31.6 us
    all_to_all x3, starting transfers between devices, exchanged(): return lax.all_to_all(value, axis, split_axis=0, concat_axis=0, tiled=True)  23.6 us
    ppermute x4, starting transfers between devices, body(): lax.ppermute(part, ('pp', 'yh'), [(s * n_yh + h, (s - 1) % n_pp * n_yh +...  15.2 us
    all_to_all x1, blocking collectives, exchanged(): return lax.all_to_all(value, axis, split_axis=0, concat_axis=0, tiled=True)  13.7 us
    ppermute x2, starting transfers between devices, fetched(): return lax.ppermute(value, square, pairs)  10.5 us
    pallas_call x11, Pallas kernels, run(): pl.pallas_call(kernel, out_shape=outs, in_specs=specs, out_specs=jax.tree...  9.79 us
    unnamed x30, local copies, waits for them, and re-layouts  9.5 us
  transfers between devices with their start and end apart: 19, of which 10 were waited for; matrix products, arithmetic and copies ran while one was open for 4% of the time, Pallas kernels for 4%

profile of v7, /device:TPU:1, one launch (start us, length us, event | category | flops | bytes accessed | tf_op | source)
XLA Modules:
  0.0 183.6 jit_solution(7686839236567117781)
XLA Ops:
  0.6 4.0 %collective-permute-start = (bf16[128,2048]{1,0:T(8,128)(2,1)}, bf16[128,2048]{1,0:T(8,128)(2,1)S(1)}, u32[]{:S(2)}, u32[]{:S(2)}) collective-permute-start(bf16[128,2048]{1,0:T(8,128)(2,1)} %bitcast.45), channel_id=1, source_target_pairs={{98,0},{67,1},{32,2},{1,3},{2,32},{35,33},{64,34},{97,35},{34,64},... | collective-permute-start | bytes 1572872 | tf_op jit(solution)/shard_map/ppermute | solution.py:284
  4.7 0.7 convert_bitcast_fusion
  5.4 0.7 pad_maximum_fusion.1
  6.0 6.4 %collective-permute-start.1 = (f32[16,128]{1,0:T(8,128)S(1)}, f32[16,128]{1,0:T(8,128)S(1)}, u32[]{:S(2)}, u32[]{:S(2)}) collective-permute-start(f32[16,128]{1,0:T(8,128)S(1)} %pad_maximum_fusion.1), channel_id=1, source_target_pairs={{98,0},{67,1},{32,2},{1,3},{2,32},{35,33},{64,34},{97,35},{34,64},... | collective-permute-start | bytes 24584 | tf_op jit(solution)/shard_map/ppermute | solution.py:284
  12.5 0.0 copy-start.12
  12.5 0.7 copy-done.12
  13.2 0.7 shard_map.140
  13.9 3.4 %all-to-all-start = ((f32[8,1,3200]{2,1,0:T(1,128)}), f32[8,1,3200]{2,1,0:T(1,128)S(1)}, u32[]{:S(2)}, u32[]{:S(2)}) async-start(f32[8,1,3200]{2,1,0:T(1,128)} %shard_map.140), calls=%async_computation | async-start | bytes 204800 | tf_op jit(solution)/shard_map/all_to_all | solution.py:291
  17.2 0.0 copy-start.14
  17.2 0.0 copy-start.13
  17.2 1.8 pad_maximum_fusion.refs_0_
  19.0 0.1 collective-permute-done.1.meta
  19.1 5.3 %all-to-all-done.ring = f32[8,1,3200]{2,1,0:T(1,128)S(1)} async-done(((f32[8,1,3200]{2,1,0:T(1,128)}), f32[8,1,3200]{2,1,0:T(1,128)S(1)}, u32[]{:S(2)}, u32[]{:S(2)}) %all-to-all-start) | async-done | bytes 102432 | tf_op jit(solution)/shard_map/all_to_all | solution.py:291
  24.4 0.0 collective-permute-done.toks
  24.4 2.6 %collective-permute-start.2 = (bf16[576,2048]{1,0:T(8,128)(2,1)S(1)}, bf16[576,2048]{1,0:T(8,128)(2,1)}, u32[]{:S(2)}, u32[]{:S(2)}) collective-permute-start(bf16[576,2048]{1,0:T(8,128)(2,1)S(1)} %pad_maximum_fusion.refs_0_), channel_id=1, source_target_pairs={{0,2},{2,0},{1,3},{3,1},{4,6},{6,4},{5,7},{7,5},{8,10},{10,8},{9,1... | collective-permute-start | bytes 7077896 | tf_op jit(solution)/shard_map/ppermute | solution.py:288
  27.1 0.7 dynamic_slice.3
  27.8 0.8 pad_add_fusion.where
  28.5 2.6 %shard_map.141 = bf16[448,2048]{1,0:T(8,128)(2,1)} custom-call(s32[4]{0:T(128)S(1)} %pad_add_fusion.where, f32[16,128]{1,0:T(8,128)S(1)} %collective-permute-done.1.meta, bf16[128,2048]{1,0:T(8,128)(2,1)S(1)} %collective-permute-done.toks, f32[1,2048]{1,0:T(1,128)S(1)} %copy-done.13, f32[8,1,3200]{2,1,0:T(1,128)S(1)} %all-to-all-done.ring), custom_call_target="tpu_custom_call" | custom-call | tf_op jit(solution)/shard_map/pallas_call | solution.py:38
  31.1 10.1 %all-to-all-start.1 = ((bf16[8,56,2048]{2,1,0:T(8,128)(2,1)}), bf16[8,56,2048]{2,1,0:T(8,128)(2,1)}, u32[]{:S(2)}, u32[]{:S(2)}) async-start(bf16[8,56,2048]{2,1,0:T(8,128)(2,1)} %bitcast.37), calls=%async_computation.1 | async-start | bytes 3670016 | tf_op jit(solution)/shard_map/all_to_all | solution.py:291
  41.2 5.5 %collective-permute-start.3 = (bf16[100,3200]{1,0:T(8,128)(2,1)S(1)}, bf16[100,3200]{1,0:T(8,128)(2,1)S(1)}, u32[]{:S(2)}, u32[]{:S(2)}) collective-permute-start(bf16[100,3200]{1,0:T(8,128)(2,1)S(1)} %bitcast.32), channel_id=1, source_target_pairs={{0,1},{1,0},{2,3},{3,2},{4,5},{5,4},{6,7},{7,6},{8,9},{9,8},{10,11... | collective-permute-start | bytes 1920008 | tf_op jit(solution)/shard_map/ppermute | solution.py:288
  46.7 1.9 %collective-permute-start.4 = (bf16[100,3200]{1,0:T(8,128)(2,1)}, bf16[100,3200]{1,0:T(8,128)(2,1)S(1)}, u32[]{:S(2)}, u32[]{:S(2)}) collective-permute-start(bf16[100,3200]{1,0:T(8,128)(2,1)} %bitcast.34), channel_id=1, source_target_pairs={{0,1},{1,0},{2,3},{3,2},{4,5},{5,4},{6,7},{7,6},{8,9},{9,8},{10,11... | collective-permute-start | bytes 1920008 | tf_op jit(solution)/shard_map/ppermute | solution.py:288
  48.6 2.4 %collective-permute-start.10 = (bf16[576,2048]{1,0:T(8,128)(2,1)S(1)}, bf16[576,2048]{1,0:T(8,128)(2,1)S(1)}, u32[]{:S(2)}, u32[]{:S(2)}) collective-permute-start(bf16[576,2048]{1,0:T(8,128)(2,1)S(1)} %pad_maximum_fusion.refs_0_), channel_id=1, source_target_pairs={{0,1},{1,0},{2,3},{3,2},{4,5},{5,4},{6,7},{7,6},{8,9},{9,8},{10,11... | collective-permute-start | bytes 7077896 | tf_op jit(solution)/shard_map/ppermute | solution.py:288
  51.1 0.0 collective-permute-done.3.first_other
  51.1 0.8 copy-done.4
  51.9 0.9 copy-done.6
  52.8 21.3 %collective-permute-done.2.refs_2_ = bf16[576,2048]{1,0:T(8,128)(2,1)} collective-permute-done((bf16[576,2048]{1,0:T(8,128)(2,1)S(1)}, bf16[576,2048]{1,0:T(8,128)(2,1)}, u32[]{:S(2)}, u32[]{:S(2)}) %collective-permute-start.2) | collective-permute-done | bytes 2359328 | tf_op jit(solution)/shard_map/ppermute | solution.py:288
  74.1 7.9 %collective-permute-start.11 = (bf16[576,2048]{1,0:T(8,128)(2,1)}, bf16[576,2048]{1,0:T(8,128)(2,1)}, u32[]{:S(2)}, u32[]{:S(2)}) collective-permute-start(bf16[576,2048]{1,0:T(8,128)(2,1)} %collective-permute-done.2.refs_2_), channel_id=1, source_target_pairs={{0,1},{1,0},{2,3},{3,2},{4,5},{5,4},{6,7},{7,6},{8,9},{9,8},{10,11... | collective-permute-start | bytes 7077896 | tf_op jit(solution)/shard_map/ppermute | solution.py:288
  82.0 1.4 copy-done
  83.4 0.9 all-to-all-done.1
  84.3 2.2 %collective-permute-done.11.refs_3_ = bf16[576,2048]{1,0:T(8,128)(2,1)} collective-permute-done((bf16[576,2048]{1,0:T(8,128)(2,1)}, bf16[576,2048]{1,0:T(8,128)(2,1)}, u32[]{:S(2)}, u32[]{:S(2)}) %collective-permute-start.11) | collective-permute-done | bytes 2359328 | tf_op jit(solution)/shard_map/ppermute | solution.py:288
  86.5 1.7 copy-done.1
  88.1 7.2 %shard_map.145 = bf16[320,2048]{1,0:T(8,128)(2,1)} custom-call(bf16[448,2048]{1,0:T(8,128)(2,1)} %bitcast.20.rows, bf16[576,2048]{1,0:T(8,128)(2,1)S(1)} %pad_maximum_fusion.refs_0_, bf16[576,2048]{1,0:T(8,128)(2,1)S(1)} %copy-done.1, bf16[576,2048]{1,0:T(8,128)(2,1)} %collective-permute-done.2.refs_2_, bf16[576,2048]{1,0:T(8,128)(2,1)} %collective-permute-done.11.refs_3_), custom_call_target="tpu_custom_call" | custom-call | flops 3019898880 | bytes 9437184 | tf_op jit(solution)/shard_map/pallas_call | solution.py:156
  95.4 0.0 copy-start.10
  95.4 10.2 %all-to-all-start.2 = ((bf16[8,40,2048]{2,1,0:T(8,128)(2,1)}), bf16[8,40,2048]{2,1,0:T(8,128)(2,1)S(1)}, u32[]{:S(2)}, u32[]{:S(2)}) async-start(bf16[8,40,2048]{2,1,0:T(8,128)(2,1)} %bitcast.38), calls=%async_computation.2 | async-start | bytes 2621440 | tf_op jit(solution)/shard_map/all_to_all | solution.py:291
  105.5 0.9 slice.9
  106.4 1.0 slice.8
  107.4 0.0 copy-start.9
  107.5 0.0 copy-start.3
  107.5 1.1 copy-done.3
  108.6 1.1 copy-done.5
  109.7 1.1 copy-done.7
  110.8 0.7 copy-done.11
  111.5 2.2 %shard_map.142 = (f32[32,3200]{1,0:T(8,128)S(1)}, bf16[32,3200]{1,0:T(8,128)(2,1)S(1)}) custom-call(s32[4]{0:T(128)S(1)} %pad_add_fusion.where, bf16[64,3200]{1,0:T(8,128)(2,1)S(1)} %maximum_bitcast_fusion.rows, f32[1,3200]{1,0:T(1,128)S(1)} %copy-done.10, f32[1,3200]{1,0:T(1,128)S(1)} %copy-done.11, bf16[100,3200]{1,0:T(8,128)(2,1)S(1)} %bitcast.33, ...), custom_call_target="tpu_custom_call" | custom-call | flops 163840000 | bytes 2560000 | tf_op jit(solution)/shard_map/pallas_call | solution.py:38
  113.7 2.5 %collective-permute-start.5 = (bf16[32,3200]{1,0:T(8,128)(2,1)S(1)}, bf16[32,3200]{1,0:T(8,128)(2,1)S(1)}, u32[]{:S(2)}, u32[]{:S(2)}) collective-permute-start(bf16[32,3200]{1,0:T(8,128)(2,1)S(1)} %get-tuple-element.33), channel_id=1, source_target_pairs={{0,2},{2,0},{1,3},{3,1},{4,6},{6,4},{5,7},{7,5},{8,10},{10,8},{9,1... | collective-permute-start | bytes 614408 | tf_op jit(solution)/shard_map/ppermute | solution.py:288
  116.2 5.4 %collective-permute-done.5.came = bf16[32,3200]{1,0:T(8,128)(2,1)S(1)} collective-permute-done((bf16[32,3200]{1,0:T(8,128)(2,1)S(1)}, bf16[32,3200]{1,0:T(8,128)(2,1)S(1)}, u32[]{:S(2)}, u32[]{:S(2)}) %collective-permute-start.5) | collective-permute-done | bytes 204832 | tf_op jit(solution)/shard_map/ppermute | solution.py:288
  121.6 4.4 %collective-permute-start.6 = (f32[8,3200]{1,0:T(8,128)S(1)}, f32[8,3200]{1,0:T(8,128)S(1)}, u32[]{:S(2)}, u32[]{:S(2)}) collective-permute-start(f32[8,3200]{1,0:T(8,128)S(1)} %get-tuple-element.34), channel_id=1, source_target_pairs={{0,384},{32,416},{64,448},{96,480},{128,0},{160,32},{192,64},{224,... | collective-permute-start | bytes 307208 | tf_op jit(solution)/shard_map/ppermute | solution.py:332
  126.0 2.6 %collective-permute-start.7 = (bf16[8,3200]{1,0:T(8,128)(2,1)S(1)}, bf16[8,3200]{1,0:T(8,128)(2,1)S(1)}, u32[]{:S(2)}, u32[]{:S(2)}) collective-permute-start(bf16[8,3200]{1,0:T(8,128)(2,1)S(1)} %get-tuple-element.35), channel_id=1, source_target_pairs={{0,416},{32,448},{64,480},{96,384},{128,32},{160,64},{192,96},{224... | collective-permute-start | bytes 153608 | tf_op jit(solution)/shard_map/ppermute | solution.py:332
  128.6 4.0 %collective-permute-start.8 = (bf16[8,3200]{1,0:T(8,128)(2,1)S(1)}, bf16[8,3200]{1,0:T(8,128)(2,1)S(1)}, u32[]{:S(2)}, u32[]{:S(2)}) collective-permute-start(bf16[8,3200]{1,0:T(8,128)(2,1)S(1)} %get-tuple-element.36), channel_id=1, source_target_pairs={{0,448},{32,480},{64,384},{96,416},{128,64},{160,96},{192,0},{224,... | collective-permute-start | bytes 153608 | tf_op jit(solution)/shard_map/ppermute | solution.py:332
  132.7 4.2 %collective-permute-start.9 = (bf16[8,3200]{1,0:T(8,128)(2,1)S(1)}, bf16[8,3200]{1,0:T(8,128)(2,1)S(1)}, u32[]{:S(2)}, u32[]{:S(2)}) collective-permute-start(bf16[8,3200]{1,0:T(8,128)(2,1)S(1)} %get-tuple-element.37), channel_id=1, source_target_pairs={{0,480},{32,384},{64,416},{96,448},{128,96},{160,0},{192,32},{224,... | collective-permute-start | bytes 153608 | tf_op jit(solution)/shard_map/ppermute | solution.py:332
  136.9 1.4 collective-permute-done.8.refs_1_
  138.3 3.4 %collective-permute-done.9.refs_2_ = bf16[8,3200]{1,0:T(8,128)(2,1)S(1)} collective-permute-done((bf16[8,3200]{1,0:T(8,128)(2,1)S(1)}, bf16[8,3200]{1,0:T(8,128)(2,1)S(1)}, u32[]{:S(2)}, u32[]{:S(2)}) %collective-permute-start.9) | collective-permute-done | bytes 51232 | tf_op jit(solution)/shard_map/ppermute | solution.py:332
  141.8 0.8 shard_map.146
  142.6 1.3 shard_map.147
  143.9 3.1 %collective-permute-start.12 = (bf16[128,1024]{1,0:T(8,128)(2,1)S(1)}, bf16[128,1024]{1,0:T(8,128)(2,1)S(1)}, u32[]{:S(2)}, u32[]{:S(2)}) collective-permute-start(bf16[128,1024]{1,0:T(8,128)(2,1)S(1)} %get-tuple-element.45), channel_id=1, source_target_pairs={{0,226},{1,195},{2,160},{3,129},{32,130},{33,163},{34,192},{35,225... | collective-permute-start | bytes 786440 | tf_op jit(solution)/shard_map/ppermute | solution.py:347
  147.0 5.0 %collective-permute-start.13 = (bf16[128,1024]{1,0:T(8,128)(2,1)S(1)}, bf16[128,1024]{1,0:T(8,128)(2,1)S(1)}, u32[]{:S(2)}, u32[]{:S(2)}) collective-permute-start(bf16[128,1024]{1,0:T(8,128)(2,1)S(1)} %get-tuple-element.46), channel_id=1, source_target_pairs={{0,224},{1,193},{2,162},{3,131},{32,128},{33,161},{34,194},{35,227... | collective-permute-start | bytes 786440 | tf_op jit(solution)/shard_map/ppermute | solution.py:347
  152.0 13.7 %all_to_all.20.spread = f32[8,1,3200]{2,1,0:T(1,128)S(1)} all-to-all(f32[8,1,3200]{2,1,0:T(1,128)S(1)} %shard_map.144), channel_id=1, replica_groups=mesh['pp'=4,'yh'=4,'z'=8,'yl'=2,'core'=2] {'z'}, dimensions={0} | all-to-all | bytes 204800 | tf_op jit(solution)/shard_map/all_to_all | solution.py:291
  165.8 0.1 shard_map.148.left
  165.8 5.8 %collective-permute-start.14 = (bf16[128,1024]{1,0:T(8,128)(2,1)S(1)}, bf16[128,1024]{1,0:T(8,128)(2,1)S(1)}, u32[]{:S(2)}, u32[]{:S(2)}) collective-permute-start(bf16[128,1024]{1,0:T(8,128)(2,1)S(1)} %shard_map.148.left), channel_id=1, source_target_pairs={{0,1},{1,0},{2,3},{3,2},{4,5},{5,4},{6,7},{7,6},{8,9},{9,8},{10,11... | collective-permute-start | bytes 786440 | tf_op jit(solution)/shard_map/ppermute | solution.py:288
  171.6 1.1 collective-permute-done.14.right
  172.8 0.1 shard_map.149.own
  172.8 2.9 %collective-permute-start.15 = (bf16[128,1024]{1,0:T(8,128)(2,1)S(1)}, bf16[128,1024]{1,0:T(8,128)(2,1)S(1)}, u32[]{:S(2)}, u32[]{:S(2)}) collective-permute-start(bf16[128,1024]{1,0:T(8,128)(2,1)S(1)} %shard_map.149.own), channel_id=1, source_target_pairs={{0,2},{2,0},{1,3},{3,1},{4,6},{6,4},{5,7},{7,5},{8,10},{10,8},{9,1... | collective-permute-start | bytes 786440 | tf_op jit(solution)/shard_map/ppermute | solution.py:288
  175.8 0.6 shard_map.151
  176.4 5.8 %collective-permute-done.15.across = bf16[128,1024]{1,0:T(8,128)(2,1)S(1)} collective-permute-done((bf16[128,1024]{1,0:T(8,128)(2,1)S(1)}, bf16[128,1024]{1,0:T(8,128)(2,1)S(1)}, u32[]{:S(2)}, u32[]{:S(2)}) %collective-permute-start.15) | collective-permute-done | bytes 262176 | tf_op jit(solution)/shard_map/ppermute | solution.py:288
  182.2 1.4 shard_map.150
  (25 shorter events, 0.2 us)
Async XLA Ops:
  0.6 23.8 %collective-permute-start = (bf16[128,2048]{1,0:T(8,128)(2,1)}, bf16[128,2048]{1,0:T(8,128)(2,1)S(1)}, u32[]{:S(2)}, u32[]{:S(2)}) collective-permute-start(bf16[128,2048]{1,0:T(8,128)(2,1)} %bitcast.45), channel_id=1, source_target_pairs={{98,0},{67,1},{32,2},{1,3},{2,32},{35,33},{64,34},{97,35},{34,64},... | collective-permute-start | bytes 1572872 | tf_op jit(solution)/shard_map/ppermute | solution.py:284
  6.0 13.1 %collective-permute-start.1 = (f32[16,128]{1,0:T(8,128)S(1)}, f32[16,128]{1,0:T(8,128)S(1)}, u32[]{:S(2)}, u32[]{:S(2)}) collective-permute-start(f32[16,128]{1,0:T(8,128)S(1)} %pad_maximum_fusion.1), channel_id=1, source_target_pairs={{98,0},{67,1},{32,2},{1,3},{2,32},{35,33},{64,34},{97,35},{34,64},... | collective-permute-start | bytes 24584 | tf_op jit(solution)/shard_map/ppermute | solution.py:284
  12.5 0.7 copy-start.12
  13.9 10.6 %all-to-all-start = ((f32[8,1,3200]{2,1,0:T(1,128)}), f32[8,1,3200]{2,1,0:T(1,128)S(1)}, u32[]{:S(2)}, u32[]{:S(2)}) async-start(f32[8,1,3200]{2,1,0:T(1,128)} %shard_map.140), calls=%async_computation | async-start | bytes 204800 | tf_op jit(solution)/shard_map/all_to_all | solution.py:291
  17.2 9.9 %copy-start.14 = (s32[16]{0:T(128)S(1)}, s32[16]{0:T(128)}, u32[]{:S(2)}) copy-start(s32[16]{0:T(128)} %constant.27.clone) | copy-start | bytes 196
  17.2 11.3 %copy-start.13 = (f32[1,2048]{1,0:T(1,128)S(1)}, f32[1,2048]{1,0:T(1,128)}, u32[]{:S(2)}) copy-start(f32[1,2048]{1,0:T(1,128)} %gain.2) | copy-start | bytes 24580
  19.1 9.4 %copy-start.8 = (f32[16,128]{1,0:T(8,128)}, f32[16,128]{1,0:T(8,128)S(1)}, u32[]{:S(2)}) copy-start(f32[16,128]{1,0:T(8,128)S(1)} %collective-permute-done.1.meta) | copy-start | bytes 24580
  24.4 49.7 %collective-permute-start.2 = (bf16[576,2048]{1,0:T(8,128)(2,1)S(1)}, bf16[576,2048]{1,0:T(8,128)(2,1)}, u32[]{:S(2)}, u32[]{:S(2)}) collective-permute-start(bf16[576,2048]{1,0:T(8,128)(2,1)S(1)} %pad_maximum_fusion.refs_0_), channel_id=1, source_target_pairs={{0,2},{2,0},{1,3},{3,1},{4,6},{6,4},{5,7},{7,5},{8,10},{10,8},{9,1... | collective-permute-start | bytes 7077896 | tf_op jit(solution)/shard_map/ppermute | solution.py:288
  31.1 10.1 %copy-start.2 = (bf16[1,3200,100]{1,2,0:T(8,128)(2,1)S(1)}, bf16[1,3200,100]{1,2,0:T(8,128)(2,1)}, u32[]{:S(2)}) copy-start(bf16[1,3200,100]{1,2,0:T(8,128)(2,1)} %param.22) | copy-start | bytes 1920004
  31.1 53.2 %all-to-all-start.1 = ((bf16[8,56,2048]{2,1,0:T(8,128)(2,1)}), bf16[8,56,2048]{2,1,0:T(8,128)(2,1)}, u32[]{:S(2)}, u32[]{:S(2)}) async-start(bf16[8,56,2048]{2,1,0:T(8,128)(2,1)} %bitcast.37), calls=%async_computation.1 | async-start | bytes 3670016 | tf_op jit(solution)/shard_map/all_to_all | solution.py:291
  41.2 9.9 %collective-permute-start.3 = (bf16[100,3200]{1,0:T(8,128)(2,1)S(1)}, bf16[100,3200]{1,0:T(8,128)(2,1)S(1)}, u32[]{:S(2)}, u32[]{:S(2)}) collective-permute-start(bf16[100,3200]{1,0:T(8,128)(2,1)S(1)} %bitcast.32), channel_id=1, source_target_pairs={{0,1},{1,0},{2,3},{3,2},{4,5},{5,4},{6,7},{7,6},{8,9},{9,8},{10,11... | collective-permute-start | bytes 1920008 | tf_op jit(solution)/shard_map/ppermute | solution.py:288
  46.7 5.2 %collective-permute-start.4 = (bf16[100,3200]{1,0:T(8,128)(2,1)}, bf16[100,3200]{1,0:T(8,128)(2,1)S(1)}, u32[]{:S(2)}, u32[]{:S(2)}) collective-permute-start(bf16[100,3200]{1,0:T(8,128)(2,1)} %bitcast.34), channel_id=1, source_target_pairs={{0,1},{1,0},{2,3},{3,2},{4,5},{5,4},{6,7},{7,6},{8,9},{9,8},{10,11... | collective-permute-start | bytes 1920008 | tf_op jit(solution)/shard_map/ppermute | solution.py:288
  48.6 33.3 %collective-permute-start.10 = (bf16[576,2048]{1,0:T(8,128)(2,1)S(1)}, bf16[576,2048]{1,0:T(8,128)(2,1)S(1)}, u32[]{:S(2)}, u32[]{:S(2)}) collective-permute-start(bf16[576,2048]{1,0:T(8,128)(2,1)S(1)} %pad_maximum_fusion.refs_0_), channel_id=1, source_target_pairs={{0,1},{1,0},{2,3},{3,2},{4,5},{5,4},{6,7},{7,6},{8,9},{9,8},{10,11... | collective-permute-start | bytes 7077896 | tf_op jit(solution)/shard_map/ppermute | solution.py:288
  51.1 0.8 copy-start.4
  51.9 0.9 copy-start.6
  74.1 12.4 %collective-permute-start.11 = (bf16[576,2048]{1,0:T(8,128)(2,1)}, bf16[576,2048]{1,0:T(8,128)(2,1)}, u32[]{:S(2)}, u32[]{:S(2)}) collective-permute-start(bf16[576,2048]{1,0:T(8,128)(2,1)} %collective-permute-done.2.refs_2_), channel_id=1, source_target_pairs={{0,1},{1,0},{2,3},{3,2},{4,5},{5,4},{6,7},{7,6},{8,9},{9,8},{10,11... | collective-permute-start | bytes 7077896 | tf_op jit(solution)/shard_map/ppermute | solution.py:288
  82.0 1.4 copy-start
  86.5 1.7 copy-start.1
  95.4 12.1 %copy-start.10 = (f32[1,3200]{1,0:T(1,128)S(1)}, f32[1,3200]{1,0:T(1,128)}, u32[]{:S(2)}) copy-start(f32[1,3200]{1,0:T(1,128)} %gain.3) | copy-start | bytes 38404
  95.4 47.2 %all-to-all-start.2 = ((bf16[8,40,2048]{2,1,0:T(8,128)(2,1)}), bf16[8,40,2048]{2,1,0:T(8,128)(2,1)S(1)}, u32[]{:S(2)}, u32[]{:S(2)}) async-start(bf16[8,40,2048]{2,1,0:T(8,128)(2,1)} %bitcast.38), calls=%async_computation.2 | async-start | bytes 2621440 | tf_op jit(solution)/shard_map/all_to_all | solution.py:291
  107.4 34.3 %copy-start.9 = (f32[16,128]{1,0:T(8,128)S(1)}, f32[16,128]{1,0:T(8,128)}, u32[]{:S(2)}) copy-start(f32[16,128]{1,0:T(8,128)} %copy-done.8) | copy-start | bytes 24580
  107.5 1.1 copy-start.3
  108.6 1.1 copy-start.5
  109.7 1.1 copy-start.7
  110.8 0.7 copy-start.11
  113.7 7.8 %collective-permute-start.5 = (bf16[32,3200]{1,0:T(8,128)(2,1)S(1)}, bf16[32,3200]{1,0:T(8,128)(2,1)S(1)}, u32[]{:S(2)}, u32[]{:S(2)}) collective-permute-start(bf16[32,3200]{1,0:T(8,128)(2,1)S(1)} %get-tuple-element.33), channel_id=1, source_target_pairs={{0,2},{2,0},{1,3},{3,1},{4,6},{6,4},{5,7},{7,5},{8,10},{10,8},{9,1... | collective-permute-start | bytes 614408 | tf_op jit(solution)/shard_map/ppermute | solution.py:288
  121.6 20.1 %collective-permute-start.6 = (f32[8,3200]{1,0:T(8,128)S(1)}, f32[8,3200]{1,0:T(8,128)S(1)}, u32[]{:S(2)}, u32[]{:S(2)}) collective-permute-start(f32[8,3200]{1,0:T(8,128)S(1)} %get-tuple-element.34), channel_id=1, source_target_pairs={{0,384},{32,416},{64,448},{96,480},{128,0},{160,32},{192,64},{224,... | collective-permute-start | bytes 307208 | tf_op jit(solution)/shard_map/ppermute | solution.py:332
  126.0 10.8 %collective-permute-start.7 = (bf16[8,3200]{1,0:T(8,128)(2,1)S(1)}, bf16[8,3200]{1,0:T(8,128)(2,1)S(1)}, u32[]{:S(2)}, u32[]{:S(2)}) collective-permute-start(bf16[8,3200]{1,0:T(8,128)(2,1)S(1)} %get-tuple-element.35), channel_id=1, source_target_pairs={{0,416},{32,448},{64,480},{96,384},{128,32},{160,64},{192,96},{224... | collective-permute-start | bytes 153608 | tf_op jit(solution)/shard_map/ppermute | solution.py:332
  128.6 9.7 %collective-permute-start.8 = (bf16[8,3200]{1,0:T(8,128)(2,1)S(1)}, bf16[8,3200]{1,0:T(8,128)(2,1)S(1)}, u32[]{:S(2)}, u32[]{:S(2)}) collective-permute-start(bf16[8,3200]{1,0:T(8,128)(2,1)S(1)} %get-tuple-element.36), channel_id=1, source_target_pairs={{0,448},{32,480},{64,384},{96,416},{128,64},{160,96},{192,0},{224,... | collective-permute-start | bytes 153608 | tf_op jit(solution)/shard_map/ppermute | solution.py:332
  132.7 9.1 %collective-permute-start.9 = (bf16[8,3200]{1,0:T(8,128)(2,1)S(1)}, bf16[8,3200]{1,0:T(8,128)(2,1)S(1)}, u32[]{:S(2)}, u32[]{:S(2)}) collective-permute-start(bf16[8,3200]{1,0:T(8,128)(2,1)S(1)} %get-tuple-element.37), channel_id=1, source_target_pairs={{0,480},{32,384},{64,416},{96,448},{128,96},{160,0},{192,32},{224,... | collective-permute-start | bytes 153608 | tf_op jit(solution)/shard_map/ppermute | solution.py:332
  143.9 21.9 %collective-permute-start.12 = (bf16[128,1024]{1,0:T(8,128)(2,1)S(1)}, bf16[128,1024]{1,0:T(8,128)(2,1)S(1)}, u32[]{:S(2)}, u32[]{:S(2)}) collective-permute-start(bf16[128,1024]{1,0:T(8,128)(2,1)S(1)} %get-tuple-element.45), channel_id=1, source_target_pairs={{0,226},{1,195},{2,160},{3,129},{32,130},{33,163},{34,192},{35,225... | collective-permute-start | bytes 786440 | tf_op jit(solution)/shard_map/ppermute | solution.py:347
  147.0 18.7 %collective-permute-start.13 = (bf16[128,1024]{1,0:T(8,128)(2,1)S(1)}, bf16[128,1024]{1,0:T(8,128)(2,1)S(1)}, u32[]{:S(2)}, u32[]{:S(2)}) collective-permute-start(bf16[128,1024]{1,0:T(8,128)(2,1)S(1)} %get-tuple-element.46), channel_id=1, source_target_pairs={{0,224},{1,193},{2,162},{3,131},{32,128},{33,161},{34,194},{35,227... | collective-permute-start | bytes 786440 | tf_op jit(solution)/shard_map/ppermute | solution.py:347
  165.8 6.9 %collective-permute-start.14 = (bf16[128,1024]{1,0:T(8,128)(2,1)S(1)}, bf16[128,1024]{1,0:T(8,128)(2,1)S(1)}, u32[]{:S(2)}, u32[]{:S(2)}) collective-permute-start(bf16[128,1024]{1,0:T(8,128)(2,1)S(1)} %shard_map.148.left), channel_id=1, source_target_pairs={{0,1},{1,0},{2,3},{3,2},{4,5},{5,4},{6,7},{7,6},{8,9},{9,8},{10,11... | collective-permute-start | bytes 786440 | tf_op jit(solution)/shard_map/ppermute | solution.py:288
  172.8 9.4 %collective-permute-start.15 = (bf16[128,1024]{1,0:T(8,128)(2,1)S(1)}, bf16[128,1024]{1,0:T(8,128)(2,1)S(1)}, u32[]{:S(2)}, u32[]{:S(2)}) collective-permute-start(bf16[128,1024]{1,0:T(8,128)(2,1)S(1)} %shard_map.149.own), channel_id=1, source_target_pairs={{0,2},{2,0},{1,3},{3,1},{4,6},{6,4},{5,7},{7,5},{8,10},{10,8},{9,1... | collective-permute-start | bytes 786440 | tf_op jit(solution)/shard_map/ppermute | solution.py:288

commit v8 on v7

--- a/solution.py
+++ b/solution.py
@@ -17,17 +17,11 @@
 
 
 def served(n):
-    table = {}
+    blocks = {}
     for a in range(n):
         for t, c in enumerate((a - 1, a + 2 if a % 2 == 0 else a, a + 1, a if a % 2 == 0 else a + 2)):
-            c %= n
-            apart = (a - c) % n
-            if apart % 2 == 1:
-                copy = 2 if apart == 1 else 0
-            else:
-                copy = 3 if (apart == 2) == (c % 2 == 0) else 1
-            table[a, t] = (c, copy)
-    return table
+            blocks[a, t] = (c % n, t ^ 2)
+    return blocks
 SMALL = 12 * 1024 * 1024
 LARGE = 24 * 1024 * 1024
 
@@ -45,6 +39,10 @@
         )(*operands)
 
     return run
+
+
+def in_hbm(value):
+    return pltpu.with_memory_space_constraint(value, pltpu.HBM)
 
 
 def shaped(dims, kind=BF16):
@@ -69,8 +67,8 @@
         weight = jnp.where(same, meta[topk + k : topk + k + 1, :] / total, weight)
     earlier = lax.broadcasted_iota(jnp.int32, (toks, toks), 0) < lax.broadcasted_iota(jnp.int32, (toks, toks), 1)
     rank = jnp.dot(member.astype(BF16), earlier.astype(F32).astype(BF16), preferred_element_type=F32)
-    rank = jnp.where(member > 0.5, rank, -1.0)
-    slot = lax.broadcasted_iota(jnp.int32, (group, slots, toks), 1).astype(F32)
+    rank = jnp.where(member > 0.5, rank, -100.0)
+    slot = (lax.broadcasted_iota(jnp.int32, (group, slots, toks), 1) - (slots - CAP)).astype(F32)
     return jnp.where(rank[:, None, :] == slot, 1.0, 0.0), weight
 
 
@@ -85,7 +83,7 @@
     count, dv = images.shape
     spare = jnp.zeros((count, 2 * width - dv), F32)
     empty = jnp.zeros((CAP, width), F32)
-    added = jnp.concatenate([empty, images[:, :width], jnp.concatenate([images[:, width:], spare], axis=1)], axis=0)
+    added = jnp.concatenate([images[:, :width], jnp.concatenate([images[:, width:], spare], axis=1), empty], axis=0)
     made = jnp.dot(hit.reshape(n, hit.shape[2]).astype(BF16), normed, preferred_element_type=F32)
     rows[...] = (made + jnp.concatenate([added] * group, axis=0)).astype(BF16)
 
@@ -98,6 +96,9 @@
     top = scaled.astype(BF16)
     high[...] = top
     low[...] = (scaled - top.astype(F32)).astype(BF16)
+
+
+ANYWHERE = pl.BlockSpec(memory_space=pl.ANY)
 
 
 def expert_kernel(rows, *refs):
@@ -129,8 +130,8 @@
             copies[3 * seen + 1].wait()
             seen += 1
         block = slice(c * step, (c + 1) * step)
-        gate = nt(flat, gate_v[block, :]).reshape(-1, ROWS, step)[:, :CAP].reshape(-1, step)
-        upval = nt(flat, up_v[block, :]).reshape(-1, ROWS, step)[:, :CAP].reshape(-1, step)
+        gate = nt(flat, gate_v[block, :]).reshape(-1, ROWS, step)[:, ROWS - CAP :].reshape(-1, step)
+        upval = nt(flat, up_v[block, :]).reshape(-1, ROWS, step)[:, ROWS - CAP :].reshape(-1, step)
         hidden_v[:, block] = (gate * jax.nn.sigmoid(gate) * upval).astype(BF16)
     for s in range(4):
         copies[3 * s + 2].wait()
@@ -152,12 +153,11 @@
     given, width = rows.shape
     n = given // ROWS * CAP
     count = shards[0].shape[0] // 3 * 4
-    anywhere = pl.BlockSpec(memory_space=pl.ANY)
     return pl.pallas_call(
         expert_kernel,
         out_shape=pltpu.HBM((n, width), BF16),
-        in_specs=[anywhere] * 5,
-        out_specs=anywhere,
+        in_specs=[ANYWHERE] * 5,
+        out_specs=ANYWHERE,
         scratch_shapes=[
             pltpu.VMEM((given, width), BF16),
             pltpu.VMEM((count, width), BF16),
@@ -171,12 +171,12 @@
         ],
         compiler_params=pltpu.CompilerParams(vmem_limit_bytes=LARGE),
         cost_estimate=pl.CostEstimate(flops=6 * n * width * count, bytes_accessed=6 * count * width, transcendentals=0),
-    )(rows, *shards)
+    )(in_hbm(rows), *[in_hbm(shard) for shard in shards])
 
 
 def combine_kernel(where, toks, high, low, made, kept, given):
     half = made.shape[1] // 2
-    low_side, core = where[2] // 2, lax.rem(where[2], 2)
+    low_side, core = 1 - where[1] // 2, lax.rem(where[1], 2)
     for out, h in ((kept, low_side), (given, 1 - low_side)):
         block = pl.ds(pl.multiple_of(h * half, half), half)
         part = made[:, block]
@@ -204,10 +204,28 @@
         out[i] = wide
 
 
-def image_kernel(sizes, where, rows, gain, weigh, first, first_other, second, second_other, mine, theirs):
+def image_kernel(sizes, where, arrived, gain, weigh, first, first_other, second, second_other, mine, theirs, *scratch):
     n_yh, n_z = sizes
-    n = rows.shape[0]
-    wide = rows[...].astype(F32)
+    rows_v, first_v, first_other_v, second_v, second_other_v, sem = scratch
+    count = 2 * n_yh
+    copies = [
+        pltpu.make_async_copy(arrived.at[i, pl.ds(0, 2 * count)], rows_v.at[i], sem.at[i]) for i in range(n_z)
+    ]
+    held = ((first, first_v), (first_other, first_other_v), (second, second_v), (second_other, second_other_v))
+    for i, (source, target) in enumerate(held):
+        copies.append(pltpu.make_async_copy(source, target, sem.at[n_z + i]))
+    for copy in copies:
+        copy.start()
+    for copy in copies:
+        copy.wait()
+    dv = gain.shape[1]
+    wide = rows_v[...].astype(F32)
+    width = wide.shape[2]
+    n = n_z * count
+    wide = jnp.concatenate(
+        [wide[:, :count].reshape(n, width), wide[:, count:, : dv - width].reshape(n, dv - width)], axis=1
+    )
+    rows = wide.astype(BF16)
     scale = lax.rsqrt(jnp.mean(wide * wide, axis=-1, keepdims=True) + 1e-06)
     normed = (wide * scale * gain[...]).astype(BF16)
     yh, yl = where[0], where[1] // 2
@@ -218,18 +236,35 @@
     source = (z * n_yh + high) * 2 + low
     order = jnp.where(lax.broadcasted_iota(jnp.int32, (n, n), 1) == source, 1.0, 0.0).astype(BF16)
     whole = None
-    for w_in, w_out in ((first, second), (first_other, second_other)):
+    for w_in, w_out in ((first_v, second_v), (first_other_v, second_other_v)):
         made = nt(normed, w_in[...])
         hidden = (0.5 * made * (1.0 + lax.erf(made * np.float32(0.5**0.5)))).astype(BF16)
         turned = jnp.dot(order, hidden, preferred_element_type=F32).astype(BF16)
         part = jnp.dot(turned, w_out[...], preferred_element_type=F32)
         whole = part if whole is None else whole + part
     whole = whole * weigh[...]
-    images = jnp.dot(order, rows[...], preferred_element_type=F32)
-    mark = lax.broadcasted_iota(jnp.int32, (n, 1), 0) == where[3]
+    images = jnp.dot(order, rows, preferred_element_type=F32)
+    mark = lax.broadcasted_iota(jnp.int32, (n, 1), 0) == where[2]
     whole = whole + jnp.where(mark, images, 0.0)
     mine[...] = whole[: n // 2]
     theirs[...] = whole[n // 2 :].astype(BF16)
+
+
+def encoder_part(where, arrived, gain, weigh, weights, n_yh):
+    n_z, _, width = arrived.shape
+    hidden, dv = weights[0].shape
+    half = n_z * n_yh
+    return pl.pallas_call(
+        functools.partial(image_kernel, (n_yh, n_z)),
+        out_shape=(shaped((half, dv), F32), shaped((half, dv))),
+        in_specs=[SM, ANYWHERE, VM, VM] + [ANYWHERE] * 4,
+        out_specs=(VM, VM),
+        scratch_shapes=[pltpu.VMEM((n_z, 4 * n_yh, width), BF16)]
+        + [pltpu.VMEM((hidden, dv), BF16)] * 4
+        + [pltpu.SemaphoreType.DMA((n_z + 4,))],
+        compiler_params=pltpu.CompilerParams(vmem_limit_bytes=SMALL),
+        cost_estimate=pl.CostEstimate(flops=16 * half * dv * hidden, bytes_accessed=8 * hidden * dv, transcendentals=0),
+    )(where, in_hbm(arrived), gain, weigh, *[in_hbm(w) for w in weights])
 
 
 def fold_kernel(held, came, keep, *sends):
@@ -275,9 +310,7 @@
     n_square = n_yh * n_tp
     square = ("yh", "yl", "core")
     serve = served(n_yh)
-    copies = np.array([serve[a, t][1] for a in range(n_yh) for t in range(n_tp)], np.int32)
-    yh, t = lax.axis_index("yh"), lax.axis_index(("yl", "core"))
-    where = jnp.stack([yh, t, jnp.asarray(copies)[yh * n_tp + t], lax.axis_index("z")]).astype(jnp.int32)
+    where = jnp.stack([lax.axis_index("yh"), lax.axis_index(("yl", "core")), lax.axis_index("z")]).astype(jnp.int32)
 
     def fetched(value):
         pairs = [(c * n_tp + copy, a * n_tp + t) for (a, t), (c, copy) in serve.items()]
@@ -298,7 +331,7 @@
     image = image_in[0]
     dv = image.shape[1]
     ring = exchanged(call(spread_kernel, shaped((n_yh * 2, 1, dv), F32))(image), ("yh", "yl"))
-    own, sent, meta, ring = lax.optimization_barrier((own, sent, meta, ring))
+    own, sent, meta, ring, where = lax.optimization_barrier((own, sent, meta, ring, where))
     across = shifted(own, "yl", 1)
     other = shifted(own, "core", 1)
     first, second = fc_in[0].T, fc_out[0]
@@ -315,16 +348,7 @@
     returned = exchanged(made.reshape(n_z, CAP, width), "z").reshape(n_rows, width)
     high, low = call(weigh_kernel, (shaped((toks, n_rows)), shaped((toks, n_rows))), scalars=1)(where, meta)
 
-    images = [arrived[:, CAP : CAP + 8, :], arrived[:, CAP + 8 : CAP + 16, : dv - width]]
-    images = jnp.concatenate(images, axis=2).reshape(-1, dv)
-    n_image = images.shape[0]
-    mine, theirs = call(
-        functools.partial(image_kernel, (n_yh, n_z)),
-        (shaped((n_image // 2, dv), F32), shaped((n_image // 2, dv))),
-        scalars=1,
-        flops=8 * n_image * dv * 100,
-        moved=8 * 100 * dv,
-    )(where, images, image_gain, layer_scale, first, first_other, second, second_other)
+    mine, theirs = encoder_part(where, arrived, image_gain, layer_scale, (first, first_other, second, second_other), n_yh)
     mine, *theirs = call(
         fold_kernel, (shaped((n_z, dv), F32),) + tuple(shaped((n_z, dv)) for _ in range(n_yh - 1))
     )(mine, shifted(theirs, "yl", 1))

time: 186 us -> 182 us (0.978)
  local copies, waits for them, and re-layouts: 12.1 us -> 0.74 us
  waiting for transfers between devices: 47 us -> 53 us
  Pallas kernels: 17 us -> 21.8 us
  blocking collectives: 13.7 us -> 10 us
  starting transfers between devices: 89 us -> 90.9 us
    unnamed x30 -> x14, local copies, waits for them, and re-layouts: 9.5 us -> 0.74 us
    ppermute x8, waiting for transfers between devices: 35.9 us -> 40.5 us  [shifted(): return lax.ppermute(value, axis, [(i, (i + by) % n) for i in range(n)])]
    pallas_call x0 -> x1, Pallas kernels: none -> 4.31 us  [encoder_part(): pl.pallas_call(functools.partial(image_kernel, (n_yh, n_z)), out_shape=(s...]
    all_to_all x1, blocking collectives: 13.7 us -> 10 us  [exchanged(): return lax.all_to_all(value, axis, split_axis=0, concat_axis=0, tiled=True)]
    pallas_call x1, Pallas kernels: 7.22 us -> 9.79 us  [experts(): pl.pallas_call(expert_kernel, out_shape=pltpu.HBM((n, width), BF16), in_s...]
    ppermute x2, starting transfers between devices: 8.14 us -> 10.4 us  [body(): lax.ppermute(piece, ('pp',) + square, [(s * n_square + a * n_tp + t, (s +...]
    pallas_call x11 -> x10, Pallas kernels: 9.79 us -> 7.66 us  [run(): pl.pallas_call(kernel, out_shape=outs, in_specs=specs, out_specs=jax.tree...]
    slice x2 -> x0, local copies, waits for them, and re-layouts: 1.89 us -> none  [the longest x1 0.97 us: body(): arrived[:, CAP:CAP + 8, :]]
  transfers between devices with their start and end apart: 19 -> 19, of which waited for: 10 -> 10; matrix products, arithmetic and copies ran while one was open for 4% -> 2% of each run, Pallas kernels for 4% -> 5%
where the time goes in v8:
time: 182 us; the launch traced here: 181 us
  starting transfers between devices  90.9 us (50%)
  waiting for transfers between devices  53 us (29%)
  Pallas kernels  21.8 us (12%)
  blocking collectives  10 us (5%)
  other arithmetic  3.33 us (2%)
    ppermute x8, waiting for transfers between devices, shifted(): return lax.ppermute(value, axis, [(i, (i + by) % n) for i in range(n)])  40.5 us
    ppermute x8, starting transfers between devices, shifted(): return lax.ppermute(value, axis, [(i, (i + by) % n) for i in range(n)])  31.4 us
    all_to_all x3, starting transfers between devices, exchanged(): return lax.all_to_all(value, axis, split_axis=0, concat_axis=0, tiled=True)  23.4 us
    ppermute x4, starting transfers between devices, body(): lax.ppermute(part, ('pp', 'yh'), [(s * n_yh + h, (s - 1) % n_pp * n_yh +...  15.2 us
    ppermute x2, starting transfers between devices, fetched(): return lax.ppermute(value, square, pairs)  10.5 us
    ppermute x2, starting transfers between devices, body(): lax.ppermute(piece, ('pp',) + square, [(s * n_square + a * n_tp + t, (s +...  10.4 us
    all_to_all x1, blocking collectives, exchanged(): return lax.all_to_all(value, axis, split_axis=0, concat_axis=0, tiled=True)  10 us
    pallas_call x1, Pallas kernels, experts(): pl.pallas_call(expert_kernel, out_shape=pltpu.HBM((n, width), BF16), in_s...  9.79 us
  transfers between devices with their start and end apart: 19, of which 10 were waited for; matrix products, arithmetic and copies ran while one was open for 2% of the time, Pallas kernels for 5%

profile of v8, /device:TPU:1, one launch (start us, length us, event | category | flops | bytes accessed | tf_op | source)
XLA Modules:
  0.0 180.7 jit_solution(5114407785707495916)
XLA Ops:
  0.6 4.0 %collective-permute-start = (bf16[128,2048]{1,0:T(8,128)(2,1)}, bf16[128,2048]{1,0:T(8,128)(2,1)S(1)}, u32[]{:S(2)}, u32[]{:S(2)}) collective-permute-start(bf16[128,2048]{1,0:T(8,128)(2,1)} %bitcast.43), channel_id=1, source_target_pairs={{98,0},{67,1},{32,2},{1,3},{2,32},{35,33},{64,34},{97,35},{34,64},... | collective-permute-start | bytes 1572872 | tf_op jit(solution)/shard_map/ppermute | solution.py:317
  4.7 0.7 convert_bitcast_fusion
  5.4 0.7 pad_maximum_fusion.1
  6.0 6.4 %collective-permute-start.1 = (f32[16,128]{1,0:T(8,128)S(1)}, f32[16,128]{1,0:T(8,128)S(1)}, u32[]{:S(2)}, u32[]{:S(2)}) collective-permute-start(f32[16,128]{1,0:T(8,128)S(1)} %pad_maximum_fusion.1), channel_id=1, source_target_pairs={{98,0},{67,1},{32,2},{1,3},{2,32},{35,33},{64,34},{97,35},{34,64},... | collective-permute-start | bytes 24584 | tf_op jit(solution)/shard_map/ppermute | solution.py:317
  12.5 0.0 copy-start.2
  12.5 0.7 copy-done.2
  13.2 0.7 shard_map.131
  13.9 3.4 %all-to-all-start = ((f32[8,1,3200]{2,1,0:T(1,128)}), f32[8,1,3200]{2,1,0:T(1,128)S(1)}, u32[]{:S(2)}, u32[]{:S(2)}) async-start(f32[8,1,3200]{2,1,0:T(1,128)} %shard_map.131), calls=%async_computation | async-start | bytes 204800 | tf_op jit(solution)/shard_map/all_to_all | solution.py:324
  17.2 0.0 copy-start.3
  17.2 1.9 %pad_maximum_fusion.refs_0_ = bf16[576,2048]{1,0:T(8,128)(2,1)S(1)} fusion(bf16[192,2048]{1,0:T(8,128)(2,1)} %bitcast.33, bf16[192,2048]{1,0:T(8,128)(2,1)} %bitcast.34, bf16[192,2048]{1,0:T(8,128)(2,1)} %bitcast.35), kind=kLoop, calls=%fused_computation | loop fusion | flops 7077888 | bytes 4718592 | tf_op jit(solution)/shard_map/concatenate | solution.py:330
  19.1 0.0 copy-start.4
  19.1 0.1 pad_add_fusion.where
  19.2 0.0 collective-permute-done.1.meta
  19.2 5.2 %all-to-all-done.ring = f32[8,1,3200]{2,1,0:T(1,128)S(1)} async-done(((f32[8,1,3200]{2,1,0:T(1,128)}), f32[8,1,3200]{2,1,0:T(1,128)S(1)}, u32[]{:S(2)}, u32[]{:S(2)}) %all-to-all-start) | async-done | bytes 102432 | tf_op jit(solution)/shard_map/all_to_all | solution.py:324
  24.4 0.0 collective-permute-done.toks
  24.4 2.6 %collective-permute-start.2 = (bf16[576,2048]{1,0:T(8,128)(2,1)S(1)}, bf16[576,2048]{1,0:T(8,128)(2,1)}, u32[]{:S(2)}, u32[]{:S(2)}) collective-permute-start(bf16[576,2048]{1,0:T(8,128)(2,1)S(1)} %pad_maximum_fusion.refs_0_), channel_id=1, source_target_pairs={{0,2},{2,0},{1,3},{3,1},{4,6},{6,4},{5,7},{7,5},{8,10},{10,8},{9,1... | collective-permute-start | bytes 7077896 | tf_op jit(solution)/shard_map/ppermute | solution.py:321
  27.1 0.0 copy-done.3
  27.1 2.7 %shard_map.132 = bf16[448,2048]{1,0:T(8,128)(2,1)} custom-call(s32[3]{0:T(128)S(1)} %pad_add_fusion.where, f32[16,128]{1,0:T(8,128)S(1)} %collective-permute-done.1.meta, bf16[128,2048]{1,0:T(8,128)(2,1)S(1)} %collective-permute-done.toks, f32[1,2048]{1,0:T(1,128)S(1)} %copy-done.3, f32[8,1,3200]{2,1,0:T(1,128)S(1)} %all-to-all-done.ring), custom_call_target="tpu_custom_call" | custom-call | tf_op jit(solution)/shard_map/pallas_call | solution.py:32
  29.8 9.9 %all-to-all-start.1 = ((bf16[8,56,2048]{2,1,0:T(8,128)(2,1)}), bf16[8,56,2048]{2,1,0:T(8,128)(2,1)}, u32[]{:S(2)}, u32[]{:S(2)}) async-start(bf16[8,56,2048]{2,1,0:T(8,128)(2,1)} %bitcast.31), calls=%async_computation.1 | async-start | bytes 3670016 | tf_op jit(solution)/shard_map/all_to_all | solution.py:324
  39.7 5.5 %collective-permute-start.3 = (bf16[100,3200]{1,0:T(8,128)(2,1)}, bf16[100,3200]{1,0:T(8,128)(2,1)S(1)}, u32[]{:S(2)}, u32[]{:S(2)}) collective-permute-start(bf16[100,3200]{1,0:T(8,128)(2,1)} %bitcast.36), channel_id=1, source_target_pairs={{0,1},{1,0},{2,3},{3,2},{4,5},{5,4},{6,7},{7,6},{8,9},{9,8},{10,11... | collective-permute-start | bytes 1920008 | tf_op jit(solution)/shard_map/ppermute | solution.py:321
  45.2 1.9 %collective-permute-start.4 = (bf16[100,3200]{1,0:T(8,128)(2,1)}, bf16[100,3200]{1,0:T(8,128)(2,1)S(1)}, u32[]{:S(2)}, u32[]{:S(2)}) collective-permute-start(bf16[100,3200]{1,0:T(8,128)(2,1)} %bitcast.38), channel_id=1, source_target_pairs={{0,1},{1,0},{2,3},{3,2},{4,5},{5,4},{6,7},{7,6},{8,9},{9,8},{10,11... | collective-permute-start | bytes 1920008 | tf_op jit(solution)/shard_map/ppermute | solution.py:321
  47.2 0.0 copy-done.4
  47.2 2.4 %collective-permute-start.10 = (bf16[576,2048]{1,0:T(8,128)(2,1)S(1)}, bf16[576,2048]{1,0:T(8,128)(2,1)}, u32[]{:S(2)}, u32[]{:S(2)}) collective-permute-start(bf16[576,2048]{1,0:T(8,128)(2,1)S(1)} %pad_maximum_fusion.refs_0_), channel_id=1, source_target_pairs={{0,1},{1,0},{2,3},{3,2},{4,5},{5,4},{6,7},{7,6},{8,9},{9,8},{10,11... | collective-permute-start | bytes 7077896 | tf_op jit(solution)/shard_map/ppermute | solution.py:321
  49.6 0.0 collective-permute-done.3.first_other
  49.6 0.0 copy-start.5
  49.6 0.0 collective-permute-done.4.second_other
  49.6 0.0 copy-start.6
  49.6 24.5 %collective-permute-done.2.refs_2_ = bf16[576,2048]{1,0:T(8,128)(2,1)} collective-permute-done((bf16[576,2048]{1,0:T(8,128)(2,1)S(1)}, bf16[576,2048]{1,0:T(8,128)(2,1)}, u32[]{:S(2)}, u32[]{:S(2)}) %collective-permute-start.2) | collective-permute-done | bytes 2359328 | tf_op jit(solution)/shard_map/ppermute | solution.py:321
  74.1 0.0 copy-done.5
  74.1 7.9 %collective-permute-start.11 = (bf16[576,2048]{1,0:T(8,128)(2,1)}, bf16[576,2048]{1,0:T(8,128)(2,1)}, u32[]{:S(2)}, u32[]{:S(2)}) collective-permute-start(bf16[576,2048]{1,0:T(8,128)(2,1)} %collective-permute-done.2.refs_2_), channel_id=1, source_target_pairs={{0,1},{1,0},{2,3},{3,2},{4,5},{5,4},{6,7},{7,6},{8,9},{9,8},{10,11... | collective-permute-start | bytes 7077896 | tf_op jit(solution)/shard_map/ppermute | solution.py:321
  82.0 0.0 collective-permute-done.10.refs_1_
  82.0 0.8 all-to-all-done.1.arrived
  82.8 3.6 %collective-permute-done.11.refs_3_ = bf16[576,2048]{1,0:T(8,128)(2,1)} collective-permute-done((bf16[576,2048]{1,0:T(8,128)(2,1)}, bf16[576,2048]{1,0:T(8,128)(2,1)}, u32[]{:S(2)}, u32[]{:S(2)}) %collective-permute-start.11) | collective-permute-done | bytes 2359328 | tf_op jit(solution)/shard_map/ppermute | solution.py:321
  86.5 9.8 %shard_map.136 = bf16[320,2048]{1,0:T(8,128)(2,1)} custom-call(bf16[448,2048]{1,0:T(8,128)(2,1)} %bitcast.19.rows, bf16[576,2048]{1,0:T(8,128)(2,1)} %copy-done.4, bf16[576,2048]{1,0:T(8,128)(2,1)} %collective-permute-done.10.refs_1_, bf16[576,2048]{1,0:T(8,128)(2,1)} %collective-permute-done.2.refs_2_, bf16[576,2048]{1,0:T(8,128)(2,1)} %collective-permute-done.11.refs_3_), custom_call_target="tpu_custom_call" | custom-call | flops 3019898880 | bytes 9437184 | tf_op jit(solution)/shard_map/pallas_call | solution.py:156
  96.3 0.0 copy-start
  96.3 0.0 copy-start.1
  96.3 10.1 %all-to-all-start.2 = ((bf16[8,40,2048]{2,1,0:T(8,128)(2,1)}), bf16[8,40,2048]{2,1,0:T(8,128)(2,1)S(1)}, u32[]{:S(2)}, u32[]{:S(2)}) async-start(bf16[8,40,2048]{2,1,0:T(8,128)(2,1)} %bitcast.32), calls=%async_computation.2 | async-start | bytes 2621440 | tf_op jit(solution)/shard_map/all_to_all | solution.py:324
  106.4 4.3 %shard_map.133 = (f32[32,3200]{1,0:T(8,128)S(1)}, bf16[32,3200]{1,0:T(8,128)(2,1)S(1)}) custom-call(s32[3]{0:T(128)S(1)} %pad_add_fusion.where, bf16[8,56,2048]{2,1,0:T(8,128)(2,1)} %all-to-all-done.1.arrived, f32[1,3200]{1,0:T(1,128)S(1)} %copy-done, f32[1,3200]{1,0:T(1,128)S(1)} %copy-done.1, bf16[100,3200]{1,0:T(8,128)(2,1)} %bitcast.37, ...), custom_call_target="tpu_custom_call" | custom-call | flops 163840000 | bytes 2560000 | tf_op jit(solution)/shard_map/pallas_call | solution.py:257
  110.8 2.4 %collective-permute-start.5 = (bf16[32,3200]{1,0:T(8,128)(2,1)S(1)}, bf16[32,3200]{1,0:T(8,128)(2,1)S(1)}, u32[]{:S(2)}, u32[]{:S(2)}) collective-permute-start(bf16[32,3200]{1,0:T(8,128)(2,1)S(1)} %get-tuple-element.35), channel_id=1, source_target_pairs={{0,2},{2,0},{1,3},{3,1},{4,6},{6,4},{5,7},{7,5},{8,10},{10,8},{9,1... | collective-permute-start | bytes 614408 | tf_op jit(solution)/shard_map/ppermute | solution.py:321
  113.2 5.4 %collective-permute-done.5.came = bf16[32,3200]{1,0:T(8,128)(2,1)S(1)} collective-permute-done((bf16[32,3200]{1,0:T(8,128)(2,1)S(1)}, bf16[32,3200]{1,0:T(8,128)(2,1)S(1)}, u32[]{:S(2)}, u32[]{:S(2)}) %collective-permute-start.5) | collective-permute-done | bytes 204832 | tf_op jit(solution)/shard_map/ppermute | solution.py:321
  118.7 4.4 %collective-permute-start.6 = (f32[8,3200]{1,0:T(8,128)S(1)}, f32[8,3200]{1,0:T(8,128)S(1)}, u32[]{:S(2)}, u32[]{:S(2)}) collective-permute-start(f32[8,3200]{1,0:T(8,128)S(1)} %get-tuple-element.36), channel_id=1, source_target_pairs={{0,384},{32,416},{64,448},{96,480},{128,0},{160,32},{192,64},{224,... | collective-permute-start | bytes 307208 | tf_op jit(solution)/shard_map/ppermute | solution.py:356
  123.1 2.6 %collective-permute-start.7 = (bf16[8,3200]{1,0:T(8,128)(2,1)S(1)}, bf16[8,3200]{1,0:T(8,128)(2,1)S(1)}, u32[]{:S(2)}, u32[]{:S(2)}) collective-permute-start(bf16[8,3200]{1,0:T(8,128)(2,1)S(1)} %get-tuple-element.37), channel_id=1, source_target_pairs={{0,416},{32,448},{64,480},{96,384},{128,32},{160,64},{192,96},{224... | collective-permute-start | bytes 153608 | tf_op jit(solution)/shard_map/ppermute | solution.py:356
  125.6 4.0 %collective-permute-start.8 = (bf16[8,3200]{1,0:T(8,128)(2,1)S(1)}, bf16[8,3200]{1,0:T(8,128)(2,1)S(1)}, u32[]{:S(2)}, u32[]{:S(2)}) collective-permute-start(bf16[8,3200]{1,0:T(8,128)(2,1)S(1)} %get-tuple-element.38), channel_id=1, source_target_pairs={{0,448},{32,480},{64,384},{96,416},{128,64},{160,96},{192,0},{224,... | collective-permute-start | bytes 153608 | tf_op jit(solution)/shard_map/ppermute | solution.py:356
  129.7 4.2 %collective-permute-start.9 = (bf16[8,3200]{1,0:T(8,128)(2,1)S(1)}, bf16[8,3200]{1,0:T(8,128)(2,1)S(1)}, u32[]{:S(2)}, u32[]{:S(2)}) collective-permute-start(bf16[8,3200]{1,0:T(8,128)(2,1)S(1)} %get-tuple-element.39), channel_id=1, source_target_pairs={{0,480},{32,384},{64,416},{96,448},{128,96},{160,0},{192,32},{224,... | collective-permute-start | bytes 153608 | tf_op jit(solution)/shard_map/ppermute | solution.py:356
  133.9 0.0 collective-permute-done.7.refs_0_
  133.9 1.4 collective-permute-done.8.refs_1_
  135.3 3.8 %collective-permute-done.9.refs_2_ = bf16[8,3200]{1,0:T(8,128)(2,1)S(1)} collective-permute-done((bf16[8,3200]{1,0:T(8,128)(2,1)S(1)}, bf16[8,3200]{1,0:T(8,128)(2,1)S(1)}, u32[]{:S(2)}, u32[]{:S(2)}) %collective-permute-start.9) | collective-permute-done | bytes 51232 | tf_op jit(solution)/shard_map/ppermute | solution.py:356
  139.1 0.0 collective-permute-done.6.held
  139.1 0.8 shard_map.137
  139.9 1.3 all-to-all-done.2
  141.2 1.3 shard_map.138
  142.5 3.6 %collective-permute-start.12 = (bf16[128,1024]{1,0:T(8,128)(2,1)S(1)}, bf16[128,1024]{1,0:T(8,128)(2,1)S(1)}, u32[]{:S(2)}, u32[]{:S(2)}) collective-permute-start(bf16[128,1024]{1,0:T(8,128)(2,1)S(1)} %get-tuple-element.47), channel_id=1, source_target_pairs={{0,226},{1,195},{2,160},{3,129},{32,130},{33,163},{34,192},{35,225... | collective-permute-start | bytes 786440 | tf_op jit(solution)/shard_map/ppermute | solution.py:371
  146.1 6.8 %collective-permute-start.13 = (bf16[128,1024]{1,0:T(8,128)(2,1)S(1)}, bf16[128,1024]{1,0:T(8,128)(2,1)S(1)}, u32[]{:S(2)}, u32[]{:S(2)}) collective-permute-start(bf16[128,1024]{1,0:T(8,128)(2,1)S(1)} %get-tuple-element.48), channel_id=1, source_target_pairs={{0,224},{1,193},{2,162},{3,131},{32,128},{33,161},{34,194},{35,227... | collective-permute-start | bytes 786440 | tf_op jit(solution)/shard_map/ppermute | solution.py:371
  152.9 10.0 %all_to_all.20.spread = f32[8,1,3200]{2,1,0:T(1,128)S(1)} all-to-all(f32[8,1,3200]{2,1,0:T(1,128)S(1)} %shard_map.135), channel_id=1, replica_groups=mesh['pp'=4,'yh'=4,'z'=8,'yl'=2,'core'=2] {'z'}, dimensions={0} | all-to-all | bytes 204800 | tf_op jit(solution)/shard_map/all_to_all | solution.py:324
  162.9 0.0 collective-permute-done.12.left
  162.9 0.0 collective-permute-done.13.right
  162.9 0.1 shard_map.139.left
  163.0 5.6 %collective-permute-start.14 = (bf16[128,1024]{1,0:T(8,128)(2,1)S(1)}, bf16[128,1024]{1,0:T(8,128)(2,1)S(1)}, u32[]{:S(2)}, u32[]{:S(2)}) collective-permute-start(bf16[128,1024]{1,0:T(8,128)(2,1)S(1)} %shard_map.139.left), channel_id=1, source_target_pairs={{0,1},{1,0},{2,3},{3,2},{4,5},{5,4},{6,7},{7,6},{8,9},{9,8},{10,11... | collective-permute-start | bytes 786440 | tf_op jit(solution)/shard_map/ppermute | solution.py:321
  168.7 1.1 collective-permute-done.14.right
  169.8 0.1 shard_map.140.own
  169.9 3.0 %collective-permute-start.15 = (bf16[128,1024]{1,0:T(8,128)(2,1)S(1)}, bf16[128,1024]{1,0:T(8,128)(2,1)S(1)}, u32[]{:S(2)}, u32[]{:S(2)}) collective-permute-start(bf16[128,1024]{1,0:T(8,128)(2,1)S(1)} %shard_map.140.own), channel_id=1, source_target_pairs={{0,2},{2,0},{1,3},{3,1},{4,6},{6,4},{5,7},{7,5},{8,10},{10,8},{9,1... | collective-permute-start | bytes 786440 | tf_op jit(solution)/shard_map/ppermute | solution.py:321
  172.8 0.6 shard_map.142
  173.4 5.8 %collective-permute-done.15.across = bf16[128,1024]{1,0:T(8,128)(2,1)S(1)} collective-permute-done((bf16[128,1024]{1,0:T(8,128)(2,1)S(1)}, bf16[128,1024]{1,0:T(8,128)(2,1)S(1)}, u32[]{:S(2)}, u32[]{:S(2)}) %collective-permute-start.15) | collective-permute-done | bytes 262176 | tf_op jit(solution)/shard_map/ppermute | solution.py:321
  179.3 1.4 shard_map.141
  (5 shorter events, 0.1 us)
Async XLA Ops:
  0.6 23.8 %collective-permute-start = (bf16[128,2048]{1,0:T(8,128)(2,1)}, bf16[128,2048]{1,0:T(8,128)(2,1)S(1)}, u32[]{:S(2)}, u32[]{:S(2)}) collective-permute-start(bf16[128,2048]{1,0:T(8,128)(2,1)} %bitcast.43), channel_id=1, source_target_pairs={{98,0},{67,1},{32,2},{1,3},{2,32},{35,33},{64,34},{97,35},{34,64},... | collective-permute-start | bytes 1572872 | tf_op jit(solution)/shard_map/ppermute | solution.py:317
  6.0 13.2 %collective-permute-start.1 = (f32[16,128]{1,0:T(8,128)S(1)}, f32[16,128]{1,0:T(8,128)S(1)}, u32[]{:S(2)}, u32[]{:S(2)}) collective-permute-start(f32[16,128]{1,0:T(8,128)S(1)} %pad_maximum_fusion.1), channel_id=1, source_target_pairs={{98,0},{67,1},{32,2},{1,3},{2,32},{35,33},{64,34},{97,35},{34,64},... | collective-permute-start | bytes 24584 | tf_op jit(solution)/shard_map/ppermute | solution.py:317
  12.5 0.7 copy-start.2
  13.9 10.6 %all-to-all-start = ((f32[8,1,3200]{2,1,0:T(1,128)}), f32[8,1,3200]{2,1,0:T(1,128)S(1)}, u32[]{:S(2)}, u32[]{:S(2)}) async-start(f32[8,1,3200]{2,1,0:T(1,128)} %shard_map.131), calls=%async_computation | async-start | bytes 204800 | tf_op jit(solution)/shard_map/all_to_all | solution.py:324
  17.2 9.8 %copy-start.3 = (f32[1,2048]{1,0:T(1,128)S(1)}, f32[1,2048]{1,0:T(1,128)}, u32[]{:S(2)}) copy-start(f32[1,2048]{1,0:T(1,128)} %gain.2) | copy-start | bytes 24580
  19.1 28.0 %copy-start.4 = (bf16[576,2048]{1,0:T(8,128)(2,1)}, bf16[576,2048]{1,0:T(8,128)(2,1)S(1)}, u32[]{:S(2)}) copy-start(bf16[576,2048]{1,0:T(8,128)(2,1)S(1)} %pad_maximum_fusion.refs_0_) | copy-start | bytes 7077892
  24.4 49.7 %collective-permute-start.2 = (bf16[576,2048]{1,0:T(8,128)(2,1)S(1)}, bf16[576,2048]{1,0:T(8,128)(2,1)}, u32[]{:S(2)}, u32[]{:S(2)}) collective-permute-start(bf16[576,2048]{1,0:T(8,128)(2,1)S(1)} %pad_maximum_fusion.refs_0_), channel_id=1, source_target_pairs={{0,2},{2,0},{1,3},{3,1},{4,6},{6,4},{5,7},{7,5},{8,10},{10,8},{9,1... | collective-permute-start | bytes 7077896 | tf_op jit(solution)/shard_map/ppermute | solution.py:321
  29.8 53.0 %all-to-all-start.1 = ((bf16[8,56,2048]{2,1,0:T(8,128)(2,1)}), bf16[8,56,2048]{2,1,0:T(8,128)(2,1)}, u32[]{:S(2)}, u32[]{:S(2)}) async-start(bf16[8,56,2048]{2,1,0:T(8,128)(2,1)} %bitcast.31), calls=%async_computation.1 | async-start | bytes 3670016 | tf_op jit(solution)/shard_map/all_to_all | solution.py:324
  39.7 9.9 %collective-permute-start.3 = (bf16[100,3200]{1,0:T(8,128)(2,1)}, bf16[100,3200]{1,0:T(8,128)(2,1)S(1)}, u32[]{:S(2)}, u32[]{:S(2)}) collective-permute-start(bf16[100,3200]{1,0:T(8,128)(2,1)} %bitcast.36), channel_id=1, source_target_pairs={{0,1},{1,0},{2,3},{3,2},{4,5},{5,4},{6,7},{7,6},{8,9},{9,8},{10,11... | collective-permute-start | bytes 1920008 | tf_op jit(solution)/shard_map/ppermute | solution.py:321
  45.2 4.4 %collective-permute-start.4 = (bf16[100,3200]{1,0:T(8,128)(2,1)}, bf16[100,3200]{1,0:T(8,128)(2,1)S(1)}, u32[]{:S(2)}, u32[]{:S(2)}) collective-permute-start(bf16[100,3200]{1,0:T(8,128)(2,1)} %bitcast.38), channel_id=1, source_target_pairs={{0,1},{1,0},{2,3},{3,2},{4,5},{5,4},{6,7},{7,6},{8,9},{9,8},{10,11... | collective-permute-start | bytes 1920008 | tf_op jit(solution)/shard_map/ppermute | solution.py:321
  47.2 34.8 %collective-permute-start.10 = (bf16[576,2048]{1,0:T(8,128)(2,1)S(1)}, bf16[576,2048]{1,0:T(8,128)(2,1)}, u32[]{:S(2)}, u32[]{:S(2)}) collective-permute-start(bf16[576,2048]{1,0:T(8,128)(2,1)S(1)} %pad_maximum_fusion.refs_0_), channel_id=1, source_target_pairs={{0,1},{1,0},{2,3},{3,2},{4,5},{5,4},{6,7},{7,6},{8,9},{9,8},{10,11... | collective-permute-start | bytes 7077896 | tf_op jit(solution)/shard_map/ppermute | solution.py:321
  49.6 24.5 %copy-start.5 = (bf16[100,3200]{1,0:T(8,128)(2,1)}, bf16[100,3200]{1,0:T(8,128)(2,1)S(1)}, u32[]{:S(2)}) copy-start(bf16[100,3200]{1,0:T(8,128)(2,1)S(1)} %collective-permute-done.3.first_other) | copy-start | bytes 1920004
  49.6 32.4 %copy-start.6 = (bf16[100,3200]{1,0:T(8,128)(2,1)}, bf16[100,3200]{1,0:T(8,128)(2,1)S(1)}, u32[]{:S(2)}) copy-start(bf16[100,3200]{1,0:T(8,128)(2,1)S(1)} %collective-permute-done.4.second_other) | copy-start | bytes 1920004
  74.1 12.4 %collective-permute-start.11 = (bf16[576,2048]{1,0:T(8,128)(2,1)}, bf16[576,2048]{1,0:T(8,128)(2,1)}, u32[]{:S(2)}, u32[]{:S(2)}) collective-permute-start(bf16[576,2048]{1,0:T(8,128)(2,1)} %collective-permute-done.2.refs_2_), channel_id=1, source_target_pairs={{0,1},{1,0},{2,3},{3,2},{4,5},{5,4},{6,7},{7,6},{8,9},{9,8},{10,11... | collective-permute-start | bytes 7077896 | tf_op jit(solution)/shard_map/ppermute | solution.py:321
  96.3 10.2 %copy-start = (f32[1,3200]{1,0:T(1,128)S(1)}, f32[1,3200]{1,0:T(1,128)}, u32[]{:S(2)}) copy-start(f32[1,3200]{1,0:T(1,128)} %gain.3) | copy-start | bytes 38404
  96.3 10.2 %copy-start.1 = (f32[1,3200]{1,0:T(1,128)S(1)}, f32[1,3200]{1,0:T(1,128)}, u32[]{:S(2)}) copy-start(f32[1,3200]{1,0:T(1,128)} %weigh.1) | copy-start | bytes 38404
  96.3 45.0 %all-to-all-start.2 = ((bf16[8,40,2048]{2,1,0:T(8,128)(2,1)}), bf16[8,40,2048]{2,1,0:T(8,128)(2,1)S(1)}, u32[]{:S(2)}, u32[]{:S(2)}) async-start(bf16[8,40,2048]{2,1,0:T(8,128)(2,1)} %bitcast.32), calls=%async_computation.2 | async-start | bytes 2621440 | tf_op jit(solution)/shard_map/all_to_all | solution.py:324
  110.8 7.9 %collective-permute-start.5 = (bf16[32,3200]{1,0:T(8,128)(2,1)S(1)}, bf16[32,3200]{1,0:T(8,128)(2,1)S(1)}, u32[]{:S(2)}, u32[]{:S(2)}) collective-permute-start(bf16[32,3200]{1,0:T(8,128)(2,1)S(1)} %get-tuple-element.35), channel_id=1, source_target_pairs={{0,2},{2,0},{1,3},{3,1},{4,6},{6,4},{5,7},{7,5},{8,10},{10,8},{9,1... | collective-permute-start | bytes 614408 | tf_op jit(solution)/shard_map/ppermute | solution.py:321
  118.7 20.4 %collective-permute-start.6 = (f32[8,3200]{1,0:T(8,128)S(1)}, f32[8,3200]{1,0:T(8,128)S(1)}, u32[]{:S(2)}, u32[]{:S(2)}) collective-permute-start(f32[8,3200]{1,0:T(8,128)S(1)} %get-tuple-element.36), channel_id=1, source_target_pairs={{0,384},{32,416},{64,448},{96,480},{128,0},{160,32},{192,64},{224,... | collective-permute-start | bytes 307208 | tf_op jit(solution)/shard_map/ppermute | solution.py:356
  123.1 10.8 %collective-permute-start.7 = (bf16[8,3200]{1,0:T(8,128)(2,1)S(1)}, bf16[8,3200]{1,0:T(8,128)(2,1)S(1)}, u32[]{:S(2)}, u32[]{:S(2)}) collective-permute-start(bf16[8,3200]{1,0:T(8,128)(2,1)S(1)} %get-tuple-element.37), channel_id=1, source_target_pairs={{0,416},{32,448},{64,480},{96,384},{128,32},{160,64},{192,96},{224... | collective-permute-start | bytes 153608 | tf_op jit(solution)/shard_map/ppermute | solution.py:356
  125.6 9.7 %collective-permute-start.8 = (bf16[8,3200]{1,0:T(8,128)(2,1)S(1)}, bf16[8,3200]{1,0:T(8,128)(2,1)S(1)}, u32[]{:S(2)}, u32[]{:S(2)}) collective-permute-start(bf16[8,3200]{1,0:T(8,128)(2,1)S(1)} %get-tuple-element.38), channel_id=1, source_target_pairs={{0,448},{32,480},{64,384},{96,416},{128,64},{160,96},{192,0},{224,... | collective-permute-start | bytes 153608 | tf_op jit(solution)/shard_map/ppermute | solution.py:356
  129.7 9.4 %collective-permute-start.9 = (bf16[8,3200]{1,0:T(8,128)(2,1)S(1)}, bf16[8,3200]{1,0:T(8,128)(2,1)S(1)}, u32[]{:S(2)}, u32[]{:S(2)}) collective-permute-start(bf16[8,3200]{1,0:T(8,128)(2,1)S(1)} %get-tuple-element.39), channel_id=1, source_target_pairs={{0,480},{32,384},{64,416},{96,448},{128,96},{160,0},{192,32},{224,... | collective-permute-start | bytes 153608 | tf_op jit(solution)/shard_map/ppermute | solution.py:356
  142.5 20.4 %collective-permute-start.12 = (bf16[128,1024]{1,0:T(8,128)(2,1)S(1)}, bf16[128,1024]{1,0:T(8,128)(2,1)S(1)}, u32[]{:S(2)}, u32[]{:S(2)}) collective-permute-start(bf16[128,1024]{1,0:T(8,128)(2,1)S(1)} %get-tuple-element.47), channel_id=1, source_target_pairs={{0,226},{1,195},{2,160},{3,129},{32,130},{33,163},{34,192},{35,225... | collective-permute-start | bytes 786440 | tf_op jit(solution)/shard_map/ppermute | solution.py:371
  146.1 16.8 %collective-permute-start.13 = (bf16[128,1024]{1,0:T(8,128)(2,1)S(1)}, bf16[128,1024]{1,0:T(8,128)(2,1)S(1)}, u32[]{:S(2)}, u32[]{:S(2)}) collective-permute-start(bf16[128,1024]{1,0:T(8,128)(2,1)S(1)} %get-tuple-element.48), channel_id=1, source_target_pairs={{0,224},{1,193},{2,162},{3,131},{32,128},{33,161},{34,194},{35,227... | collective-permute-start | bytes 786440 | tf_op jit(solution)/shard_map/ppermute | solution.py:371
  163.0 6.8 %collective-permute-start.14 = (bf16[128,1024]{1,0:T(8,128)(2,1)S(1)}, bf16[128,1024]{1,0:T(8,128)(2,1)S(1)}, u32[]{:S(2)}, u32[]{:S(2)}) collective-permute-start(bf16[128,1024]{1,0:T(8,128)(2,1)S(1)} %shard_map.139.left), channel_id=1, source_target_pairs={{0,1},{1,0},{2,3},{3,2},{4,5},{5,4},{6,7},{7,6},{8,9},{9,8},{10,11... | collective-permute-start | bytes 786440 | tf_op jit(solution)/shard_map/ppermute | solution.py:321
  169.9 9.4 %collective-permute-start.15 = (bf16[128,1024]{1,0:T(8,128)(2,1)S(1)}, bf16[128,1024]{1,0:T(8,128)(2,1)S(1)}, u32[]{:S(2)}, u32[]{:S(2)}) collective-permute-start(bf16[128,1024]{1,0:T(8,128)(2,1)S(1)} %shard_map.140.own), channel_id=1, source_target_pairs={{0,2},{2,0},{1,3},{3,1},{4,6},{6,4},{5,7},{7,5},{8,10},{10,8},{9,1... | collective-permute-start | bytes 786440 | tf_op jit(solution)/shard_map/ppermute | solution.py:321

commit v9 on v8

--- a/solution.py
+++ b/solution.py
@@ -115,16 +115,23 @@
                     shard.at[pl.ds(p * count, count)], held.at[pl.ds(s * count, count)], in_sem.at[3 * s + p]
                 )
             )
-    for s in range(4):
+    for s in (0, 1):
         copies[3 * s].start()
         copies[3 * s + 1].start()
-    for s in range(4):
-        copies[3 * s + 2].start()
     row_copy.wait()
+    for s in (0, 1):
+        copies[3 * s].wait()
+        copies[3 * s + 1].wait()
+    for s in (2, 3):
+        copies[3 * s].start()
+        copies[3 * s + 1].start()
     flat = rows_v[...]
     step = 256
-    seen = 0
+    seen = 2
     for c in range(4 * count // step):
+        if c == 1:
+            for s in range(4):
+                copies[3 * s + 2].start()
         while seen * count < (c + 1) * step:
             copies[3 * seen].wait()
             copies[3 * seen + 1].wait()
@@ -331,24 +338,26 @@
     image = image_in[0]
     dv = image.shape[1]
     ring = exchanged(call(spread_kernel, shaped((n_yh * 2, 1, dv), F32))(image), ("yh", "yl"))
+    other = shifted(own, "core", 1)
     own, sent, meta, ring, where = lax.optimization_barrier((own, sent, meta, ring, where))
     across = shifted(own, "yl", 1)
-    other = shifted(own, "core", 1)
+
+    rows = call(pack_kernel, pltpu.HBM((n_z * ROWS, width), BF16), scalars=1)(where, meta, sent, trunk_gain, ring)
+    arrived = exchanged(rows.reshape(n_z, ROWS, width), "z")
+
     first, second = fc_in[0].T, fc_out[0]
     first_other, second_other = shifted(first, "core", 1), shifted(second, "core", 1)
-    across, first_other, second_other = lax.optimization_barrier((across, first_other, second_other))
+    across, other, first_other, second_other = lax.optimization_barrier((across, other, first_other, second_other))
     both = shifted(across, "core", 1)
 
-    rows = call(pack_kernel, pltpu.HBM((n_z * ROWS, width), BF16), scalars=1)(where, meta, sent, trunk_gain, ring)
-    arrived = exchanged(rows.reshape(n_z, ROWS, width), "z")
-
+    mine, theirs = encoder_part(where, arrived, image_gain, layer_scale, (first, first_other, second, second_other), n_yh)
+    both, theirs = lax.optimization_barrier((both, theirs))
     made = experts(arrived.reshape(-1, width), (own, other, across, both))
     made, meta = lax.optimization_barrier((made, meta))
     n_rows = n_z * CAP
     returned = exchanged(made.reshape(n_z, CAP, width), "z").reshape(n_rows, width)
     high, low = call(weigh_kernel, (shaped((toks, n_rows)), shaped((toks, n_rows))), scalars=1)(where, meta)
 
-    mine, theirs = encoder_part(where, arrived, image_gain, layer_scale, (first, first_other, second, second_other), n_yh)
     mine, *theirs = call(
         fold_kernel, (shaped((n_z, dv), F32),) + tuple(shaped((n_z, dv)) for _ in range(n_yh - 1))
     )(mine, shifted(theirs, "yl", 1))
@@ -379,8 +388,8 @@
         )
         for flip, piece in zip((0, 2), pieces)
     ]
-    spread, pieces = lax.optimization_barrier((exchanged(column, "z"), pieces))
     part = call(add_kernel, shaped((toks, half)))(*pieces)
+    spread, part = lax.optimization_barrier((exchanged(column, "z"), part))
     layer = call(add_kernel, shaped((toks, half)))(part, shifted(part, "core", 1))
     trunk_out = call(join_kernel, shaped((toks, width)), scalars=1)(where, layer, shifted(layer, "yl", 1))
 

time: 182 us -> 180 us (0.989)
  blocking collectives: 10 us -> 0 us
  waiting for transfers between devices: 53 us -> 58 us
  starting transfers between devices: 90.9 us -> 93.9 us
    all_to_all x1 -> x0, blocking collectives: 10 us -> none  [exchanged(): return lax.all_to_all(value, axis, split_axis=0, concat_axis=0, tiled=True)]
    ppermute x2, waiting for transfers between devices: 0.01 us -> 8.52 us  [body(): lax.ppermute(piece, ('pp',) + square, [(s * n_square + a * n_tp + t, (s +...]
    ppermute x4, starting transfers between devices: 15.2 us -> 19.3 us  [body(): lax.ppermute(part, ('pp', 'yh'), [(s * n_yh + h, (s - 1) % n_pp * n_yh +...]
    ppermute x4, waiting for transfers between devices: 5.16 us -> 1.54 us  [body(): lax.ppermute(part, ('pp', 'yh'), [(s * n_yh + h, (s - 1) % n_pp * n_yh +...]
    ppermute x8, waiting for transfers between devices: 40.5 us -> 42.9 us  [shifted(): return lax.ppermute(value, axis, [(i, (i + by) % n) for i in range(n)])]
    all_to_all x3 -> x4, waiting for transfers between devices: 7.32 us -> 5.05 us  [exchanged(): return lax.all_to_all(value, axis, split_axis=0, concat_axis=0, tiled=True)]
    ppermute x8, starting transfers between devices: 31.4 us -> 29.4 us  [shifted(): return lax.ppermute(value, axis, [(i, (i + by) % n) for i in range(n)])]
    all_to_all x3 -> x4, starting transfers between devices: 23.4 us -> 23.5 us  [exchanged(): return lax.all_to_all(value, axis, split_axis=0, concat_axis=0, tiled=True)]
  transfers between devices with their start and end apart: 19 -> 20, of which waited for: 10 -> 9; matrix products, arithmetic and copies ran while one was open for 2% -> 3% of each run, Pallas kernels for 5% -> 6%
where the time goes in v9:
time: 180 us; the launch traced here: 179 us
  starting transfers between devices  93.9 us (52%)
  waiting for transfers between devices  58 us (32%)
  Pallas kernels  20.8 us (12%)
  other arithmetic  4.78 us (3%)
    ppermute x8, waiting for transfers between devices, shifted(): return lax.ppermute(value, axis, [(i, (i + by) % n) for i in range(n)])  42.9 us
    ppermute x8, starting transfers between devices, shifted(): return lax.ppermute(value, axis, [(i, (i + by) % n) for i in range(n)])  29.4 us
    all_to_all x4, starting transfers between devices, exchanged(): return lax.all_to_all(value, axis, split_axis=0, concat_axis=0, tiled=True)  23.5 us
    ppermute x4, starting transfers between devices, body(): lax.ppermute(part, ('pp', 'yh'), [(s * n_yh + h, (s - 1) % n_pp * n_yh +...  19.3 us
    ppermute x2, starting transfers between devices, body(): lax.ppermute(piece, ('pp',) + square, [(s * n_square + a * n_tp + t, (s +...  11.3 us
    ppermute x2, starting transfers between devices, fetched(): return lax.ppermute(value, square, pairs)  10.5 us
    ppermute x2, waiting for transfers between devices, body(): lax.ppermute(piece, ('pp',) + square, [(s * n_square + a * n_tp + t, (s +...  8.52 us
    pallas_call x10, Pallas kernels, run(): pl.pallas_call(kernel, out_shape=outs, in_specs=specs, out_specs=jax.tree...  8.32 us
  transfers between devices with their start and end apart: 20, of which 9 were waited for; matrix products, arithmetic and copies ran while one was open for 3% of the time, Pallas kernels for 6%

profile of v9, /device:TPU:1, one launch (start us, length us, event | category | flops | bytes accessed | tf_op | source)
XLA Modules:
  0.0 179.2 jit_solution(2208858181384228667)
XLA Ops:
  0.6 4.0 %collective-permute-start = (bf16[128,2048]{1,0:T(8,128)(2,1)}, bf16[128,2048]{1,0:T(8,128)(2,1)S(1)}, u32[]{:S(2)}, u32[]{:S(2)}) collective-permute-start(bf16[128,2048]{1,0:T(8,128)(2,1)} %bitcast.43), channel_id=1, source_target_pairs={{98,0},{67,1},{32,2},{1,3},{2,32},{35,33},{64,34},{97,35},{34,64},... | collective-permute-start | bytes 1572872 | tf_op jit(solution)/shard_map/ppermute | solution.py:324
  4.7 0.7 convert_bitcast_fusion
  5.4 0.7 pad_maximum_fusion.1
  6.0 6.4 %collective-permute-start.1 = (f32[16,128]{1,0:T(8,128)S(1)}, f32[16,128]{1,0:T(8,128)S(1)}, u32[]{:S(2)}, u32[]{:S(2)}) collective-permute-start(f32[16,128]{1,0:T(8,128)S(1)} %pad_maximum_fusion.1), channel_id=1, source_target_pairs={{98,0},{67,1},{32,2},{1,3},{2,32},{35,33},{64,34},{97,35},{34,64},... | collective-permute-start | bytes 24584 | tf_op jit(solution)/shard_map/ppermute | solution.py:324
  12.5 0.0 copy-start.2
  12.5 0.7 copy-done.2
  13.2 0.7 shard_map.131
  13.9 3.4 %all-to-all-start = ((f32[8,1,3200]{2,1,0:T(1,128)}), f32[8,1,3200]{2,1,0:T(1,128)S(1)}, u32[]{:S(2)}, u32[]{:S(2)}) async-start(f32[8,1,3200]{2,1,0:T(1,128)} %shard_map.131), calls=%async_computation | async-start | bytes 204800 | tf_op jit(solution)/shard_map/all_to_all | solution.py:331
  17.2 0.0 copy-start.3
  17.2 3.3 %pad_maximum_fusion.refs_0_ = bf16[576,2048]{1,0:T(8,128)(2,1)} fusion(bf16[192,2048]{1,0:T(8,128)(2,1)} %bitcast.33, bf16[192,2048]{1,0:T(8,128)(2,1)} %bitcast.34, bf16[192,2048]{1,0:T(8,128)(2,1)} %bitcast.35), kind=kLoop, calls=%fused_computation | loop fusion | flops 7077888 | bytes 4718592 | tf_op jit(solution)/shard_map/concatenate | solution.py:337
  20.6 5.4 %collective-permute-start.3 = (bf16[576,2048]{1,0:T(8,128)(2,1)}, bf16[576,2048]{1,0:T(8,128)(2,1)S(1)}, u32[]{:S(2)}, u32[]{:S(2)}) collective-permute-start(bf16[576,2048]{1,0:T(8,128)(2,1)} %pad_maximum_fusion.refs_0_), channel_id=1, source_target_pairs={{0,1},{1,0},{2,3},{3,2},{4,5},{5,4},{6,7},{7,6},{8,9},{9,8},{10,11... | collective-permute-start | bytes 7077896 | tf_op jit(solution)/shard_map/ppermute | solution.py:328
  25.9 0.1 pad_add_fusion.where
  26.0 0.0 collective-permute-done.1.meta
  26.0 0.0 all-to-all-done.ring
  26.0 0.0 collective-permute-done.toks
  26.0 3.5 %collective-permute-start.2 = (bf16[576,2048]{1,0:T(8,128)(2,1)}, bf16[576,2048]{1,0:T(8,128)(2,1)}, u32[]{:S(2)}, u32[]{:S(2)}) collective-permute-start(bf16[576,2048]{1,0:T(8,128)(2,1)} %pad_maximum_fusion.refs_0_), channel_id=1, source_target_pairs={{0,2},{2,0},{1,3},{3,1},{4,6},{6,4},{5,7},{7,5},{8,10},{10,8},{9,1... | collective-permute-start | bytes 7077896 | tf_op jit(solution)/shard_map/ppermute | solution.py:328
  29.6 0.0 copy-done.3
  29.6 2.7 %shard_map.132 = bf16[448,2048]{1,0:T(8,128)(2,1)} custom-call(s32[3]{0:T(128)S(1)} %pad_add_fusion.where, f32[16,128]{1,0:T(8,128)S(1)} %collective-permute-done.1.meta, bf16[128,2048]{1,0:T(8,128)(2,1)S(1)} %collective-permute-done.toks, f32[1,2048]{1,0:T(1,128)S(1)} %copy-done.3, f32[8,1,3200]{2,1,0:T(1,128)S(1)} %all-to-all-done.ring), custom_call_target="tpu_custom_call" | custom-call | tf_op jit(solution)/shard_map/pallas_call | solution.py:32
  32.3 8.6 %all-to-all-start.1 = ((bf16[8,56,2048]{2,1,0:T(8,128)(2,1)}), bf16[8,56,2048]{2,1,0:T(8,128)(2,1)}, u32[]{:S(2)}, u32[]{:S(2)}) async-start(bf16[8,56,2048]{2,1,0:T(8,128)(2,1)} %bitcast.31), calls=%async_computation.1 | async-start | bytes 3670016 | tf_op jit(solution)/shard_map/all_to_all | solution.py:331
  40.9 4.4 %collective-permute-start.4 = (bf16[100,3200]{1,0:T(8,128)(2,1)}, bf16[100,3200]{1,0:T(8,128)(2,1)S(1)}, u32[]{:S(2)}, u32[]{:S(2)}) collective-permute-start(bf16[100,3200]{1,0:T(8,128)(2,1)} %bitcast.36), channel_id=1, source_target_pairs={{0,1},{1,0},{2,3},{3,2},{4,5},{5,4},{6,7},{7,6},{8,9},{9,8},{10,11... | collective-permute-start | bytes 1920008 | tf_op jit(solution)/shard_map/ppermute | solution.py:328
  45.4 1.9 %collective-permute-start.5 = (bf16[100,3200]{1,0:T(8,128)(2,1)}, bf16[100,3200]{1,0:T(8,128)(2,1)S(1)}, u32[]{:S(2)}, u32[]{:S(2)}) collective-permute-start(bf16[100,3200]{1,0:T(8,128)(2,1)} %bitcast.38), channel_id=1, source_target_pairs={{0,1},{1,0},{2,3},{3,2},{4,5},{5,4},{6,7},{7,6},{8,9},{9,8},{10,11... | collective-permute-start | bytes 1920008 | tf_op jit(solution)/shard_map/ppermute | solution.py:328
  47.3 0.0 collective-permute-done.4.first_other
  47.3 0.0 copy-start.5
  47.3 2.3 %collective-permute-done.5.second_other = bf16[100,3200]{1,0:T(8,128)(2,1)S(1)} collective-permute-done((bf16[100,3200]{1,0:T(8,128)(2,1)}, bf16[100,3200]{1,0:T(8,128)(2,1)S(1)}, u32[]{:S(2)}, u32[]{:S(2)}) %collective-permute-start.5) | collective-permute-done | bytes 640032 | tf_op jit(solution)/shard_map/ppermute | solution.py:328
  49.6 0.0 collective-permute-done.3.refs_1_
  49.6 0.0 copy-done.5
  49.6 0.0 copy-start.4
  49.6 28.8 %collective-permute-done.2.refs_2_ = bf16[576,2048]{1,0:T(8,128)(2,1)} collective-permute-done((bf16[576,2048]{1,0:T(8,128)(2,1)}, bf16[576,2048]{1,0:T(8,128)(2,1)}, u32[]{:S(2)}, u32[]{:S(2)}) %collective-permute-start.2) | collective-permute-done | bytes 2359328 | tf_op jit(solution)/shard_map/ppermute | solution.py:328
  78.4 5.6 %collective-permute-start.6 = (bf16[576,2048]{1,0:T(8,128)(2,1)}, bf16[576,2048]{1,0:T(8,128)(2,1)}, u32[]{:S(2)}, u32[]{:S(2)}) collective-permute-start(bf16[576,2048]{1,0:T(8,128)(2,1)} %collective-permute-done.2.refs_2_), channel_id=1, source_target_pairs={{0,1},{1,0},{2,3},{3,2},{4,5},{5,4},{6,7},{7,6},{8,9},{9,8},{10,11... | collective-permute-start | bytes 7077896 | tf_op jit(solution)/shard_map/ppermute | solution.py:328
  84.0 0.5 all-to-all-done.1.arrived
  84.5 0.0 copy-done
  84.5 4.3 %shard_map.133 = (f32[32,3200]{1,0:T(8,128)S(1)}, bf16[32,3200]{1,0:T(8,128)(2,1)S(1)}) custom-call(s32[3]{0:T(128)S(1)} %pad_add_fusion.where, bf16[8,56,2048]{2,1,0:T(8,128)(2,1)} %all-to-all-done.1.arrived, f32[1,3200]{1,0:T(1,128)S(1)} %copy-done, f32[1,3200]{1,0:T(1,128)S(1)} %copy-done.1, bf16[100,3200]{1,0:T(8,128)(2,1)} %bitcast.37, ...), custom_call_target="tpu_custom_call" | custom-call | flops 163840000 | bytes 2560000 | tf_op jit(solution)/shard_map/pallas_call | solution.py:264
  88.8 0.0 collective-permute-done.6.refs_3_
  88.8 8.2 %shard_map.136 = bf16[320,2048]{1,0:T(8,128)(2,1)} custom-call(bf16[448,2048]{1,0:T(8,128)(2,1)} %bitcast.19.rows, bf16[576,2048]{1,0:T(8,128)(2,1)} %pad_maximum_fusion.refs_0_, bf16[576,2048]{1,0:T(8,128)(2,1)} %copy-done.4, bf16[576,2048]{1,0:T(8,128)(2,1)} %collective-permute-done.2.refs_2_, bf16[576,2048]{1,0:T(8,128)(2,1)} %collective-permute-done.6.refs_3_), custom_call_target="tpu_custom_call" | custom-call | flops 3019898880 | bytes 9437184 | tf_op jit(solution)/shard_map/pallas_call | solution.py:163
  97.0 8.2 %all-to-all-start.2 = ((bf16[8,40,2048]{2,1,0:T(8,128)(2,1)}), bf16[8,40,2048]{2,1,0:T(8,128)(2,1)S(1)}, u32[]{:S(2)}, u32[]{:S(2)}) async-start(bf16[8,40,2048]{2,1,0:T(8,128)(2,1)} %bitcast.32), calls=%async_computation.2 | async-start | bytes 2621440 | tf_op jit(solution)/shard_map/all_to_all | solution.py:331
  105.2 3.3 %collective-permute-start.7 = (bf16[32,3200]{1,0:T(8,128)(2,1)S(1)}, bf16[32,3200]{1,0:T(8,128)(2,1)S(1)}, u32[]{:S(2)}, u32[]{:S(2)}) collective-permute-start(bf16[32,3200]{1,0:T(8,128)(2,1)S(1)} %get-tuple-element.39), channel_id=1, source_target_pairs={{0,2},{2,0},{1,3},{3,1},{4,6},{6,4},{5,7},{7,5},{8,10},{10,8},{9,1... | collective-permute-start | bytes 614408 | tf_op jit(solution)/shard_map/ppermute | solution.py:328
  108.5 4.5 %collective-permute-done.7.came = bf16[32,3200]{1,0:T(8,128)(2,1)S(1)} collective-permute-done((bf16[32,3200]{1,0:T(8,128)(2,1)S(1)}, bf16[32,3200]{1,0:T(8,128)(2,1)S(1)}, u32[]{:S(2)}, u32[]{:S(2)}) %collective-permute-start.7) | collective-permute-done | bytes 204832 | tf_op jit(solution)/shard_map/ppermute | solution.py:328
  113.0 0.1 shard_map.134
  113.1 4.4 %collective-permute-start.8 = (f32[8,3200]{1,0:T(8,128)S(1)}, f32[8,3200]{1,0:T(8,128)S(1)}, u32[]{:S(2)}, u32[]{:S(2)}) collective-permute-start(f32[8,3200]{1,0:T(8,128)S(1)} %get-tuple-element.40), channel_id=1, source_target_pairs={{0,384},{32,416},{64,448},{96,480},{128,0},{160,32},{192,64},{224,... | collective-permute-start | bytes 307208 | tf_op jit(solution)/shard_map/ppermute | solution.py:365
  117.5 4.5 %collective-permute-start.9 = (bf16[8,3200]{1,0:T(8,128)(2,1)S(1)}, bf16[8,3200]{1,0:T(8,128)(2,1)S(1)}, u32[]{:S(2)}, u32[]{:S(2)}) collective-permute-start(bf16[8,3200]{1,0:T(8,128)(2,1)S(1)} %get-tuple-element.41), channel_id=1, source_target_pairs={{0,416},{32,448},{64,480},{96,384},{128,32},{160,64},{192,96},{224... | collective-permute-start | bytes 153608 | tf_op jit(solution)/shard_map/ppermute | solution.py:365
  122.0 5.2 %collective-permute-start.10 = (bf16[8,3200]{1,0:T(8,128)(2,1)S(1)}, bf16[8,3200]{1,0:T(8,128)(2,1)S(1)}, u32[]{:S(2)}, u32[]{:S(2)}) collective-permute-start(bf16[8,3200]{1,0:T(8,128)(2,1)S(1)} %get-tuple-element.42), channel_id=1, source_target_pairs={{0,448},{32,480},{64,384},{96,416},{128,64},{160,96},{192,0},{224,... | collective-permute-start | bytes 153608 | tf_op jit(solution)/shard_map/ppermute | solution.py:365
  127.2 5.2 %collective-permute-start.11 = (bf16[8,3200]{1,0:T(8,128)(2,1)S(1)}, bf16[8,3200]{1,0:T(8,128)(2,1)S(1)}, u32[]{:S(2)}, u32[]{:S(2)}) collective-permute-start(bf16[8,3200]{1,0:T(8,128)(2,1)S(1)} %get-tuple-element.43), channel_id=1, source_target_pairs={{0,480},{32,384},{64,416},{96,448},{128,96},{160,0},{192,32},{224,... | collective-permute-start | bytes 153608 | tf_op jit(solution)/shard_map/ppermute | solution.py:365
  132.4 0.8 shard_map.137
  133.2 0.0 collective-permute-done.9.refs_0_
  133.2 0.0 collective-permute-done.10.refs_1_
  133.2 1.5 collective-permute-done.11.refs_2_
  134.7 0.0 collective-permute-done.8.held
  134.7 0.7 shard_map.135
  135.4 4.6 %all-to-all-done.2 = bf16[8,40,2048]{2,1,0:T(8,128)(2,1)S(1)} async-done(((bf16[8,40,2048]{2,1,0:T(8,128)(2,1)}), bf16[8,40,2048]{2,1,0:T(8,128)(2,1)S(1)}, u32[]{:S(2)}, u32[]{:S(2)}) %all-to-all-start.2) | async-done | bytes 1310752 | tf_op jit(solution)/shard_map/all_to_all | solution.py:331
  140.0 1.3 shard_map.138
  141.3 7.3 %collective-permute-start.12 = (bf16[128,1024]{1,0:T(8,128)(2,1)S(1)}, bf16[128,1024]{1,0:T(8,128)(2,1)S(1)}, u32[]{:S(2)}, u32[]{:S(2)}) collective-permute-start(bf16[128,1024]{1,0:T(8,128)(2,1)S(1)} %get-tuple-element.52), channel_id=1, source_target_pairs={{0,226},{1,195},{2,160},{3,129},{32,130},{33,163},{34,192},{35,225... | collective-permute-start | bytes 786440 | tf_op jit(solution)/shard_map/ppermute | solution.py:380
  148.6 4.0 %collective-permute-start.13 = (bf16[128,1024]{1,0:T(8,128)(2,1)S(1)}, bf16[128,1024]{1,0:T(8,128)(2,1)S(1)}, u32[]{:S(2)}, u32[]{:S(2)}) collective-permute-start(bf16[128,1024]{1,0:T(8,128)(2,1)S(1)} %get-tuple-element.53), channel_id=1, source_target_pairs={{0,224},{1,193},{2,162},{3,131},{32,128},{33,161},{34,194},{35,227... | collective-permute-start | bytes 786440 | tf_op jit(solution)/shard_map/ppermute | solution.py:380
  152.6 3.4 %all-to-all-start.3 = ((f32[8,1,3200]{2,1,0:T(1,128)}), f32[8,1,3200]{2,1,0:T(1,128)S(1)}, u32[]{:S(2)}, u32[]{:S(2)}) async-start(f32[8,1,3200]{2,1,0:T(1,128)} %shard_map.135), calls=%async_computation.3 | async-start | bytes 204800 | tf_op jit(solution)/shard_map/all_to_all | solution.py:331
  156.0 0.0 collective-permute-done.12.left
  156.0 8.5 %collective-permute-done.13.right = bf16[128,1024]{1,0:T(8,128)(2,1)S(1)} collective-permute-done((bf16[128,1024]{1,0:T(8,128)(2,1)S(1)}, bf16[128,1024]{1,0:T(8,128)(2,1)S(1)}, u32[]{:S(2)}, u32[]{:S(2)}) %collective-permute-start.13) | collective-permute-done | bytes 262176 | tf_op jit(solution)/shard_map/ppermute | solution.py:380
  164.5 0.1 shard_map.139.left
  164.6 0.0 all-to-all-done.3.spread
  164.6 2.6 %collective-permute-start.14 = (bf16[128,1024]{1,0:T(8,128)(2,1)S(1)}, bf16[128,1024]{1,0:T(8,128)(2,1)S(1)}, u32[]{:S(2)}, u32[]{:S(2)}) collective-permute-start(bf16[128,1024]{1,0:T(8,128)(2,1)S(1)} %shard_map.139.left), channel_id=1, source_target_pairs={{0,1},{1,0},{2,3},{3,2},{4,5},{5,4},{6,7},{7,6},{8,9},{9,8},{10,11... | collective-permute-start | bytes 786440 | tf_op jit(solution)/shard_map/ppermute | solution.py:328
  167.2 1.1 collective-permute-done.14.right
  168.3 0.1 shard_map.140.own
  168.4 2.6 %collective-permute-start.15 = (bf16[128,1024]{1,0:T(8,128)(2,1)S(1)}, bf16[128,1024]{1,0:T(8,128)(2,1)S(1)}, u32[]{:S(2)}, u32[]{:S(2)}) collective-permute-start(bf16[128,1024]{1,0:T(8,128)(2,1)S(1)} %shard_map.140.own), channel_id=1, source_target_pairs={{0,2},{2,0},{1,3},{3,1},{4,6},{6,4},{5,7},{7,5},{8,10},{10,8},{9,1... | collective-permute-start | bytes 786440 | tf_op jit(solution)/shard_map/ppermute | solution.py:328
  171.0 0.6 shard_map.142
  171.7 6.1 %collective-permute-done.15.across = bf16[128,1024]{1,0:T(8,128)(2,1)S(1)} collective-permute-done((bf16[128,1024]{1,0:T(8,128)(2,1)S(1)}, bf16[128,1024]{1,0:T(8,128)(2,1)S(1)}, u32[]{:S(2)}, u32[]{:S(2)}) %collective-permute-start.15) | collective-permute-done | bytes 262176 | tf_op jit(solution)/shard_map/ppermute | solution.py:328
  177.8 1.4 shard_map.141
  (6 shorter events, 0.0 us)
Async XLA Ops:
  0.6 25.4 %collective-permute-start = (bf16[128,2048]{1,0:T(8,128)(2,1)}, bf16[128,2048]{1,0:T(8,128)(2,1)S(1)}, u32[]{:S(2)}, u32[]{:S(2)}) collective-permute-start(bf16[128,2048]{1,0:T(8,128)(2,1)} %bitcast.43), channel_id=1, source_target_pairs={{98,0},{67,1},{32,2},{1,3},{2,32},{35,33},{64,34},{97,35},{34,64},... | collective-permute-start | bytes 1572872 | tf_op jit(solution)/shard_map/ppermute | solution.py:324
  6.0 20.0 %collective-permute-start.1 = (f32[16,128]{1,0:T(8,128)S(1)}, f32[16,128]{1,0:T(8,128)S(1)}, u32[]{:S(2)}, u32[]{:S(2)}) collective-permute-start(f32[16,128]{1,0:T(8,128)S(1)} %pad_maximum_fusion.1), channel_id=1, source_target_pairs={{98,0},{67,1},{32,2},{1,3},{2,32},{35,33},{64,34},{97,35},{34,64},... | collective-permute-start | bytes 24584 | tf_op jit(solution)/shard_map/ppermute | solution.py:324
  12.5 0.7 copy-start.2
  13.9 12.2 %all-to-all-start = ((f32[8,1,3200]{2,1,0:T(1,128)}), f32[8,1,3200]{2,1,0:T(1,128)S(1)}, u32[]{:S(2)}, u32[]{:S(2)}) async-start(f32[8,1,3200]{2,1,0:T(1,128)} %shard_map.131), calls=%async_computation | async-start | bytes 204800 | tf_op jit(solution)/shard_map/all_to_all | solution.py:331
  17.2 12.4 %copy-start.3 = (f32[1,2048]{1,0:T(1,128)S(1)}, f32[1,2048]{1,0:T(1,128)}, u32[]{:S(2)}) copy-start(f32[1,2048]{1,0:T(1,128)} %gain.2) | copy-start | bytes 24580
  20.6 29.0 %collective-permute-start.3 = (bf16[576,2048]{1,0:T(8,128)(2,1)}, bf16[576,2048]{1,0:T(8,128)(2,1)S(1)}, u32[]{:S(2)}, u32[]{:S(2)}) collective-permute-start(bf16[576,2048]{1,0:T(8,128)(2,1)} %pad_maximum_fusion.refs_0_), channel_id=1, source_target_pairs={{0,1},{1,0},{2,3},{3,2},{4,5},{5,4},{6,7},{7,6},{8,9},{9,8},{10,11... | collective-permute-start | bytes 7077896 | tf_op jit(solution)/shard_map/ppermute | solution.py:328
  26.0 52.4 %collective-permute-start.2 = (bf16[576,2048]{1,0:T(8,128)(2,1)}, bf16[576,2048]{1,0:T(8,128)(2,1)}, u32[]{:S(2)}, u32[]{:S(2)}) collective-permute-start(bf16[576,2048]{1,0:T(8,128)(2,1)} %pad_maximum_fusion.refs_0_), channel_id=1, source_target_pairs={{0,2},{2,0},{1,3},{3,1},{4,6},{6,4},{5,7},{7,5},{8,10},{10,8},{9,1... | collective-permute-start | bytes 7077896 | tf_op jit(solution)/shard_map/ppermute | solution.py:328
  32.3 52.2 %copy-start = (f32[1,3200]{1,0:T(1,128)S(1)}, f32[1,3200]{1,0:T(1,128)}, u32[]{:S(2)}) copy-start(f32[1,3200]{1,0:T(1,128)} %gain.3) | copy-start | bytes 38404
  32.3 52.2 %copy-start.1 = (f32[1,3200]{1,0:T(1,128)S(1)}, f32[1,3200]{1,0:T(1,128)}, u32[]{:S(2)}) copy-start(f32[1,3200]{1,0:T(1,128)} %weigh.1) | copy-start | bytes 38404
  32.3 52.2 %all-to-all-start.1 = ((bf16[8,56,2048]{2,1,0:T(8,128)(2,1)}), bf16[8,56,2048]{2,1,0:T(8,128)(2,1)}, u32[]{:S(2)}, u32[]{:S(2)}) async-start(bf16[8,56,2048]{2,1,0:T(8,128)(2,1)} %bitcast.31), calls=%async_computation.1 | async-start | bytes 3670016 | tf_op jit(solution)/shard_map/all_to_all | solution.py:331
  40.9 6.4 %collective-permute-start.4 = (bf16[100,3200]{1,0:T(8,128)(2,1)}, bf16[100,3200]{1,0:T(8,128)(2,1)S(1)}, u32[]{:S(2)}, u32[]{:S(2)}) collective-permute-start(bf16[100,3200]{1,0:T(8,128)(2,1)} %bitcast.36), channel_id=1, source_target_pairs={{0,1},{1,0},{2,3},{3,2},{4,5},{5,4},{6,7},{7,6},{8,9},{9,8},{10,11... | collective-permute-start | bytes 1920008 | tf_op jit(solution)/shard_map/ppermute | solution.py:328
  45.4 4.2 %collective-permute-start.5 = (bf16[100,3200]{1,0:T(8,128)(2,1)}, bf16[100,3200]{1,0:T(8,128)(2,1)S(1)}, u32[]{:S(2)}, u32[]{:S(2)}) collective-permute-start(bf16[100,3200]{1,0:T(8,128)(2,1)} %bitcast.38), channel_id=1, source_target_pairs={{0,1},{1,0},{2,3},{3,2},{4,5},{5,4},{6,7},{7,6},{8,9},{9,8},{10,11... | collective-permute-start | bytes 1920008 | tf_op jit(solution)/shard_map/ppermute | solution.py:328
  47.3 2.3 %copy-start.5 = (bf16[100,3200]{1,0:T(8,128)(2,1)}, bf16[100,3200]{1,0:T(8,128)(2,1)S(1)}, u32[]{:S(2)}) copy-start(bf16[100,3200]{1,0:T(8,128)(2,1)S(1)} %collective-permute-done.4.first_other) | copy-start | bytes 1920004
  49.6 28.8 %copy-start.6 = (bf16[100,3200]{1,0:T(8,128)(2,1)}, bf16[100,3200]{1,0:T(8,128)(2,1)S(1)}, u32[]{:S(2)}) copy-start(bf16[100,3200]{1,0:T(8,128)(2,1)S(1)} %collective-permute-done.5.second_other) | copy-start | bytes 1920004
  49.6 34.4 %copy-start.4 = (bf16[576,2048]{1,0:T(8,128)(2,1)}, bf16[576,2048]{1,0:T(8,128)(2,1)S(1)}, u32[]{:S(2)}) copy-start(bf16[576,2048]{1,0:T(8,128)(2,1)S(1)} %collective-permute-done.3.refs_1_) | copy-start | bytes 7077892
  78.4 10.4 %collective-permute-start.6 = (bf16[576,2048]{1,0:T(8,128)(2,1)}, bf16[576,2048]{1,0:T(8,128)(2,1)}, u32[]{:S(2)}, u32[]{:S(2)}) collective-permute-start(bf16[576,2048]{1,0:T(8,128)(2,1)} %collective-permute-done.2.refs_2_), channel_id=1, source_target_pairs={{0,1},{1,0},{2,3},{3,2},{4,5},{5,4},{6,7},{7,6},{8,9},{9,8},{10,11... | collective-permute-start | bytes 7077896 | tf_op jit(solution)/shard_map/ppermute | solution.py:328
  97.0 43.0 %all-to-all-start.2 = ((bf16[8,40,2048]{2,1,0:T(8,128)(2,1)}), bf16[8,40,2048]{2,1,0:T(8,128)(2,1)S(1)}, u32[]{:S(2)}, u32[]{:S(2)}) async-start(bf16[8,40,2048]{2,1,0:T(8,128)(2,1)} %bitcast.32), calls=%async_computation.2 | async-start | bytes 2621440 | tf_op jit(solution)/shard_map/all_to_all | solution.py:331
  105.2 7.8 %collective-permute-start.7 = (bf16[32,3200]{1,0:T(8,128)(2,1)S(1)}, bf16[32,3200]{1,0:T(8,128)(2,1)S(1)}, u32[]{:S(2)}, u32[]{:S(2)}) collective-permute-start(bf16[32,3200]{1,0:T(8,128)(2,1)S(1)} %get-tuple-element.39), channel_id=1, source_target_pairs={{0,2},{2,0},{1,3},{3,1},{4,6},{6,4},{5,7},{7,5},{8,10},{10,8},{9,1... | collective-permute-start | bytes 614408 | tf_op jit(solution)/shard_map/ppermute | solution.py:328
  113.1 21.7 %collective-permute-start.8 = (f32[8,3200]{1,0:T(8,128)S(1)}, f32[8,3200]{1,0:T(8,128)S(1)}, u32[]{:S(2)}, u32[]{:S(2)}) collective-permute-start(f32[8,3200]{1,0:T(8,128)S(1)} %get-tuple-element.40), channel_id=1, source_target_pairs={{0,384},{32,416},{64,448},{96,480},{128,0},{160,32},{192,64},{224,... | collective-permute-start | bytes 307208 | tf_op jit(solution)/shard_map/ppermute | solution.py:365
  117.5 15.7 %collective-permute-start.9 = (bf16[8,3200]{1,0:T(8,128)(2,1)S(1)}, bf16[8,3200]{1,0:T(8,128)(2,1)S(1)}, u32[]{:S(2)}, u32[]{:S(2)}) collective-permute-start(bf16[8,3200]{1,0:T(8,128)(2,1)S(1)} %get-tuple-element.41), channel_id=1, source_target_pairs={{0,416},{32,448},{64,480},{96,384},{128,32},{160,64},{192,96},{224... | collective-permute-start | bytes 153608 | tf_op jit(solution)/shard_map/ppermute | solution.py:365
  122.0 11.2 %collective-permute-start.10 = (bf16[8,3200]{1,0:T(8,128)(2,1)S(1)}, bf16[8,3200]{1,0:T(8,128)(2,1)S(1)}, u32[]{:S(2)}, u32[]{:S(2)}) collective-permute-start(bf16[8,3200]{1,0:T(8,128)(2,1)S(1)} %get-tuple-element.42), channel_id=1, source_target_pairs={{0,448},{32,480},{64,384},{96,416},{128,64},{160,96},{192,0},{224,... | collective-permute-start | bytes 153608 | tf_op jit(solution)/shard_map/ppermute | solution.py:365
  127.2 7.5 %collective-permute-start.11 = (bf16[8,3200]{1,0:T(8,128)(2,1)S(1)}, bf16[8,3200]{1,0:T(8,128)(2,1)S(1)}, u32[]{:S(2)}, u32[]{:S(2)}) collective-permute-start(bf16[8,3200]{1,0:T(8,128)(2,1)S(1)} %get-tuple-element.43), channel_id=1, source_target_pairs={{0,480},{32,384},{64,416},{96,448},{128,96},{160,0},{192,32},{224,... | collective-permute-start | bytes 153608 | tf_op jit(solution)/shard_map/ppermute | solution.py:365
  141.3 14.7 %collective-permute-start.12 = (bf16[128,1024]{1,0:T(8,128)(2,1)S(1)}, bf16[128,1024]{1,0:T(8,128)(2,1)S(1)}, u32[]{:S(2)}, u32[]{:S(2)}) collective-permute-start(bf16[128,1024]{1,0:T(8,128)(2,1)S(1)} %get-tuple-element.52), channel_id=1, source_target_pairs={{0,226},{1,195},{2,160},{3,129},{32,130},{33,163},{34,192},{35,225... | collective-permute-start | bytes 786440 | tf_op jit(solution)/shard_map/ppermute | solution.py:380
  148.6 15.9 %collective-permute-start.13 = (bf16[128,1024]{1,0:T(8,128)(2,1)S(1)}, bf16[128,1024]{1,0:T(8,128)(2,1)S(1)}, u32[]{:S(2)}, u32[]{:S(2)}) collective-permute-start(bf16[128,1024]{1,0:T(8,128)(2,1)S(1)} %get-tuple-element.53), channel_id=1, source_target_pairs={{0,224},{1,193},{2,162},{3,131},{32,128},{33,161},{34,194},{35,227... | collective-permute-start | bytes 786440 | tf_op jit(solution)/shard_map/ppermute | solution.py:380
  152.6 12.0 %all-to-all-start.3 = ((f32[8,1,3200]{2,1,0:T(1,128)}), f32[8,1,3200]{2,1,0:T(1,128)S(1)}, u32[]{:S(2)}, u32[]{:S(2)}) async-start(f32[8,1,3200]{2,1,0:T(1,128)} %shard_map.135), calls=%async_computation.3 | async-start | bytes 204800 | tf_op jit(solution)/shard_map/all_to_all | solution.py:331
  164.6 3.8 %collective-permute-start.14 = (bf16[128,1024]{1,0:T(8,128)(2,1)S(1)}, bf16[128,1024]{1,0:T(8,128)(2,1)S(1)}, u32[]{:S(2)}, u32[]{:S(2)}) collective-permute-start(bf16[128,1024]{1,0:T(8,128)(2,1)S(1)} %shard_map.139.left), channel_id=1, source_target_pairs={{0,1},{1,0},{2,3},{3,2},{4,5},{5,4},{6,7},{7,6},{8,9},{9,8},{10,11... | collective-permute-start | bytes 786440 | tf_op jit(solution)/shard_map/ppermute | solution.py:328
  168.4 9.4 %collective-permute-start.15 = (bf16[128,1024]{1,0:T(8,128)(2,1)S(1)}, bf16[128,1024]{1,0:T(8,128)(2,1)S(1)}, u32[]{:S(2)}, u32[]{:S(2)}) collective-permute-start(bf16[128,1024]{1,0:T(8,128)(2,1)S(1)} %shard_map.140.own), channel_id=1, source_target_pairs={{0,2},{2,0},{1,3},{3,1},{4,6},{6,4},{5,7},{7,5},{8,10},{10,8},{9,1... | collective-permute-start | bytes 786440 | tf_op jit(solution)/shard_map/ppermute | solution.py:328

commit v10 on v9

--- a/solution.py
+++ b/solution.py
@@ -101,47 +101,62 @@
 ANYWHERE = pl.BlockSpec(memory_space=pl.ANY)
 
 
-def expert_kernel(rows, *refs):
-    shards, out = refs[:4], refs[4]
-    rows_v, gate_v, up_v, down_v, hidden_v, out_v, row_sem, in_sem, out_sem = refs[5:]
-    count = shards[0].shape[0] // 3
-    row_copy = pltpu.make_async_copy(rows, rows_v, row_sem)
+def products(flat, gate_v, up_v):
+    gate = nt(flat, gate_v)
+    return (gate * jax.nn.sigmoid(gate) * nt(flat, up_v)).astype(BF16)
+
+
+def gate_up(shards, starts, stops, gate_v, up_v, sem):
+    copies, at = [], 0
+    for shard, start, stop in zip(shards, starts, stops):
+        count = shard.shape[0] // 3
+        for p, held in enumerate((gate_v, up_v)):
+            source = shard.at[pl.ds(p * count + start, stop - start)]
+            copies.append(pltpu.make_async_copy(source, held.at[pl.ds(at, stop - start)], sem.at[len(copies)]))
+        at += stop - start
+    return copies
+
+
+def first_kernel(arrived, own, other, across, rows, out, arrived_v, gate_v, up_v, row_sem, in_sem):
+    count = own.shape[0] // 3
+    row_copy = pltpu.make_async_copy(arrived, arrived_v, row_sem)
     row_copy.start()
-    copies = []
-    for s, shard in enumerate(shards):
-        for p, held in enumerate((gate_v, up_v, down_v)):
-            copies.append(
-                pltpu.make_async_copy(
-                    shard.at[pl.ds(p * count, count)], held.at[pl.ds(s * count, count)], in_sem.at[3 * s + p]
-                )
-            )
-    for s in (0, 1):
-        copies[3 * s].start()
-        copies[3 * s + 1].start()
+    copies = gate_up((own, other, across), (0, 0, 0), (count, count, out.shape[1] - 2 * count), gate_v, up_v, in_sem)
+    for copy in copies[:4]:
+        copy.start()
     row_copy.wait()
-    for s in (0, 1):
-        copies[3 * s].wait()
-        copies[3 * s + 1].wait()
-    for s in (2, 3):
-        copies[3 * s].start()
-        copies[3 * s + 1].start()
-    flat = rows_v[...]
+    wide = arrived_v[...].astype(F32)
+    flat = wide[:, ROWS - CAP :].reshape(rows.shape).astype(BF16)
+    rows[...] = flat
+    for copy in copies[:4]:
+        copy.wait()
+    for copy in copies[4:]:
+        copy.start()
     step = 256
-    seen = 2
-    for c in range(4 * count // step):
+    for c in range(out.shape[1] // step):
         if c == 1:
-            for s in range(4):
-                copies[3 * s + 2].start()
-        while seen * count < (c + 1) * step:
-            copies[3 * seen].wait()
-            copies[3 * seen + 1].wait()
-            seen += 1
+            for copy in copies[4:]:
+                copy.wait()
         block = slice(c * step, (c + 1) * step)
-        gate = nt(flat, gate_v[block, :]).reshape(-1, ROWS, step)[:, ROWS - CAP :].reshape(-1, step)
-        upval = nt(flat, up_v[block, :]).reshape(-1, ROWS, step)[:, ROWS - CAP :].reshape(-1, step)
-        hidden_v[:, block] = (gate * jax.nn.sigmoid(gate) * upval).astype(BF16)
-    for s in range(4):
-        copies[3 * s + 2].wait()
+        out[:, block] = products(flat, gate_v[block, :], up_v[block, :])
+
+
+def second_kernel(rows, begun, own, other, across, both, out, gate_v, up_v, down_v, hidden_v, out_v, in_sem, down_sem, out_sem):
+    count = own.shape[0] // 3
+    done = begun.shape[1]
+    copies = gate_up((across, both), (done - 2 * count, 0), (count, count), gate_v, up_v, in_sem)
+    downs = [
+        pltpu.make_async_copy(shard.at[pl.ds(2 * count, count)], down_v.at[pl.ds(s * count, count)], down_sem.at[s])
+        for s, shard in enumerate((own, other, across, both))
+    ]
+    for copy in copies + downs:
+        copy.start()
+    hidden_v[:, :done] = begun[...]
+    for copy in copies:
+        copy.wait()
+    hidden_v[:, done:] = products(rows[...], gate_v[...], up_v[...])
+    for copy in downs:
+        copy.wait()
     cols = out_v.shape[1] // 4
     leaving = []
     for j in range(4):
@@ -156,29 +171,45 @@
         copy.wait()
 
 
-def experts(rows, shards):
-    given, width = rows.shape
-    n = given // ROWS * CAP
-    count = shards[0].shape[0] // 3 * 4
+def experts(arrived, own, other, across, both):
+    groups, _, width = arrived.shape
+    n = groups * CAP
+    count = own.shape[0] // 3 * 4
+    begun, left = count // 3 * 2, count // 3
+    own, other, across = (in_hbm(shard) for shard in (own, other, across))
+    rows, hidden = pl.pallas_call(
+        first_kernel,
+        out_shape=(shaped((n, width)), shaped((n, begun))),
+        in_specs=[ANYWHERE] * 4,
+        out_specs=(VM, VM),
+        scratch_shapes=[
+            pltpu.VMEM(arrived.shape, BF16),
+            pltpu.VMEM((begun, width), BF16),
+            pltpu.VMEM((begun, width), BF16),
+            pltpu.SemaphoreType.DMA,
+            pltpu.SemaphoreType.DMA((6,)),
+        ],
+        compiler_params=pltpu.CompilerParams(vmem_limit_bytes=LARGE),
+        cost_estimate=pl.CostEstimate(flops=4 * n * width * begun, bytes_accessed=4 * begun * width, transcendentals=0),
+    )(in_hbm(arrived), own, other, across)
     return pl.pallas_call(
-        expert_kernel,
+        second_kernel,
         out_shape=pltpu.HBM((n, width), BF16),
-        in_specs=[ANYWHERE] * 5,
+        in_specs=[VM, VM] + [ANYWHERE] * 4,
         out_specs=ANYWHERE,
         scratch_shapes=[
-            pltpu.VMEM((given, width), BF16),
-            pltpu.VMEM((count, width), BF16),
-            pltpu.VMEM((count, width), BF16),
+            pltpu.VMEM((left, width), BF16),
+            pltpu.VMEM((left, width), BF16),
             pltpu.VMEM((count, width), BF16),
             pltpu.VMEM((n, count), BF16),
             pltpu.VMEM((n, width), BF16),
-            pltpu.SemaphoreType.DMA,
-            pltpu.SemaphoreType.DMA((12,)),
+            pltpu.SemaphoreType.DMA((4,)),
+            pltpu.SemaphoreType.DMA((4,)),
             pltpu.SemaphoreType.DMA((4,)),
         ],
         compiler_params=pltpu.CompilerParams(vmem_limit_bytes=LARGE),
-        cost_estimate=pl.CostEstimate(flops=6 * n * width * count, bytes_accessed=6 * count * width, transcendentals=0),
-    )(in_hbm(rows), *[in_hbm(shard) for shard in shards])
+        cost_estimate=pl.CostEstimate(flops=2 * n * width * (2 * left + count), bytes_accessed=4 * count * width, transcendentals=0),
+    )(rows, hidden, own, other, across, both)
 
 
 def combine_kernel(where, toks, high, low, made, kept, given):
@@ -198,11 +229,29 @@
     out[...] = (left[...].astype(F32) + right[...].astype(F32)).astype(out.dtype)
 
 
-def join_kernel(where, own, across, out):
+def join_kernel(where, own, across, out, sem):
     cols = own.shape[1]
     yl = where[1] // 2
-    for ref, half in ((own, yl), (across, 1 - yl)):
-        out[:, pl.ds(pl.multiple_of(half * cols, cols), cols)] = ref[...]
+    copies = [
+        pltpu.make_async_copy(ref, out.at[:, pl.ds(pl.multiple_of(half * cols, cols), cols)], sem.at[i])
+        for i, (ref, half) in enumerate(((own, yl), (across, 1 - yl)))
+    ]
+    for copy in copies:
+        copy.start()
+    for copy in copies:
+        copy.wait()
+
+
+def joined(where, own, across):
+    toks, cols = own.shape
+    return pl.pallas_call(
+        join_kernel,
+        out_shape=pltpu.HBM((toks, 2 * cols), BF16),
+        in_specs=[SM, VM, VM],
+        out_specs=ANYWHERE,
+        scratch_shapes=[pltpu.SemaphoreType.DMA((2,))],
+        compiler_params=pltpu.CompilerParams(vmem_limit_bytes=SMALL),
+    )(where, own, across)
 
 
 def spread_kernel(row, out):
@@ -350,14 +399,13 @@
     across, other, first_other, second_other = lax.optimization_barrier((across, other, first_other, second_other))
     both = shifted(across, "core", 1)
 
-    mine, theirs = encoder_part(where, arrived, image_gain, layer_scale, (first, first_other, second, second_other), n_yh)
-    both, theirs = lax.optimization_barrier((both, theirs))
-    made = experts(arrived.reshape(-1, width), (own, other, across, both))
+    made = experts(arrived, own, other, across, both)
     made, meta = lax.optimization_barrier((made, meta))
     n_rows = n_z * CAP
     returned = exchanged(made.reshape(n_z, CAP, width), "z").reshape(n_rows, width)
     high, low = call(weigh_kernel, (shaped((toks, n_rows)), shaped((toks, n_rows))), scalars=1)(where, meta)
 
+    mine, theirs = encoder_part(where, arrived, image_gain, layer_scale, (first, first_other, second, second_other), n_yh)
     mine, *theirs = call(
         fold_kernel, (shaped((n_z, dv), F32),) + tuple(shaped((n_z, dv)) for _ in range(n_yh - 1))
     )(mine, shifted(theirs, "yl", 1))
@@ -391,7 +439,7 @@
     part = call(add_kernel, shaped((toks, half)))(*pieces)
     spread, part = lax.optimization_barrier((exchanged(column, "z"), part))
     layer = call(add_kernel, shaped((toks, half)))(part, shifted(part, "core", 1))
-    trunk_out = call(join_kernel, shaped((toks, width)), scalars=1)(where, layer, shifted(layer, "yl", 1))
+    trunk_out = joined(where, layer, shifted(layer, "yl", 1))
 
     image_out = call(encoded_kernel, shaped((1, dv)))(spread)[None]
     return (trunk_out[None], image_out)

time: 180 us -> 181 us (level)
  starting transfers between devices: 93.9 us -> 98.5 us
  waiting for transfers between devices: 58 us -> 54.1 us
    ppermute x8, starting transfers between devices: 29.4 us -> 33.1 us  [shifted(): return lax.ppermute(value, axis, [(i, (i + by) % n) for i in range(n)])]
    all_to_all x4, waiting for transfers between devices: 5.05 us -> 1.82 us  [exchanged(): return lax.all_to_all(value, axis, split_axis=0, concat_axis=0, tiled=True)]
    ppermute x2, waiting for transfers between devices: 8.52 us -> 6.11 us  [body(): lax.ppermute(piece, ('pp',) + square, [(s * n_square + a * n_tp + t, (s +...]
    pallas_call x1 -> x3, Pallas kernels: 8.2 us -> 9.91 us  [the longest x1 4.54 us: experts(): pl.pallas_call(first_kernel, out_shape=(shaped((n, width)), shaped((n, be...]
    pallas_call x10 -> x9, Pallas kernels: 8.32 us -> 6.8 us  [run(): pl.pallas_call(kernel, out_shape=outs, in_specs=specs, out_specs=jax.tree...]
  transfers between devices with their start and end apart: 20 -> 20, of which waited for: 9 -> 9; matrix products, arithmetic and copies ran while one was open for 3% -> 3% of each run, Pallas kernels for 6% -> 8%
where the time goes in v10:
time: 181 us; the launch traced here: 180 us
  starting transfers between devices  98.5 us (54%)
  waiting for transfers between devices  54.1 us (30%)
  Pallas kernels  21 us (12%)
  other arithmetic  4.77 us (3%)
    ppermute x8, waiting for transfers between devices, shifted(): return lax.ppermute(value, axis, [(i, (i + by) % n) for i in range(n)])  43.9 us
    ppermute x8, starting transfers between devices, shifted(): return lax.ppermute(value, axis, [(i, (i + by) % n) for i in range(n)])  33.1 us
    all_to_all x4, starting transfers between devices, exchanged(): return lax.all_to_all(value, axis, split_axis=0, concat_axis=0, tiled=True)  25.1 us
    ppermute x4, starting transfers between devices, body(): lax.ppermute(part, ('pp', 'yh'), [(s * n_yh + h, (s - 1) % n_pp * n_yh +...  19.3 us
    ppermute x2, starting transfers between devices, body(): lax.ppermute(piece, ('pp',) + square, [(s * n_square + a * n_tp + t, (s +...  10.5 us
    ppermute x2, starting transfers between devices, fetched(): return lax.ppermute(value, square, pairs)  10.5 us
    pallas_call x9, Pallas kernels, run(): pl.pallas_call(kernel, out_shape=outs, in_specs=specs, out_specs=jax.tree...  6.8 us
    ppermute x2, waiting for transfers between devices, body(): lax.ppermute(piece, ('pp',) + square, [(s * n_square + a * n_tp + t, (s +...  6.11 us
  transfers between devices with their start and end apart: 20, of which 9 were waited for; matrix products, arithmetic and copies ran while one was open for 3% of the time, Pallas kernels for 8%

profile of v10, /device:TPU:1, one launch (start us, length us, event | category | flops | bytes accessed | tf_op | source)
XLA Modules:
  0.0 180.1 jit_solution(1114237754783477420)
XLA Ops:
  0.6 4.0 %collective-permute-start = (bf16[128,2048]{1,0:T(8,128)(2,1)}, bf16[128,2048]{1,0:T(8,128)(2,1)S(1)}, u32[]{:S(2)}, u32[]{:S(2)}) collective-permute-start(bf16[128,2048]{1,0:T(8,128)(2,1)} %bitcast.42), channel_id=1, source_target_pairs={{98,0},{67,1},{32,2},{1,3},{2,32},{35,33},{64,34},{97,35},{34,64},... | collective-permute-start | bytes 1572872 | tf_op jit(solution)/shard_map/ppermute | solution.py:373
  4.7 0.7 convert_bitcast_fusion
  5.4 0.7 pad_maximum_fusion.1
  6.0 6.4 %collective-permute-start.1 = (f32[16,128]{1,0:T(8,128)S(1)}, f32[16,128]{1,0:T(8,128)S(1)}, u32[]{:S(2)}, u32[]{:S(2)}) collective-permute-start(f32[16,128]{1,0:T(8,128)S(1)} %pad_maximum_fusion.1), channel_id=1, source_target_pairs={{98,0},{67,1},{32,2},{1,3},{2,32},{35,33},{64,34},{97,35},{34,64},... | collective-permute-start | bytes 24584 | tf_op jit(solution)/shard_map/ppermute | solution.py:373
  12.5 0.0 copy-start.2
  12.5 0.7 copy-done.2
  13.2 0.7 shard_map.131
  13.9 3.4 %all-to-all-start = ((f32[8,1,3200]{2,1,0:T(1,128)}), f32[8,1,3200]{2,1,0:T(1,128)S(1)}, u32[]{:S(2)}, u32[]{:S(2)}) async-start(f32[8,1,3200]{2,1,0:T(1,128)} %shard_map.131), calls=%async_computation | async-start | bytes 204800 | tf_op jit(solution)/shard_map/all_to_all | solution.py:380
  17.2 0.0 copy-start.3
  17.2 3.3 %pad_maximum_fusion.own = bf16[576,2048]{1,0:T(8,128)(2,1)} fusion(bf16[192,2048]{1,0:T(8,128)(2,1)} %bitcast.32, bf16[192,2048]{1,0:T(8,128)(2,1)} %bitcast.33, bf16[192,2048]{1,0:T(8,128)(2,1)} %bitcast.34), kind=kLoop, calls=%fused_computation | loop fusion | flops 7077888 | bytes 4718592 | tf_op jit(solution)/shard_map/concatenate | solution.py:386
  20.6 5.4 %collective-permute-start.3 = (bf16[576,2048]{1,0:T(8,128)(2,1)}, bf16[576,2048]{1,0:T(8,128)(2,1)}, u32[]{:S(2)}, u32[]{:S(2)}) collective-permute-start(bf16[576,2048]{1,0:T(8,128)(2,1)} %pad_maximum_fusion.own), channel_id=1, source_target_pairs={{0,1},{1,0},{2,3},{3,2},{4,5},{5,4},{6,7},{7,6},{8,9},{9,8},{10,11... | collective-permute-start | bytes 7077896 | tf_op jit(solution)/shard_map/ppermute | solution.py:377
  25.9 0.1 pad_add_fusion.where
  26.0 0.0 collective-permute-done.1.meta
  26.0 0.0 all-to-all-done.ring
  26.0 0.0 collective-permute-done.toks
  26.0 3.5 %collective-permute-start.2 = (bf16[576,2048]{1,0:T(8,128)(2,1)}, bf16[576,2048]{1,0:T(8,128)(2,1)}, u32[]{:S(2)}, u32[]{:S(2)}) collective-permute-start(bf16[576,2048]{1,0:T(8,128)(2,1)} %pad_maximum_fusion.own), channel_id=1, source_target_pairs={{0,2},{2,0},{1,3},{3,1},{4,6},{6,4},{5,7},{7,5},{8,10},{10,8},{9,1... | collective-permute-start | bytes 7077896 | tf_op jit(solution)/shard_map/ppermute | solution.py:377
  29.6 2.6 %shard_map.132 = bf16[448,2048]{1,0:T(8,128)(2,1)} custom-call(s32[3]{0:T(128)S(1)} %pad_add_fusion.where, f32[16,128]{1,0:T(8,128)S(1)} %collective-permute-done.1.meta, bf16[128,2048]{1,0:T(8,128)(2,1)S(1)} %collective-permute-done.toks, f32[1,2048]{1,0:T(1,128)S(1)} %copy-done.3, f32[8,1,3200]{2,1,0:T(1,128)S(1)} %all-to-all-done.ring), custom_call_target="tpu_custom_call" | custom-call | tf_op jit(solution)/shard_map/pallas_call | solution.py:32
  32.2 8.6 %all-to-all-start.1 = ((bf16[8,56,2048]{2,1,0:T(8,128)(2,1)}), bf16[8,56,2048]{2,1,0:T(8,128)(2,1)}, u32[]{:S(2)}, u32[]{:S(2)}) async-start(bf16[8,56,2048]{2,1,0:T(8,128)(2,1)} %bitcast.30), calls=%async_computation.1 | async-start | bytes 3670016 | tf_op jit(solution)/shard_map/all_to_all | solution.py:380
  40.8 4.4 %collective-permute-start.4 = (bf16[100,3200]{1,0:T(8,128)(2,1)S(1)}, bf16[100,3200]{1,0:T(8,128)(2,1)S(1)}, u32[]{:S(2)}, u32[]{:S(2)}) collective-permute-start(bf16[100,3200]{1,0:T(8,128)(2,1)S(1)} %bitcast.36), channel_id=1, source_target_pairs={{0,1},{1,0},{2,3},{3,2},{4,5},{5,4},{6,7},{7,6},{8,9},{9,8},{10,11... | collective-permute-start | bytes 1920008 | tf_op jit(solution)/shard_map/ppermute | solution.py:377
  45.3 1.9 %collective-permute-start.5 = (bf16[100,3200]{1,0:T(8,128)(2,1)S(1)}, bf16[100,3200]{1,0:T(8,128)(2,1)S(1)}, u32[]{:S(2)}, u32[]{:S(2)}) collective-permute-start(bf16[100,3200]{1,0:T(8,128)(2,1)S(1)} %bitcast.38), channel_id=1, source_target_pairs={{0,1},{1,0},{2,3},{3,2},{4,5},{5,4},{6,7},{7,6},{8,9},{9,8},{10,11... | collective-permute-start | bytes 1920008 | tf_op jit(solution)/shard_map/ppermute | solution.py:377
  47.2 0.0 collective-permute-done.4.first_other
  47.2 0.0 copy-start.6
  47.2 2.1 %collective-permute-done.5.second_other = bf16[100,3200]{1,0:T(8,128)(2,1)S(1)} collective-permute-done((bf16[100,3200]{1,0:T(8,128)(2,1)S(1)}, bf16[100,3200]{1,0:T(8,128)(2,1)S(1)}, u32[]{:S(2)}, u32[]{:S(2)}) %collective-permute-start.5) | collective-permute-done | bytes 640032 | tf_op jit(solution)/shard_map/ppermute | solution.py:377
  49.3 0.0 collective-permute-done.3.other
  49.3 0.0 copy-done.6
  49.3 29.1 %collective-permute-done.2.across = bf16[576,2048]{1,0:T(8,128)(2,1)} collective-permute-done((bf16[576,2048]{1,0:T(8,128)(2,1)}, bf16[576,2048]{1,0:T(8,128)(2,1)}, u32[]{:S(2)}, u32[]{:S(2)}) %collective-permute-start.2) | collective-permute-done | bytes 2359328 | tf_op jit(solution)/shard_map/ppermute | solution.py:377
  78.4 5.6 %collective-permute-start.11 = (bf16[576,2048]{1,0:T(8,128)(2,1)}, bf16[576,2048]{1,0:T(8,128)(2,1)S(1)}, u32[]{:S(2)}, u32[]{:S(2)}) collective-permute-start(bf16[576,2048]{1,0:T(8,128)(2,1)} %collective-permute-done.2.across), channel_id=1, source_target_pairs={{0,1},{1,0},{2,3},{3,2},{4,5},{5,4},{6,7},{7,6},{8,9},{9,8},{10,11... | collective-permute-start | bytes 7077896 | tf_op jit(solution)/shard_map/ppermute | solution.py:377
  84.0 0.4 all-to-all-done.1.arrived
  84.3 4.5 %shard_map.136 = (bf16[320,2048]{1,0:T(8,128)(2,1)S(1)}, bf16[320,512]{1,0:T(8,128)(2,1)S(1)}) custom-call(bf16[8,56,2048]{2,1,0:T(8,128)(2,1)} %all-to-all-done.1.arrived, bf16[576,2048]{1,0:T(8,128)(2,1)} %pad_maximum_fusion.own, bf16[576,2048]{1,0:T(8,128)(2,1)} %collective-permute-done.3.other, bf16[576,2048]{1,0:T(8,128)(2,1)} %collective-permute-done.2.across), custom_call_target="tpu_custom_call" | custom-call | flops 1342177280 | bytes 4194304 | tf_op jit(solution)/shard_map/pallas_call | solution.py:180
  88.9 0.0 collective-permute-done.11.both
  88.9 4.0 %shard_map.137 = bf16[320,2048]{1,0:T(8,128)(2,1)} custom-call(bf16[320,2048]{1,0:T(8,128)(2,1)S(1)} %get-tuple-element.44.rows, bf16[320,512]{1,0:T(8,128)(2,1)S(1)} %get-tuple-element.45.begun, bf16[576,2048]{1,0:T(8,128)(2,1)} %pad_maximum_fusion.own, bf16[576,2048]{1,0:T(8,128)(2,1)} %collective-permute-done.3.other, ...), custom_call_target="tpu_custom_call" | custom-call | flops 1677721600 | bytes 6291456 | tf_op jit(solution)/shard_map/pallas_call | solution.py:195
  92.9 0.0 copy-start
  92.9 0.0 copy-start.1
  93.0 8.2 %all-to-all-start.2 = ((bf16[8,40,2048]{2,1,0:T(8,128)(2,1)}), bf16[8,40,2048]{2,1,0:T(8,128)(2,1)S(1)}, u32[]{:S(2)}, u32[]{:S(2)}) async-start(bf16[8,40,2048]{2,1,0:T(8,128)(2,1)} %bitcast.31), calls=%async_computation.2 | async-start | bytes 2621440 | tf_op jit(solution)/shard_map/all_to_all | solution.py:380
  101.1 0.0 copy-done
  101.1 4.3 %shard_map.133 = (f32[32,3200]{1,0:T(8,128)S(1)}, bf16[32,3200]{1,0:T(8,128)(2,1)S(1)}) custom-call(s32[3]{0:T(128)S(1)} %pad_add_fusion.where, bf16[8,56,2048]{2,1,0:T(8,128)(2,1)} %all-to-all-done.1.arrived, f32[1,3200]{1,0:T(1,128)S(1)} %copy-done, f32[1,3200]{1,0:T(1,128)S(1)} %copy-done.1, bf16[100,3200]{1,0:T(8,128)(2,1)} %bitcast.35, ...), custom_call_target="tpu_custom_call" | custom-call | flops 163840000 | bytes 2560000 | tf_op jit(solution)/shard_map/pallas_call | solution.py:313
  105.4 3.4 %collective-permute-start.6 = (bf16[32,3200]{1,0:T(8,128)(2,1)S(1)}, bf16[32,3200]{1,0:T(8,128)(2,1)S(1)}, u32[]{:S(2)}, u32[]{:S(2)}) collective-permute-start(bf16[32,3200]{1,0:T(8,128)(2,1)S(1)} %get-tuple-element.37), channel_id=1, source_target_pairs={{0,2},{2,0},{1,3},{3,1},{4,6},{6,4},{5,7},{7,5},{8,10},{10,8},{9,1... | collective-permute-start | bytes 614408 | tf_op jit(solution)/shard_map/ppermute | solution.py:377
  108.8 4.7 %collective-permute-done.6.came = bf16[32,3200]{1,0:T(8,128)(2,1)S(1)} collective-permute-done((bf16[32,3200]{1,0:T(8,128)(2,1)S(1)}, bf16[32,3200]{1,0:T(8,128)(2,1)S(1)}, u32[]{:S(2)}, u32[]{:S(2)}) %collective-permute-start.6) | collective-permute-done | bytes 204832 | tf_op jit(solution)/shard_map/ppermute | solution.py:377
  113.6 4.4 %collective-permute-start.7 = (f32[8,3200]{1,0:T(8,128)S(1)}, f32[8,3200]{1,0:T(8,128)S(1)}, u32[]{:S(2)}, u32[]{:S(2)}) collective-permute-start(f32[8,3200]{1,0:T(8,128)S(1)} %get-tuple-element.38), channel_id=1, source_target_pairs={{0,384},{32,416},{64,448},{96,480},{128,0},{160,32},{192,64},{224,... | collective-permute-start | bytes 307208 | tf_op jit(solution)/shard_map/ppermute | solution.py:413
  118.0 4.5 %collective-permute-start.8 = (bf16[8,3200]{1,0:T(8,128)(2,1)S(1)}, bf16[8,3200]{1,0:T(8,128)(2,1)S(1)}, u32[]{:S(2)}, u32[]{:S(2)}) collective-permute-start(bf16[8,3200]{1,0:T(8,128)(2,1)S(1)} %get-tuple-element.39), channel_id=1, source_target_pairs={{0,416},{32,448},{64,480},{96,384},{128,32},{160,64},{192,96},{224... | collective-permute-start | bytes 153608 | tf_op jit(solution)/shard_map/ppermute | solution.py:413
  122.5 5.2 %collective-permute-start.9 = (bf16[8,3200]{1,0:T(8,128)(2,1)S(1)}, bf16[8,3200]{1,0:T(8,128)(2,1)S(1)}, u32[]{:S(2)}, u32[]{:S(2)}) collective-permute-start(bf16[8,3200]{1,0:T(8,128)(2,1)S(1)} %get-tuple-element.40), channel_id=1, source_target_pairs={{0,448},{32,480},{64,384},{96,416},{128,64},{160,96},{192,0},{224,... | collective-permute-start | bytes 153608 | tf_op jit(solution)/shard_map/ppermute | solution.py:413
  127.7 5.2 %collective-permute-start.10 = (bf16[8,3200]{1,0:T(8,128)(2,1)S(1)}, bf16[8,3200]{1,0:T(8,128)(2,1)S(1)}, u32[]{:S(2)}, u32[]{:S(2)}) collective-permute-start(bf16[8,3200]{1,0:T(8,128)(2,1)S(1)} %get-tuple-element.41), channel_id=1, source_target_pairs={{0,480},{32,384},{64,416},{96,448},{128,96},{160,0},{192,32},{224,... | collective-permute-start | bytes 153608 | tf_op jit(solution)/shard_map/ppermute | solution.py:413
  132.9 0.0 collective-permute-done.8.refs_0_
  132.9 0.0 collective-permute-done.9.refs_1_
  132.9 2.3 %collective-permute-done.10.refs_2_ = bf16[8,3200]{1,0:T(8,128)(2,1)S(1)} collective-permute-done((bf16[8,3200]{1,0:T(8,128)(2,1)S(1)}, bf16[8,3200]{1,0:T(8,128)(2,1)S(1)}, u32[]{:S(2)}, u32[]{:S(2)}) %collective-permute-start.10) | collective-permute-done | bytes 51232 | tf_op jit(solution)/shard_map/ppermute | solution.py:413
  135.2 0.0 collective-permute-done.7.held
  135.2 0.7 shard_map.135
  135.9 0.8 shard_map.138
  136.7 0.0 all-to-all-done.2
  136.7 1.3 shard_map.139
  138.0 6.5 %collective-permute-start.12 = (bf16[128,1024]{1,0:T(8,128)(2,1)S(1)}, bf16[128,1024]{1,0:T(8,128)(2,1)S(1)}, u32[]{:S(2)}, u32[]{:S(2)}) collective-permute-start(bf16[128,1024]{1,0:T(8,128)(2,1)S(1)} %get-tuple-element.52), channel_id=1, source_target_pairs={{0,226},{1,195},{2,160},{3,129},{32,130},{33,163},{34,192},{35,225... | collective-permute-start | bytes 786440 | tf_op jit(solution)/shard_map/ppermute | solution.py:428
  144.5 4.0 %collective-permute-start.13 = (bf16[128,1024]{1,0:T(8,128)(2,1)S(1)}, bf16[128,1024]{1,0:T(8,128)(2,1)S(1)}, u32[]{:S(2)}, u32[]{:S(2)}) collective-permute-start(bf16[128,1024]{1,0:T(8,128)(2,1)S(1)} %get-tuple-element.53), channel_id=1, source_target_pairs={{0,224},{1,193},{2,162},{3,131},{32,128},{33,161},{34,194},{35,227... | collective-permute-start | bytes 786440 | tf_op jit(solution)/shard_map/ppermute | solution.py:428
  148.5 5.0 %all-to-all-start.3 = ((f32[8,1,3200]{2,1,0:T(1,128)}), f32[8,1,3200]{2,1,0:T(1,128)S(1)}, u32[]{:S(2)}, u32[]{:S(2)}) async-start(f32[8,1,3200]{2,1,0:T(1,128)} %shard_map.135), calls=%async_computation.3 | async-start | bytes 204800 | tf_op jit(solution)/shard_map/all_to_all | solution.py:380
  153.5 0.0 collective-permute-done.12.left
  153.5 6.1 %collective-permute-done.13.right = bf16[128,1024]{1,0:T(8,128)(2,1)S(1)} collective-permute-done((bf16[128,1024]{1,0:T(8,128)(2,1)S(1)}, bf16[128,1024]{1,0:T(8,128)(2,1)S(1)}, u32[]{:S(2)}, u32[]{:S(2)}) %collective-permute-start.13) | collective-permute-done | bytes 262176 | tf_op jit(solution)/shard_map/ppermute | solution.py:428
  159.6 0.1 shard_map.140.left
  159.7 1.4 all-to-all-done.3.spread
  161.1 7.0 %collective-permute-start.14 = (bf16[128,1024]{1,0:T(8,128)(2,1)S(1)}, bf16[128,1024]{1,0:T(8,128)(2,1)S(1)}, u32[]{:S(2)}, u32[]{:S(2)}) collective-permute-start(bf16[128,1024]{1,0:T(8,128)(2,1)S(1)} %shard_map.140.left), channel_id=1, source_target_pairs={{0,1},{1,0},{2,3},{3,2},{4,5},{5,4},{6,7},{7,6},{8,9},{9,8},{10,11... | collective-permute-start | bytes 786440 | tf_op jit(solution)/shard_map/ppermute | solution.py:377
  168.1 1.1 collective-permute-done.14.right
  169.3 0.1 shard_map.141.own
  169.3 1.9 %collective-permute-start.15 = (bf16[128,1024]{1,0:T(8,128)(2,1)S(1)}, bf16[128,1024]{1,0:T(8,128)(2,1)S(1)}, u32[]{:S(2)}, u32[]{:S(2)}) collective-permute-start(bf16[128,1024]{1,0:T(8,128)(2,1)S(1)} %shard_map.141.own), channel_id=1, source_target_pairs={{0,2},{2,0},{1,3},{3,1},{4,6},{6,4},{5,7},{7,5},{8,10},{10,8},{9,1... | collective-permute-start | bytes 786440 | tf_op jit(solution)/shard_map/ppermute | solution.py:377
  171.3 0.6 shard_map.143
  171.9 6.9 %collective-permute-done.15.across = bf16[128,1024]{1,0:T(8,128)(2,1)S(1)} collective-permute-done((bf16[128,1024]{1,0:T(8,128)(2,1)S(1)}, bf16[128,1024]{1,0:T(8,128)(2,1)S(1)}, u32[]{:S(2)}, u32[]{:S(2)}) %collective-permute-start.15) | collective-permute-done | bytes 262176 | tf_op jit(solution)/shard_map/ppermute | solution.py:377
  178.7 1.4 shard_map.142
  (9 shorter events, 0.1 us)
Async XLA Ops:
  0.6 25.4 %collective-permute-start = (bf16[128,2048]{1,0:T(8,128)(2,1)}, bf16[128,2048]{1,0:T(8,128)(2,1)S(1)}, u32[]{:S(2)}, u32[]{:S(2)}) collective-permute-start(bf16[128,2048]{1,0:T(8,128)(2,1)} %bitcast.42), channel_id=1, source_target_pairs={{98,0},{67,1},{32,2},{1,3},{2,32},{35,33},{64,34},{97,35},{34,64},... | collective-permute-start | bytes 1572872 | tf_op jit(solution)/shard_map/ppermute | solution.py:373
  6.0 20.0 %collective-permute-start.1 = (f32[16,128]{1,0:T(8,128)S(1)}, f32[16,128]{1,0:T(8,128)S(1)}, u32[]{:S(2)}, u32[]{:S(2)}) collective-permute-start(f32[16,128]{1,0:T(8,128)S(1)} %pad_maximum_fusion.1), channel_id=1, source_target_pairs={{98,0},{67,1},{32,2},{1,3},{2,32},{35,33},{64,34},{97,35},{34,64},... | collective-permute-start | bytes 24584 | tf_op jit(solution)/shard_map/ppermute | solution.py:373
  12.5 0.7 copy-start.2
  13.9 12.2 %all-to-all-start = ((f32[8,1,3200]{2,1,0:T(1,128)}), f32[8,1,3200]{2,1,0:T(1,128)S(1)}, u32[]{:S(2)}, u32[]{:S(2)}) async-start(f32[8,1,3200]{2,1,0:T(1,128)} %shard_map.131), calls=%async_computation | async-start | bytes 204800 | tf_op jit(solution)/shard_map/all_to_all | solution.py:380
  17.2 12.3 %copy-start.3 = (f32[1,2048]{1,0:T(1,128)S(1)}, f32[1,2048]{1,0:T(1,128)}, u32[]{:S(2)}) copy-start(f32[1,2048]{1,0:T(1,128)} %gain.2) | copy-start | bytes 24580
  20.6 28.7 %collective-permute-start.3 = (bf16[576,2048]{1,0:T(8,128)(2,1)}, bf16[576,2048]{1,0:T(8,128)(2,1)}, u32[]{:S(2)}, u32[]{:S(2)}) collective-permute-start(bf16[576,2048]{1,0:T(8,128)(2,1)} %pad_maximum_fusion.own), channel_id=1, source_target_pairs={{0,1},{1,0},{2,3},{3,2},{4,5},{5,4},{6,7},{7,6},{8,9},{9,8},{10,11... | collective-permute-start | bytes 7077896 | tf_op jit(solution)/shard_map/ppermute | solution.py:377
  26.0 52.4 %collective-permute-start.2 = (bf16[576,2048]{1,0:T(8,128)(2,1)}, bf16[576,2048]{1,0:T(8,128)(2,1)}, u32[]{:S(2)}, u32[]{:S(2)}) collective-permute-start(bf16[576,2048]{1,0:T(8,128)(2,1)} %pad_maximum_fusion.own), channel_id=1, source_target_pairs={{0,2},{2,0},{1,3},{3,1},{4,6},{6,4},{5,7},{7,5},{8,10},{10,8},{9,1... | collective-permute-start | bytes 7077896 | tf_op jit(solution)/shard_map/ppermute | solution.py:377
  32.2 8.6 %copy-start.4 = (bf16[1,3200,100]{1,2,0:T(8,128)(2,1)S(1)}, bf16[1,3200,100]{1,2,0:T(8,128)(2,1)}, u32[]{:S(2)}) copy-start(bf16[1,3200,100]{1,2,0:T(8,128)(2,1)} %param.21) | copy-start | bytes 1920004
  32.2 13.1 %copy-start.5 = (bf16[1,100,3200]{2,1,0:T(8,128)(2,1)S(1)}, bf16[1,100,3200]{2,1,0:T(8,128)(2,1)}, u32[]{:S(2)}) copy-start(bf16[1,100,3200]{2,1,0:T(8,128)(2,1)} %param.22) | copy-start | bytes 1920004
  32.2 52.2 %all-to-all-start.1 = ((bf16[8,56,2048]{2,1,0:T(8,128)(2,1)}), bf16[8,56,2048]{2,1,0:T(8,128)(2,1)}, u32[]{:S(2)}, u32[]{:S(2)}) async-start(bf16[8,56,2048]{2,1,0:T(8,128)(2,1)} %bitcast.30), calls=%async_computation.1 | async-start | bytes 3670016 | tf_op jit(solution)/shard_map/all_to_all | solution.py:380
  40.8 6.4 %collective-permute-start.4 = (bf16[100,3200]{1,0:T(8,128)(2,1)S(1)}, bf16[100,3200]{1,0:T(8,128)(2,1)S(1)}, u32[]{:S(2)}, u32[]{:S(2)}) collective-permute-start(bf16[100,3200]{1,0:T(8,128)(2,1)S(1)} %bitcast.36), channel_id=1, source_target_pairs={{0,1},{1,0},{2,3},{3,2},{4,5},{5,4},{6,7},{7,6},{8,9},{9,8},{10,11... | collective-permute-start | bytes 1920008 | tf_op jit(solution)/shard_map/ppermute | solution.py:377
  45.3 4.0 %collective-permute-start.5 = (bf16[100,3200]{1,0:T(8,128)(2,1)S(1)}, bf16[100,3200]{1,0:T(8,128)(2,1)S(1)}, u32[]{:S(2)}, u32[]{:S(2)}) collective-permute-start(bf16[100,3200]{1,0:T(8,128)(2,1)S(1)} %bitcast.38), channel_id=1, source_target_pairs={{0,1},{1,0},{2,3},{3,2},{4,5},{5,4},{6,7},{7,6},{8,9},{9,8},{10,11... | collective-permute-start | bytes 1920008 | tf_op jit(solution)/shard_map/ppermute | solution.py:377
  47.2 2.1 %copy-start.6 = (bf16[100,3200]{1,0:T(8,128)(2,1)}, bf16[100,3200]{1,0:T(8,128)(2,1)S(1)}, u32[]{:S(2)}) copy-start(bf16[100,3200]{1,0:T(8,128)(2,1)S(1)} %collective-permute-done.4.first_other) | copy-start | bytes 1920004
  49.3 29.1 %copy-start.7 = (bf16[100,3200]{1,0:T(8,128)(2,1)}, bf16[100,3200]{1,0:T(8,128)(2,1)S(1)}, u32[]{:S(2)}) copy-start(bf16[100,3200]{1,0:T(8,128)(2,1)S(1)} %collective-permute-done.5.second_other) | copy-start | bytes 1920004
  78.4 10.5 %collective-permute-start.11 = (bf16[576,2048]{1,0:T(8,128)(2,1)}, bf16[576,2048]{1,0:T(8,128)(2,1)S(1)}, u32[]{:S(2)}, u32[]{:S(2)}) collective-permute-start(bf16[576,2048]{1,0:T(8,128)(2,1)} %collective-permute-done.2.across), channel_id=1, source_target_pairs={{0,1},{1,0},{2,3},{3,2},{4,5},{5,4},{6,7},{7,6},{8,9},{9,8},{10,11... | collective-permute-start | bytes 7077896 | tf_op jit(solution)/shard_map/ppermute | solution.py:377
  92.9 8.2 %copy-start = (f32[1,3200]{1,0:T(1,128)S(1)}, f32[1,3200]{1,0:T(1,128)}, u32[]{:S(2)}) copy-start(f32[1,3200]{1,0:T(1,128)} %gain.3) | copy-start | bytes 38404
  92.9 8.2 %copy-start.1 = (f32[1,3200]{1,0:T(1,128)S(1)}, f32[1,3200]{1,0:T(1,128)}, u32[]{:S(2)}) copy-start(f32[1,3200]{1,0:T(1,128)} %weigh.1) | copy-start | bytes 38404
  93.0 43.8 %all-to-all-start.2 = ((bf16[8,40,2048]{2,1,0:T(8,128)(2,1)}), bf16[8,40,2048]{2,1,0:T(8,128)(2,1)S(1)}, u32[]{:S(2)}, u32[]{:S(2)}) async-start(bf16[8,40,2048]{2,1,0:T(8,128)(2,1)} %bitcast.31), calls=%async_computation.2 | async-start | bytes 2621440 | tf_op jit(solution)/shard_map/all_to_all | solution.py:380
  105.4 8.1 %collective-permute-start.6 = (bf16[32,3200]{1,0:T(8,128)(2,1)S(1)}, bf16[32,3200]{1,0:T(8,128)(2,1)S(1)}, u32[]{:S(2)}, u32[]{:S(2)}) collective-permute-start(bf16[32,3200]{1,0:T(8,128)(2,1)S(1)} %get-tuple-element.37), channel_id=1, source_target_pairs={{0,2},{2,0},{1,3},{3,1},{4,6},{6,4},{5,7},{7,5},{8,10},{10,8},{9,1... | collective-permute-start | bytes 614408 | tf_op jit(solution)/shard_map/ppermute | solution.py:377
  113.6 21.6 %collective-permute-start.7 = (f32[8,3200]{1,0:T(8,128)S(1)}, f32[8,3200]{1,0:T(8,128)S(1)}, u32[]{:S(2)}, u32[]{:S(2)}) collective-permute-start(f32[8,3200]{1,0:T(8,128)S(1)} %get-tuple-element.38), channel_id=1, source_target_pairs={{0,384},{32,416},{64,448},{96,480},{128,0},{160,32},{192,64},{224,... | collective-permute-start | bytes 307208 | tf_op jit(solution)/shard_map/ppermute | solution.py:413
  118.0 14.9 %collective-permute-start.8 = (bf16[8,3200]{1,0:T(8,128)(2,1)S(1)}, bf16[8,3200]{1,0:T(8,128)(2,1)S(1)}, u32[]{:S(2)}, u32[]{:S(2)}) collective-permute-start(bf16[8,3200]{1,0:T(8,128)(2,1)S(1)} %get-tuple-element.39), channel_id=1, source_target_pairs={{0,416},{32,448},{64,480},{96,384},{128,32},{160,64},{192,96},{224... | collective-permute-start | bytes 153608 | tf_op jit(solution)/shard_map/ppermute | solution.py:413
  122.5 10.4 %collective-permute-start.9 = (bf16[8,3200]{1,0:T(8,128)(2,1)S(1)}, bf16[8,3200]{1,0:T(8,128)(2,1)S(1)}, u32[]{:S(2)}, u32[]{:S(2)}) collective-permute-start(bf16[8,3200]{1,0:T(8,128)(2,1)S(1)} %get-tuple-element.40), channel_id=1, source_target_pairs={{0,448},{32,480},{64,384},{96,416},{128,64},{160,96},{192,0},{224,... | collective-permute-start | bytes 153608 | tf_op jit(solution)/shard_map/ppermute | solution.py:413
  127.7 7.5 %collective-permute-start.10 = (bf16[8,3200]{1,0:T(8,128)(2,1)S(1)}, bf16[8,3200]{1,0:T(8,128)(2,1)S(1)}, u32[]{:S(2)}, u32[]{:S(2)}) collective-permute-start(bf16[8,3200]{1,0:T(8,128)(2,1)S(1)} %get-tuple-element.41), channel_id=1, source_target_pairs={{0,480},{32,384},{64,416},{96,448},{128,96},{160,0},{192,32},{224,... | collective-permute-start | bytes 153608 | tf_op jit(solution)/shard_map/ppermute | solution.py:413
  138.0 15.5 %collective-permute-start.12 = (bf16[128,1024]{1,0:T(8,128)(2,1)S(1)}, bf16[128,1024]{1,0:T(8,128)(2,1)S(1)}, u32[]{:S(2)}, u32[]{:S(2)}) collective-permute-start(bf16[128,1024]{1,0:T(8,128)(2,1)S(1)} %get-tuple-element.52), channel_id=1, source_target_pairs={{0,226},{1,195},{2,160},{3,129},{32,130},{33,163},{34,192},{35,225... | collective-permute-start | bytes 786440 | tf_op jit(solution)/shard_map/ppermute | solution.py:428
  144.5 15.1 %collective-permute-start.13 = (bf16[128,1024]{1,0:T(8,128)(2,1)S(1)}, bf16[128,1024]{1,0:T(8,128)(2,1)S(1)}, u32[]{:S(2)}, u32[]{:S(2)}) collective-permute-start(bf16[128,1024]{1,0:T(8,128)(2,1)S(1)} %get-tuple-element.53), channel_id=1, source_target_pairs={{0,224},{1,193},{2,162},{3,131},{32,128},{33,161},{34,194},{35,227... | collective-permute-start | bytes 786440 | tf_op jit(solution)/shard_map/ppermute | solution.py:428
  148.5 12.6 %all-to-all-start.3 = ((f32[8,1,3200]{2,1,0:T(1,128)}), f32[8,1,3200]{2,1,0:T(1,128)S(1)}, u32[]{:S(2)}, u32[]{:S(2)}) async-start(f32[8,1,3200]{2,1,0:T(1,128)} %shard_map.135), calls=%async_computation.3 | async-start | bytes 204800 | tf_op jit(solution)/shard_map/all_to_all | solution.py:380
  161.1 8.1 %collective-permute-start.14 = (bf16[128,1024]{1,0:T(8,128)(2,1)S(1)}, bf16[128,1024]{1,0:T(8,128)(2,1)S(1)}, u32[]{:S(2)}, u32[]{:S(2)}) collective-permute-start(bf16[128,1024]{1,0:T(8,128)(2,1)S(1)} %shard_map.140.left), channel_id=1, source_target_pairs={{0,1},{1,0},{2,3},{3,2},{4,5},{5,4},{6,7},{7,6},{8,9},{9,8},{10,11... | collective-permute-start | bytes 786440 | tf_op jit(solution)/shard_map/ppermute | solution.py:377
  169.3 9.4 %collective-permute-start.15 = (bf16[128,1024]{1,0:T(8,128)(2,1)S(1)}, bf16[128,1024]{1,0:T(8,128)(2,1)S(1)}, u32[]{:S(2)}, u32[]{:S(2)}) collective-permute-start(bf16[128,1024]{1,0:T(8,128)(2,1)S(1)} %shard_map.141.own), channel_id=1, source_target_pairs={{0,2},{2,0},{1,3},{3,1},{4,6},{6,4},{5,7},{7,5},{8,10},{10,8},{9,1... | collective-permute-start | bytes 786440 | tf_op jit(solution)/shard_map/ppermute | solution.py:377

commit v11 on v10

--- a/solution.py
+++ b/solution.py
@@ -396,27 +396,21 @@
 
     first, second = fc_in[0].T, fc_out[0]
     first_other, second_other = shifted(first, "core", 1), shifted(second, "core", 1)
-    across, other, first_other, second_other = lax.optimization_barrier((across, other, first_other, second_other))
+    n_rows = n_z * CAP
+    meta, second_other = lax.optimization_barrier((meta, second_other))
+    high, low = call(weigh_kernel, (shaped((toks, n_rows)), shaped((toks, n_rows))), scalars=1)(where, meta)
+    across, other, first_other, second_other, high, low = lax.optimization_barrier(
+        (across, other, first_other, second_other, high, low)
+    )
     both = shifted(across, "core", 1)
 
     made = experts(arrived, own, other, across, both)
-    made, meta = lax.optimization_barrier((made, meta))
-    n_rows = n_z * CAP
     returned = exchanged(made.reshape(n_z, CAP, width), "z").reshape(n_rows, width)
-    high, low = call(weigh_kernel, (shaped((toks, n_rows)), shaped((toks, n_rows))), scalars=1)(where, meta)
-
     mine, theirs = encoder_part(where, arrived, image_gain, layer_scale, (first, first_other, second, second_other), n_yh)
     mine, *theirs = call(
         fold_kernel, (shaped((n_z, dv), F32),) + tuple(shaped((n_z, dv)) for _ in range(n_yh - 1))
     )(mine, shifted(theirs, "yl", 1))
-    parts = [
-        lax.ppermute(
-            part,
-            ("pp", "yh"),
-            [(s * n_yh + h, (s - 1) % n_pp * n_yh + (h + k) % n_yh) for s in range(n_pp) for h in range(n_yh)],
-        )
-        for k, part in enumerate([mine, *theirs])
-    ]
+    parts = [mine] + [shifted(part, "yh", k + 1) for k, part in enumerate(theirs)]
     column = call(column_kernel, shaped((n_z, 1, dv), F32))(*parts)
 
     column, returned = lax.optimization_barrier((column, returned))
@@ -441,7 +435,8 @@
     layer = call(add_kernel, shaped((toks, half)))(part, shifted(part, "core", 1))
     trunk_out = joined(where, layer, shifted(layer, "yl", 1))
 
-    image_out = call(encoded_kernel, shaped((1, dv)))(spread)[None]
+    encoded = call(encoded_kernel, shaped((1, dv)))(spread)
+    image_out = shifted(encoded[None], "pp", -1)
     return (trunk_out[None], image_out)
 
 

time: 181 us -> 177 us (0.978)
  starting transfers between devices: 98.5 us -> 92.7 us
    ppermute x4 -> x0, starting transfers between devices: 19.3 us -> none  [body(): lax.ppermute(part, ('pp', 'yh'), [(s * n_yh + h, (s - 1) % n_pp * n_yh +...]
    ppermute x8 -> x12, starting transfers between devices: 33.1 us -> 47.5 us  [shifted(): return lax.ppermute(value, axis, [(i, (i + by) % n) for i in range(n)])]
    all_to_all x4, waiting for transfers between devices: 1.82 us -> 5.4 us  [exchanged(): return lax.all_to_all(value, axis, split_axis=0, concat_axis=0, tiled=True)]
    ppermute x2, waiting for transfers between devices: 6.11 us -> 8.52 us  [body(): lax.ppermute(piece, ('pp',) + square, [(s * n_square + a * n_tp + t, (s +...]
    ppermute x8 -> x12, waiting for transfers between devices: 43.9 us -> 41.6 us  [shifted(): return lax.ppermute(value, axis, [(i, (i + by) % n) for i in range(n)])]
    ppermute x4 -> x0, waiting for transfers between devices: 2.31 us -> none  [body(): lax.ppermute(part, ('pp', 'yh'), [(s * n_yh + h, (s - 1) % n_pp * n_yh +...]
  transfers between devices with their start and end apart: 20 -> 20, of which waited for: 9 -> 10; matrix products, arithmetic and copies ran while one was open for 3% -> 3% of each run, Pallas kernels for 8% -> 8%
where the time goes in v11:
time: 177 us; the launch traced here: 176 us
  starting transfers between devices  92.7 us (52%)
  waiting for transfers between devices  55.5 us (31%)
  Pallas kernels  20.4 us (12%)
  other arithmetic  4.77 us (3%)
    ppermute x12, starting transfers between devices, shifted(): return lax.ppermute(value, axis, [(i, (i + by) % n) for i in range(n)])  47.5 us
    ppermute x12, waiting for transfers between devices, shifted(): return lax.ppermute(value, axis, [(i, (i + by) % n) for i in range(n)])  41.6 us
    all_to_all x4, starting transfers between devices, exchanged(): return lax.all_to_all(value, axis, split_axis=0, concat_axis=0, tiled=True)  23.5 us
    ppermute x2, starting transfers between devices, body(): lax.ppermute(piece, ('pp',) + square, [(s * n_square + a * n_tp + t, (s +...  11.3 us
    ppermute x2, starting transfers between devices, fetched(): return lax.ppermute(value, square, pairs)  10.5 us
    ppermute x2, waiting for transfers between devices, body(): lax.ppermute(piece, ('pp',) + square, [(s * n_square + a * n_tp + t, (s +...  8.52 us
    pallas_call x9, Pallas kernels, run(): pl.pallas_call(kernel, out_shape=outs, in_specs=specs, out_specs=jax.tree...  6.21 us
    all_to_all x4, waiting for transfers between devices, exchanged(): return lax.all_to_all(value, axis, split_axis=0, concat_axis=0, tiled=True)  5.4 us
  transfers between devices with their start and end apart: 20, of which 10 were waited for; matrix products, arithmetic and copies ran while one was open for 3% of the time, Pallas kernels for 8%

profile of v11, /device:TPU:1, one launch (start us, length us, event | category | flops | bytes accessed | tf_op | source)
XLA Modules:
  0.0 175.7 jit_solution(18384013349203969208)
XLA Ops:
  0.6 4.0 %collective-permute-start = (bf16[128,2048]{1,0:T(8,128)(2,1)}, bf16[128,2048]{1,0:T(8,128)(2,1)S(1)}, u32[]{:S(2)}, u32[]{:S(2)}) collective-permute-start(bf16[128,2048]{1,0:T(8,128)(2,1)} %bitcast.42), channel_id=1, source_target_pairs={{98,0},{67,1},{32,2},{1,3},{2,32},{35,33},{64,34},{97,35},{34,64},... | collective-permute-start | bytes 1572872 | tf_op jit(solution)/shard_map/ppermute | solution.py:373
  4.7 0.7 convert_bitcast_fusion
  5.4 0.7 pad_maximum_fusion.1
  6.0 6.4 %collective-permute-start.1 = (f32[16,128]{1,0:T(8,128)S(1)}, f32[16,128]{1,0:T(8,128)S(1)}, u32[]{:S(2)}, u32[]{:S(2)}) collective-permute-start(f32[16,128]{1,0:T(8,128)S(1)} %pad_maximum_fusion.1), channel_id=1, source_target_pairs={{98,0},{67,1},{32,2},{1,3},{2,32},{35,33},{64,34},{97,35},{34,64},... | collective-permute-start | bytes 24584 | tf_op jit(solution)/shard_map/ppermute | solution.py:373
  12.5 0.0 copy-start.2
  12.5 0.7 copy-done.2
  13.2 0.7 shard_map.131
  13.9 3.4 %all-to-all-start = ((f32[8,1,3200]{2,1,0:T(1,128)}), f32[8,1,3200]{2,1,0:T(1,128)S(1)}, u32[]{:S(2)}, u32[]{:S(2)}) async-start(f32[8,1,3200]{2,1,0:T(1,128)} %shard_map.131), calls=%async_computation | async-start | bytes 204800 | tf_op jit(solution)/shard_map/all_to_all | solution.py:380
  17.2 0.0 copy-start.3
  17.2 3.3 %pad_maximum_fusion.own = bf16[576,2048]{1,0:T(8,128)(2,1)} fusion(bf16[192,2048]{1,0:T(8,128)(2,1)} %bitcast.33, bf16[192,2048]{1,0:T(8,128)(2,1)} %bitcast.34, bf16[192,2048]{1,0:T(8,128)(2,1)} %bitcast.35), kind=kLoop, calls=%fused_computation | loop fusion | flops 7077888 | bytes 4718592 | tf_op jit(solution)/shard_map/concatenate | solution.py:386
  20.6 5.4 %collective-permute-start.3 = (bf16[576,2048]{1,0:T(8,128)(2,1)}, bf16[576,2048]{1,0:T(8,128)(2,1)}, u32[]{:S(2)}, u32[]{:S(2)}) collective-permute-start(bf16[576,2048]{1,0:T(8,128)(2,1)} %pad_maximum_fusion.own), channel_id=1, source_target_pairs={{0,1},{1,0},{2,3},{3,2},{4,5},{5,4},{6,7},{7,6},{8,9},{9,8},{10,11... | collective-permute-start | bytes 7077896 | tf_op jit(solution)/shard_map/ppermute | solution.py:377
  25.9 0.1 pad_add_fusion.where
  26.0 0.0 collective-permute-done.1.meta
  26.0 0.0 all-to-all-done.ring
  26.0 0.0 collective-permute-done.toks
  26.0 3.5 %collective-permute-start.2 = (bf16[576,2048]{1,0:T(8,128)(2,1)}, bf16[576,2048]{1,0:T(8,128)(2,1)}, u32[]{:S(2)}, u32[]{:S(2)}) collective-permute-start(bf16[576,2048]{1,0:T(8,128)(2,1)} %pad_maximum_fusion.own), channel_id=1, source_target_pairs={{0,2},{2,0},{1,3},{3,1},{4,6},{6,4},{5,7},{7,5},{8,10},{10,8},{9,1... | collective-permute-start | bytes 7077896 | tf_op jit(solution)/shard_map/ppermute | solution.py:377
  29.6 2.6 %shard_map.132 = bf16[448,2048]{1,0:T(8,128)(2,1)} custom-call(s32[3]{0:T(128)S(1)} %pad_add_fusion.where, f32[16,128]{1,0:T(8,128)S(1)} %collective-permute-done.1.meta, bf16[128,2048]{1,0:T(8,128)(2,1)S(1)} %collective-permute-done.toks, f32[1,2048]{1,0:T(1,128)S(1)} %copy-done.3, f32[8,1,3200]{2,1,0:T(1,128)S(1)} %all-to-all-done.ring), custom_call_target="tpu_custom_call" | custom-call | tf_op jit(solution)/shard_map/pallas_call | solution.py:32
  32.2 8.6 %all-to-all-start.1 = ((bf16[8,56,2048]{2,1,0:T(8,128)(2,1)}), bf16[8,56,2048]{2,1,0:T(8,128)(2,1)}, u32[]{:S(2)}, u32[]{:S(2)}) async-start(bf16[8,56,2048]{2,1,0:T(8,128)(2,1)} %bitcast.31), calls=%async_computation.1 | async-start | bytes 3670016 | tf_op jit(solution)/shard_map/all_to_all | solution.py:380
  40.8 0.0 copy-done.5
  40.8 4.4 %collective-permute-start.5 = (bf16[100,3200]{1,0:T(8,128)(2,1)S(1)}, bf16[100,3200]{1,0:T(8,128)(2,1)}, u32[]{:S(2)}, u32[]{:S(2)}) collective-permute-start(bf16[100,3200]{1,0:T(8,128)(2,1)S(1)} %bitcast.39), channel_id=1, source_target_pairs={{0,1},{1,0},{2,3},{3,2},{4,5},{5,4},{6,7},{7,6},{8,9},{9,8},{10,11... | collective-permute-start | bytes 1920008 | tf_op jit(solution)/shard_map/ppermute | solution.py:377
  45.3 0.0 copy-done.4
  45.3 1.9 %collective-permute-start.4 = (bf16[100,3200]{1,0:T(8,128)(2,1)S(1)}, bf16[100,3200]{1,0:T(8,128)(2,1)S(1)}, u32[]{:S(2)}, u32[]{:S(2)}) collective-permute-start(bf16[100,3200]{1,0:T(8,128)(2,1)S(1)} %bitcast.37), channel_id=1, source_target_pairs={{0,1},{1,0},{2,3},{3,2},{4,5},{5,4},{6,7},{7,6},{8,9},{9,8},{10,11... | collective-permute-start | bytes 1920008 | tf_op jit(solution)/shard_map/ppermute | solution.py:377
  47.2 0.0 collective-permute-done.5.second_other
  47.2 0.8 shard_map.133
  48.0 1.2 collective-permute-done.4.first_other
  49.3 0.0 collective-permute-done.3.other
  49.3 29.1 %collective-permute-done.2.across = bf16[576,2048]{1,0:T(8,128)(2,1)} collective-permute-done((bf16[576,2048]{1,0:T(8,128)(2,1)}, bf16[576,2048]{1,0:T(8,128)(2,1)}, u32[]{:S(2)}, u32[]{:S(2)}) %collective-permute-start.2) | collective-permute-done | bytes 2359328 | tf_op jit(solution)/shard_map/ppermute | solution.py:377
  78.4 0.0 copy-done.6
  78.4 5.6 %collective-permute-start.10 = (bf16[576,2048]{1,0:T(8,128)(2,1)}, bf16[576,2048]{1,0:T(8,128)(2,1)S(1)}, u32[]{:S(2)}, u32[]{:S(2)}) collective-permute-start(bf16[576,2048]{1,0:T(8,128)(2,1)} %collective-permute-done.2.across), channel_id=1, source_target_pairs={{0,1},{1,0},{2,3},{3,2},{4,5},{5,4},{6,7},{7,6},{8,9},{9,8},{10,11... | collective-permute-start | bytes 7077896 | tf_op jit(solution)/shard_map/ppermute | solution.py:377
  84.0 0.4 all-to-all-done.1.arrived
  84.4 4.5 %shard_map.137 = (bf16[320,2048]{1,0:T(8,128)(2,1)S(1)}, bf16[320,512]{1,0:T(8,128)(2,1)S(1)}) custom-call(bf16[8,56,2048]{2,1,0:T(8,128)(2,1)} %all-to-all-done.1.arrived, bf16[576,2048]{1,0:T(8,128)(2,1)} %pad_maximum_fusion.own, bf16[576,2048]{1,0:T(8,128)(2,1)} %collective-permute-done.3.other, bf16[576,2048]{1,0:T(8,128)(2,1)} %collective-permute-done.2.across), custom_call_target="tpu_custom_call" | custom-call | flops 1342177280 | bytes 4194304 | tf_op jit(solution)/shard_map/pallas_call | solution.py:180
  88.9 0.0 collective-permute-done.10.both
  88.9 4.0 %shard_map.138 = bf16[320,2048]{1,0:T(8,128)(2,1)} custom-call(bf16[320,2048]{1,0:T(8,128)(2,1)S(1)} %get-tuple-element.50.rows, bf16[320,512]{1,0:T(8,128)(2,1)S(1)} %get-tuple-element.51.begun, bf16[576,2048]{1,0:T(8,128)(2,1)} %pad_maximum_fusion.own, bf16[576,2048]{1,0:T(8,128)(2,1)} %collective-permute-done.3.other, ...), custom_call_target="tpu_custom_call" | custom-call | flops 1677721600 | bytes 6291456 | tf_op jit(solution)/shard_map/pallas_call | solution.py:195
  92.9 0.0 copy-start
  92.9 0.0 copy-start.1
  92.9 8.1 %all-to-all-start.2 = ((bf16[8,40,2048]{2,1,0:T(8,128)(2,1)}), bf16[8,40,2048]{2,1,0:T(8,128)(2,1)S(1)}, u32[]{:S(2)}, u32[]{:S(2)}) async-start(bf16[8,40,2048]{2,1,0:T(8,128)(2,1)} %bitcast.32), calls=%async_computation.2 | async-start | bytes 2621440 | tf_op jit(solution)/shard_map/all_to_all | solution.py:380
  101.1 4.3 %shard_map.134 = (f32[32,3200]{1,0:T(8,128)S(1)}, bf16[32,3200]{1,0:T(8,128)(2,1)S(1)}) custom-call(s32[3]{0:T(128)S(1)} %pad_add_fusion.where, bf16[8,56,2048]{2,1,0:T(8,128)(2,1)} %all-to-all-done.1.arrived, f32[1,3200]{1,0:T(1,128)S(1)} %copy-done, f32[1,3200]{1,0:T(1,128)S(1)} %copy-done.1, bf16[100,3200]{1,0:T(8,128)(2,1)} %bitcast.36, ...), custom_call_target="tpu_custom_call" | custom-call | flops 163840000 | bytes 2560000 | tf_op jit(solution)/shard_map/pallas_call | solution.py:313
  105.4 3.4 %collective-permute-start.6 = (bf16[32,3200]{1,0:T(8,128)(2,1)S(1)}, bf16[32,3200]{1,0:T(8,128)(2,1)S(1)}, u32[]{:S(2)}, u32[]{:S(2)}) collective-permute-start(bf16[32,3200]{1,0:T(8,128)(2,1)S(1)} %get-tuple-element.43), channel_id=1, source_target_pairs={{0,2},{2,0},{1,3},{3,1},{4,6},{6,4},{5,7},{7,5},{8,10},{10,8},{9,1... | collective-permute-start | bytes 614408 | tf_op jit(solution)/shard_map/ppermute | solution.py:377
  108.8 4.7 %collective-permute-done.6.came = bf16[32,3200]{1,0:T(8,128)(2,1)S(1)} collective-permute-done((bf16[32,3200]{1,0:T(8,128)(2,1)S(1)}, bf16[32,3200]{1,0:T(8,128)(2,1)S(1)}, u32[]{:S(2)}, u32[]{:S(2)}) %collective-permute-start.6) | collective-permute-done | bytes 204832 | tf_op jit(solution)/shard_map/ppermute | solution.py:377
  113.6 4.3 %collective-permute-start.7 = (bf16[8,3200]{1,0:T(8,128)(2,1)S(1)}, bf16[8,3200]{1,0:T(8,128)(2,1)S(1)}, u32[]{:S(2)}, u32[]{:S(2)}) collective-permute-start(bf16[8,3200]{1,0:T(8,128)(2,1)S(1)} %get-tuple-element.45), channel_id=1, source_target_pairs={{0,32},{32,64},{64,96},{96,0},{1,33},{33,65},{65,97},{97,1},{2,34}... | collective-permute-start | bytes 153608 | tf_op jit(solution)/shard_map/ppermute | solution.py:377
  117.8 5.2 %collective-permute-start.8 = (bf16[8,3200]{1,0:T(8,128)(2,1)S(1)}, bf16[8,3200]{1,0:T(8,128)(2,1)S(1)}, u32[]{:S(2)}, u32[]{:S(2)}) collective-permute-start(bf16[8,3200]{1,0:T(8,128)(2,1)S(1)} %get-tuple-element.46), channel_id=1, source_target_pairs={{0,64},{32,96},{64,0},{96,32},{1,65},{33,97},{65,1},{97,33},{2,66}... | collective-permute-start | bytes 153608 | tf_op jit(solution)/shard_map/ppermute | solution.py:377
  123.0 5.2 %collective-permute-start.9 = (bf16[8,3200]{1,0:T(8,128)(2,1)S(1)}, bf16[8,3200]{1,0:T(8,128)(2,1)S(1)}, u32[]{:S(2)}, u32[]{:S(2)}) collective-permute-start(bf16[8,3200]{1,0:T(8,128)(2,1)S(1)} %get-tuple-element.47), channel_id=1, source_target_pairs={{0,96},{32,0},{64,32},{96,64},{1,97},{33,1},{65,33},{97,65},{2,98}... | collective-permute-start | bytes 153608 | tf_op jit(solution)/shard_map/ppermute | solution.py:377
  128.2 0.0 collective-permute-done.7.refs_0_
  128.3 0.0 collective-permute-done.8.refs_1_
  128.3 1.9 %collective-permute-done.9.refs_2_ = bf16[8,3200]{1,0:T(8,128)(2,1)S(1)} collective-permute-done((bf16[8,3200]{1,0:T(8,128)(2,1)S(1)}, bf16[8,3200]{1,0:T(8,128)(2,1)S(1)}, u32[]{:S(2)}, u32[]{:S(2)}) %collective-permute-start.9) | collective-permute-done | bytes 51232 | tf_op jit(solution)/shard_map/ppermute | solution.py:377
  130.2 0.7 shard_map.136
  130.9 5.0 %all-to-all-done.2 = bf16[8,40,2048]{2,1,0:T(8,128)(2,1)S(1)} async-done(((bf16[8,40,2048]{2,1,0:T(8,128)(2,1)}), bf16[8,40,2048]{2,1,0:T(8,128)(2,1)S(1)}, u32[]{:S(2)}, u32[]{:S(2)}) %all-to-all-start.2) | async-done | bytes 1310752 | tf_op jit(solution)/shard_map/all_to_all | solution.py:380
  135.9 1.3 shard_map.139
  137.2 7.3 %collective-permute-start.11 = (bf16[128,1024]{1,0:T(8,128)(2,1)S(1)}, bf16[128,1024]{1,0:T(8,128)(2,1)S(1)}, u32[]{:S(2)}, u32[]{:S(2)}) collective-permute-start(bf16[128,1024]{1,0:T(8,128)(2,1)S(1)} %get-tuple-element.56), channel_id=1, source_target_pairs={{0,226},{1,195},{2,160},{3,129},{32,130},{33,163},{34,192},{35,225... | collective-permute-start | bytes 786440 | tf_op jit(solution)/shard_map/ppermute | solution.py:422
  144.5 4.0 %collective-permute-start.12 = (bf16[128,1024]{1,0:T(8,128)(2,1)S(1)}, bf16[128,1024]{1,0:T(8,128)(2,1)S(1)}, u32[]{:S(2)}, u32[]{:S(2)}) collective-permute-start(bf16[128,1024]{1,0:T(8,128)(2,1)S(1)} %get-tuple-element.57), channel_id=1, source_target_pairs={{0,224},{1,193},{2,162},{3,131},{32,128},{33,161},{34,194},{35,227... | collective-permute-start | bytes 786440 | tf_op jit(solution)/shard_map/ppermute | solution.py:422
  148.5 3.4 %all-to-all-start.3 = ((f32[8,1,3200]{2,1,0:T(1,128)}), f32[8,1,3200]{2,1,0:T(1,128)S(1)}, u32[]{:S(2)}, u32[]{:S(2)}) async-start(f32[8,1,3200]{2,1,0:T(1,128)} %shard_map.136), calls=%async_computation.3 | async-start | bytes 204800 | tf_op jit(solution)/shard_map/all_to_all | solution.py:380
  151.9 0.0 collective-permute-done.11.left
  151.9 8.5 %collective-permute-done.12.right = bf16[128,1024]{1,0:T(8,128)(2,1)S(1)} collective-permute-done((bf16[128,1024]{1,0:T(8,128)(2,1)S(1)}, bf16[128,1024]{1,0:T(8,128)(2,1)S(1)}, u32[]{:S(2)}, u32[]{:S(2)}) %collective-permute-start.12) | collective-permute-done | bytes 262176 | tf_op jit(solution)/shard_map/ppermute | solution.py:422
  160.4 0.1 shard_map.140.left
  160.5 0.0 all-to-all-done.3.spread
  160.5 2.6 %collective-permute-start.13 = (bf16[128,1024]{1,0:T(8,128)(2,1)S(1)}, bf16[128,1024]{1,0:T(8,128)(2,1)S(1)}, u32[]{:S(2)}, u32[]{:S(2)}) collective-permute-start(bf16[128,1024]{1,0:T(8,128)(2,1)S(1)} %shard_map.140.left), channel_id=1, source_target_pairs={{0,1},{1,0},{2,3},{3,2},{4,5},{5,4},{6,7},{7,6},{8,9},{9,8},{10,11... | collective-permute-start | bytes 786440 | tf_op jit(solution)/shard_map/ppermute | solution.py:377
  163.1 1.1 collective-permute-done.13.right
  164.2 0.1 shard_map.141.own
  164.3 2.6 %collective-permute-start.14 = (bf16[128,1024]{1,0:T(8,128)(2,1)S(1)}, bf16[128,1024]{1,0:T(8,128)(2,1)S(1)}, u32[]{:S(2)}, u32[]{:S(2)}) collective-permute-start(bf16[128,1024]{1,0:T(8,128)(2,1)S(1)} %shard_map.141.own), channel_id=1, source_target_pairs={{0,2},{2,0},{1,3},{3,1},{4,6},{6,4},{5,7},{7,5},{8,10},{10,8},{9,1... | collective-permute-start | bytes 786440 | tf_op jit(solution)/shard_map/ppermute | solution.py:377
  167.0 3.4 %collective-permute-start.15 = (bf16[1,1,3200]{2,1,0:T(2,128)(2,1)S(1)}, bf16[1,1,3200]{2,1,0:T(2,128)(2,1)S(1)}, u32[]{:S(2)}, u32[]{:S(2)}) collective-permute-start(bf16[1,1,3200]{2,1,0:T(2,128)(2,1)S(1)} %bitcast.30), channel_id=1, source_target_pairs={{0,384},{128,0},{256,128},{384,256},{1,385},{129,1},{257,129},{385... | collective-permute-start | bytes 19208 | tf_op jit(solution)/shard_map/ppermute | solution.py:377
  170.4 1.4 collective-permute-done.15
  171.7 2.0 %collective-permute-done.14.across = bf16[128,1024]{1,0:T(8,128)(2,1)S(1)} collective-permute-done((bf16[128,1024]{1,0:T(8,128)(2,1)S(1)}, bf16[128,1024]{1,0:T(8,128)(2,1)S(1)}, u32[]{:S(2)}, u32[]{:S(2)}) %collective-permute-start.14) | collective-permute-done | bytes 262176 | tf_op jit(solution)/shard_map/ppermute | solution.py:377
  173.7 1.4 shard_map.142
  175.1 0.6 copy.15
  (8 shorter events, 0.1 us)
Async XLA Ops:
  0.6 25.4 %collective-permute-start = (bf16[128,2048]{1,0:T(8,128)(2,1)}, bf16[128,2048]{1,0:T(8,128)(2,1)S(1)}, u32[]{:S(2)}, u32[]{:S(2)}) collective-permute-start(bf16[128,2048]{1,0:T(8,128)(2,1)} %bitcast.42), channel_id=1, source_target_pairs={{98,0},{67,1},{32,2},{1,3},{2,32},{35,33},{64,34},{97,35},{34,64},... | collective-permute-start | bytes 1572872 | tf_op jit(solution)/shard_map/ppermute | solution.py:373
  6.0 20.0 %collective-permute-start.1 = (f32[16,128]{1,0:T(8,128)S(1)}, f32[16,128]{1,0:T(8,128)S(1)}, u32[]{:S(2)}, u32[]{:S(2)}) collective-permute-start(f32[16,128]{1,0:T(8,128)S(1)} %pad_maximum_fusion.1), channel_id=1, source_target_pairs={{98,0},{67,1},{32,2},{1,3},{2,32},{35,33},{64,34},{97,35},{34,64},... | collective-permute-start | bytes 24584 | tf_op jit(solution)/shard_map/ppermute | solution.py:373
  12.5 0.7 copy-start.2
  13.9 12.2 %all-to-all-start = ((f32[8,1,3200]{2,1,0:T(1,128)}), f32[8,1,3200]{2,1,0:T(1,128)S(1)}, u32[]{:S(2)}, u32[]{:S(2)}) async-start(f32[8,1,3200]{2,1,0:T(1,128)} %shard_map.131), calls=%async_computation | async-start | bytes 204800 | tf_op jit(solution)/shard_map/all_to_all | solution.py:380
  17.2 12.3 %copy-start.3 = (f32[1,2048]{1,0:T(1,128)S(1)}, f32[1,2048]{1,0:T(1,128)}, u32[]{:S(2)}) copy-start(f32[1,2048]{1,0:T(1,128)} %gain.2) | copy-start | bytes 24580
  20.6 28.7 %collective-permute-start.3 = (bf16[576,2048]{1,0:T(8,128)(2,1)}, bf16[576,2048]{1,0:T(8,128)(2,1)}, u32[]{:S(2)}, u32[]{:S(2)}) collective-permute-start(bf16[576,2048]{1,0:T(8,128)(2,1)} %pad_maximum_fusion.own), channel_id=1, source_target_pairs={{0,1},{1,0},{2,3},{3,2},{4,5},{5,4},{6,7},{7,6},{8,9},{9,8},{10,11... | collective-permute-start | bytes 7077896 | tf_op jit(solution)/shard_map/ppermute | solution.py:377
  26.0 52.4 %collective-permute-start.2 = (bf16[576,2048]{1,0:T(8,128)(2,1)}, bf16[576,2048]{1,0:T(8,128)(2,1)}, u32[]{:S(2)}, u32[]{:S(2)}) collective-permute-start(bf16[576,2048]{1,0:T(8,128)(2,1)} %pad_maximum_fusion.own), channel_id=1, source_target_pairs={{0,2},{2,0},{1,3},{3,1},{4,6},{6,4},{5,7},{7,5},{8,10},{10,8},{9,1... | collective-permute-start | bytes 7077896 | tf_op jit(solution)/shard_map/ppermute | solution.py:377
  32.2 8.6 %copy-start.5 = (bf16[1,100,3200]{2,1,0:T(8,128)(2,1)S(1)}, bf16[1,100,3200]{2,1,0:T(8,128)(2,1)}, u32[]{:S(2)}) copy-start(bf16[1,100,3200]{2,1,0:T(8,128)(2,1)} %param.22) | copy-start | bytes 1920004
  32.2 13.1 %copy-start.4 = (bf16[1,3200,100]{1,2,0:T(8,128)(2,1)S(1)}, bf16[1,3200,100]{1,2,0:T(8,128)(2,1)}, u32[]{:S(2)}) copy-start(bf16[1,3200,100]{1,2,0:T(8,128)(2,1)} %param.21) | copy-start | bytes 1920004
  32.2 52.2 %all-to-all-start.1 = ((bf16[8,56,2048]{2,1,0:T(8,128)(2,1)}), bf16[8,56,2048]{2,1,0:T(8,128)(2,1)}, u32[]{:S(2)}, u32[]{:S(2)}) async-start(bf16[8,56,2048]{2,1,0:T(8,128)(2,1)} %bitcast.31), calls=%async_computation.1 | async-start | bytes 3670016 | tf_op jit(solution)/shard_map/all_to_all | solution.py:380
  40.8 6.4 %collective-permute-start.5 = (bf16[100,3200]{1,0:T(8,128)(2,1)S(1)}, bf16[100,3200]{1,0:T(8,128)(2,1)}, u32[]{:S(2)}, u32[]{:S(2)}) collective-permute-start(bf16[100,3200]{1,0:T(8,128)(2,1)S(1)} %bitcast.39), channel_id=1, source_target_pairs={{0,1},{1,0},{2,3},{3,2},{4,5},{5,4},{6,7},{7,6},{8,9},{9,8},{10,11... | collective-permute-start | bytes 1920008 | tf_op jit(solution)/shard_map/ppermute | solution.py:377
  45.3 4.0 %collective-permute-start.4 = (bf16[100,3200]{1,0:T(8,128)(2,1)S(1)}, bf16[100,3200]{1,0:T(8,128)(2,1)S(1)}, u32[]{:S(2)}, u32[]{:S(2)}) collective-permute-start(bf16[100,3200]{1,0:T(8,128)(2,1)S(1)} %bitcast.37), channel_id=1, source_target_pairs={{0,1},{1,0},{2,3},{3,2},{4,5},{5,4},{6,7},{7,6},{8,9},{9,8},{10,11... | collective-permute-start | bytes 1920008 | tf_op jit(solution)/shard_map/ppermute | solution.py:377
  49.3 29.1 %copy-start.6 = (bf16[100,3200]{1,0:T(8,128)(2,1)}, bf16[100,3200]{1,0:T(8,128)(2,1)S(1)}, u32[]{:S(2)}) copy-start(bf16[100,3200]{1,0:T(8,128)(2,1)S(1)} %collective-permute-done.4.first_other) | copy-start | bytes 1920004
  78.4 10.5 %collective-permute-start.10 = (bf16[576,2048]{1,0:T(8,128)(2,1)}, bf16[576,2048]{1,0:T(8,128)(2,1)S(1)}, u32[]{:S(2)}, u32[]{:S(2)}) collective-permute-start(bf16[576,2048]{1,0:T(8,128)(2,1)} %collective-permute-done.2.across), channel_id=1, source_target_pairs={{0,1},{1,0},{2,3},{3,2},{4,5},{5,4},{6,7},{7,6},{8,9},{9,8},{10,11... | collective-permute-start | bytes 7077896 | tf_op jit(solution)/shard_map/ppermute | solution.py:377
  92.9 8.2 %copy-start = (f32[1,3200]{1,0:T(1,128)S(1)}, f32[1,3200]{1,0:T(1,128)}, u32[]{:S(2)}) copy-start(f32[1,3200]{1,0:T(1,128)} %gain.3) | copy-start | bytes 38404
  92.9 8.2 %copy-start.1 = (f32[1,3200]{1,0:T(1,128)S(1)}, f32[1,3200]{1,0:T(1,128)}, u32[]{:S(2)}) copy-start(f32[1,3200]{1,0:T(1,128)} %weigh.1) | copy-start | bytes 38404
  92.9 43.0 %all-to-all-start.2 = ((bf16[8,40,2048]{2,1,0:T(8,128)(2,1)}), bf16[8,40,2048]{2,1,0:T(8,128)(2,1)S(1)}, u32[]{:S(2)}, u32[]{:S(2)}) async-start(bf16[8,40,2048]{2,1,0:T(8,128)(2,1)} %bitcast.32), calls=%async_computation.2 | async-start | bytes 2621440 | tf_op jit(solution)/shard_map/all_to_all | solution.py:380
  105.4 8.1 %collective-permute-start.6 = (bf16[32,3200]{1,0:T(8,128)(2,1)S(1)}, bf16[32,3200]{1,0:T(8,128)(2,1)S(1)}, u32[]{:S(2)}, u32[]{:S(2)}) collective-permute-start(bf16[32,3200]{1,0:T(8,128)(2,1)S(1)} %get-tuple-element.43), channel_id=1, source_target_pairs={{0,2},{2,0},{1,3},{3,1},{4,6},{6,4},{5,7},{7,5},{8,10},{10,8},{9,1... | collective-permute-start | bytes 614408 | tf_op jit(solution)/shard_map/ppermute | solution.py:377
  113.6 14.7 %collective-permute-start.7 = (bf16[8,3200]{1,0:T(8,128)(2,1)S(1)}, bf16[8,3200]{1,0:T(8,128)(2,1)S(1)}, u32[]{:S(2)}, u32[]{:S(2)}) collective-permute-start(bf16[8,3200]{1,0:T(8,128)(2,1)S(1)} %get-tuple-element.45), channel_id=1, source_target_pairs={{0,32},{32,64},{64,96},{96,0},{1,33},{33,65},{65,97},{97,1},{2,34}... | collective-permute-start | bytes 153608 | tf_op jit(solution)/shard_map/ppermute | solution.py:377
  117.8 10.4 %collective-permute-start.8 = (bf16[8,3200]{1,0:T(8,128)(2,1)S(1)}, bf16[8,3200]{1,0:T(8,128)(2,1)S(1)}, u32[]{:S(2)}, u32[]{:S(2)}) collective-permute-start(bf16[8,3200]{1,0:T(8,128)(2,1)S(1)} %get-tuple-element.46), channel_id=1, source_target_pairs={{0,64},{32,96},{64,0},{96,32},{1,65},{33,97},{65,1},{97,33},{2,66}... | collective-permute-start | bytes 153608 | tf_op jit(solution)/shard_map/ppermute | solution.py:377
  123.0 7.1 %collective-permute-start.9 = (bf16[8,3200]{1,0:T(8,128)(2,1)S(1)}, bf16[8,3200]{1,0:T(8,128)(2,1)S(1)}, u32[]{:S(2)}, u32[]{:S(2)}) collective-permute-start(bf16[8,3200]{1,0:T(8,128)(2,1)S(1)} %get-tuple-element.47), channel_id=1, source_target_pairs={{0,96},{32,0},{64,32},{96,64},{1,97},{33,1},{65,33},{97,65},{2,98}... | collective-permute-start | bytes 153608 | tf_op jit(solution)/shard_map/ppermute | solution.py:377
  137.2 14.7 %collective-permute-start.11 = (bf16[128,1024]{1,0:T(8,128)(2,1)S(1)}, bf16[128,1024]{1,0:T(8,128)(2,1)S(1)}, u32[]{:S(2)}, u32[]{:S(2)}) collective-permute-start(bf16[128,1024]{1,0:T(8,128)(2,1)S(1)} %get-tuple-element.56), channel_id=1, source_target_pairs={{0,226},{1,195},{2,160},{3,129},{32,130},{33,163},{34,192},{35,225... | collective-permute-start | bytes 786440 | tf_op jit(solution)/shard_map/ppermute | solution.py:422
  144.5 15.9 %collective-permute-start.12 = (bf16[128,1024]{1,0:T(8,128)(2,1)S(1)}, bf16[128,1024]{1,0:T(8,128)(2,1)S(1)}, u32[]{:S(2)}, u32[]{:S(2)}) collective-permute-start(bf16[128,1024]{1,0:T(8,128)(2,1)S(1)} %get-tuple-element.57), channel_id=1, source_target_pairs={{0,224},{1,193},{2,162},{3,131},{32,128},{33,161},{34,194},{35,227... | collective-permute-start | bytes 786440 | tf_op jit(solution)/shard_map/ppermute | solution.py:422
  148.5 12.0 %all-to-all-start.3 = ((f32[8,1,3200]{2,1,0:T(1,128)}), f32[8,1,3200]{2,1,0:T(1,128)S(1)}, u32[]{:S(2)}, u32[]{:S(2)}) async-start(f32[8,1,3200]{2,1,0:T(1,128)} %shard_map.136), calls=%async_computation.3 | async-start | bytes 204800 | tf_op jit(solution)/shard_map/all_to_all | solution.py:380
  160.5 3.8 %collective-permute-start.13 = (bf16[128,1024]{1,0:T(8,128)(2,1)S(1)}, bf16[128,1024]{1,0:T(8,128)(2,1)S(1)}, u32[]{:S(2)}, u32[]{:S(2)}) collective-permute-start(bf16[128,1024]{1,0:T(8,128)(2,1)S(1)} %shard_map.140.left), channel_id=1, source_target_pairs={{0,1},{1,0},{2,3},{3,2},{4,5},{5,4},{6,7},{7,6},{8,9},{9,8},{10,11... | collective-permute-start | bytes 786440 | tf_op jit(solution)/shard_map/ppermute | solution.py:377
  164.3 9.4 %collective-permute-start.14 = (bf16[128,1024]{1,0:T(8,128)(2,1)S(1)}, bf16[128,1024]{1,0:T(8,128)(2,1)S(1)}, u32[]{:S(2)}, u32[]{:S(2)}) collective-permute-start(bf16[128,1024]{1,0:T(8,128)(2,1)S(1)} %shard_map.141.own), channel_id=1, source_target_pairs={{0,2},{2,0},{1,3},{3,1},{4,6},{6,4},{5,7},{7,5},{8,10},{10,8},{9,1... | collective-permute-start | bytes 786440 | tf_op jit(solution)/shard_map/ppermute | solution.py:377
  167.0 4.7 %collective-permute-start.15 = (bf16[1,1,3200]{2,1,0:T(2,128)(2,1)S(1)}, bf16[1,1,3200]{2,1,0:T(2,128)(2,1)S(1)}, u32[]{:S(2)}, u32[]{:S(2)}) collective-permute-start(bf16[1,1,3200]{2,1,0:T(2,128)(2,1)S(1)} %bitcast.30), channel_id=1, source_target_pairs={{0,384},{128,0},{256,128},{384,256},{1,385},{129,1},{257,129},{385... | collective-permute-start | bytes 19208 | tf_op jit(solution)/shard_map/ppermute | solution.py:377

commit v12 on v11

--- a/solution.py
+++ b/solution.py
@@ -12,6 +12,7 @@
 F32 = jnp.float32
 VM = pl.BlockSpec(memory_space=pltpu.VMEM)
 SM = pl.BlockSpec(memory_space=pltpu.SMEM)
+ANYWHERE = pl.BlockSpec(memory_space=pl.ANY)
 CAP = 40
 ROWS = 56
 
@@ -53,7 +54,7 @@
     return lax.dot_general(a, b, (((1,), (1,)), ((), ())), preferred_element_type=F32)
 
 
-def table(group, slots, first, meta):
+def table(group, first, meta):
     toks = meta.shape[1]
     topk = meta.shape[0] // 2
     wanted = (lax.broadcasted_iota(jnp.int32, (group, toks), 0) + first).astype(F32)
@@ -67,38 +68,51 @@
         weight = jnp.where(same, meta[topk + k : topk + k + 1, :] / total, weight)
     earlier = lax.broadcasted_iota(jnp.int32, (toks, toks), 0) < lax.broadcasted_iota(jnp.int32, (toks, toks), 1)
     rank = jnp.dot(member.astype(BF16), earlier.astype(F32).astype(BF16), preferred_element_type=F32)
-    rank = jnp.where(member > 0.5, rank, -100.0)
-    slot = (lax.broadcasted_iota(jnp.int32, (group, slots, toks), 1) - (slots - CAP)).astype(F32)
+    rank = jnp.where(member > 0.5, rank, -1.0)
+    slot = lax.broadcasted_iota(jnp.int32, (group, CAP, toks), 1).astype(F32)
     return jnp.where(rank[:, None, :] == slot, 1.0, 0.0), weight
 
 
-def pack_kernel(where, meta, toks, gain, ring, rows):
-    n, width = rows.shape
-    group = n // ROWS
-    hit, _ = table(group, ROWS, where[0] * group, meta[...])
+def pack_kernel(where, meta, toks, gain, ring, rows, rows_v, sem):
+    group, _, width = rows.shape
+    hit, _ = table(group, where[0] * group, meta[...])
     wide = toks[...].astype(F32)
     scale = lax.rsqrt(jnp.mean(wide * wide, axis=-1, keepdims=True) + 1e-06)
     normed = (wide * scale * gain[...]).astype(BF16)
     images = jnp.concatenate([ring[i] for i in range(ring.shape[0])], axis=0)
     count, dv = images.shape
     spare = jnp.zeros((count, 2 * width - dv), F32)
-    empty = jnp.zeros((CAP, width), F32)
-    added = jnp.concatenate([images[:, :width], jnp.concatenate([images[:, width:], spare], axis=1), empty], axis=0)
-    made = jnp.dot(hit.reshape(n, hit.shape[2]).astype(BF16), normed, preferred_element_type=F32)
-    rows[...] = (made + jnp.concatenate([added] * group, axis=0)).astype(BF16)
+    images = jnp.concatenate([images[:, :width], jnp.concatenate([images[:, width:], spare], axis=1)], axis=0)
+    made = jnp.dot(hit.reshape(group * CAP, -1).astype(BF16), normed, preferred_element_type=F32)
+    copies = []
+    for i in range(group):
+        rows_v[i] = jnp.concatenate([images, made[i * CAP : (i + 1) * CAP]], axis=0).astype(BF16)
+        copies.append(pltpu.make_async_copy(rows_v.at[i], rows.at[i], sem.at[i]))
+        copies[-1].start()
+    for copy in copies:
+        copy.wait()
+
+
+def packed(where, meta, toks, gain, ring, group):
+    dims = (group, ROWS, toks.shape[1])
+    return pl.pallas_call(
+        pack_kernel,
+        out_shape=pltpu.HBM(dims, BF16),
+        in_specs=[SM, VM, VM, VM, VM],
+        out_specs=ANYWHERE,
+        scratch_shapes=[pltpu.VMEM(dims, BF16), pltpu.SemaphoreType.DMA((group,))],
+        compiler_params=pltpu.CompilerParams(vmem_limit_bytes=SMALL),
+    )(where, meta, toks, gain, ring)
 
 
 def weigh_kernel(where, meta, high, low):
     toks, n = high.shape
     group = n // CAP
-    hit, weight = table(group, CAP, where[0] * group, meta[...])
+    hit, weight = table(group, where[0] * group, meta[...])
     scaled = (hit * weight[:, None, :]).reshape(n, toks).T
     top = scaled.astype(BF16)
     high[...] = top
     low[...] = (scaled - top.astype(F32)).astype(BF16)
-
-
-ANYWHERE = pl.BlockSpec(memory_space=pl.ANY)
 
 
 def products(flat, gate_v, up_v):
@@ -391,8 +405,7 @@
     own, sent, meta, ring, where = lax.optimization_barrier((own, sent, meta, ring, where))
     across = shifted(own, "yl", 1)
 
-    rows = call(pack_kernel, pltpu.HBM((n_z * ROWS, width), BF16), scalars=1)(where, meta, sent, trunk_gain, ring)
-    arrived = exchanged(rows.reshape(n_z, ROWS, width), "z")
+    arrived = exchanged(packed(where, meta, sent, trunk_gain, ring, n_z), "z")
 
     first, second = fc_in[0].T, fc_out[0]
     first_other, second_other = shifted(first, "core", 1), shifted(second, "core", 1)

time: 177 us -> 177 us (level)
    pallas_call x9 -> x8, Pallas kernels: 6.21 us -> 3.61 us  [run(): pl.pallas_call(kernel, out_shape=outs, in_specs=specs, out_specs=jax.tree...]
    pallas_call x0 -> x1, Pallas kernels: none -> 2.47 us  [packed(): pl.pallas_call(pack_kernel, out_shape=pltpu.HBM(dims, BF16), in_specs=[SM...]
where the time goes in v12:
time: 177 us; the launch traced here: 176 us
  starting transfers between devices  92.8 us (52%)
  waiting for transfers between devices  55.5 us (31%)
  Pallas kernels  20.3 us (11%)
  other arithmetic  4.77 us (3%)
    ppermute x12, starting transfers between devices, shifted(): return lax.ppermute(value, axis, [(i, (i + by) % n) for i in range(n)])  47.4 us
    ppermute x12, waiting for transfers between devices, shifted(): return lax.ppermute(value, axis, [(i, (i + by) % n) for i in range(n)])  41.6 us
    all_to_all x4, starting transfers between devices, exchanged(): return lax.all_to_all(value, axis, split_axis=0, concat_axis=0, tiled=True)  23.6 us
    ppermute x2, starting transfers between devices, body(): lax.ppermute(piece, ('pp',) + square, [(s * n_square + a * n_tp + t, (s +...  11.3 us
    ppermute x2, starting transfers between devices, fetched(): return lax.ppermute(value, square, pairs)  10.5 us
    ppermute x2, waiting for transfers between devices, body(): lax.ppermute(piece, ('pp',) + square, [(s * n_square + a * n_tp + t, (s +...  8.53 us
    all_to_all x4, waiting for transfers between devices, exchanged(): return lax.all_to_all(value, axis, split_axis=0, concat_axis=0, tiled=True)  5.34 us
    pallas_call x1, Pallas kernels, experts(): pl.pallas_call(first_kernel, out_shape=(shaped((n, width)), shaped((n, be...  4.54 us
  transfers between devices with their start and end apart: 20, of which 10 were waited for; matrix products, arithmetic and copies ran while one was open for 3% of the time, Pallas kernels for 8%

profile of v12, /device:TPU:1, one launch (start us, length us, event | category | flops | bytes accessed | tf_op | source)
XLA Modules:
  0.0 175.7 jit_solution(7213322000235124380)
XLA Ops:
  0.6 4.0 %collective-permute-start = (bf16[128,2048]{1,0:T(8,128)(2,1)}, bf16[128,2048]{1,0:T(8,128)(2,1)S(1)}, u32[]{:S(2)}, u32[]{:S(2)}) collective-permute-start(bf16[128,2048]{1,0:T(8,128)(2,1)} %bitcast.40), channel_id=1, source_target_pairs={{98,0},{67,1},{32,2},{1,3},{2,32},{35,33},{64,34},{97,35},{34,64},... | collective-permute-start | bytes 1572872 | tf_op jit(solution)/shard_map/ppermute | solution.py:387
  4.7 0.7 convert_bitcast_fusion
  5.4 0.7 pad_maximum_fusion.1
  6.0 6.4 %collective-permute-start.1 = (f32[16,128]{1,0:T(8,128)S(1)}, f32[16,128]{1,0:T(8,128)S(1)}, u32[]{:S(2)}, u32[]{:S(2)}) collective-permute-start(f32[16,128]{1,0:T(8,128)S(1)} %pad_maximum_fusion.1), channel_id=1, source_target_pairs={{98,0},{67,1},{32,2},{1,3},{2,32},{35,33},{64,34},{97,35},{34,64},... | collective-permute-start | bytes 24584 | tf_op jit(solution)/shard_map/ppermute | solution.py:387
  12.5 0.0 copy-start.2
  12.5 0.7 copy-done.2
  13.2 0.7 shard_map.131
  13.9 3.4 %all-to-all-start = ((f32[8,1,3200]{2,1,0:T(1,128)}), f32[8,1,3200]{2,1,0:T(1,128)S(1)}, u32[]{:S(2)}, u32[]{:S(2)}) async-start(f32[8,1,3200]{2,1,0:T(1,128)} %shard_map.131), calls=%async_computation | async-start | bytes 204800 | tf_op jit(solution)/shard_map/all_to_all | solution.py:394
  17.2 0.0 copy-start.3
  17.2 3.3 %pad_maximum_fusion.own = bf16[576,2048]{1,0:T(8,128)(2,1)} fusion(bf16[192,2048]{1,0:T(8,128)(2,1)} %bitcast.31, bf16[192,2048]{1,0:T(8,128)(2,1)} %bitcast.32, bf16[192,2048]{1,0:T(8,128)(2,1)} %bitcast.33), kind=kLoop, calls=%fused_computation | loop fusion | flops 7077888 | bytes 4718592 | tf_op jit(solution)/shard_map/concatenate | solution.py:400
  20.6 5.4 %collective-permute-start.3 = (bf16[576,2048]{1,0:T(8,128)(2,1)}, bf16[576,2048]{1,0:T(8,128)(2,1)}, u32[]{:S(2)}, u32[]{:S(2)}) collective-permute-start(bf16[576,2048]{1,0:T(8,128)(2,1)} %pad_maximum_fusion.own), channel_id=1, source_target_pairs={{0,1},{1,0},{2,3},{3,2},{4,5},{5,4},{6,7},{7,6},{8,9},{9,8},{10,11... | collective-permute-start | bytes 7077896 | tf_op jit(solution)/shard_map/ppermute | solution.py:391
  25.9 0.1 pad_add_fusion.where
  26.0 0.0 collective-permute-done.1.meta
  26.0 0.0 all-to-all-done.ring
  26.0 0.0 collective-permute-done.toks
  26.0 3.5 %collective-permute-start.2 = (bf16[576,2048]{1,0:T(8,128)(2,1)}, bf16[576,2048]{1,0:T(8,128)(2,1)}, u32[]{:S(2)}, u32[]{:S(2)}) collective-permute-start(bf16[576,2048]{1,0:T(8,128)(2,1)} %pad_maximum_fusion.own), channel_id=1, source_target_pairs={{0,2},{2,0},{1,3},{3,1},{4,6},{6,4},{5,7},{7,5},{8,10},{10,8},{9,1... | collective-permute-start | bytes 7077896 | tf_op jit(solution)/shard_map/ppermute | solution.py:391
  29.6 0.0 copy-done.3
  29.6 2.5 %shard_map.132 = bf16[8,56,2048]{2,1,0:T(8,128)(2,1)} custom-call(s32[3]{0:T(128)S(1)} %pad_add_fusion.where, f32[16,128]{1,0:T(8,128)S(1)} %collective-permute-done.1.meta, bf16[128,2048]{1,0:T(8,128)(2,1)S(1)} %collective-permute-done.toks, f32[1,2048]{1,0:T(1,128)S(1)} %copy-done.3, f32[8,1,3200]{2,1,0:T(1,128)S(1)} %all-to-all-done.ring), custom_call_target="tpu_custom_call" | custom-call | tf_op jit(solution)/shard_map/pallas_call | solution.py:98
  32.1 0.0 copy-start.5
  32.1 0.0 copy-start.4
  32.1 8.6 %all-to-all-start.1 = ((bf16[8,56,2048]{2,1,0:T(8,128)(2,1)}), bf16[8,56,2048]{2,1,0:T(8,128)(2,1)}, u32[]{:S(2)}, u32[]{:S(2)}) async-start(bf16[8,56,2048]{2,1,0:T(8,128)(2,1)} %shard_map.132), calls=%async_computation.1 | async-start | bytes 3670016 | tf_op jit(solution)/shard_map/all_to_all | solution.py:394
  40.7 4.4 %collective-permute-start.5 = (bf16[100,3200]{1,0:T(8,128)(2,1)S(1)}, bf16[100,3200]{1,0:T(8,128)(2,1)}, u32[]{:S(2)}, u32[]{:S(2)}) collective-permute-start(bf16[100,3200]{1,0:T(8,128)(2,1)S(1)} %bitcast.37), channel_id=1, source_target_pairs={{0,1},{1,0},{2,3},{3,2},{4,5},{5,4},{6,7},{7,6},{8,9},{9,8},{10,11... | collective-permute-start | bytes 1920008 | tf_op jit(solution)/shard_map/ppermute | solution.py:391
  45.2 1.9 %collective-permute-start.4 = (bf16[100,3200]{1,0:T(8,128)(2,1)S(1)}, bf16[100,3200]{1,0:T(8,128)(2,1)S(1)}, u32[]{:S(2)}, u32[]{:S(2)}) collective-permute-start(bf16[100,3200]{1,0:T(8,128)(2,1)S(1)} %bitcast.35), channel_id=1, source_target_pairs={{0,1},{1,0},{2,3},{3,2},{4,5},{5,4},{6,7},{7,6},{8,9},{9,8},{10,11... | collective-permute-start | bytes 1920008 | tf_op jit(solution)/shard_map/ppermute | solution.py:391
  47.1 0.0 collective-permute-done.5.second_other
  47.1 0.8 shard_map.133
  48.0 1.2 collective-permute-done.4.first_other
  49.2 0.0 collective-permute-done.3.other
  49.2 29.2 %collective-permute-done.2.across = bf16[576,2048]{1,0:T(8,128)(2,1)} collective-permute-done((bf16[576,2048]{1,0:T(8,128)(2,1)}, bf16[576,2048]{1,0:T(8,128)(2,1)}, u32[]{:S(2)}, u32[]{:S(2)}) %collective-permute-start.2) | collective-permute-done | bytes 2359328 | tf_op jit(solution)/shard_map/ppermute | solution.py:391
  78.4 5.6 %collective-permute-start.10 = (bf16[576,2048]{1,0:T(8,128)(2,1)}, bf16[576,2048]{1,0:T(8,128)(2,1)S(1)}, u32[]{:S(2)}, u32[]{:S(2)}) collective-permute-start(bf16[576,2048]{1,0:T(8,128)(2,1)} %collective-permute-done.2.across), channel_id=1, source_target_pairs={{0,1},{1,0},{2,3},{3,2},{4,5},{5,4},{6,7},{7,6},{8,9},{9,8},{10,11... | collective-permute-start | bytes 7077896 | tf_op jit(solution)/shard_map/ppermute | solution.py:391
  84.0 0.3 all-to-all-done.1.arrived
  84.3 4.5 %shard_map.137 = (bf16[320,2048]{1,0:T(8,128)(2,1)S(1)}, bf16[320,512]{1,0:T(8,128)(2,1)S(1)}) custom-call(bf16[8,56,2048]{2,1,0:T(8,128)(2,1)} %all-to-all-done.1.arrived, bf16[576,2048]{1,0:T(8,128)(2,1)} %pad_maximum_fusion.own, bf16[576,2048]{1,0:T(8,128)(2,1)} %collective-permute-done.3.other, bf16[576,2048]{1,0:T(8,128)(2,1)} %collective-permute-done.2.across), custom_call_target="tpu_custom_call" | custom-call | flops 1342177280 | bytes 4194304 | tf_op jit(solution)/shard_map/pallas_call | solution.py:194
  88.8 0.0 collective-permute-done.10.both
  88.8 4.0 %shard_map.138 = bf16[320,2048]{1,0:T(8,128)(2,1)} custom-call(bf16[320,2048]{1,0:T(8,128)(2,1)S(1)} %get-tuple-element.50.rows, bf16[320,512]{1,0:T(8,128)(2,1)S(1)} %get-tuple-element.51.begun, bf16[576,2048]{1,0:T(8,128)(2,1)} %pad_maximum_fusion.own, bf16[576,2048]{1,0:T(8,128)(2,1)} %collective-permute-done.3.other, ...), custom_call_target="tpu_custom_call" | custom-call | flops 1677721600 | bytes 6291456 | tf_op jit(solution)/shard_map/pallas_call | solution.py:209
  92.8 0.0 copy-start
  92.8 0.0 copy-start.1
  92.8 8.2 %all-to-all-start.2 = ((bf16[8,40,2048]{2,1,0:T(8,128)(2,1)}), bf16[8,40,2048]{2,1,0:T(8,128)(2,1)S(1)}, u32[]{:S(2)}, u32[]{:S(2)}) async-start(bf16[8,40,2048]{2,1,0:T(8,128)(2,1)} %bitcast.30), calls=%async_computation.2 | async-start | bytes 2621440 | tf_op jit(solution)/shard_map/all_to_all | solution.py:394
  101.1 4.3 %shard_map.134 = (f32[32,3200]{1,0:T(8,128)S(1)}, bf16[32,3200]{1,0:T(8,128)(2,1)S(1)}) custom-call(s32[3]{0:T(128)S(1)} %pad_add_fusion.where, bf16[8,56,2048]{2,1,0:T(8,128)(2,1)} %all-to-all-done.1.arrived, f32[1,3200]{1,0:T(1,128)S(1)} %copy-done, f32[1,3200]{1,0:T(1,128)S(1)} %copy-done.1, bf16[100,3200]{1,0:T(8,128)(2,1)} %bitcast.34, ...), custom_call_target="tpu_custom_call" | custom-call | flops 163840000 | bytes 2560000 | tf_op jit(solution)/shard_map/pallas_call | solution.py:327
  105.4 3.4 %collective-permute-start.6 = (bf16[32,3200]{1,0:T(8,128)(2,1)S(1)}, bf16[32,3200]{1,0:T(8,128)(2,1)S(1)}, u32[]{:S(2)}, u32[]{:S(2)}) collective-permute-start(bf16[32,3200]{1,0:T(8,128)(2,1)S(1)} %get-tuple-element.43), channel_id=1, source_target_pairs={{0,2},{2,0},{1,3},{3,1},{4,6},{6,4},{5,7},{7,5},{8,10},{10,8},{9,1... | collective-permute-start | bytes 614408 | tf_op jit(solution)/shard_map/ppermute | solution.py:391
  108.8 4.7 %collective-permute-done.6.came = bf16[32,3200]{1,0:T(8,128)(2,1)S(1)} collective-permute-done((bf16[32,3200]{1,0:T(8,128)(2,1)S(1)}, bf16[32,3200]{1,0:T(8,128)(2,1)S(1)}, u32[]{:S(2)}, u32[]{:S(2)}) %collective-permute-start.6) | collective-permute-done | bytes 204832 | tf_op jit(solution)/shard_map/ppermute | solution.py:391
  113.6 4.3 %collective-permute-start.7 = (bf16[8,3200]{1,0:T(8,128)(2,1)S(1)}, bf16[8,3200]{1,0:T(8,128)(2,1)S(1)}, u32[]{:S(2)}, u32[]{:S(2)}) collective-permute-start(bf16[8,3200]{1,0:T(8,128)(2,1)S(1)} %get-tuple-element.45), channel_id=1, source_target_pairs={{0,32},{32,64},{64,96},{96,0},{1,33},{33,65},{65,97},{97,1},{2,34}... | collective-permute-start | bytes 153608 | tf_op jit(solution)/shard_map/ppermute | solution.py:391
  117.8 5.2 %collective-permute-start.8 = (bf16[8,3200]{1,0:T(8,128)(2,1)S(1)}, bf16[8,3200]{1,0:T(8,128)(2,1)S(1)}, u32[]{:S(2)}, u32[]{:S(2)}) collective-permute-start(bf16[8,3200]{1,0:T(8,128)(2,1)S(1)} %get-tuple-element.46), channel_id=1, source_target_pairs={{0,64},{32,96},{64,0},{96,32},{1,65},{33,97},{65,1},{97,33},{2,66}... | collective-permute-start | bytes 153608 | tf_op jit(solution)/shard_map/ppermute | solution.py:391
  123.0 5.2 %collective-permute-start.9 = (bf16[8,3200]{1,0:T(8,128)(2,1)S(1)}, bf16[8,3200]{1,0:T(8,128)(2,1)S(1)}, u32[]{:S(2)}, u32[]{:S(2)}) collective-permute-start(bf16[8,3200]{1,0:T(8,128)(2,1)S(1)} %get-tuple-element.47), channel_id=1, source_target_pairs={{0,96},{32,0},{64,32},{96,64},{1,97},{33,1},{65,33},{97,65},{2,98}... | collective-permute-start | bytes 153608 | tf_op jit(solution)/shard_map/ppermute | solution.py:391
  128.2 0.0 collective-permute-done.7.refs_0_
  128.3 0.0 collective-permute-done.8.refs_1_
  128.3 1.9 %collective-permute-done.9.refs_2_ = bf16[8,3200]{1,0:T(8,128)(2,1)S(1)} collective-permute-done((bf16[8,3200]{1,0:T(8,128)(2,1)S(1)}, bf16[8,3200]{1,0:T(8,128)(2,1)S(1)}, u32[]{:S(2)}, u32[]{:S(2)}) %collective-permute-start.9) | collective-permute-done | bytes 51232 | tf_op jit(solution)/shard_map/ppermute | solution.py:391
  130.2 0.7 shard_map.136
  130.9 5.0 %all-to-all-done.2 = bf16[8,40,2048]{2,1,0:T(8,128)(2,1)S(1)} async-done(((bf16[8,40,2048]{2,1,0:T(8,128)(2,1)}), bf16[8,40,2048]{2,1,0:T(8,128)(2,1)S(1)}, u32[]{:S(2)}, u32[]{:S(2)}) %all-to-all-start.2) | async-done | bytes 1310752 | tf_op jit(solution)/shard_map/all_to_all | solution.py:394
  135.9 1.3 shard_map.139
  137.2 7.3 %collective-permute-start.11 = (bf16[128,1024]{1,0:T(8,128)(2,1)S(1)}, bf16[128,1024]{1,0:T(8,128)(2,1)S(1)}, u32[]{:S(2)}, u32[]{:S(2)}) collective-permute-start(bf16[128,1024]{1,0:T(8,128)(2,1)S(1)} %get-tuple-element.56), channel_id=1, source_target_pairs={{0,226},{1,195},{2,160},{3,129},{32,130},{33,163},{34,192},{35,225... | collective-permute-start | bytes 786440 | tf_op jit(solution)/shard_map/ppermute | solution.py:435
  144.5 4.0 %collective-permute-start.12 = (bf16[128,1024]{1,0:T(8,128)(2,1)S(1)}, bf16[128,1024]{1,0:T(8,128)(2,1)S(1)}, u32[]{:S(2)}, u32[]{:S(2)}) collective-permute-start(bf16[128,1024]{1,0:T(8,128)(2,1)S(1)} %get-tuple-element.57), channel_id=1, source_target_pairs={{0,224},{1,193},{2,162},{3,131},{32,128},{33,161},{34,194},{35,227... | collective-permute-start | bytes 786440 | tf_op jit(solution)/shard_map/ppermute | solution.py:435
  148.5 3.4 %all-to-all-start.3 = ((f32[8,1,3200]{2,1,0:T(1,128)}), f32[8,1,3200]{2,1,0:T(1,128)S(1)}, u32[]{:S(2)}, u32[]{:S(2)}) async-start(f32[8,1,3200]{2,1,0:T(1,128)} %shard_map.136), calls=%async_computation.3 | async-start | bytes 204800 | tf_op jit(solution)/shard_map/all_to_all | solution.py:394
  151.9 0.0 collective-permute-done.11.left
  151.9 8.5 %collective-permute-done.12.right = bf16[128,1024]{1,0:T(8,128)(2,1)S(1)} collective-permute-done((bf16[128,1024]{1,0:T(8,128)(2,1)S(1)}, bf16[128,1024]{1,0:T(8,128)(2,1)S(1)}, u32[]{:S(2)}, u32[]{:S(2)}) %collective-permute-start.12) | collective-permute-done | bytes 262176 | tf_op jit(solution)/shard_map/ppermute | solution.py:435
  160.4 0.1 shard_map.140.left
  160.5 0.0 all-to-all-done.3.spread
  160.5 2.6 %collective-permute-start.13 = (bf16[128,1024]{1,0:T(8,128)(2,1)S(1)}, bf16[128,1024]{1,0:T(8,128)(2,1)S(1)}, u32[]{:S(2)}, u32[]{:S(2)}) collective-permute-start(bf16[128,1024]{1,0:T(8,128)(2,1)S(1)} %shard_map.140.left), channel_id=1, source_target_pairs={{0,1},{1,0},{2,3},{3,2},{4,5},{5,4},{6,7},{7,6},{8,9},{9,8},{10,11... | collective-permute-start | bytes 786440 | tf_op jit(solution)/shard_map/ppermute | solution.py:391
  163.1 1.1 collective-permute-done.13.right
  164.2 0.1 shard_map.141.own
  164.3 2.6 %collective-permute-start.14 = (bf16[128,1024]{1,0:T(8,128)(2,1)S(1)}, bf16[128,1024]{1,0:T(8,128)(2,1)S(1)}, u32[]{:S(2)}, u32[]{:S(2)}) collective-permute-start(bf16[128,1024]{1,0:T(8,128)(2,1)S(1)} %shard_map.141.own), channel_id=1, source_target_pairs={{0,2},{2,0},{1,3},{3,1},{4,6},{6,4},{5,7},{7,5},{8,10},{10,8},{9,1... | collective-permute-start | bytes 786440 | tf_op jit(solution)/shard_map/ppermute | solution.py:391
  167.0 3.4 %collective-permute-start.15 = (bf16[1,1,3200]{2,1,0:T(2,128)(2,1)S(1)}, bf16[1,1,3200]{2,1,0:T(2,128)(2,1)S(1)}, u32[]{:S(2)}, u32[]{:S(2)}) collective-permute-start(bf16[1,1,3200]{2,1,0:T(2,128)(2,1)S(1)} %bitcast.29), channel_id=1, source_target_pairs={{0,384},{128,0},{256,128},{384,256},{1,385},{129,1},{257,129},{385... | collective-permute-start | bytes 19208 | tf_op jit(solution)/shard_map/ppermute | solution.py:391
  170.3 1.4 collective-permute-done.15
  171.7 2.0 %collective-permute-done.14.across = bf16[128,1024]{1,0:T(8,128)(2,1)S(1)} collective-permute-done((bf16[128,1024]{1,0:T(8,128)(2,1)S(1)}, bf16[128,1024]{1,0:T(8,128)(2,1)S(1)}, u32[]{:S(2)}, u32[]{:S(2)}) %collective-permute-start.14) | collective-permute-done | bytes 262176 | tf_op jit(solution)/shard_map/ppermute | solution.py:391
  173.7 1.4 shard_map.142
  175.1 0.6 copy.15
  (8 shorter events, 0.1 us)
Async XLA Ops:
  0.6 25.4 %collective-permute-start = (bf16[128,2048]{1,0:T(8,128)(2,1)}, bf16[128,2048]{1,0:T(8,128)(2,1)S(1)}, u32[]{:S(2)}, u32[]{:S(2)}) collective-permute-start(bf16[128,2048]{1,0:T(8,128)(2,1)} %bitcast.40), channel_id=1, source_target_pairs={{98,0},{67,1},{32,2},{1,3},{2,32},{35,33},{64,34},{97,35},{34,64},... | collective-permute-start | bytes 1572872 | tf_op jit(solution)/shard_map/ppermute | solution.py:387
  6.0 20.0 %collective-permute-start.1 = (f32[16,128]{1,0:T(8,128)S(1)}, f32[16,128]{1,0:T(8,128)S(1)}, u32[]{:S(2)}, u32[]{:S(2)}) collective-permute-start(f32[16,128]{1,0:T(8,128)S(1)} %pad_maximum_fusion.1), channel_id=1, source_target_pairs={{98,0},{67,1},{32,2},{1,3},{2,32},{35,33},{64,34},{97,35},{34,64},... | collective-permute-start | bytes 24584 | tf_op jit(solution)/shard_map/ppermute | solution.py:387
  12.5 0.7 copy-start.2
  13.9 12.2 %all-to-all-start = ((f32[8,1,3200]{2,1,0:T(1,128)}), f32[8,1,3200]{2,1,0:T(1,128)S(1)}, u32[]{:S(2)}, u32[]{:S(2)}) async-start(f32[8,1,3200]{2,1,0:T(1,128)} %shard_map.131), calls=%async_computation | async-start | bytes 204800 | tf_op jit(solution)/shard_map/all_to_all | solution.py:394
  17.2 12.3 %copy-start.3 = (f32[1,2048]{1,0:T(1,128)S(1)}, f32[1,2048]{1,0:T(1,128)}, u32[]{:S(2)}) copy-start(f32[1,2048]{1,0:T(1,128)} %gain.2) | copy-start | bytes 24580
  20.6 28.6 %collective-permute-start.3 = (bf16[576,2048]{1,0:T(8,128)(2,1)}, bf16[576,2048]{1,0:T(8,128)(2,1)}, u32[]{:S(2)}, u32[]{:S(2)}) collective-permute-start(bf16[576,2048]{1,0:T(8,128)(2,1)} %pad_maximum_fusion.own), channel_id=1, source_target_pairs={{0,1},{1,0},{2,3},{3,2},{4,5},{5,4},{6,7},{7,6},{8,9},{9,8},{10,11... | collective-permute-start | bytes 7077896 | tf_op jit(solution)/shard_map/ppermute | solution.py:391
  26.0 52.4 %collective-permute-start.2 = (bf16[576,2048]{1,0:T(8,128)(2,1)}, bf16[576,2048]{1,0:T(8,128)(2,1)}, u32[]{:S(2)}, u32[]{:S(2)}) collective-permute-start(bf16[576,2048]{1,0:T(8,128)(2,1)} %pad_maximum_fusion.own), channel_id=1, source_target_pairs={{0,2},{2,0},{1,3},{3,1},{4,6},{6,4},{5,7},{7,5},{8,10},{10,8},{9,1... | collective-permute-start | bytes 7077896 | tf_op jit(solution)/shard_map/ppermute | solution.py:391
  32.1 8.7 %copy-start.5 = (bf16[1,100,3200]{2,1,0:T(8,128)(2,1)S(1)}, bf16[1,100,3200]{2,1,0:T(8,128)(2,1)}, u32[]{:S(2)}) copy-start(bf16[1,100,3200]{2,1,0:T(8,128)(2,1)} %param.22) | copy-start | bytes 1920004
  32.1 13.1 %copy-start.4 = (bf16[1,3200,100]{1,2,0:T(8,128)(2,1)S(1)}, bf16[1,3200,100]{1,2,0:T(8,128)(2,1)}, u32[]{:S(2)}) copy-start(bf16[1,3200,100]{1,2,0:T(8,128)(2,1)} %param.21) | copy-start | bytes 1920004
  32.1 52.2 %all-to-all-start.1 = ((bf16[8,56,2048]{2,1,0:T(8,128)(2,1)}), bf16[8,56,2048]{2,1,0:T(8,128)(2,1)}, u32[]{:S(2)}, u32[]{:S(2)}) async-start(bf16[8,56,2048]{2,1,0:T(8,128)(2,1)} %shard_map.132), calls=%async_computation.1 | async-start | bytes 3670016 | tf_op jit(solution)/shard_map/all_to_all | solution.py:394
  40.7 6.4 %collective-permute-start.5 = (bf16[100,3200]{1,0:T(8,128)(2,1)S(1)}, bf16[100,3200]{1,0:T(8,128)(2,1)}, u32[]{:S(2)}, u32[]{:S(2)}) collective-permute-start(bf16[100,3200]{1,0:T(8,128)(2,1)S(1)} %bitcast.37), channel_id=1, source_target_pairs={{0,1},{1,0},{2,3},{3,2},{4,5},{5,4},{6,7},{7,6},{8,9},{9,8},{10,11... | collective-permute-start | bytes 1920008 | tf_op jit(solution)/shard_map/ppermute | solution.py:391
  45.2 4.0 %collective-permute-start.4 = (bf16[100,3200]{1,0:T(8,128)(2,1)S(1)}, bf16[100,3200]{1,0:T(8,128)(2,1)S(1)}, u32[]{:S(2)}, u32[]{:S(2)}) collective-permute-start(bf16[100,3200]{1,0:T(8,128)(2,1)S(1)} %bitcast.35), channel_id=1, source_target_pairs={{0,1},{1,0},{2,3},{3,2},{4,5},{5,4},{6,7},{7,6},{8,9},{9,8},{10,11... | collective-permute-start | bytes 1920008 | tf_op jit(solution)/shard_map/ppermute | solution.py:391
  49.2 29.2 %copy-start.6 = (bf16[100,3200]{1,0:T(8,128)(2,1)}, bf16[100,3200]{1,0:T(8,128)(2,1)S(1)}, u32[]{:S(2)}) copy-start(bf16[100,3200]{1,0:T(8,128)(2,1)S(1)} %collective-permute-done.4.first_other) | copy-start | bytes 1920004
  78.4 10.4 %collective-permute-start.10 = (bf16[576,2048]{1,0:T(8,128)(2,1)}, bf16[576,2048]{1,0:T(8,128)(2,1)S(1)}, u32[]{:S(2)}, u32[]{:S(2)}) collective-permute-start(bf16[576,2048]{1,0:T(8,128)(2,1)} %collective-permute-done.2.across), channel_id=1, source_target_pairs={{0,1},{1,0},{2,3},{3,2},{4,5},{5,4},{6,7},{7,6},{8,9},{9,8},{10,11... | collective-permute-start | bytes 7077896 | tf_op jit(solution)/shard_map/ppermute | solution.py:391
  92.8 8.2 %copy-start = (f32[1,3200]{1,0:T(1,128)S(1)}, f32[1,3200]{1,0:T(1,128)}, u32[]{:S(2)}) copy-start(f32[1,3200]{1,0:T(1,128)} %gain.3) | copy-start | bytes 38404
  92.8 8.2 %copy-start.1 = (f32[1,3200]{1,0:T(1,128)S(1)}, f32[1,3200]{1,0:T(1,128)}, u32[]{:S(2)}) copy-start(f32[1,3200]{1,0:T(1,128)} %weigh.1) | copy-start | bytes 38404
  92.8 43.0 %all-to-all-start.2 = ((bf16[8,40,2048]{2,1,0:T(8,128)(2,1)}), bf16[8,40,2048]{2,1,0:T(8,128)(2,1)S(1)}, u32[]{:S(2)}, u32[]{:S(2)}) async-start(bf16[8,40,2048]{2,1,0:T(8,128)(2,1)} %bitcast.30), calls=%async_computation.2 | async-start | bytes 2621440 | tf_op jit(solution)/shard_map/all_to_all | solution.py:394
  105.4 8.1 %collective-permute-start.6 = (bf16[32,3200]{1,0:T(8,128)(2,1)S(1)}, bf16[32,3200]{1,0:T(8,128)(2,1)S(1)}, u32[]{:S(2)}, u32[]{:S(2)}) collective-permute-start(bf16[32,3200]{1,0:T(8,128)(2,1)S(1)} %get-tuple-element.43), channel_id=1, source_target_pairs={{0,2},{2,0},{1,3},{3,1},{4,6},{6,4},{5,7},{7,5},{8,10},{10,8},{9,1... | collective-permute-start | bytes 614408 | tf_op jit(solution)/shard_map/ppermute | solution.py:391
  113.6 14.7 %collective-permute-start.7 = (bf16[8,3200]{1,0:T(8,128)(2,1)S(1)}, bf16[8,3200]{1,0:T(8,128)(2,1)S(1)}, u32[]{:S(2)}, u32[]{:S(2)}) collective-permute-start(bf16[8,3200]{1,0:T(8,128)(2,1)S(1)} %get-tuple-element.45), channel_id=1, source_target_pairs={{0,32},{32,64},{64,96},{96,0},{1,33},{33,65},{65,97},{97,1},{2,34}... | collective-permute-start | bytes 153608 | tf_op jit(solution)/shard_map/ppermute | solution.py:391
  117.8 10.4 %collective-permute-start.8 = (bf16[8,3200]{1,0:T(8,128)(2,1)S(1)}, bf16[8,3200]{1,0:T(8,128)(2,1)S(1)}, u32[]{:S(2)}, u32[]{:S(2)}) collective-permute-start(bf16[8,3200]{1,0:T(8,128)(2,1)S(1)} %get-tuple-element.46), channel_id=1, source_target_pairs={{0,64},{32,96},{64,0},{96,32},{1,65},{33,97},{65,1},{97,33},{2,66}... | collective-permute-start | bytes 153608 | tf_op jit(solution)/shard_map/ppermute | solution.py:391
  123.0 7.1 %collective-permute-start.9 = (bf16[8,3200]{1,0:T(8,128)(2,1)S(1)}, bf16[8,3200]{1,0:T(8,128)(2,1)S(1)}, u32[]{:S(2)}, u32[]{:S(2)}) collective-permute-start(bf16[8,3200]{1,0:T(8,128)(2,1)S(1)} %get-tuple-element.47), channel_id=1, source_target_pairs={{0,96},{32,0},{64,32},{96,64},{1,97},{33,1},{65,33},{97,65},{2,98}... | collective-permute-start | bytes 153608 | tf_op jit(solution)/shard_map/ppermute | solution.py:391
  137.2 14.7 %collective-permute-start.11 = (bf16[128,1024]{1,0:T(8,128)(2,1)S(1)}, bf16[128,1024]{1,0:T(8,128)(2,1)S(1)}, u32[]{:S(2)}, u32[]{:S(2)}) collective-permute-start(bf16[128,1024]{1,0:T(8,128)(2,1)S(1)} %get-tuple-element.56), channel_id=1, source_target_pairs={{0,226},{1,195},{2,160},{3,129},{32,130},{33,163},{34,192},{35,225... | collective-permute-start | bytes 786440 | tf_op jit(solution)/shard_map/ppermute | solution.py:435
  144.5 15.9 %collective-permute-start.12 = (bf16[128,1024]{1,0:T(8,128)(2,1)S(1)}, bf16[128,1024]{1,0:T(8,128)(2,1)S(1)}, u32[]{:S(2)}, u32[]{:S(2)}) collective-permute-start(bf16[128,1024]{1,0:T(8,128)(2,1)S(1)} %get-tuple-element.57), channel_id=1, source_target_pairs={{0,224},{1,193},{2,162},{3,131},{32,128},{33,161},{34,194},{35,227... | collective-permute-start | bytes 786440 | tf_op jit(solution)/shard_map/ppermute | solution.py:435
  148.5 12.0 %all-to-all-start.3 = ((f32[8,1,3200]{2,1,0:T(1,128)}), f32[8,1,3200]{2,1,0:T(1,128)S(1)}, u32[]{:S(2)}, u32[]{:S(2)}) async-start(f32[8,1,3200]{2,1,0:T(1,128)} %shard_map.136), calls=%async_computation.3 | async-start | bytes 204800 | tf_op jit(solution)/shard_map/all_to_all | solution.py:394
  160.5 3.7 %collective-permute-start.13 = (bf16[128,1024]{1,0:T(8,128)(2,1)S(1)}, bf16[128,1024]{1,0:T(8,128)(2,1)S(1)}, u32[]{:S(2)}, u32[]{:S(2)}) collective-permute-start(bf16[128,1024]{1,0:T(8,128)(2,1)S(1)} %shard_map.140.left), channel_id=1, source_target_pairs={{0,1},{1,0},{2,3},{3,2},{4,5},{5,4},{6,7},{7,6},{8,9},{9,8},{10,11... | collective-permute-start | bytes 786440 | tf_op jit(solution)/shard_map/ppermute | solution.py:391
  164.3 9.4 %collective-permute-start.14 = (bf16[128,1024]{1,0:T(8,128)(2,1)S(1)}, bf16[128,1024]{1,0:T(8,128)(2,1)S(1)}, u32[]{:S(2)}, u32[]{:S(2)}) collective-permute-start(bf16[128,1024]{1,0:T(8,128)(2,1)S(1)} %shard_map.141.own), channel_id=1, source_target_pairs={{0,2},{2,0},{1,3},{3,1},{4,6},{6,4},{5,7},{7,5},{8,10},{10,8},{9,1... | collective-permute-start | bytes 786440 | tf_op jit(solution)/shard_map/ppermute | solution.py:391
  167.0 4.7 %collective-permute-start.15 = (bf16[1,1,3200]{2,1,0:T(2,128)(2,1)S(1)}, bf16[1,1,3200]{2,1,0:T(2,128)(2,1)S(1)}, u32[]{:S(2)}, u32[]{:S(2)}) collective-permute-start(bf16[1,1,3200]{2,1,0:T(2,128)(2,1)S(1)} %bitcast.29), channel_id=1, source_target_pairs={{0,384},{128,0},{256,128},{384,256},{1,385},{129,1},{257,129},{385... | collective-permute-start | bytes 19208 | tf_op jit(solution)/shard_map/ppermute | solution.py:391

commit v13 on v12

--- a/solution.py
+++ b/solution.py
@@ -190,7 +190,7 @@
     n = groups * CAP
     count = own.shape[0] // 3 * 4
     begun, left = count // 3 * 2, count // 3
-    own, other, across = (in_hbm(shard) for shard in (own, other, across))
+    other, across = in_hbm(other), in_hbm(across)
     rows, hidden = pl.pallas_call(
         first_kernel,
         out_shape=(shaped((n, width)), shaped((n, begun))),
@@ -396,11 +396,13 @@
     tokens = trunk_in[0]
     toks, width = tokens.shape
     sent = fetched(tokens)
-    meta = fetched(jnp.concatenate([expert_ids[0].T.astype(F32), gate_scores[0].T], axis=0))
-    own = jnp.concatenate([w_gate[0, 0].T, w_up[0, 0].T, w_down[0, 0]], axis=0)
     image = image_in[0]
     dv = image.shape[1]
-    ring = exchanged(call(spread_kernel, shaped((n_yh * 2, 1, dv), F32))(image), ("yh", "yl"))
+    ring = call(spread_kernel, shaped((n_yh * 2, 1, dv), F32))(image)
+    ids, ring = lax.optimization_barrier((expert_ids, ring))
+    ring = exchanged(ring, ("yh", "yl"))
+    meta = fetched(jnp.concatenate([ids[0].T.astype(F32), gate_scores[0].T], axis=0))
+    own = jnp.concatenate([w_gate[0, 0].T, w_up[0, 0].T, w_down[0, 0]], axis=0)
     other = shifted(own, "core", 1)
     own, sent, meta, ring, where = lax.optimization_barrier((own, sent, meta, ring, where))
     across = shifted(own, "yl", 1)

time: 177 us -> 179 us (1.011)
  waiting for transfers between devices: 55.5 us -> 61.6 us
  starting transfers between devices: 92.8 us -> 90.7 us
    all_to_all x4, starting transfers between devices: 23.6 us -> 30.5 us  [exchanged(): return lax.all_to_all(value, axis, split_axis=0, concat_axis=0, tiled=True)]
    ppermute x12, starting transfers between devices: 47.4 us -> 41 us  [shifted(): return lax.ppermute(value, axis, [(i, (i + by) % n) for i in range(n)])]
    ppermute x2, waiting for transfers between devices: 0.01 us -> 2.87 us  [fetched(): return lax.ppermute(value, square, pairs)]
    all_to_all x4, waiting for transfers between devices: 5.34 us -> 7.45 us  [exchanged(): return lax.all_to_all(value, axis, split_axis=0, concat_axis=0, tiled=True)]
  transfers between devices with their start and end apart: 20 -> 20, of which waited for: 10 -> 12; matrix products, arithmetic and copies ran while one was open for 3% -> 2% of each run, Pallas kernels for 8% -> 7%
where the time goes in v13:
time: 179 us; the launch traced here: 178 us
  starting transfers between devices  90.7 us (51%)
  waiting for transfers between devices  61.6 us (34%)
  Pallas kernels  20.3 us (11%)
  other arithmetic  3.22 us (2%)
    ppermute x12, waiting for transfers between devices, shifted(): return lax.ppermute(value, axis, [(i, (i + by) % n) for i in range(n)])  42.4 us
    ppermute x12, starting transfers between devices, shifted(): return lax.ppermute(value, axis, [(i, (i + by) % n) for i in range(n)])  41 us
    all_to_all x4, starting transfers between devices, exchanged(): return lax.all_to_all(value, axis, split_axis=0, concat_axis=0, tiled=True)  30.5 us
    ppermute x2, starting transfers between devices, body(): lax.ppermute(piece, ('pp',) + square, [(s * n_square + a * n_tp + t, (s +...  9.88 us
    ppermute x2, starting transfers between devices, fetched(): return lax.ppermute(value, square, pairs)  9.45 us
    ppermute x2, waiting for transfers between devices, body(): lax.ppermute(piece, ('pp',) + square, [(s * n_square + a * n_tp + t, (s +...  8.88 us
    all_to_all x4, waiting for transfers between devices, exchanged(): return lax.all_to_all(value, axis, split_axis=0, concat_axis=0, tiled=True)  7.45 us
    pallas_call x1, Pallas kernels, experts(): pl.pallas_call(second_kernel, out_shape=pltpu.HBM((n, width), BF16), in_s...  4.48 us
  transfers between devices with their start and end apart: 20, of which 12 were waited for; matrix products, arithmetic and copies ran while one was open for 2% of the time, Pallas kernels for 7%

profile of v13, /device:TPU:1, one launch (start us, length us, event | category | flops | bytes accessed | tf_op | source)
XLA Modules:
  0.0 178.2 jit_solution(3645966076477644686)
XLA Ops:
  0.6 0.0 copy-start.2
  0.6 0.7 copy-done.2
  1.3 0.7 shard_map.131
  2.0 7.7 %all-to-all-start = ((f32[8,1,3200]{2,1,0:T(1,128)}), f32[8,1,3200]{2,1,0:T(1,128)S(1)}, u32[]{:S(2)}, u32[]{:S(2)}) async-start(f32[8,1,3200]{2,1,0:T(1,128)} %shard_map.131), calls=%async_computation | async-start | bytes 204800 | tf_op jit(solution)/shard_map/all_to_all | solution.py:394
  9.6 3.4 %collective-permute-start = (bf16[128,2048]{1,0:T(8,128)(2,1)}, bf16[128,2048]{1,0:T(8,128)(2,1)S(1)}, u32[]{:S(2)}, u32[]{:S(2)}) collective-permute-start(bf16[128,2048]{1,0:T(8,128)(2,1)} %bitcast.40), channel_id=1, source_target_pairs={{98,0},{67,1},{32,2},{1,3},{2,32},{35,33},{64,34},{97,35},{34,64},... | collective-permute-start | bytes 1572872 | tf_op jit(solution)/shard_map/ppermute | solution.py:387
  13.0 0.7 convert_bitcast_fusion
  13.7 0.7 pad_maximum_fusion.1
  14.4 6.1 %collective-permute-start.1 = (f32[16,128]{1,0:T(8,128)S(1)}, f32[16,128]{1,0:T(8,128)S(1)}, u32[]{:S(2)}, u32[]{:S(2)}) collective-permute-start(f32[16,128]{1,0:T(8,128)S(1)} %pad_maximum_fusion.1), channel_id=1, source_target_pairs={{98,0},{67,1},{32,2},{1,3},{2,32},{35,33},{64,34},{97,35},{34,64},... | collective-permute-start | bytes 24584 | tf_op jit(solution)/shard_map/ppermute | solution.py:387
  20.5 0.0 copy-start.3
  20.5 1.8 pad_maximum_fusion.own
  22.3 2.1 %collective-permute-start.3 = (bf16[576,2048]{1,0:T(8,128)(2,1)S(1)}, bf16[576,2048]{1,0:T(8,128)(2,1)}, u32[]{:S(2)}, u32[]{:S(2)}) collective-permute-start(bf16[576,2048]{1,0:T(8,128)(2,1)S(1)} %pad_maximum_fusion.own), channel_id=1, source_target_pairs={{0,1},{1,0},{2,3},{3,2},{4,5},{5,4},{6,7},{7,6},{8,9},{9,8},{10,11... | collective-permute-start | bytes 7077896 | tf_op jit(solution)/shard_map/ppermute | solution.py:391
  24.4 0.1 pad_add_fusion.where
  24.5 2.9 %collective-permute-done.1.meta = f32[16,128]{1,0:T(8,128)S(1)} collective-permute-done((f32[16,128]{1,0:T(8,128)S(1)}, f32[16,128]{1,0:T(8,128)S(1)}, u32[]{:S(2)}, u32[]{:S(2)}) %collective-permute-start.1) | collective-permute-done | bytes 8224 | tf_op jit(solution)/shard_map/ppermute | solution.py:387
  27.3 0.0 all-to-all-done.ring
  27.3 0.0 collective-permute-done.toks
  27.3 3.8 %collective-permute-start.2 = (bf16[576,2048]{1,0:T(8,128)(2,1)S(1)}, bf16[576,2048]{1,0:T(8,128)(2,1)}, u32[]{:S(2)}, u32[]{:S(2)}) collective-permute-start(bf16[576,2048]{1,0:T(8,128)(2,1)S(1)} %pad_maximum_fusion.own), channel_id=1, source_target_pairs={{0,2},{2,0},{1,3},{3,1},{4,6},{6,4},{5,7},{7,5},{8,10},{10,8},{9,1... | collective-permute-start | bytes 7077896 | tf_op jit(solution)/shard_map/ppermute | solution.py:391
  31.1 0.0 copy-done.3
  31.1 2.5 %shard_map.132 = bf16[8,56,2048]{2,1,0:T(8,128)(2,1)} custom-call(s32[3]{0:T(128)S(1)} %pad_add_fusion.where, f32[16,128]{1,0:T(8,128)S(1)} %collective-permute-done.1.meta, bf16[128,2048]{1,0:T(8,128)(2,1)S(1)} %collective-permute-done.toks, f32[1,2048]{1,0:T(1,128)S(1)} %copy-done.3, f32[8,1,3200]{2,1,0:T(1,128)S(1)} %all-to-all-done.ring), custom_call_target="tpu_custom_call" | custom-call | tf_op jit(solution)/shard_map/pallas_call | solution.py:98
  33.6 9.2 %all-to-all-start.1 = ((bf16[8,56,2048]{2,1,0:T(8,128)(2,1)}), bf16[8,56,2048]{2,1,0:T(8,128)(2,1)}, u32[]{:S(2)}, u32[]{:S(2)}) async-start(bf16[8,56,2048]{2,1,0:T(8,128)(2,1)} %shard_map.132), calls=%async_computation.1 | async-start | bytes 3670016 | tf_op jit(solution)/shard_map/all_to_all | solution.py:394
  42.8 3.6 %collective-permute-start.5 = (bf16[100,3200]{1,0:T(8,128)(2,1)}, bf16[100,3200]{1,0:T(8,128)(2,1)}, u32[]{:S(2)}, u32[]{:S(2)}) collective-permute-start(bf16[100,3200]{1,0:T(8,128)(2,1)} %bitcast.36), channel_id=1, source_target_pairs={{0,1},{1,0},{2,3},{3,2},{4,5},{5,4},{6,7},{7,6},{8,9},{9,8},{10,11... | collective-permute-start | bytes 1920008 | tf_op jit(solution)/shard_map/ppermute | solution.py:391
  46.4 1.9 %collective-permute-start.4 = (bf16[100,3200]{1,0:T(8,128)(2,1)}, bf16[100,3200]{1,0:T(8,128)(2,1)S(1)}, u32[]{:S(2)}, u32[]{:S(2)}) collective-permute-start(bf16[100,3200]{1,0:T(8,128)(2,1)} %bitcast.34), channel_id=1, source_target_pairs={{0,1},{1,0},{2,3},{3,2},{4,5},{5,4},{6,7},{7,6},{8,9},{9,8},{10,11... | collective-permute-start | bytes 1920008 | tf_op jit(solution)/shard_map/ppermute | solution.py:391
  48.3 0.1 collective-permute-done.5.second_other
  48.5 0.8 shard_map.133
  49.3 1.3 collective-permute-done.4.first_other
  50.6 0.0 collective-permute-done.3.other
  50.6 29.7 %collective-permute-done.2.across = bf16[576,2048]{1,0:T(8,128)(2,1)} collective-permute-done((bf16[576,2048]{1,0:T(8,128)(2,1)S(1)}, bf16[576,2048]{1,0:T(8,128)(2,1)}, u32[]{:S(2)}, u32[]{:S(2)}) %collective-permute-start.2) | collective-permute-done | bytes 2359328 | tf_op jit(solution)/shard_map/ppermute | solution.py:391
  80.4 0.0 copy-done.4
  80.4 4.9 %collective-permute-start.10 = (bf16[576,2048]{1,0:T(8,128)(2,1)}, bf16[576,2048]{1,0:T(8,128)(2,1)}, u32[]{:S(2)}, u32[]{:S(2)}) collective-permute-start(bf16[576,2048]{1,0:T(8,128)(2,1)} %collective-permute-done.2.across), channel_id=1, source_target_pairs={{0,1},{1,0},{2,3},{3,2},{4,5},{5,4},{6,7},{7,6},{8,9},{9,8},{10,11... | collective-permute-start | bytes 7077896 | tf_op jit(solution)/shard_map/ppermute | solution.py:391
  85.3 0.7 all-to-all-done.1.arrived
  86.1 4.1 %shard_map.137 = (bf16[320,2048]{1,0:T(8,128)(2,1)S(1)}, bf16[320,512]{1,0:T(8,128)(2,1)S(1)}) custom-call(bf16[8,56,2048]{2,1,0:T(8,128)(2,1)} %all-to-all-done.1.arrived, bf16[576,2048]{1,0:T(8,128)(2,1)S(1)} %pad_maximum_fusion.own, bf16[576,2048]{1,0:T(8,128)(2,1)} %collective-permute-done.3.other, bf16[576,2048]{1,0:T(8,128)(2,1)} %collective-permute-done.2.across), custom_call_target="tpu_custom_call" | custom-call | flops 1342177280 | bytes 4194304 | tf_op jit(solution)/shard_map/pallas_call | solution.py:194
  90.1 0.0 collective-permute-done.10.both
  90.2 4.5 %shard_map.138 = bf16[320,2048]{1,0:T(8,128)(2,1)} custom-call(bf16[320,2048]{1,0:T(8,128)(2,1)S(1)} %get-tuple-element.54.rows, bf16[320,512]{1,0:T(8,128)(2,1)S(1)} %get-tuple-element.55.begun, bf16[576,2048]{1,0:T(8,128)(2,1)S(1)} %pad_maximum_fusion.own, bf16[576,2048]{1,0:T(8,128)(2,1)} %collective-permute-done.3.other, ...), custom_call_target="tpu_custom_call" | custom-call | flops 1677721600 | bytes 6291456 | tf_op jit(solution)/shard_map/pallas_call | solution.py:209
  94.7 0.0 copy-start
  94.7 0.0 copy-start.1
  94.7 10.3 %all-to-all-start.2 = ((bf16[8,40,2048]{2,1,0:T(8,128)(2,1)}), bf16[8,40,2048]{2,1,0:T(8,128)(2,1)S(1)}, u32[]{:S(2)}, u32[]{:S(2)}) async-start(bf16[8,40,2048]{2,1,0:T(8,128)(2,1)} %bitcast.30), calls=%async_computation.2 | async-start | bytes 2621440 | tf_op jit(solution)/shard_map/all_to_all | solution.py:394
  104.9 0.0 copy-done
  105.0 4.3 %shard_map.134 = (f32[32,3200]{1,0:T(8,128)S(1)}, bf16[32,3200]{1,0:T(8,128)(2,1)S(1)}) custom-call(s32[3]{0:T(128)S(1)} %pad_add_fusion.where, bf16[8,56,2048]{2,1,0:T(8,128)(2,1)} %all-to-all-done.1.arrived, f32[1,3200]{1,0:T(1,128)S(1)} %copy-done, f32[1,3200]{1,0:T(1,128)S(1)} %copy-done.1, bf16[100,3200]{1,0:T(8,128)(2,1)} %bitcast.35, ...), custom_call_target="tpu_custom_call" | custom-call | flops 163840000 | bytes 2560000 | tf_op jit(solution)/shard_map/pallas_call | solution.py:327
  109.3 1.9 %collective-permute-start.6 = (bf16[32,3200]{1,0:T(8,128)(2,1)S(1)}, bf16[32,3200]{1,0:T(8,128)(2,1)S(1)}, u32[]{:S(2)}, u32[]{:S(2)}) collective-permute-start(bf16[32,3200]{1,0:T(8,128)(2,1)S(1)} %get-tuple-element.47), channel_id=1, source_target_pairs={{0,2},{2,0},{1,3},{3,1},{4,6},{6,4},{5,7},{7,5},{8,10},{10,8},{9,1... | collective-permute-start | bytes 614408 | tf_op jit(solution)/shard_map/ppermute | solution.py:391
  111.2 5.9 %collective-permute-done.6.came = bf16[32,3200]{1,0:T(8,128)(2,1)S(1)} collective-permute-done((bf16[32,3200]{1,0:T(8,128)(2,1)S(1)}, bf16[32,3200]{1,0:T(8,128)(2,1)S(1)}, u32[]{:S(2)}, u32[]{:S(2)}) %collective-permute-start.6) | collective-permute-done | bytes 204832 | tf_op jit(solution)/shard_map/ppermute | solution.py:391
  117.2 3.5 %collective-permute-start.7 = (bf16[8,3200]{1,0:T(8,128)(2,1)S(1)}, bf16[8,3200]{1,0:T(8,128)(2,1)S(1)}, u32[]{:S(2)}, u32[]{:S(2)}) collective-permute-start(bf16[8,3200]{1,0:T(8,128)(2,1)S(1)} %get-tuple-element.49), channel_id=1, source_target_pairs={{0,32},{32,64},{64,96},{96,0},{1,33},{33,65},{65,97},{97,1},{2,34}... | collective-permute-start | bytes 153608 | tf_op jit(solution)/shard_map/ppermute | solution.py:391
  120.7 5.0 %collective-permute-start.8 = (bf16[8,3200]{1,0:T(8,128)(2,1)S(1)}, bf16[8,3200]{1,0:T(8,128)(2,1)S(1)}, u32[]{:S(2)}, u32[]{:S(2)}) collective-permute-start(bf16[8,3200]{1,0:T(8,128)(2,1)S(1)} %get-tuple-element.50), channel_id=1, source_target_pairs={{0,64},{32,96},{64,0},{96,32},{1,65},{33,97},{65,1},{97,33},{2,66}... | collective-permute-start | bytes 153608 | tf_op jit(solution)/shard_map/ppermute | solution.py:391
  125.7 5.3 %collective-permute-start.9 = (bf16[8,3200]{1,0:T(8,128)(2,1)S(1)}, bf16[8,3200]{1,0:T(8,128)(2,1)S(1)}, u32[]{:S(2)}, u32[]{:S(2)}) collective-permute-start(bf16[8,3200]{1,0:T(8,128)(2,1)S(1)} %get-tuple-element.51), channel_id=1, source_target_pairs={{0,96},{32,0},{64,32},{96,64},{1,97},{33,1},{65,33},{97,65},{2,98}... | collective-permute-start | bytes 153608 | tf_op jit(solution)/shard_map/ppermute | solution.py:391
  131.0 0.0 collective-permute-done.7.refs_0_
  131.1 0.0 collective-permute-done.8.refs_1_
  131.1 1.3 collective-permute-done.9.refs_2_
  132.3 0.7 shard_map.136
  133.0 6.7 %all-to-all-done.2 = bf16[8,40,2048]{2,1,0:T(8,128)(2,1)S(1)} async-done(((bf16[8,40,2048]{2,1,0:T(8,128)(2,1)}), bf16[8,40,2048]{2,1,0:T(8,128)(2,1)S(1)}, u32[]{:S(2)}, u32[]{:S(2)}) %all-to-all-start.2) | async-done | bytes 1310752 | tf_op jit(solution)/shard_map/all_to_all | solution.py:394
  139.7 1.3 shard_map.139
  141.0 6.2 %collective-permute-start.11 = (bf16[128,1024]{1,0:T(8,128)(2,1)S(1)}, bf16[128,1024]{1,0:T(8,128)(2,1)S(1)}, u32[]{:S(2)}, u32[]{:S(2)}) collective-permute-start(bf16[128,1024]{1,0:T(8,128)(2,1)S(1)} %get-tuple-element.60), channel_id=1, source_target_pairs={{0,226},{1,195},{2,160},{3,129},{32,130},{33,163},{34,192},{35,225... | collective-permute-start | bytes 786440 | tf_op jit(solution)/shard_map/ppermute | solution.py:437
  147.2 3.7 %collective-permute-start.12 = (bf16[128,1024]{1,0:T(8,128)(2,1)S(1)}, bf16[128,1024]{1,0:T(8,128)(2,1)S(1)}, u32[]{:S(2)}, u32[]{:S(2)}) collective-permute-start(bf16[128,1024]{1,0:T(8,128)(2,1)S(1)} %get-tuple-element.61), channel_id=1, source_target_pairs={{0,224},{1,193},{2,162},{3,131},{32,128},{33,161},{34,194},{35,227... | collective-permute-start | bytes 786440 | tf_op jit(solution)/shard_map/ppermute | solution.py:437
  150.9 3.4 %all-to-all-start.3 = ((f32[8,1,3200]{2,1,0:T(1,128)}), f32[8,1,3200]{2,1,0:T(1,128)S(1)}, u32[]{:S(2)}, u32[]{:S(2)}) async-start(f32[8,1,3200]{2,1,0:T(1,128)} %shard_map.136), calls=%async_computation.3 | async-start | bytes 204800 | tf_op jit(solution)/shard_map/all_to_all | solution.py:394
  154.3 0.0 collective-permute-done.11.left
  154.3 8.9 %collective-permute-done.12.right = bf16[128,1024]{1,0:T(8,128)(2,1)S(1)} collective-permute-done((bf16[128,1024]{1,0:T(8,128)(2,1)S(1)}, bf16[128,1024]{1,0:T(8,128)(2,1)S(1)}, u32[]{:S(2)}, u32[]{:S(2)}) %collective-permute-start.12) | collective-permute-done | bytes 262176 | tf_op jit(solution)/shard_map/ppermute | solution.py:437
  163.2 0.1 shard_map.140.left
  163.3 0.0 all-to-all-done.3.spread
  163.3 2.3 %collective-permute-start.13 = (bf16[128,1024]{1,0:T(8,128)(2,1)S(1)}, bf16[128,1024]{1,0:T(8,128)(2,1)S(1)}, u32[]{:S(2)}, u32[]{:S(2)}) collective-permute-start(bf16[128,1024]{1,0:T(8,128)(2,1)S(1)} %shard_map.140.left), channel_id=1, source_target_pairs={{0,1},{1,0},{2,3},{3,2},{4,5},{5,4},{6,7},{7,6},{8,9},{9,8},{10,11... | collective-permute-start | bytes 786440 | tf_op jit(solution)/shard_map/ppermute | solution.py:391
  165.5 1.2 collective-permute-done.13.right
  166.7 0.1 shard_map.141.own
  166.8 3.2 %collective-permute-start.14 = (bf16[128,1024]{1,0:T(8,128)(2,1)S(1)}, bf16[128,1024]{1,0:T(8,128)(2,1)S(1)}, u32[]{:S(2)}, u32[]{:S(2)}) collective-permute-start(bf16[128,1024]{1,0:T(8,128)(2,1)S(1)} %shard_map.141.own), channel_id=1, source_target_pairs={{0,2},{2,0},{1,3},{3,1},{4,6},{6,4},{5,7},{7,5},{8,10},{10,8},{9,1... | collective-permute-start | bytes 786440 | tf_op jit(solution)/shard_map/ppermute | solution.py:391
  170.0 3.4 %collective-permute-start.15 = (bf16[1,1,3200]{2,1,0:T(2,128)(2,1)S(1)}, bf16[1,1,3200]{2,1,0:T(2,128)(2,1)S(1)}, u32[]{:S(2)}, u32[]{:S(2)}) collective-permute-start(bf16[1,1,3200]{2,1,0:T(2,128)(2,1)S(1)} %bitcast.29), channel_id=1, source_target_pairs={{0,384},{128,0},{256,128},{384,256},{1,385},{129,1},{257,129},{385... | collective-permute-start | bytes 19208 | tf_op jit(solution)/shard_map/ppermute | solution.py:391
  173.4 1.4 collective-permute-done.15
  174.7 1.5 collective-permute-done.14.across
  176.2 1.4 shard_map.142
  177.6 0.6 copy.15
  (4 shorter events, 0.1 us)
Async XLA Ops:
  0.6 0.7 copy-start.2
  2.0 25.3 %all-to-all-start = ((f32[8,1,3200]{2,1,0:T(1,128)}), f32[8,1,3200]{2,1,0:T(1,128)S(1)}, u32[]{:S(2)}, u32[]{:S(2)}) async-start(f32[8,1,3200]{2,1,0:T(1,128)} %shard_map.131), calls=%async_computation | async-start | bytes 204800 | tf_op jit(solution)/shard_map/all_to_all | solution.py:394
  9.6 17.7 %collective-permute-start = (bf16[128,2048]{1,0:T(8,128)(2,1)}, bf16[128,2048]{1,0:T(8,128)(2,1)S(1)}, u32[]{:S(2)}, u32[]{:S(2)}) collective-permute-start(bf16[128,2048]{1,0:T(8,128)(2,1)} %bitcast.40), channel_id=1, source_target_pairs={{98,0},{67,1},{32,2},{1,3},{2,32},{35,33},{64,34},{97,35},{34,64},... | collective-permute-start | bytes 1572872 | tf_op jit(solution)/shard_map/ppermute | solution.py:387
  14.4 12.9 %collective-permute-start.1 = (f32[16,128]{1,0:T(8,128)S(1)}, f32[16,128]{1,0:T(8,128)S(1)}, u32[]{:S(2)}, u32[]{:S(2)}) collective-permute-start(f32[16,128]{1,0:T(8,128)S(1)} %pad_maximum_fusion.1), channel_id=1, source_target_pairs={{98,0},{67,1},{32,2},{1,3},{2,32},{35,33},{64,34},{97,35},{34,64},... | collective-permute-start | bytes 24584 | tf_op jit(solution)/shard_map/ppermute | solution.py:387
  20.5 10.6 %copy-start.3 = (f32[1,2048]{1,0:T(1,128)S(1)}, f32[1,2048]{1,0:T(1,128)}, u32[]{:S(2)}) copy-start(f32[1,2048]{1,0:T(1,128)} %gain.2) | copy-start | bytes 24580
  22.3 28.4 %collective-permute-start.3 = (bf16[576,2048]{1,0:T(8,128)(2,1)S(1)}, bf16[576,2048]{1,0:T(8,128)(2,1)}, u32[]{:S(2)}, u32[]{:S(2)}) collective-permute-start(bf16[576,2048]{1,0:T(8,128)(2,1)S(1)} %pad_maximum_fusion.own), channel_id=1, source_target_pairs={{0,1},{1,0},{2,3},{3,2},{4,5},{5,4},{6,7},{7,6},{8,9},{9,8},{10,11... | collective-permute-start | bytes 7077896 | tf_op jit(solution)/shard_map/ppermute | solution.py:391
  27.3 53.0 %collective-permute-start.2 = (bf16[576,2048]{1,0:T(8,128)(2,1)S(1)}, bf16[576,2048]{1,0:T(8,128)(2,1)}, u32[]{:S(2)}, u32[]{:S(2)}) collective-permute-start(bf16[576,2048]{1,0:T(8,128)(2,1)S(1)} %pad_maximum_fusion.own), channel_id=1, source_target_pairs={{0,2},{2,0},{1,3},{3,1},{4,6},{6,4},{5,7},{7,5},{8,10},{10,8},{9,1... | collective-permute-start | bytes 7077896 | tf_op jit(solution)/shard_map/ppermute | solution.py:391
  33.6 52.5 %all-to-all-start.1 = ((bf16[8,56,2048]{2,1,0:T(8,128)(2,1)}), bf16[8,56,2048]{2,1,0:T(8,128)(2,1)}, u32[]{:S(2)}, u32[]{:S(2)}) async-start(bf16[8,56,2048]{2,1,0:T(8,128)(2,1)} %shard_map.132), calls=%async_computation.1 | async-start | bytes 3670016 | tf_op jit(solution)/shard_map/all_to_all | solution.py:394
  42.8 5.7 %collective-permute-start.5 = (bf16[100,3200]{1,0:T(8,128)(2,1)}, bf16[100,3200]{1,0:T(8,128)(2,1)}, u32[]{:S(2)}, u32[]{:S(2)}) collective-permute-start(bf16[100,3200]{1,0:T(8,128)(2,1)} %bitcast.36), channel_id=1, source_target_pairs={{0,1},{1,0},{2,3},{3,2},{4,5},{5,4},{6,7},{7,6},{8,9},{9,8},{10,11... | collective-permute-start | bytes 1920008 | tf_op jit(solution)/shard_map/ppermute | solution.py:391
  46.4 4.2 %collective-permute-start.4 = (bf16[100,3200]{1,0:T(8,128)(2,1)}, bf16[100,3200]{1,0:T(8,128)(2,1)S(1)}, u32[]{:S(2)}, u32[]{:S(2)}) collective-permute-start(bf16[100,3200]{1,0:T(8,128)(2,1)} %bitcast.34), channel_id=1, source_target_pairs={{0,1},{1,0},{2,3},{3,2},{4,5},{5,4},{6,7},{7,6},{8,9},{9,8},{10,11... | collective-permute-start | bytes 1920008 | tf_op jit(solution)/shard_map/ppermute | solution.py:391
  50.6 29.8 %copy-start.4 = (bf16[100,3200]{1,0:T(8,128)(2,1)}, bf16[100,3200]{1,0:T(8,128)(2,1)S(1)}, u32[]{:S(2)}) copy-start(bf16[100,3200]{1,0:T(8,128)(2,1)S(1)} %collective-permute-done.4.first_other) | copy-start | bytes 1920004
  80.4 9.8 %collective-permute-start.10 = (bf16[576,2048]{1,0:T(8,128)(2,1)}, bf16[576,2048]{1,0:T(8,128)(2,1)}, u32[]{:S(2)}, u32[]{:S(2)}) collective-permute-start(bf16[576,2048]{1,0:T(8,128)(2,1)} %collective-permute-done.2.across), channel_id=1, source_target_pairs={{0,1},{1,0},{2,3},{3,2},{4,5},{5,4},{6,7},{7,6},{8,9},{9,8},{10,11... | collective-permute-start | bytes 7077896 | tf_op jit(solution)/shard_map/ppermute | solution.py:391
  94.7 10.3 %copy-start = (f32[1,3200]{1,0:T(1,128)S(1)}, f32[1,3200]{1,0:T(1,128)}, u32[]{:S(2)}) copy-start(f32[1,3200]{1,0:T(1,128)} %gain.3) | copy-start | bytes 38404
  94.7 10.3 %copy-start.1 = (f32[1,3200]{1,0:T(1,128)S(1)}, f32[1,3200]{1,0:T(1,128)}, u32[]{:S(2)}) copy-start(f32[1,3200]{1,0:T(1,128)} %weigh.1) | copy-start | bytes 38404
  94.7 45.1 %all-to-all-start.2 = ((bf16[8,40,2048]{2,1,0:T(8,128)(2,1)}), bf16[8,40,2048]{2,1,0:T(8,128)(2,1)S(1)}, u32[]{:S(2)}, u32[]{:S(2)}) async-start(bf16[8,40,2048]{2,1,0:T(8,128)(2,1)} %bitcast.30), calls=%async_computation.2 | async-start | bytes 2621440 | tf_op jit(solution)/shard_map/all_to_all | solution.py:394
  109.3 7.9 %collective-permute-start.6 = (bf16[32,3200]{1,0:T(8,128)(2,1)S(1)}, bf16[32,3200]{1,0:T(8,128)(2,1)S(1)}, u32[]{:S(2)}, u32[]{:S(2)}) collective-permute-start(bf16[32,3200]{1,0:T(8,128)(2,1)S(1)} %get-tuple-element.47), channel_id=1, source_target_pairs={{0,2},{2,0},{1,3},{3,1},{4,6},{6,4},{5,7},{7,5},{8,10},{10,8},{9,1... | collective-permute-start | bytes 614408 | tf_op jit(solution)/shard_map/ppermute | solution.py:391
  117.2 13.9 %collective-permute-start.7 = (bf16[8,3200]{1,0:T(8,128)(2,1)S(1)}, bf16[8,3200]{1,0:T(8,128)(2,1)S(1)}, u32[]{:S(2)}, u32[]{:S(2)}) collective-permute-start(bf16[8,3200]{1,0:T(8,128)(2,1)S(1)} %get-tuple-element.49), channel_id=1, source_target_pairs={{0,32},{32,64},{64,96},{96,0},{1,33},{33,65},{65,97},{97,1},{2,34}... | collective-permute-start | bytes 153608 | tf_op jit(solution)/shard_map/ppermute | solution.py:391
  120.7 10.4 %collective-permute-start.8 = (bf16[8,3200]{1,0:T(8,128)(2,1)S(1)}, bf16[8,3200]{1,0:T(8,128)(2,1)S(1)}, u32[]{:S(2)}, u32[]{:S(2)}) collective-permute-start(bf16[8,3200]{1,0:T(8,128)(2,1)S(1)} %get-tuple-element.50), channel_id=1, source_target_pairs={{0,64},{32,96},{64,0},{96,32},{1,65},{33,97},{65,1},{97,33},{2,66}... | collective-permute-start | bytes 153608 | tf_op jit(solution)/shard_map/ppermute | solution.py:391
  125.7 6.6 %collective-permute-start.9 = (bf16[8,3200]{1,0:T(8,128)(2,1)S(1)}, bf16[8,3200]{1,0:T(8,128)(2,1)S(1)}, u32[]{:S(2)}, u32[]{:S(2)}) collective-permute-start(bf16[8,3200]{1,0:T(8,128)(2,1)S(1)} %get-tuple-element.51), channel_id=1, source_target_pairs={{0,96},{32,0},{64,32},{96,64},{1,97},{33,1},{65,33},{97,65},{2,98}... | collective-permute-start | bytes 153608 | tf_op jit(solution)/shard_map/ppermute | solution.py:391
  141.0 13.3 %collective-permute-start.11 = (bf16[128,1024]{1,0:T(8,128)(2,1)S(1)}, bf16[128,1024]{1,0:T(8,128)(2,1)S(1)}, u32[]{:S(2)}, u32[]{:S(2)}) collective-permute-start(bf16[128,1024]{1,0:T(8,128)(2,1)S(1)} %get-tuple-element.60), channel_id=1, source_target_pairs={{0,226},{1,195},{2,160},{3,129},{32,130},{33,163},{34,192},{35,225... | collective-permute-start | bytes 786440 | tf_op jit(solution)/shard_map/ppermute | solution.py:437
  147.2 15.9 %collective-permute-start.12 = (bf16[128,1024]{1,0:T(8,128)(2,1)S(1)}, bf16[128,1024]{1,0:T(8,128)(2,1)S(1)}, u32[]{:S(2)}, u32[]{:S(2)}) collective-permute-start(bf16[128,1024]{1,0:T(8,128)(2,1)S(1)} %get-tuple-element.61), channel_id=1, source_target_pairs={{0,224},{1,193},{2,162},{3,131},{32,128},{33,161},{34,194},{35,227... | collective-permute-start | bytes 786440 | tf_op jit(solution)/shard_map/ppermute | solution.py:437
  150.9 12.3 %all-to-all-start.3 = ((f32[8,1,3200]{2,1,0:T(1,128)}), f32[8,1,3200]{2,1,0:T(1,128)S(1)}, u32[]{:S(2)}, u32[]{:S(2)}) async-start(f32[8,1,3200]{2,1,0:T(1,128)} %shard_map.136), calls=%async_computation.3 | async-start | bytes 204800 | tf_op jit(solution)/shard_map/all_to_all | solution.py:394
  163.3 3.4 %collective-permute-start.13 = (bf16[128,1024]{1,0:T(8,128)(2,1)S(1)}, bf16[128,1024]{1,0:T(8,128)(2,1)S(1)}, u32[]{:S(2)}, u32[]{:S(2)}) collective-permute-start(bf16[128,1024]{1,0:T(8,128)(2,1)S(1)} %shard_map.140.left), channel_id=1, source_target_pairs={{0,1},{1,0},{2,3},{3,2},{4,5},{5,4},{6,7},{7,6},{8,9},{9,8},{10,11... | collective-permute-start | bytes 786440 | tf_op jit(solution)/shard_map/ppermute | solution.py:391
  166.8 9.4 %collective-permute-start.14 = (bf16[128,1024]{1,0:T(8,128)(2,1)S(1)}, bf16[128,1024]{1,0:T(8,128)(2,1)S(1)}, u32[]{:S(2)}, u32[]{:S(2)}) collective-permute-start(bf16[128,1024]{1,0:T(8,128)(2,1)S(1)} %shard_map.141.own), channel_id=1, source_target_pairs={{0,2},{2,0},{1,3},{3,1},{4,6},{6,4},{5,7},{7,5},{8,10},{10,8},{9,1... | collective-permute-start | bytes 786440 | tf_op jit(solution)/shard_map/ppermute | solution.py:391
  170.0 4.7 %collective-permute-start.15 = (bf16[1,1,3200]{2,1,0:T(2,128)(2,1)S(1)}, bf16[1,1,3200]{2,1,0:T(2,128)(2,1)S(1)}, u32[]{:S(2)}, u32[]{:S(2)}) collective-permute-start(bf16[1,1,3200]{2,1,0:T(2,128)(2,1)S(1)} %bitcast.29), channel_id=1, source_target_pairs={{0,384},{128,0},{256,128},{384,256},{1,385},{129,1},{257,129},{385... | collective-permute-start | bytes 19208 | tf_op jit(solution)/shard_map/ppermute | solution.py:391
